TPU v7x, 32 devices: a whole 2x2x4 slice. The times are simulated.
32 devices in a mesh: seq: 4 (over y, core), head: 8 (over z, x).
Axes of the slice: x: 2, y: 2, z: 4, core: 2. Of those that a mesh axis runs over, the one named last changes fastest.
Arguments:
- tokens: bfloat16 [8192, 1024], P(('seq', 'head')), may hold values from -6 to 6
- leading_layer_value: bfloat16 [8192, 1024], P(('seq', 'head')), may hold values from -6 to 6
- output_gradient: bfloat16 [8192, 1024], P(('seq', 'head')), may hold values from -6 to 6
- lengths: int32 [4, 4], P('seq'), may hold values from 1 to 1024, 2048 in all within a row
- sequence_block_of: int32 [4, 16], P('seq'), may hold values from 0 to 15, as said below
- stored_block_of: int32 [4, 16], P('seq'), may hold values from 0 to 15, as said below
- channel_settings: bfloat16 [1024, 19], P(('seq', 'head')), may hold values from -6 to 2, as said below
- receptance_matrix: bfloat16 [1024, 1024], P(('seq', 'head')), may hold values from -0.1875 to 0.1875
- key_matrix: bfloat16 [1024, 1024], P(('seq', 'head')), may hold values from -0.1875 to 0.1875
- value_matrix: bfloat16 [1024, 1024], P(('seq', 'head')), may hold values from -0.1875 to 0.1875
- output_matrix: bfloat16 [1024, 1024], P(('seq', 'head')), may hold values from -0.1875 to 0.1875
- branch_down_weight: bfloat16 [1024, 288], P(('seq', 'head')), may hold values from -0.1875 to 0.1875
- branch_up_weight: bfloat16 [1024, 288], P(('seq', 'head')), may hold values from -0.75 to 0.75
- channel_key_weight: bfloat16 [1024, 4096], P(('seq', 'head')), may hold values from -0.1875 to 0.1875
- channel_value_weight: bfloat16 [1024, 4096], P(('seq', 'head')), may hold values from -0.09375 to 0.09375
Outputs:
- layer_out: bfloat16 [8192, 1024], P(('seq', 'head'))
- tokens_grad: float32 [8192, 1024], P(('seq', 'head'))
- first_value_grad: float32 [8192, 1024], P(('seq', 'head'))
- channel_grad: float32 [1024, 19], P(('seq', 'head'))
- recept_grad: float32 [1024, 1024], P('head', 'seq')
- key_grad: float32 [1024, 1024], P('head', 'seq')
- value_grad: float32 [1024, 1024], P('head', 'seq')
- output_grad: float32 [1024, 1024], P('head', 'seq')
- lora_down_grad: float32 [1024, 288], P('head', 'seq')
- lora_up_grad: float32 [1024, 288], P('head', 'seq')
- ffn_key_grad: float32 [1024, 4096], P('head', 'seq')
- ffn_value_grad: float32 [1024, 4096], P('head', 'seq')
Inputs may be any that keep to these rules, and one draw needn't show every extreme that they name: Row s lists the lengths of group s's 4 sequences in order; they sum to 2048 and the longest is exactly 1024. `sequence_block_of`: each row is a permutation of 0 to 15. stored_block_of[s, sequence_block_of[s, j]] = j for every s and j. `channel_settings`: Columns: 0, 1 first norm's gain and bias; 2 to 7 token-shift mixes of receptance, decay, key, value, rate, gate; 8 decay base; 9 rate base; 10 value-residual base; 11 key scale; 12 key rate; 13 bonus scale; 14, 15 group norm's gain and bias; 16, 17 second norm's gain and bias; 18 channel-mix token-shift mix.
All inputs are finite; a program needn't handle non-finite values.
Results may differ from a plain program's by a relative error of at most 0.013.
The roundings to bfloat16 on the way count: a program that leaves them out, or rounds other values in their place, can miss the bound.
Values may be sent and summed in bfloat16 or wider, within the bound.
No kernel may reach another device: no remote copies, remote signals or barrier semaphores. Data moves between devices by JAX's collectives and lax.ppermute only.
A program may use at most 320 MiB of HBM per device.

v0:
```python
import jax
import jax.numpy as jnp
from jax import lax
from jax.sharding import PartitionSpec as P

ATTENTION_SPAN = 64
DECAY_RANK = 64
DA = 64
DV = 32
BLOCK = 128
SPAN = 32


HIGHEST = lax.Precision.HIGHEST


def rounded(array):
    return array.astype(jnp.bfloat16)


def matrix_product(left, right):
    return jnp.dot(left, right, preferred_element_type=jnp.float32)


def transposed_product(left, right):
    return lax.dot_general(
        left, right, (((1,), (1,)), ((), ())), preferred_element_type=jnp.float32
    )


def product_tn(left, right):
    return lax.dot_general(
        left, right, (((0,), (0,)), ((), ())), preferred_element_type=jnp.float32
    )


def linear_back(inputs, weight_matrix, grad):
    grad_low = rounded(grad)
    return (transposed_product(grad_low, weight_matrix), product_tn(inputs, grad_low))


def linear_t_back(inputs, weight_matrix, grad):
    grad_low = rounded(grad)
    return (matrix_product(grad_low, weight_matrix), product_tn(grad_low, inputs))


def layer_norm(inputs, gain, bias):
    center = inputs - jnp.mean(inputs, -1, keepdims=True)
    spread = jnp.mean(center * center, -1, keepdims=True)
    return center * lax.rsqrt(spread + 1e-05) * gain + bias


def start_flags(positions, begins):
    return jnp.any(positions[:, None] == begins[None, :], -1).astype(jnp.float32)


def shift_rows(rows_in, edge, keep):
    grid = rows_in.reshape(edge.shape[0], -1, rows_in.shape[1])
    moved = jnp.concatenate([edge[:, None, :], grid[:, :-1, :]], 1)
    return moved.reshape(rows_in.shape) * keep[:, None]


def add_last(rows_in, size):
    element_tally, width = rows_in.shape
    padding = jnp.zeros((element_tally, size - 1, width), jnp.float32)
    return jnp.concatenate([padding, rows_in[:, None, :]], 1).reshape(element_tally * size, width)


def mix_inputs(rows_in, edge, column_list, keep):
    standardized_entries = layer_norm(rows_in, column_list[:, 0], column_list[:, 1])
    edge_normed = layer_norm(edge, column_list[:, 0], column_list[:, 1])
    shift_diff = shift_rows(standardized_entries, edge_normed, keep) - standardized_entries
    return tuple((standardized_entries + shift_diff * column_list[:, slot] for slot in range(2, 8)))


def ffn_mix(rows_in, edge, column_list, keep):
    standardized_entries = layer_norm(rows_in, column_list[:, 16], column_list[:, 17])
    edge_normed = layer_norm(edge, column_list[:, 16], column_list[:, 17])
    return (
        standardized_entries
        + (shift_rows(standardized_entries, edge_normed, keep) - standardized_entries)
        * column_list[:, 18]
    )


def head_inputs(
    recept_pre, key_pre, value_pre, decay_raised, rate_raised, value_raised, first_vals, column_list
):
    log_decay = -jnp.exp(-jax.nn.softplus(-(column_list[:, 8] + decay_raised)) - 0.5)
    learn_rate = jax.nn.sigmoid(column_list[:, 9] + rate_raised)
    element_tally = key_pre.shape[0]
    scaled = (key_pre * column_list[:, 11]).reshape(element_tally, -1, ATTENTION_SPAN)
    key_norm = (scaled * lax.rsqrt(jnp.sum(scaled * scaled, -1, keepdims=True) + 1e-06)).reshape(
        key_pre.shape
    )
    main_lookup_vector = key_pre * (1.0 + (learn_rate - 1.0) * column_list[:, 12])
    payload_entries = value_pre + (first_vals - value_pre) * jax.nn.sigmoid(
        column_list[:, 10] + value_raised
    )
    return (recept_pre, log_decay, main_lookup_vector, key_norm, learn_rate, payload_entries)


def attention_answer(
    prefix_recurrence_answer,
    acceptance_entries,
    main_lookup_vector,
    payload_entries,
    extra_multiplier,
    cluster_multiplier,
    cluster_offset_term,
):
    element_tally = prefix_recurrence_answer.shape[0]
    per_head = prefix_recurrence_answer.reshape(element_tally, -1, ATTENTION_SPAN)
    center = per_head - jnp.mean(per_head, -1, keepdims=True)
    spread = jnp.mean(center * center, -1, keepdims=True)
    standardized_entries = (center * lax.rsqrt(spread + 0.00064)).reshape(
        prefix_recurrence_answer.shape
    ) * cluster_multiplier + cluster_offset_term
    extra_shift_term = jnp.sum(
        (acceptance_entries * main_lookup_vector * extra_multiplier).reshape(
            element_tally, -1, ATTENTION_SPAN
        ),
        -1,
        keepdims=True,
    )
    return standardized_entries + (
        extra_shift_term * payload_entries.reshape(element_tally, -1, ATTENTION_SPAN)
    ).reshape(prefix_recurrence_answer.shape)


def to_order(array, table):
    blocks = array.reshape(table.shape[0], -1, array.shape[-1])
    return jnp.take(blocks, table, axis=0).reshape(array.shape)


def pairs(left, right, mask):
    return jnp.where(mask, jnp.einsum("nhtk,nhsk->nhts", left, right, precision=HIGHEST), 0.0)


def span_scan(
    acceptance_entries, log_decay, main_lookup_vector, key_norm, learn_rate, payload_entries, starts
):
    total, width = acceptance_entries.shape
    element_tally = total // SPAN

    def blocked(array):
        return array.reshape(
            element_tally, SPAN, width // ATTENTION_SPAN, ATTENTION_SPAN
        ).transpose(0, 2, 1, 3)

    recept_b, decay_b, key_b, norm_b, rate_b, value_b = [
        blocked(array)
        for array in (
            acceptance_entries,
            log_decay,
            main_lookup_vector,
            key_norm,
            learn_rate,
            payload_entries,
        )
    ]
    alpha = -norm_b
    beta = norm_b * rate_b
    segment = jnp.cumsum(starts.reshape(element_tally, SPAN), axis=1)
    same = segment[:, :, None] == segment[:, None, :]
    index = jnp.arange(SPAN)
    strict = (same & (index[:, None] > index[None, :]))[:, None]
    upto = (same & (index[:, None] >= index[None, :]))[:, None]
    carried = (segment == 0.0).astype(jnp.float32)[:, None, :, None]
    final = (segment == segment[:, -1:]).astype(jnp.float32)[:, None, :, None]
    running = jnp.cumsum(decay_b, axis=2)
    decay_in = jnp.exp(running)
    a_hat = alpha * jnp.exp(running - decay_b)
    b_hat = beta / decay_in
    k_hat = key_b / decay_in
    r_hat = recept_b * decay_in
    decay_end = decay_in[:, :, -1:, :]
    l_ab = pairs(a_hat, b_hat, strict)
    l_ak = pairs(a_hat, k_hat, strict)
    system = jnp.eye(SPAN, dtype=jnp.float32) - l_ab
    ends_b = b_hat * decay_end * final
    ends_k = k_hat * decay_end * final
    solved = lax.linalg.triangular_solve(
        system, ends_b, left_side=True, lower=True, transpose_a=True, unit_diagonal=True
    )
    eye_key = jnp.eye(ATTENTION_SPAN, dtype=jnp.float32)
    through = eye_key * (decay_end * carried[:, :, -1:, :])[:, :, 0, :, None]
    through = through + jnp.einsum("nhtk,nhtj->nhkj", a_hat * carried, solved, precision=HIGHEST)
    mapped = jnp.einsum("nhts,nhtk->nhsk", l_ak, solved, precision=HIGHEST) + ends_k
    offset = jnp.einsum("nhsv,nhsk->nhvk", value_b, mapped, precision=HIGHEST)

    def combine(early, late):
        return (
            jnp.einsum("nhkj,nhji->nhki", early[0], late[0], precision=HIGHEST),
            jnp.einsum("nhvj,nhji->nhvi", early[1], late[0], precision=HIGHEST) + late[1],
        )

    _, reached = lax.associative_scan(combine, (through, offset), axis=0)
    begin = jnp.concatenate([jnp.zeros_like(reached[:1]), reached[:-1]], 0)
    right_side = carried * jnp.einsum("nhtk,nhvk->nhtv", a_hat, begin, precision=HIGHEST)
    right_side = right_side + jnp.einsum("nhts,nhsv->nhtv", l_ak, value_b, precision=HIGHEST)
    update = lax.linalg.triangular_solve(
        system, right_side, left_side=True, lower=True, unit_diagonal=True
    )
    l_rb = pairs(r_hat, b_hat, upto)
    l_rk = pairs(r_hat, k_hat, upto)
    result = carried * jnp.einsum("nhtk,nhvk->nhtv", r_hat, begin, precision=HIGHEST)
    result = result + jnp.einsum("nhts,nhsv->nhtv", l_rb, update, precision=HIGHEST)
    result = result + jnp.einsum("nhts,nhsv->nhtv", l_rk, value_b, precision=HIGHEST)
    return result.transpose(0, 2, 1, 3).reshape(total, width)


def head_mix(parts, head_cols, starts, home, order):
    acceptance_entries, log_decay, main_lookup_vector, key_norm, learn_rate, payload_entries = [
        to_order(array, home) for array in parts
    ]
    prefix_recurrence_answer = span_scan(
        acceptance_entries,
        log_decay,
        main_lookup_vector,
        key_norm,
        learn_rate,
        payload_entries,
        starts,
    )
    joined = attention_answer(
        prefix_recurrence_answer,
        acceptance_entries,
        main_lookup_vector,
        payload_entries,
        head_cols[:, 0],
        head_cols[:, 1],
        head_cols[:, 2],
    )
    return to_order(joined, order)


def body(
    tokens,
    leading_layer_value,
    output_gradient,
    lengths,
    sequence_block_of,
    stored_block_of,
    channel_settings,
    receptance_matrix,
    key_matrix,
    value_matrix,
    output_matrix,
    branch_down_weight,
    branch_up_weight,
    channel_key_weight,
    channel_value_weight,
):
    full = (
        lax.all_gather(channel_settings, ("seq", "head"), axis=0, tiled=True),
        lax.all_gather(receptance_matrix, ("seq", "head"), axis=0, tiled=True),
        lax.all_gather(key_matrix, ("seq", "head"), axis=0, tiled=True),
        lax.all_gather(value_matrix, ("seq", "head"), axis=0, tiled=True),
        lax.all_gather(output_matrix, ("seq", "head"), axis=0, tiled=True),
        lax.all_gather(branch_down_weight, ("seq", "head"), axis=0, tiled=True),
        lax.all_gather(branch_up_weight, ("seq", "head"), axis=0, tiled=True),
        lax.all_gather(channel_key_weight, ("seq", "head"), axis=0, tiled=True),
        lax.all_gather(channel_value_weight, ("seq", "head"), axis=0, tiled=True),
    )
    (
        columns_low,
        receptance_weight,
        key_weight_local,
        value_weight_local,
        output_weight_local,
        down_full,
        up_full,
        channel_key,
        channel_value,
    ) = full
    column_list = columns_low.astype(jnp.float32)
    rows_here, width = tokens.shape
    blocks_here = rows_here // BLOCK
    head_index = lax.axis_index("head")
    order = sequence_block_of[0]
    home = stored_block_of[0]
    group_blocks = order.shape[0]
    begins = jnp.cumsum(lengths[0]) - lengths[0]
    local_seq = lax.dynamic_slice_in_dim(order, head_index * blocks_here, blocks_here)
    positions = local_seq[:, None] * BLOCK + jnp.arange(BLOCK, dtype=jnp.int32)[None, :]
    keep = 1.0 - start_flags(positions.reshape(rows_here), begins)
    before_block = jnp.take(home, jnp.maximum(local_seq - 1, 0))
    after_seq = local_seq + 1
    after_block = jnp.take(home, jnp.minimum(after_seq, group_blocks - 1))
    after_live = (after_seq < group_blocks).astype(jnp.float32)[:, None]
    sliced_decay = DECAY_RANK
    sliced_rate = DECAY_RANK + DA
    sliced_value = DECAY_RANK + DA + DV
    tokens_f = tokens.astype(jnp.float32)
    last_tokens = tokens.reshape(blocks_here, BLOCK, width)[:, -1, :]
    group_last = lax.all_gather(last_tokens, "head", axis=0, tiled=True)
    edge_tokens = jnp.take(group_last, before_block, axis=0).astype(jnp.float32)

    def mix_fn(rows_in, edge, cols):
        return mix_inputs(rows_in, edge, cols, keep)

    mixed, mix_pull = jax.vjp(mix_fn, tokens_f, edge_tokens, column_list)
    in_recept, decay_input, in_key, value_input, rate_input, gate_input = [
        rounded(array) for array in mixed
    ]
    decay_tanh = jnp.tanh(matrix_product(decay_input, down_full[:, :sliced_decay]))
    decay_between = rounded(decay_tanh)
    rate_between = rounded(matrix_product(rate_input, down_full[:, sliced_decay:sliced_rate]))
    value_between = rounded(matrix_product(value_input, down_full[:, sliced_rate:sliced_value]))
    gate_sig = jax.nn.sigmoid(matrix_product(gate_input, down_full[:, sliced_value:]))
    gate_between = rounded(gate_sig)
    gate_result = transposed_product(gate_between, up_full[:, sliced_value:])
    recept_pre = matrix_product(in_recept, receptance_weight)
    key_pre = matrix_product(in_key, key_weight_local)
    value_pre = matrix_product(value_input, value_weight_local)
    decay_raised = transposed_product(decay_between, up_full[:, :sliced_decay])
    rate_raised = transposed_product(rate_between, up_full[:, sliced_decay:sliced_rate])
    value_raised = transposed_product(value_between, up_full[:, sliced_rate:sliced_value])
    first_f = leading_layer_value.astype(jnp.float32)
    scan_in, heads_pull = jax.vjp(
        head_inputs,
        recept_pre,
        key_pre,
        value_pre,
        decay_raised,
        rate_raised,
        value_raised,
        first_f,
        column_list,
    )
    sent = jnp.stack([rounded(array) for array in scan_in], 0)
    grouped = lax.all_to_all(sent, "head", split_axis=2, concat_axis=1, tiled=True)
    local_width = grouped.shape[2]
    head_cols = lax.dynamic_slice(
        column_list, (head_index * local_width, jnp.int32(13)), (local_width, 3)
    )
    group_starts = start_flags(jnp.arange(grouped.shape[1], dtype=jnp.int32), begins)
    group_parts = tuple((grouped[slot].astype(jnp.float32) for slot in range(6)))

    def scan_fn(parts, cols):
        return head_mix(parts, cols, group_starts, home, order)

    joined_heads, scan_pull = jax.vjp(scan_fn, group_parts, head_cols)
    joined = lax.all_to_all(rounded(joined_heads), "head", split_axis=0, concat_axis=1, tiled=True)
    joined_f = joined.astype(jnp.float32)
    out_in = rounded(joined_f * gate_result)
    middle = tokens_f + matrix_product(out_in, output_weight_local)
    last_middle = middle.reshape(blocks_here, BLOCK, width)[:, -1, :]
    group_middle = lax.all_gather(last_middle, "head", axis=0, tiled=True)
    edge_middle = jnp.take(group_middle, before_block, axis=0)

    def ffn_fn(rows_in, edge, cols):
        return ffn_mix(rows_in, edge, cols, keep)

    ffn_mixed, ffn_pull = jax.vjp(ffn_fn, middle, edge_middle, column_list)
    ffn_in = rounded(ffn_mixed)
    active = jax.nn.relu(matrix_product(ffn_in, channel_key))
    hidden = rounded(active * active)
    layer_out = rounded(middle + transposed_product(hidden, channel_value))
    cotangent = output_gradient.astype(jnp.float32)
    grad_hidden, grad_ffn_value = linear_t_back(hidden, channel_value, cotangent)
    grad_ffn_in, grad_ffn_key = linear_back(ffn_in, channel_key, grad_hidden * 2.0 * active)
    grad_mid_part, grad_edge_mid, grad_cols_ffn = ffn_pull(grad_ffn_in)
    group_edge_mid = lax.all_gather(grad_edge_mid, "head", axis=0, tiled=True)
    grad_middle = (
        cotangent
        + grad_mid_part
        + add_last(jnp.take(group_edge_mid, after_block, axis=0) * after_live, BLOCK)
    )
    grad_out_in, grad_output = linear_back(out_in, output_weight_local, grad_middle)
    grad_joined = rounded(grad_out_in * gate_result)
    grad_gate = grad_out_in * joined_f
    grad_heads = lax.all_to_all(
        grad_joined, "head", split_axis=1, concat_axis=0, tiled=True
    ).astype(jnp.float32)
    grad_parts, grad_head_cols = scan_pull(grad_heads)
    grad_sent = jnp.stack([rounded(array) for array in grad_parts], 0)
    grad_scan_in = lax.all_to_all(grad_sent, "head", split_axis=1, concat_axis=2, tiled=True)
    pre_grads = heads_pull(tuple((grad_scan_in[slot].astype(jnp.float32) for slot in range(6))))
    (
        grad_recept_pre,
        grad_key_pre,
        grad_value_pre,
        grad_decay_up,
        grad_rate_up,
        grad_value_up,
        first_value_grad,
        grad_cols_heads,
    ) = pre_grads
    grad_in_recept, grad_recept = linear_back(in_recept, receptance_weight, grad_recept_pre)
    grad_in_key, grad_key = linear_back(in_key, key_weight_local, grad_key_pre)
    grad_in_value, grad_value = linear_back(value_input, value_weight_local, grad_value_pre)
    grad_decay_mid, up_decay = linear_t_back(
        decay_between, up_full[:, :sliced_decay], grad_decay_up
    )
    grad_in_decay, down_decay = linear_back(
        decay_input, down_full[:, :sliced_decay], grad_decay_mid * (1.0 - decay_tanh * decay_tanh)
    )
    grad_rate_mid, up_rate = linear_t_back(
        rate_between, up_full[:, sliced_decay:sliced_rate], grad_rate_up
    )
    grad_in_rate, down_rate = linear_back(
        rate_input, down_full[:, sliced_decay:sliced_rate], grad_rate_mid
    )
    grad_value_mid, up_value = linear_t_back(
        value_between, up_full[:, sliced_rate:sliced_value], grad_value_up
    )
    grad_in_mixv, down_value = linear_back(
        value_input, down_full[:, sliced_rate:sliced_value], grad_value_mid
    )
    grad_gate_mid, up_gate = linear_t_back(gate_between, up_full[:, sliced_value:], grad_gate)
    grad_in_gate, down_gate = linear_back(
        gate_input, down_full[:, sliced_value:], grad_gate_mid * gate_sig * (1.0 - gate_sig)
    )
    grad_tokens_part, grad_edge_tokens, grad_cols_mix = mix_pull(
        (
            grad_in_recept,
            grad_in_decay,
            grad_in_key,
            grad_in_value + grad_in_mixv,
            grad_in_rate,
            grad_in_gate,
        )
    )
    group_edge_tokens = lax.all_gather(grad_edge_tokens, "head", axis=0, tiled=True)
    tokens_grad = (
        grad_middle
        + grad_tokens_part
        + add_last(jnp.take(group_edge_tokens, after_block, axis=0) * after_live, BLOCK)
    )
    grad_cols_scan = lax.dynamic_update_slice(
        jnp.zeros_like(column_list), grad_head_cols, (head_index * local_width, jnp.int32(13))
    )
    grad_columns = grad_cols_mix + grad_cols_heads + grad_cols_ffn + grad_cols_scan
    grad_down = jnp.concatenate([down_decay, down_rate, down_value, down_gate], 1)
    grad_up = jnp.concatenate([up_decay, up_rate, up_value, up_gate], 1)
    seq_count = lax.axis_size("seq")
    head_count = lax.axis_size("head")
    total_rows = grad_columns.shape[0]
    regrouped = (
        grad_columns.reshape(seq_count, head_count, total_rows // (seq_count * head_count), -1)
        .transpose(1, 0, 2, 3)
        .reshape(total_rows, -1)
    )
    (
        sum_cols,
        sum_recept,
        sum_key,
        sum_value,
        sum_output,
        sum_down,
        sum_up,
        sum_ffn_key,
        sum_ffn_value,
    ) = (
        lax.psum_scatter(regrouped, "head", scatter_dimension=0, tiled=True),
        lax.psum_scatter(grad_recept, "head", scatter_dimension=0, tiled=True),
        lax.psum_scatter(grad_key, "head", scatter_dimension=0, tiled=True),
        lax.psum_scatter(grad_value, "head", scatter_dimension=0, tiled=True),
        lax.psum_scatter(grad_output, "head", scatter_dimension=0, tiled=True),
        lax.psum_scatter(grad_down, "head", scatter_dimension=0, tiled=True),
        lax.psum_scatter(grad_up, "head", scatter_dimension=0, tiled=True),
        lax.psum_scatter(grad_ffn_key, "head", scatter_dimension=0, tiled=True),
        lax.psum_scatter(grad_ffn_value, "head", scatter_dimension=0, tiled=True),
    )
    shards = (
        lax.psum_scatter(sum_cols, "seq", scatter_dimension=0, tiled=True),
        lax.psum_scatter(sum_recept, "seq", scatter_dimension=1, tiled=True),
        lax.psum_scatter(sum_key, "seq", scatter_dimension=1, tiled=True),
        lax.psum_scatter(sum_value, "seq", scatter_dimension=1, tiled=True),
        lax.psum_scatter(sum_output, "seq", scatter_dimension=1, tiled=True),
        lax.psum_scatter(sum_down, "seq", scatter_dimension=1, tiled=True),
        lax.psum_scatter(sum_up, "seq", scatter_dimension=1, tiled=True),
        lax.psum_scatter(sum_ffn_key, "seq", scatter_dimension=1, tiled=True),
        lax.psum_scatter(sum_ffn_value, "seq", scatter_dimension=1, tiled=True),
    )
    return (layer_out, tokens_grad, first_value_grad) + tuple(shards)


def solution(mesh):
    placed = (
        P(("seq", "head"), None),
        P(("seq", "head"), None),
        P(("seq", "head"), None),
        P("seq", None),
        P("seq", None),
        P("seq", None),
        P(("seq", "head"), None),
        P(("seq", "head"), None),
        P(("seq", "head"), None),
        P(("seq", "head"), None),
        P(("seq", "head"), None),
        P(("seq", "head"), None),
        P(("seq", "head"), None),
        P(("seq", "head"), None),
        P(("seq", "head"), None),
    )
    return jax.shard_map(
        body,
        mesh=mesh,
        in_specs=placed,
        out_specs=(
            P(("seq", "head"), None),
            P(("seq", "head"), None),
            P(("seq", "head"), None),
            P(("seq", "head"), None),
            P("head", "seq"),
            P("head", "seq"),
            P("head", "seq"),
            P("head", "seq"),
            P("head", "seq"),
            P("head", "seq"),
            P("head", "seq"),
            P("head", "seq"),
        ),
        check_vma=False,
    )
```

profile of v0, /device:TPU:4, one launch (start us, length us, event | category | flops | bytes accessed | tf_op | source)
XLA Modules:
  0.0 3310.2 jit_solution(496850832894413017)
XLA Ops:
  10.6 69.1 %all-gather.2 = bf16[32,32,19]{1,2,0:T(8,128)(2,1)S(1)} all-gather(bf16[1,32,19]{1,2,0:T(8,128)(2,1)} %bitcast.774), channel_id=1, replica_groups=mesh['seq'=4,'head'=8] {'seq','head'}, dimensions={0}, use_global_device_ids=true | all-gather | bytes 40128 | tf_op jit(solution)/shard_map/all_gather | solution.py:256
  81.5 30.6 all-gather
  117.7 69.6 %all_gather.42 = bf16[1024,288]{1,0:T(8,128)(2,1)S(1)} all-gather(bf16[32,288]{1,0:T(8,128)(2,1)S(1)} %copy-done.307), channel_id=1, replica_groups=mesh['seq'=4,'head'=8] {'seq','head'}, dimensions={0}, use_global_device_ids=true | all-gather | bytes 608256 | tf_op jit(solution)/shard_map/all_gather | solution.py:261
  190.9 70.6 %all_gather.43 = bf16[1024,288]{1,0:T(8,128)(2,1)S(1)} all-gather(bf16[32,288]{1,0:T(8,128)(2,1)S(1)} %copy-done.308), channel_id=1, replica_groups=mesh['seq'=4,'head'=8] {'seq','head'}, dimensions={0}, use_global_device_ids=true | all-gather | bytes 608256 | tf_op jit(solution)/shard_map/all_gather | solution.py:262
  306.7 112.2 %all-to-all-done = bf16[6,256,1024]{1,0,2:T(8,128)(2,1)} async-done(((bf16[6,256,1024]{1,0,2:T(8,128)(2,1)}), bf16[6,256,1024]{1,0,2:T(8,128)(2,1)}, u32[]{:S(2)}, u32[]{:S(2)}) %all-to-all-start) | async-done | bytes 3145760 | tf_op jit(solution)/shard_map/all_to_all | solution.py:333
  469.7 9.1 copy_exponential_fusion
  515.6 26.6 custom-call.14
  581.0 9.0 fusion.109
  590.0 8.2 multiply_add_fusion
  635.6 9.2 pad.307
  654.2 11.3 pad.309
  668.0 11.2 pad.308
  681.7 21.7 pad.543
  708.1 21.7 pad.431
  801.4 9.8 all-to-all-done.1
  818.1 31.0 all-gather.1
  882.4 32.5 all-gather.3
  1051.0 9.3 pad.345
  1060.3 9.2 pad.346
  1083.6 16.6 pad.347
  1100.3 16.6 pad.348
  1116.9 15.9 pad.319
  1142.5 32.1 pad.366
  1174.7 32.2 pad.367
  1206.9 31.4 pad.365
  1321.0 9.2 pad.358
  1338.1 16.6 pad.361
  1354.7 15.8 pad.349
  1370.5 11.6 pad.360
  1382.2 8.5 fusion.77
  1450.1 32.1 pad.363
  1482.2 31.0 pad.313
  1513.2 32.5 pad.362
  1596.5 8.2 fusion.361
  1652.1 13.3 fusion.31
  1701.1 8.9 copy.926
  1714.8 9.1 copy.927
  1725.8 9.3 copy.928
  1740.0 8.9 copy.929
  1756.0 9.0 copy.930
  1765.0 8.7 add_bitcast_fusion
  1787.0 8.9 copy.931
  1796.0 19.6 stack.37
  1822.0 78.0 %all-to-all-done.3 = bf16[6,2048,128]{2,0,1:T(8,128)(2,1)} async-done(((bf16[6,2048,128]{2,0,1:T(8,128)(2,1)}), bf16[6,2048,128]{2,0,1:T(8,128)(2,1)}, u32[]{:S(2)}, u32[]{:S(2)}) %all-to-all-start.3) | async-done | bytes 3145760 | tf_op jit(solution)/shard_map/all_to_all | solution.py:379
  1941.5 10.3 convolution_bitcast_fusion
  1974.3 9.8 fusion.382
  1984.2 14.1 reduce-scatter.25.cloned.1.call-done
  1999.8 284.0 %reduce-scatter.51.cloned.1.call-done = f32[128,4096]{0,1:T(8,128)} async-done(((f32[1024,4096]{0,1:T(8,128)}), f32[128,4096]{0,1:T(8,128)}) %reduce-scatter.51.cloned.1.call-update) | async-done | bytes 2097168 | tf_op jit(solution)/shard_map/reduce_scatter | solution.py:465
  2283.9 67.5 %reduce-scatter.43.cloned.1.call-done = f32[128,288]{0,1:T(8,128)} async-done(((f32[1024,288]{0,1:T(8,128)}), f32[128,288]{0,1:T(8,128)}) %reduce-scatter.43.cloned.1.call-update) | async-done | bytes 147472 | tf_op jit(solution)/shard_map/reduce_scatter | solution.py:462
  2351.5 67.3 %reduce-scatter.45.cloned.1.call-done = f32[128,288]{0,1:T(8,128)} async-done(((f32[1024,288]{0,1:T(8,128)}), f32[128,288]{0,1:T(8,128)}) %reduce-scatter.45.cloned.1.call-update) | async-done | bytes 147472 | tf_op jit(solution)/shard_map/reduce_scatter | solution.py:463
  2418.9 91.0 %reduce-scatter.39.cloned.1.call-done = f32[128,1024]{1,0:T(8,128)} async-done(((f32[1024,1024]{1,0:T(8,128)}), f32[128,1024]{1,0:T(8,128)}) %reduce-scatter.39.cloned.1.call-update) | async-done | bytes 524304 | tf_op jit(solution)/shard_map/reduce_scatter | solution.py:461
  2510.0 91.1 %reduce-scatter.27.cloned.1.call-done = f32[128,1024]{1,0:T(8,128)} async-done(((f32[1024,1024]{1,0:T(8,128)}), f32[128,1024]{1,0:T(8,128)}) %reduce-scatter.27.cloned.1.call-update) | async-done | bytes 524304 | tf_op jit(solution)/shard_map/reduce_scatter | solution.py:458
  2601.2 91.7 %reduce-scatter.31.cloned.1.call-done = f32[128,1024]{1,0:T(8,128)} async-done(((f32[1024,1024]{1,0:T(8,128)}), f32[128,1024]{1,0:T(8,128)}) %reduce-scatter.31.cloned.1.call-update) | async-done | bytes 524304 | tf_op jit(solution)/shard_map/reduce_scatter | solution.py:459
  2692.9 91.1 %reduce-scatter.35.cloned.1.call-done = f32[128,1024]{1,0:T(8,128)} async-done(((f32[1024,1024]{1,0:T(8,128)}), f32[128,1024]{1,0:T(8,128)}) %reduce-scatter.35.cloned.1.call-update) | async-done | bytes 524304 | tf_op jit(solution)/shard_map/reduce_scatter | solution.py:460
  2784.1 286.0 %reduce-scatter.47.cloned.1.call-done = f32[128,4096]{1,0:T(8,128)} async-done(((f32[1024,4096]{1,0:T(8,128)}), f32[128,4096]{1,0:T(8,128)}) %reduce-scatter.47.cloned.1.call-update) | async-done | bytes 2097168 | tf_op jit(solution)/shard_map/reduce_scatter | solution.py:464
  3078.4 30.5 all-gather.4
  3112.7 11.6 reduce-scatter.53.cloned.1.call-done
  3126.4 20.4 reduce-scatter.57.cloned.1.call-done
  3146.7 22.7 reduce-scatter.59.cloned.1.call-done
  3169.4 24.8 reduce-scatter.41.cloned.1.call-done
  3194.1 24.9 reduce-scatter.29.cloned.1.call-done
  3219.1 24.7 reduce-scatter.33.cloned.1.call-done
  3243.8 24.9 reduce-scatter.37.cloned.1.call-done
  3268.7 34.4 %reduce-scatter.49.cloned.1.call-done = f32[128,1024]{1,0:T(8,128)} async-done(((f32[128,4096]{1,0:T(8,128)}), f32[128,1024]{1,0:T(8,128)}) %reduce-scatter.49.cloned.1.call-update) | async-done | bytes 524304 | tf_op jit(solution)/shard_map/reduce_scatter | solution.py:475
  (1266 shorter events, 911.8 us)
Async XLA Ops:
  7.2 109.5 %copy-start.359 = (s32[1,4]{1,0:T(1,128)S(1)}, s32[1,4]{1,0:T(1,128)}, u32[]{:S(2)}) copy-start(s32[1,4]{1,0:T(1,128)} %param.28) | copy-start | bytes 52
  7.2 109.6 %copy-start.47 = (bf16[256,1024]{1,0:T(8,128)(2,1)S(1)}, bf16[256,1024]{1,0:T(8,128)(2,1)}, u32[]{:S(2)}) copy-start(bf16[256,1024]{1,0:T(8,128)(2,1)} %param.25) | copy-start | bytes 1572868
  7.2 106.9 %copy-start.2 = (s32[1,16]{1,0:T(1,128)S(1)}, s32[1,16]{1,0:T(1,128)}, u32[]{:S(2)}) copy-start(s32[1,16]{1,0:T(1,128)} %param.30) | copy-start | bytes 196
  7.2 256.4 %all-gather.12.cloned.1.call-start = ((), (), s32[]{:S(2)}) async-start(), calls=%async_computation.22 | async-start | bytes 2162688 | tf_op jit(solution)/shard_map/all_gather | solution.py:257
  7.9 261.3 %all-gather.14.cloned.1.call-start = ((), (), s32[]{:S(2)}) async-start(), calls=%async_computation.23 | async-start | bytes 2162688 | tf_op jit(solution)/shard_map/all_gather | solution.py:258
  8.7 275.7 %all-gather.16.cloned.1.call-start = ((), (), s32[]{:S(2)}) async-start(), calls=%async_computation.24 | async-start | bytes 2162688 | tf_op jit(solution)/shard_map/all_gather | solution.py:259
  9.4 804.4 %all-gather.18.cloned.1.call-start = ((), (), s32[]{:S(2)}) async-start(), calls=%async_computation.25 | async-start | bytes 2162688 | tf_op jit(solution)/shard_map/all_gather | solution.py:260
  10.0 849.9 %all-gather.20.cloned.1.call-start = ((), (), s32[]{:S(2)}) async-start(), calls=%async_computation.26 | async-start | bytes 8650752 | tf_op jit(solution)/shard_map/all_gather | solution.py:263
  116.4 71.0 %copy-start.275 = (f32[1024,1]{0,1:T(1,128)}, f32[1024,1]{0,1:T(1,128)S(1)}, u32[]{:S(2)}) copy-start(f32[1024,1]{0,1:T(1,128)S(1)} %get-tuple-element.261) | copy-start | bytes 12292
  116.4 71.7 %copy-start.251 = (f32[1024,1]{0,1:T(1,128)}, f32[1024,1]{0,1:T(1,128)S(1)}, u32[]{:S(2)}) copy-start(f32[1024,1]{0,1:T(1,128)S(1)} %get-tuple-element.271) | copy-start | bytes 12292
  116.4 71.8 %copy-start.273 = (f32[1024,1]{0,1:T(1,128)}, f32[1024,1]{0,1:T(1,128)S(1)}, u32[]{:S(2)}) copy-start(f32[1024,1]{0,1:T(1,128)S(1)} %get-tuple-element.259) | copy-start | bytes 12292
  116.4 71.8 %copy-start.277 = (f32[1024,1]{0,1:T(1,128)}, f32[1024,1]{0,1:T(1,128)S(1)}, u32[]{:S(2)}) copy-start(f32[1024,1]{0,1:T(1,128)S(1)} %get-tuple-element.264) | copy-start | bytes 12292
  116.4 71.8 %copy-start.279 = (f32[1024,1]{0,1:T(1,128)}, f32[1024,1]{0,1:T(1,128)S(1)}, u32[]{:S(2)}) copy-start(f32[1024,1]{0,1:T(1,128)S(1)} %get-tuple-element.266) | copy-start | bytes 12292
  116.4 71.8 %copy-start.281 = (f32[1024,1]{0,1:T(1,128)}, f32[1024,1]{0,1:T(1,128)S(1)}, u32[]{:S(2)}) copy-start(f32[1024,1]{0,1:T(1,128)S(1)} %get-tuple-element.267) | copy-start | bytes 12292
  116.4 71.8 %copy-start.283 = (f32[1024,1]{0,1:T(1,128)}, f32[1024,1]{0,1:T(1,128)S(1)}, u32[]{:S(2)}) copy-start(f32[1024,1]{0,1:T(1,128)S(1)} %get-tuple-element.269) | copy-start | bytes 12292
  116.4 152.8 %copy-start.270 = (f32[1024,1]{0,1:T(1,128)}, f32[1024,1]{0,1:T(1,128)S(1)}, u32[]{:S(2)}) copy-start(f32[1024,1]{0,1:T(1,128)S(1)} %get-tuple-element.263) | copy-start | bytes 12292
  116.4 164.7 %copy-start.268 = (f32[1024,1]{0,1:T(1,128)}, f32[1024,1]{0,1:T(1,128)S(1)}, u32[]{:S(2)}) copy-start(f32[1024,1]{0,1:T(1,128)S(1)} %get-tuple-element.262) | copy-start | bytes 12292
  116.9 71.3 %copy-start.285 = (f32[256]{0:T(256)}, f32[256]{0:T(256)S(1)}, u32[]{:S(2)}) copy-start(f32[256]{0:T(256)S(1)} %broadcast_multiply_fusion.4) | copy-start | bytes 3076
  117.2 70.2 %copy-start.320 = (f32[256]{0:T(256)}, f32[256]{0:T(256)S(1)}, u32[]{:S(2)}) copy-start(f32[256]{0:T(256)S(1)} %fusion.135) | copy-start | bytes 3076
  117.2 71.0 %copy-start.294 = (f32[256]{0:T(256)}, f32[256]{0:T(256)S(1)}, u32[]{:S(2)}) copy-start(f32[256]{0:T(256)S(1)} %fusion.293) | copy-start | bytes 3076
  117.7 70.4 %copy-start.314 = (f32[256]{0:T(256)}, f32[256]{0:T(256)S(1)}, u32[]{:S(2)}) copy-start(f32[256]{0:T(256)S(1)} %convert_subtract_fusion.3) | copy-start | bytes 3076
  187.8 96.5 %copy-start.92 = (bf16[256,1024]{1,0:T(8,128)(2,1)}, bf16[256,1024]{1,0:T(8,128)(2,1)S(1)}, u32[]{:S(2)}) copy-start(bf16[256,1024]{1,0:T(8,128)(2,1)S(1)} %get-tuple-element.183) | copy-start | bytes 1572868
  188.1 73.4 %copy-start.292 = (bf16[256,32]{0,1:T(8,128)(2,1)}, bf16[256,32]{0,1:T(8,128)(2,1)S(1)}, u32[]{:S(2)}) copy-start(bf16[256,32]{0,1:T(8,128)(2,1)S(1)} %convolution_convert_fusion.4) | copy-start | bytes 49156
  190.1 72.9 %copy-start.157 = (bf16[256,1024]{1,0:T(8,128)(2,1)}, bf16[256,1024]{1,0:T(8,128)(2,1)S(1)}, u32[]{:S(2)}) copy-start(bf16[256,1024]{1,0:T(8,128)(2,1)S(1)} %get-tuple-element.226) | copy-start | bytes 1572868
  190.1 72.9 %copy-start.159 = (bf16[256,1024]{1,0:T(8,128)(2,1)}, bf16[256,1024]{1,0:T(8,128)(2,1)S(1)}, u32[]{:S(2)}) copy-start(bf16[256,1024]{1,0:T(8,128)(2,1)S(1)} %get-tuple-element.223) | copy-start | bytes 1572868
  190.1 73.5 %copy-start.208 = (bf16[256,1024]{1,0:T(8,128)(2,1)}, bf16[256,1024]{1,0:T(8,128)(2,1)S(1)}, u32[]{:S(2)}) copy-start(bf16[256,1024]{1,0:T(8,128)(2,1)S(1)} %get-tuple-element.227) | copy-start | bytes 1572868
  190.6 72.5 %copy-start.266 = (bf16[256,64]{0,1:T(8,128)(2,1)}, bf16[256,64]{0,1:T(8,128)(2,1)S(1)}, u32[]{:S(2)}) copy-start(bf16[256,64]{0,1:T(8,128)(2,1)S(1)} %convolution_convert_fusion.2) | copy-start | bytes 98308
  190.9 76.2 %copy-start.248 = (f32[256,64]{0,1:T(8,128)}, f32[256,64]{0,1:T(8,128)S(1)}, u32[]{:S(2)}) copy-start(f32[256,64]{0,1:T(8,128)S(1)} %convolution_tanh_fusion) | copy-start | bytes 196612
  295.0 123.9 %all-to-all-start = ((bf16[6,256,1024]{1,0,2:T(8,128)(2,1)}), bf16[6,256,1024]{1,0,2:T(8,128)(2,1)}, u32[]{:S(2)}, u32[]{:S(2)}) async-start(bf16[6,256,1024]{1,0,2:T(8,128)(2,1)} %copy.800), calls=%async_computation | async-start | bytes 8388608 | tf_op jit(solution)/shard_map/all_to_all | solution.py:333
  299.7 568.1 %all-gather.22.cloned.1.call-start = ((), (), s32[]{:S(2)}) async-start(), calls=%async_computation.27 | async-start | bytes 8650752 | tf_op jit(solution)/shard_map/all_gather | solution.py:264
  304.7 285.4 %copy-start.253 = (f32[64,64]{1,0:T(8,128)}, f32[64,64]{1,0:T(8,128)S(1)}, u32[]{:S(2)}) copy-start(f32[64,64]{1,0:T(8,128)S(1)} %fusion.274) | copy-start | bytes 49156
  304.9 251.3 %copy-start.206 = (f32[64,32]{1,0:T(8,128)}, f32[64,32]{1,0:T(8,128)S(1)}, u32[]{:S(2)}) copy-start(f32[64,32]{1,0:T(8,128)S(1)} %get-tuple-element.274) | copy-start | bytes 24580
  304.9 687.6 %copy-start.203 = (f32[64,32]{1,0:T(8,128)}, f32[64,32]{1,0:T(8,128)S(1)}, u32[]{:S(2)}) copy-start(f32[64,32]{1,0:T(8,128)S(1)} %get-tuple-element.178) | copy-start | bytes 24580
  306.4 206.4 %copy-start.301 = (pred[32,32]{1,0:T(8,128)(4,1)}, pred[32,32]{1,0:T(8,128)(4,1)S(1)}, u32[]{:S(2)}) copy-start(pred[32,32]{1,0:T(8,128)(4,1)S(1)} %get-tuple-element.310) | copy-start | bytes 3076
  306.7 206.0 %copy-start.228 = (pred[64,32,32]{0,2,1:T(8,128)(4,1)}, pred[64,32,32]{0,2,1:T(8,128)(4,1)S(1)}, u32[]{:S(2)}) copy-start(pred[64,32,32]{0,2,1:T(8,128)(4,1)S(1)} %get-tuple-element.275) | copy-start | bytes 196612
  306.7 253.3 %copy-start.230 = (pred[64,32,32]{0,2,1:T(8,128)(4,1)}, pred[64,32,32]{0,2,1:T(8,128)(4,1)S(1)}, u32[]{:S(2)}) copy-start(pred[64,32,32]{0,2,1:T(8,128)(4,1)S(1)} %get-tuple-element.276) | copy-start | bytes 196612
  453.3 120.7 %copy-start.100 = (f32[16,128,128]{2,1,0:T(8,128)}, f32[16,128,128]{2,1,0:T(8,128)S(1)}, u32[]{:S(2)}) copy-start(f32[16,128,128]{2,1,0:T(8,128)S(1)} %get-tuple-element.283) | copy-start | bytes 3145732
  478.9 111.2 %copy-start.3 = (f32[64,2,32,64]{3,2,1,0:T(8,128)}, f32[64,2,32,64]{3,2,1,0:T(8,128)S(1)}, u32[]{:S(2)}) copy-start(f32[64,2,32,64]{3,2,1,0:T(8,128)S(1)} %get-tuple-element.222) | copy-start | bytes 3145732
  603.2 62.3 %copy-start.44 = (f32[32,2,64,64]{3,2,1,0:T(8,128)}, f32[32,2,64,64]{3,2,1,0:T(8,128)S(1)}, u32[]{:S(2)}) copy-start(f32[32,2,64,64]{3,2,1,0:T(8,128)S(1)} %fusion.55) | copy-start | bytes 3145732
  793.2 18.0 all-to-all-start.1
  813.9 39.7 %copy-start.287 = (f32[1024,1]{0,1:T(1,128)S(1)}, f32[1024,1]{0,1:T(1,128)}, u32[]{:S(2)}) copy-start(f32[1024,1]{0,1:T(1,128)} %get-tuple-element.257) | copy-start | bytes 12292
  880.3 39.8 %copy-start.298 = (f32[256]{0:T(256)S(1)}, f32[256]{0:T(256)}, u32[]{:S(2)}) copy-start(f32[256]{0:T(256)} %copy-done.297) | copy-start | bytes 3076
  928.6 14.4 all-to-all-start.2
  1815.6 84.4 %all-to-all-start.3 = ((bf16[6,2048,128]{2,0,1:T(8,128)(2,1)}), bf16[6,2048,128]{2,0,1:T(8,128)(2,1)}, u32[]{:S(2)}, u32[]{:S(2)}) async-start(bf16[6,2048,128]{2,0,1:T(8,128)(2,1)} %stack.37), calls=%async_computation.3 | async-start | bytes 8388608 | tf_op jit(solution)/shard_map/all_to_all | solution.py:379
  1820.5 177.8 %reduce-scatter.25.cloned.1.call-start = ((), (), s32[]{:S(2)}) async-start(), calls=%async_computation.28 | async-start | bytes 110592 | tf_op jit(solution)/shard_map/reduce_scatter | solution.py:457
  1941.5 342.4 %reduce-scatter.51.cloned.1.call-start = ((), (), s32[]{:S(2)}) async-start(), calls=%async_computation.41 | async-start | bytes 18874368 | tf_op jit(solution)/shard_map/reduce_scatter | solution.py:465
  1951.9 399.5 %reduce-scatter.43.cloned.1.call-start = ((), (), s32[]{:S(2)}) async-start(), calls=%async_computation.37 | async-start | bytes 1327104 | tf_op jit(solution)/shard_map/reduce_scatter | solution.py:462
  1955.0 463.8 %reduce-scatter.45.cloned.1.call-start = ((), (), s32[]{:S(2)}) async-start(), calls=%async_computation.38 | async-start | bytes 1327104 | tf_op jit(solution)/shard_map/reduce_scatter | solution.py:463
  1958.3 551.6 %reduce-scatter.39.cloned.1.call-start = ((), (), s32[]{:S(2)}) async-start(), calls=%async_computation.35 | async-start | bytes 4718592 | tf_op jit(solution)/shard_map/reduce_scatter | solution.py:461
  1961.8 639.3 %reduce-scatter.27.cloned.1.call-start = ((), (), s32[]{:S(2)}) async-start(), calls=%async_computation.29 | async-start | bytes 4718592 | tf_op jit(solution)/shard_map/reduce_scatter | solution.py:458
  1965.7 727.2 %reduce-scatter.31.cloned.1.call-start = ((), (), s32[]{:S(2)}) async-start(), calls=%async_computation.31 | async-start | bytes 4718592 | tf_op jit(solution)/shard_map/reduce_scatter | solution.py:459
  1969.6 814.5 %reduce-scatter.35.cloned.1.call-start = ((), (), s32[]{:S(2)}) async-start(), calls=%async_computation.33 | async-start | bytes 4718592 | tf_op jit(solution)/shard_map/reduce_scatter | solution.py:460
  1973.3 1096.8 %reduce-scatter.47.cloned.1.call-start = ((), (), s32[]{:S(2)}) async-start(), calls=%async_computation.39 | async-start | bytes 18874368 | tf_op jit(solution)/shard_map/reduce_scatter | solution.py:464
  1984.2 1127.2 %reduce-scatter.55.cloned.1.call-start = ((), (), s32[]{:S(2)}) async-start(), calls=%async_computation.43 | async-start | bytes 81920
  1999.8 1124.5 %reduce-scatter.53.cloned.1.call-start = ((), (), s32[]{:S(2)}) async-start(), calls=%async_computation.42 | async-start | bytes 2621440 | tf_op jit(solution)/shard_map/reduce_scatter | solution.py:476
  2283.9 862.9 %reduce-scatter.57.cloned.1.call-start = ((), (), s32[]{:S(2)}) async-start(), calls=%async_computation.44 | async-start | bytes 184320
  2351.4 818.0 %reduce-scatter.59.cloned.1.call-start = ((), (), s32[]{:S(2)}) async-start(), calls=%async_computation.45 | async-start | bytes 184320
  2418.8 775.3 %reduce-scatter.41.cloned.1.call-start = ((), (), s32[]{:S(2)}) async-start(), calls=%async_computation.36 | async-start | bytes 655360 | tf_op jit(solution)/shard_map/reduce_scatter | solution.py:472
  2509.9 560.2 %copy-start.52 = (f32[256,1024]{1,0:T(8,128)S(1)}, f32[256,1024]{1,0:T(8,128)}, u32[]{:S(2)}) copy-start(f32[256,1024]{1,0:T(8,128)} %copy-done.50) | copy-start | bytes 3145732
  2509.9 709.1 %reduce-scatter.29.cloned.1.call-start = ((), (), s32[]{:S(2)}) async-start(), calls=%async_computation.30 | async-start | bytes 655360 | tf_op jit(solution)/shard_map/reduce_scatter | solution.py:469
  2601.1 642.7 %reduce-scatter.33.cloned.1.call-start = ((), (), s32[]{:S(2)}) async-start(), calls=%async_computation.32 | async-start | bytes 655360 | tf_op jit(solution)/shard_map/reduce_scatter | solution.py:470
  2692.9 575.8 %reduce-scatter.37.cloned.1.call-start = ((), (), s32[]{:S(2)}) async-start(), calls=%async_computation.34 | async-start | bytes 655360 | tf_op jit(solution)/shard_map/reduce_scatter | solution.py:471
  2784.1 519.0 %reduce-scatter.49.cloned.1.call-start = ((), (), s32[]{:S(2)}) async-start(), calls=%async_computation.40 | async-start | bytes 2621440 | tf_op jit(solution)/shard_map/reduce_scatter | solution.py:475
  3070.2 39.6 %copy-start.296 = (f32[256]{0:T(256)S(1)}, f32[256]{0:T(256)}, u32[]{:S(2)}) copy-start(f32[256]{0:T(256)} %copy-done.294) | copy-start | bytes 3076
  (332 other events, 1808.5 us)
Sparse Core Ops, SparseCore 0:
  11.0 58.3 all-gather.11
  72.4 55.4 all-gather.13
  130.8 56.3 all-gather.15
  190.0 57.6 all-gather.17
  250.5 106.2 all-gather.19
  359.7 112.4 all-gather.21
  1941.6 56.6 reduce-scatter.24
  2002.1 281.6 reduce-scatter.50
  2287.7 63.6 reduce-scatter.42
  2355.0 63.7 reduce-scatter.44
  2422.9 86.9 reduce-scatter.38
  2513.4 87.6 reduce-scatter.26
  2605.2 87.6 reduce-scatter.30
  2696.3 87.6 reduce-scatter.34
  2788.2 281.8 reduce-scatter.46
  3073.0 17.1 reduce-scatter.54
  3092.7 31.5 reduce-scatter.52
  3127.2 19.4 reduce-scatter.56
  3149.7 19.6 reduce-scatter.58
  3172.3 21.8 reduce-scatter.40
  3197.4 21.6 reduce-scatter.28
  3222.1 21.6 reduce-scatter.32
  3247.0 21.6 reduce-scatter.36
  3271.7 31.4 reduce-scatter.48
where the time goes:
time: 3370 us; the launch traced here: 3310 us
  waiting for transfers between devices  1480 us (44%)
  local copies, waits for them, and re-layouts  830 us (25%)
  matrix products  430 us (13%)
  blocking collectives  334 us (10%)
  other arithmetic  200 us (6%)
    pad x43, local copies, waits for them, and re-layouts, span_scan(): _, reached = lax.associative_scan(combine, (through, offset), axis=0)  430 us
    reduce_scatter x1, waiting for transfers between devices, body(): lax.psum_scatter(grad_ffn_key, 'head', scatter_dimension=0, tiled=True)  286 us
    reduce_scatter x1, waiting for transfers between devices, body(): lax.psum_scatter(grad_ffn_value, 'head', scatter_dimension=0, tiled=True)  284 us
    all_to_all x1, waiting for transfers between devices, body(): lax.all_to_all(sent, 'head', split_axis=2, concat_axis=1, tiled=True)  112 us
    reduce_scatter x1, waiting for transfers between devices, body(): lax.psum_scatter(grad_key, 'head', scatter_dimension=0, tiled=True)  91.7 us
    reduce_scatter x1, waiting for transfers between devices, body(): lax.psum_scatter(grad_value, 'head', scatter_dimension=0, tiled=True)  91.1 us
    reduce_scatter x1, waiting for transfers between devices, body(): lax.psum_scatter(grad_recept, 'head', scatter_dimension=0, tiled=True)  91.1 us
    reduce_scatter x1, waiting for transfers between devices, body(): lax.psum_scatter(grad_output, 'head', scatter_dimension=0, tiled=True)  91 us
  transfers between devices with their start and end apart: 28, of which 21 were waited for; matrix products, arithmetic and copies ran while one was open for 15% of the time, Pallas kernels for 0%

commit v1 on v0

v1 whole, which is shorter than its diff:
```python
import functools
import jax
import jax.numpy as jnp
from jax import lax
from jax.experimental import pallas as pl
from jax.experimental.pallas import tpu as pltpu
from jax.sharding import Mesh
from jax.sharding import PartitionSpec as P

DECAY_RANK = 64
DA = 64
DV = 32
BLOCK = 128
SPAN = 64
HEAD = 64
FORWARD_CHUNKS = 8
BACKWARD_CHUNKS = 4
LOW = jnp.bfloat16
F32 = jnp.float32
NN = (((1,), (0,)), ((), ()))
NT = (((1,), (1,)), ((), ()))
TN = (((0,), (0,)), ((), ()))
PASSES = {"pair": 3, "inv": 3, "val": 3, "chain": 3, "bpair": 3}


def work(micros):
    return pl.CostEstimate(flops=0, bytes_accessed=int(micros * 3_000), transcendentals=0)


def dot(a, b, dims):
    return lax.dot_general(a, b, dims, preferred_element_type=F32)


def halves(x):
    high = x.astype(LOW)
    return high, (x - high.astype(F32)).astype(LOW)


def product(a, b, dims, passes):
    if passes == 1:
        return dot(a.astype(LOW), b.astype(LOW), dims)
    la, lb = dims[0][0][0], dims[0][1][0]
    a_high, a_low = halves(a)
    if passes == 2:
        b = b.astype(LOW)
        return dot(jnp.concatenate([a_high, a_low], la), jnp.concatenate([b, b], lb), dims)
    b_high, b_low = halves(b)
    first = dot(jnp.concatenate([a_high, a_low], la), jnp.concatenate([b_high, b_high], lb), dims)
    return first + dot(a_high, b_low, dims)


def head_masks(heads):
    lane = lax.broadcasted_iota(jnp.int32, (1, heads * HEAD), 1) // HEAD
    return [(lane == h).astype(F32) for h in range(heads)]


def stacked(x, masks):
    if len(masks) == 1:
        return x
    return jnp.concatenate([x * m for m in masks], 0)


def unstacked(x, heads):
    rows = x.shape[0] // heads
    out = x[:rows]
    for h in range(1, heads):
        out = out + x[h * rows : (h + 1) * rows]
    return out


def head_ones(width):
    row = lax.broadcasted_iota(jnp.int32, (width, width), 0) // HEAD
    col = lax.broadcasted_iota(jnp.int32, (width, width), 1) // HEAD
    return (row == col).astype(LOW)


def head_sum(x, ones):
    high, low = halves(x)
    return dot(jnp.concatenate([high, low], 1), jnp.concatenate([ones, ones], 0), NN)


class Chunk:
    def __init__(self, r, lw, k, kn, a, begins, start, heads):
        self.heads = heads
        masks = head_masks(heads)
        rows = heads * SPAN
        local = [jnp.where(b >= start, b - start, SPAN) for b in begins]
        row_t = lax.broadcasted_iota(jnp.int32, (rows, 1), 0) % SPAN
        col_t = lax.broadcasted_iota(jnp.int32, (1, rows), 1) % SPAN
        row_seg = sum((row_t >= b).astype(jnp.int32) for b in local)
        col_seg = sum((col_t >= b).astype(jnp.int32) for b in local)
        last = sum((b < SPAN).astype(jnp.int32) for b in local)
        same = row_seg == col_seg
        self.strict = same & (row_t > col_t)
        self.upto = same & (row_t >= col_t)
        self.carried = (row_seg == 0).astype(F32)
        self.final = (row_seg == last).astype(F32)
        self.whole = (last == 0).astype(F32)
        tri_r = lax.broadcasted_iota(jnp.int32, (SPAN, SPAN), 0)
        tri_c = lax.broadcasted_iota(jnp.int32, (SPAN, SPAN), 1)
        running = dot((tri_r >= tri_c).astype(LOW), lw, NN)
        lw = lw.astype(F32)
        decay = jnp.exp(running)
        before = jnp.exp(running - lw)
        inverse = jnp.exp(-running)
        end = running[SPAN - 1 : SPAN]
        to_end = jnp.exp(end - running)
        self.end = jnp.exp(end)
        kn = kn.astype(F32)
        beta = kn * a.astype(F32)
        k = k.astype(F32)
        self.decay, self.before, self.inverse, self.to_end = decay, before, inverse, to_end
        self.a_hat = stacked(-kn * before, masks)
        self.r_hat = stacked(r.astype(F32) * decay, masks)
        self.b_hat = stacked(beta * inverse, masks)
        self.k_hat = stacked(k * inverse, masks)
        self.b_end = stacked(beta * to_end, masks) * self.final
        self.k_end = stacked(k * to_end, masks) * self.final


def block_inverses(all_pairs, passes):
    rows = all_pairs[0].shape[0]
    row = lax.broadcasted_iota(jnp.int32, (rows, rows), 0)
    col = lax.broadcasted_iota(jnp.int32, (rows, rows), 1)
    eye = (row == col).astype(F32)

    def products(left, right):
        return [product(a, b, NN, passes) for a, b in zip(left, right)]

    within = row // 8 == col // 8
    small = [jnp.where(within, pairs, 0.0) for pairs in all_pairs]
    square = products(small, small)
    fourth = products(square, square)
    first = [eye + x for x in small]
    inverse = [a + b for a, b in zip(first, products(first, square))]
    inverse = [a + b for a, b in zip(inverse, products(inverse, fourth))]
    size = 8
    while size < SPAN:
        within = (row // (2 * size) == col // (2 * size)) & (row // size != col // size)
        cross = [jnp.where(within, pairs, 0.0) for pairs in all_pairs]
        step = products(products(inverse, cross), inverse)
        inverse = [a + b for a, b in zip(inverse, step)]
        size *= 2
    return inverse


def group_norm_parts(scanned, ones):
    center = scanned - head_sum(scanned, ones) * (1.0 / HEAD)
    spread = head_sum(center * center, ones) * (1.0 / HEAD)
    scale = lax.rsqrt(spread + 0.00064)
    return center * scale, scale


def scan_forward_kernel(
    heads, p, begins_ref, parts_ref, gate_ref, cols_ref,
    out_ref, joined_ref, scanned_ref, state_ref, mats_ref, state,
):
    step = pl.program_id(0)
    width = heads * HEAD

    @pl.when(step == 0)
    def _():
        state[...] = jnp.zeros_like(state)

    begins = [begins_ref[i] for i in range(begins_ref.shape[0])]
    masks = head_masks(heads)
    n = heads * SPAN
    eye = (
        lax.broadcasted_iota(jnp.int32, (width, width), 0)
        == lax.broadcasted_iota(jnp.int32, (width, width), 1)
    ).astype(F32)
    held = []
    for c in range(FORWARD_CHUNKS):
        rows = pl.ds(c * SPAN, SPAN)
        r, lw, k, kn, a, v = [parts_ref[i, rows] for i in range(6)]
        q = Chunk(r, lw, k, kn, a, begins, (step * FORWARD_CHUNKS + c) * SPAN, heads)
        v_st = stacked(v.astype(F32), masks).astype(LOW)
        held.append((q, r, k, v, v_st))
    all_pairs = [
        product(
            jnp.concatenate([q.a_hat, q.r_hat], 0), jnp.concatenate([q.b_hat, q.k_hat], 0), NT, p["pair"]
        )
        for q, *_ in held
    ]
    l_ab = [jnp.where(h[0].strict, x[:n, :n], 0.0) for h, x in zip(held, all_pairs)]
    l_ak = [jnp.where(h[0].strict, x[:n, n:], 0.0) for h, x in zip(held, all_pairs)]
    l_rb = [jnp.where(h[0].upto, x[n:, :n], 0.0) for h, x in zip(held, all_pairs)]
    l_rk = [jnp.where(h[0].upto, x[n:, n:], 0.0) for h, x in zip(held, all_pairs)]
    both_v = [
        product(jnp.concatenate([ak, rk], 0), h[4], NN, 2 if p["val"] == 3 else 1)
        for ak, rk, h in zip(l_ak, l_rk, held)
    ]
    inverses = block_inverses(l_ab, p["inv"])
    solved = [
        product(t, jnp.concatenate([h[0].a_hat * h[0].carried, b[:n]], 1), NN, p["val"])
        for t, h, b in zip(inverses, held, both_v)
    ]
    ends = [product(x, h[0].b_end, TN, p["val"]) for x, h in zip(solved, held)]
    grown = []
    for q, _, _, _, v_st in held:
        if p["val"] == 3:
            k_high, k_low = halves(q.k_end)
            grown.append(dot(jnp.concatenate([v_st, v_st], 0), jnp.concatenate([k_high, k_low], 0), TN))
        else:
            grown.append(dot(v_st, q.k_end.astype(LOW), TN))
    ready = []
    for c in range(FORWARD_CHUNKS):
        q, r, k, v, _ = held[c]
        through = product(l_rb[c], solved[c], NN, p["val"])
        r_thru = q.r_hat * q.carried + through[:, :width]
        o_val = both_v[c][n:] + through[:, width:]
        move = eye * (q.end * q.whole) + ends[c][:width]
        gain = ends[c][width:] + grown[c]
        mats = [
            inverses[c], l_ak[c], l_rb[c], l_rk[c], solved[c][:, :width], solved[c][:, width:], move, r_thru,
        ]
        for i, m in enumerate(mats):
            mats_ref[c, i] = m
        ready.append((move, gain, r_thru, o_val, r, k, v))
    ones = head_ones(width)
    now = state[...]
    begun = []
    for c in range(FORWARD_CHUNKS):
        begun.append(now)
        state_ref[c] = now
        now = product(now, ready[c][0], NN, p["chain"]) + ready[c][1]
    state[...] = now
    for c in range(FORWARD_CHUNKS):
        rows = pl.ds(c * SPAN, SPAN)
        _, _, r_thru, o_val, r, k, v = ready[c]
        scanned = unstacked(o_val + product(r_thru, begun[c], NT, p["val"]), heads)
        scanned_ref[rows] = scanned
        unit, _ = group_norm_parts(scanned, ones)
        bonus = head_sum(r.astype(F32) * k.astype(F32) * cols_ref[0:1], ones)
        joined = unit * cols_ref[1:2] + cols_ref[2:3] + bonus * v.astype(F32)
        joined = joined.astype(LOW)
        joined_ref[rows] = joined
        out_ref[rows] = (joined.astype(F32) * gate_ref[rows]).astype(LOW)


def scan_forward(parts, gate, cols, begins, p):
    _, total, width = parts.shape
    heads = width // HEAD
    rows = FORWARD_CHUNKS * SPAN
    n = heads * SPAN
    spans = total // SPAN
    assert n == width
    row_spec = pl.BlockSpec((rows, width), lambda i, b: (i, 0))
    return pl.pallas_call(
        functools.partial(scan_forward_kernel, heads, p),
        grid_spec=pltpu.PrefetchScalarGridSpec(
            num_scalar_prefetch=1,
            grid=(total // rows,),
            in_specs=[
                pl.BlockSpec((6, rows, width), lambda i, b: (0, i, 0)),
                row_spec,
                pl.BlockSpec(cols.shape, lambda i, b: (0, 0)),
            ],
            out_specs=[
                row_spec,
                row_spec,
                row_spec,
                pl.BlockSpec((FORWARD_CHUNKS, width, width), lambda i, b: (i, 0, 0)),
                pl.BlockSpec((FORWARD_CHUNKS, 8, n, width), lambda i, b: (i, 0, 0, 0)),
            ],
            scratch_shapes=[pltpu.VMEM((width, width), F32)],
        ),
        out_shape=[
            jax.ShapeDtypeStruct((total, width), LOW),
            jax.ShapeDtypeStruct((total, width), LOW),
            jax.ShapeDtypeStruct((total, width), F32),
            jax.ShapeDtypeStruct((spans, width, width), F32),
            jax.ShapeDtypeStruct((spans, 8, n, width), F32),
        ],
        compiler_params=pltpu.CompilerParams(vmem_limit_bytes=48 * 1024 * 1024),
        cost_estimate=work(80),
    )(begins, parts, gate, cols)


def scan_backward_kernel(
    heads, p, home_ref, begins_ref, parts_ref, joined_ref, scanned_ref, gate_ref, grad_a_ref, grad_b_ref,
    pre_ref, first_ref, cols_ref, state_ref, mats_ref, *rest,
):
    steps = pl.num_programs(0)
    step = steps - 1 - pl.program_id(0)
    grads_ref, first_grad_ref, col_grad_ref, state = rest
    width = heads * HEAD
    n = heads * SPAN

    @pl.when(pl.program_id(0) == 0)
    def _():
        state[...] = jnp.zeros_like(state)
        col_grad_ref[...] = jnp.zeros_like(col_grad_ref)

    begins = [begins_ref[i] for i in range(begins_ref.shape[0])]
    masks = head_masks(heads)
    ones = head_ones(width)
    tri_r = lax.broadcasted_iota(jnp.int32, (SPAN, SPAN), 0)
    tri_c = lax.broadcasted_iota(jnp.int32, (SPAN, SPAN), 1)
    later = (tri_c >= tri_r).astype(LOW)
    after = (tri_c > tri_r).astype(LOW)
    sums = [jnp.zeros((1, width), F32) for _ in range(8)]

    def add(slot, value):
        sums[slot] = sums[slot] + jnp.sum(value, 0, keepdims=True)

    c13, c14 = cols_ref[0:1], cols_ref[1:2]
    grads = jnp.concatenate([grad_a_ref[0], grad_b_ref[0]], 0).astype(F32)
    ready = []
    for c in range(BACKWARD_CHUNKS):
        rows = pl.ds(c * SPAN, SPAN)
        r, lw, k, kn, a, v = [parts_ref[i, rows] for i in range(6)]
        q = Chunk(r, lw, k, kn, a, begins, (step * BACKWARD_CHUNKS + c) * SPAN, heads)
        r, k, v = r.astype(F32), k.astype(F32), v.astype(F32)
        unit, scale = group_norm_parts(scanned_ref[rows], ones)
        grad_out = grads[c * SPAN : (c + 1) * SPAN]
        grad_joined = (grad_out * gate_ref[rows]).astype(LOW).astype(F32)
        grad_gate = (grad_out * joined_ref[rows].astype(F32)).astype(LOW)
        add(6, grad_joined * unit)
        add(7, grad_joined)
        grad_unit = grad_joined * c14
        grad_scan = scale * (
            grad_unit
            - head_sum(grad_unit, ones) * (1.0 / HEAD)
            - unit * (head_sum(grad_unit * unit, ones) * (1.0 / HEAD))
        )
        bonus = head_sum(r * k * c13, ones)
        grad_bonus = head_sum(grad_joined * v, ones)
        add(5, grad_bonus * r * k)
        own_r = grad_bonus * k * c13
        own_k = grad_bonus * r * c13
        own_v = grad_joined * bonus
        d_out = stacked(grad_scan, masks)
        flow = product(d_out, mats_ref[c, 7], TN, p["val"])
        ready.append((q, d_out, flow, own_r, own_k, own_v, grad_gate))
    now = state[...]
    ended = [None] * BACKWARD_CHUNKS
    for c in reversed(range(BACKWARD_CHUNKS)):
        ended[c] = now
        now = product(now, mats_ref[c, 6], NT, p["chain"]) + ready[c][2]
    state[...] = now
    span = range(BACKWARD_CHUNKS)
    mats = [[mats_ref[c, i] for i in range(6)] for c in span]
    begin = [state_ref[c] for c in span]
    chunks = [ready[c][0] for c in span]
    d_outs = [ready[c][1] for c in span]
    v_st = [stacked(parts_ref[5, pl.ds(c * SPAN, SPAN)].astype(F32), masks) for c in span]
    update = [mats[c][5] + product(mats[c][4], begin[c], NT, p["val"]) for c in span]
    through = [product(mats[c][2], d_outs[c], TN, p["val"]) for c in span]
    through = [
        through[c] + product(chunks[c].b_end, ended[c], NT, p["val"]) for c in span
    ]
    back = [product(mats[c][0], through[c], TN, p["val"]) for c in span]
    left = [jnp.concatenate([back[c], d_outs[c]], 0) for c in span]
    right = [jnp.concatenate([update[c], v_st[c]], 0) for c in span]
    d_hats = [product(left[c], begin[c], NN, p["val"]) for c in span]
    pair_grads = [product(left[c], right[c], NT, p["bpair"]) for c in span]
    for c in span:
        strict, upto = chunks[c].strict.astype(F32), chunks[c].upto.astype(F32)
        mask = jnp.concatenate(
            [jnp.concatenate([strict, strict], 1), jnp.concatenate([upto, upto], 1)], 0
        )
        pair_grads[c] = pair_grads[c] * mask
    all_asks = []
    for c in span:
        q = chunks[c]
        keys = jnp.concatenate([q.b_hat, q.k_hat], 0)
        carried = jnp.concatenate([q.carried, q.carried], 0)
        all_asks.append(d_hats[c] * carried + product(pair_grads[c], keys, NN, p["bpair"]))
    all_keys = [
        product(
            pair_grads[c], jnp.concatenate([chunks[c].a_hat, chunks[c].r_hat], 0), TN, p["bpair"]
        )
        for c in span
    ]
    all_ends = [product(right[c], ended[c], NN, p["val"]) for c in span]
    all_vals = [
        product(jnp.concatenate([mats[c][1], mats[c][3]], 0), left[c], TN, p["val"]) for c in span
    ]
    all_vals = [
        all_vals[c] + product(chunks[c].k_end, ended[c], NT, p["val"]) for c in span
    ]
    for c in span:
        rows = pl.ds(c * SPAN, SPAN)
        q, _, _, own_r, own_k, own_v, grad_gate = ready[c]
        end_grad, begin_now = ended[c], begin[c]
        r, lw, k, kn, a, v = [parts_ref[i, rows].astype(F32) for i in range(6)]
        d_asks, d_keys, d_val = all_asks[c], all_keys[c], all_vals[c]
        d_ends = all_ends[c] * jnp.concatenate([q.final, q.final], 0)
        d_a, d_r = unstacked(d_asks[:n], heads) * q.before, unstacked(d_asks[n:], heads) * q.decay
        d_b = unstacked(d_keys[:n], heads) * q.inverse
        d_k = unstacked(d_keys[n:], heads) * q.inverse
        e_b = unstacked(d_ends[:n], heads) * q.to_end
        e_k = unstacked(d_ends[n:], heads) * q.to_end
        d_v = unstacked(d_val, heads) + own_v
        beta = kn * a
        end_part = e_b * beta + e_k * k
        here = d_r * r - d_b * beta - d_k * k - end_part
        ahead = -d_a * kn
        at_end = jnp.sum(end_part, 0, keepdims=True) + q.whole * q.end * jnp.sum(
            begin_now * end_grad, 0, keepdims=True
        )
        high, low = halves(here)
        high2, low2 = halves(ahead)
        d_lw = at_end + dot(
            jnp.concatenate([later, later, after, after], 1),
            jnp.concatenate([high, low, high2, low2], 0),
            NN,
        )
        d_b = d_b + e_b
        d_k = d_k + e_k + own_k
        d_r = d_r + own_r
        d_kn = d_b * a - d_a
        d_rate = d_b * kn
        g_r, g_lw, g_k, g_kn, g_a, g_v = [
            x.astype(LOW).astype(F32) for x in (d_r, d_lw, d_k, d_kn, d_rate, d_v)
        ]
        key_pre, value_pre, decay_up, rate_up, value_up = [pre_ref[i, rows] for i in range(5)]
        first = first_ref[rows].astype(F32)
        c8, c9, c10, c11, c12 = [cols_ref[i : i + 1] for i in range(3, 8)]
        sig = jax.nn.sigmoid(c8 + decay_up)
        log_decay = -0.6065306597126334 * sig
        g_decay = g_lw * log_decay * (1.0 - sig)
        add(0, g_decay)
        rate = jax.nn.sigmoid(c9 + rate_up)
        g_rate = (g_a + g_k * key_pre * c12) * rate * (1.0 - rate)
        add(1, g_rate)
        g_key = g_k * (1.0 + (rate - 1.0) * c12)
        add(4, g_k * key_pre * (rate - 1.0))
        scaled = key_pre * c11
        norm = lax.rsqrt(head_sum(scaled * scaled, ones) + 1e-06)
        unit = scaled * norm
        g_scaled = norm * (g_kn - unit * head_sum(g_kn * unit, ones))
        g_key = g_key + g_scaled * c11
        add(3, g_scaled * key_pre)
        mix = jax.nn.sigmoid(c10 + value_up)
        g_value = g_v * (1.0 - mix)
        first_grad_ref[rows] = (g_v * mix).astype(first_grad_ref.dtype)
        g_vup = g_v * (first - value_pre) * mix * (1.0 - mix)
        add(2, g_vup)
        for i, x in enumerate((g_r, g_key, g_value, g_decay, g_rate, g_vup)):
            grads_ref[i, rows] = x.astype(LOW)
        grads_ref[6, rows] = grad_gate
    col_grad_ref[...] += jnp.concatenate(sums, 0)


def scan_backward(parts, joined, scanned, gate, grad, pre, first, cols, states, mats, home, begins, p):
    _, total, width = parts.shape
    heads = width // HEAD
    rows = BACKWARD_CHUNKS * SPAN
    n = heads * SPAN
    steps = total // rows
    row_spec = pl.BlockSpec((rows, width), lambda i, *_: (steps - 1 - i, 0))
    assert rows == 2 * BLOCK

    def stored(which):
        return pl.BlockSpec(
            (1, BLOCK, width), lambda i, home, b: (home[2 * (steps - 1 - i) + which], 0, 0)
        )

    return pl.pallas_call(
        functools.partial(scan_backward_kernel, heads, p),
        grid_spec=pltpu.PrefetchScalarGridSpec(
            num_scalar_prefetch=2,
            grid=(steps,),
            in_specs=[
                pl.BlockSpec((6, rows, width), lambda i, *_: (0, steps - 1 - i, 0)),
                row_spec,
                row_spec,
                row_spec,
                stored(0),
                stored(1),
                pl.BlockSpec((5, rows, width), lambda i, *_: (0, steps - 1 - i, 0)),
                row_spec,
                pl.BlockSpec(cols.shape, lambda i, *_: (0, 0)),
                pl.BlockSpec((BACKWARD_CHUNKS, width, width), lambda i, *_: (steps - 1 - i, 0, 0)),
                pl.BlockSpec((BACKWARD_CHUNKS, 8, n, width), lambda i, *_: (steps - 1 - i, 0, 0, 0)),
            ],
            out_specs=[
                pl.BlockSpec((7, rows, width), lambda i, *_: (0, steps - 1 - i, 0)),
                row_spec,
                pl.BlockSpec((8, width), lambda i, *_: (0, 0)),
            ],
            scratch_shapes=[pltpu.VMEM((width, width), F32)],
        ),
        out_shape=[
            jax.ShapeDtypeStruct((7, total, width), LOW),
            jax.ShapeDtypeStruct((total, width), LOW),
            jax.ShapeDtypeStruct((8, width), F32),
        ],
        compiler_params=pltpu.CompilerParams(vmem_limit_bytes=56 * 1024 * 1024),
        cost_estimate=work(60),
    )(home, begins, parts, joined, scanned, gate, grad, grad, pre, first, cols, states, mats)


def norm_rows(x):
    center = x - jnp.mean(x, -1, keepdims=True)
    scale = lax.rsqrt(jnp.mean(center * center, -1, keepdims=True) + 1e-05)
    return center * scale, scale


def keep_rows(rows, first, begins):
    position = first + lax.broadcasted_iota(jnp.int32, (rows, 1), 0)
    hit = position == begins[0]
    for b in begins[1:]:
        hit = hit | (position == b)
    return 1.0 - hit.astype(F32)


def rows_down(x, edge):
    row = lax.broadcasted_iota(jnp.int32, (x.shape[0], 1), 0)
    return jnp.where(row == 0, edge, pltpu.roll(x, 1, 0))


def rows_up(x, edge):
    row = lax.broadcasted_iota(jnp.int32, (x.shape[0], 1), 0)
    return jnp.where(row == x.shape[0] - 1, edge, pltpu.roll(x, x.shape[0] - 1, 0))


def lane_below(limit):
    return lax.broadcasted_iota(jnp.int32, (1, 128), 1) < limit


def kept(x, mask):
    return jnp.where(mask, x, jnp.zeros_like(x))


class SmallWeights:
    def __init__(self, small, up):
        self.pair, self.gate, self.value = small[:, :128], small[:, 128:256], small[:, 256:384]
        self.up_pair, self.up_gate = up[:, 384:512], up[:, 512:640]
        self.up_value = jnp.concatenate([up[:, 320:352], jnp.zeros((up.shape[0], 96), LOW)], 1)


def project_kernel(
    place_ref, home_ref, begins_ref, xa_ref, xb_ref, fa_ref, fb_ref, cols_ref, own_ref, columns_ref,
    small_ref, up_ref, parts_ref, gate_ref, pre_ref, first_ref, pair_ref, vm_ref, gs_ref, edge,
):
    step = pl.program_id(0)

    @pl.when(step == 0)
    def _():
        edge[...] = jnp.zeros_like(edge)

    begins = [begins_ref[i] for i in range(begins_ref.shape[0])]
    x = jnp.concatenate([xa_ref[0], xb_ref[0]], 0).astype(F32)
    rows = x.shape[0]
    unit, _ = norm_rows(x)
    normed = unit * cols_ref[0:1] + cols_ref[1:2]
    moved = rows_down(normed, edge[0:1]) * keep_rows(rows, step * rows, begins)
    edge[0:1] = normed[rows - 1 : rows]
    diff = moved - normed
    mixed = [(normed + diff * cols_ref[i : i + 1]).astype(LOW) for i in range(2, 8)]
    in_r, in_d, in_k, in_v, in_a, in_g = mixed
    low = SmallWeights(small_ref[...], up_ref[...])
    width = own_ref.shape[1]
    recept = dot(in_r, columns_ref[:, :width], NN)
    key_pre = dot(in_k, columns_ref[:, width : 2 * width], NN)
    values = dot(in_v, jnp.concatenate([columns_ref[:, 2 * width :], low.value], 1), NN)
    value_pre = values[:, :width]
    value_mid = kept(values[:, width:], lane_below(DV)).astype(LOW)
    decay, rate = dot(in_d, low.pair, NN), dot(in_a, low.pair, NN)
    pair = jnp.where(lane_below(DECAY_RANK), jnp.tanh(decay), rate)
    pair_low = pair.astype(LOW)
    gate_sig = jax.nn.sigmoid(dot(in_g, low.gate, NN))
    decay_up = dot(kept(pair_low, lane_below(DECAY_RANK)), low.up_pair, NT)
    rate_up = dot(kept(pair_low, ~lane_below(DECAY_RANK)), low.up_pair, NT)
    value_up = dot(value_mid, low.up_value, NT)
    gate_ref[...] = dot(gate_sig.astype(LOW), low.up_gate, NT)
    pair_ref[...] = pair
    vm_ref[...] = value_mid
    gs_ref[...] = gate_sig
    first_low = jnp.concatenate([fa_ref[0], fb_ref[0]], 0)
    first_ref[...] = first_low
    first = first_low.astype(F32)
    for i, value in enumerate((key_pre, value_pre, decay_up, rate_up, value_up)):
        pre_ref[i] = value
    c8, c9, c10, c11, c12 = [own_ref[i : i + 1] for i in range(3, 8)]
    ones = head_ones(recept.shape[1])
    log_decay = -jnp.exp(-jax.nn.softplus(-(c8 + decay_up)) - 0.5)
    rate = jax.nn.sigmoid(c9 + rate_up)
    scaled = key_pre * c11
    key_norm = scaled * lax.rsqrt(head_sum(scaled * scaled, ones) + 1e-06)
    key_main = key_pre * (1.0 + (rate - 1.0) * c12)
    values = value_pre + (first - value_pre) * jax.nn.sigmoid(c10 + value_up)
    for i, value in enumerate((recept, log_decay, key_main, key_norm, rate, values)):
        parts_ref[i] = value.astype(LOW)


def block_spec(per, which, rows, width, blocks, back, table=0):
    def index(i, *tables):
        step = blocks // 2 - 1 - i if back else i
        stored = tables[table][jnp.maximum(2 * step + which, 0)]
        return (stored // per, (stored % per) * (BLOCK // rows) + BLOCK // rows - 1, 0)

    return pl.BlockSpec((1, rows, width), index)


def whole_spec(array):
    return pl.BlockSpec(array.shape, lambda i, *_: (0,) * array.ndim)


def project(x, first, cols, own, weights, place, home, begins, per):
    blocks = home.shape[0]
    total = blocks * BLOCK
    rows = 2 * BLOCK
    width = own.shape[1]
    span = lambda w: pl.BlockSpec((rows, w), lambda i, *_: (i, 0))
    deep = lambda n: pl.BlockSpec((n, rows, width), lambda i, *_: (0, i, 0))
    shape = jax.ShapeDtypeStruct
    return pl.pallas_call(
        project_kernel,
        grid_spec=pltpu.PrefetchScalarGridSpec(
            num_scalar_prefetch=3,
            grid=(blocks // 2,),
            in_specs=[
                block_spec(per, 0, BLOCK, x.shape[2], blocks, False),
                block_spec(per, 1, BLOCK, x.shape[2], blocks, False),
                block_spec(per, 0, BLOCK, width, blocks, False, 1),
                block_spec(per, 1, BLOCK, width, blocks, False, 1),
                whole_spec(cols),
                whole_spec(own),
            ]
            + [whole_spec(w) for w in weights],
            out_specs=[deep(6), span(width), deep(5), span(width), span(128), span(128), span(128)],
            scratch_shapes=[pltpu.VMEM((8, x.shape[2]), F32)],
        ),
        out_shape=[
            shape((6, total, width), LOW),
            shape((total, width), F32),
            shape((5, total, width), F32),
            shape((total, width), LOW),
            shape((total, 128), F32),
            shape((total, 128), LOW),
            shape((total, 128), F32),
        ],
        compiler_params=pltpu.CompilerParams(vmem_limit_bytes=56 * 1024 * 1024),
        cost_estimate=work(20),
    )(place, home, begins, x, x, first, first, cols, own, *weights)


def project_back_kernel(
    place_ref, begins_ref, xa_ref, xb_ref, xp_ref, grads_ref, pair_ref, vm_ref, gs_ref, cols_ref,
    columns_ref, small_ref, up_ref, back_ref, sum_ref, up_sum_ref, edge,
):
    step = pl.num_programs(0) - 1 - pl.program_id(0)

    @pl.when(pl.program_id(0) == 0)
    def _():
        for ref in (edge, sum_ref, up_sum_ref):
            ref[...] = jnp.zeros_like(ref)

    begins = [begins_ref[i] for i in range(begins_ref.shape[0])]
    x = jnp.concatenate([xa_ref[0], xb_ref[0]], 0).astype(F32)
    rows = x.shape[0]
    unit, _ = norm_rows(x)
    normed = unit * cols_ref[0:1] + cols_ref[1:2]
    prior_unit, _ = norm_rows(xp_ref[0].astype(F32))
    prior = prior_unit * cols_ref[0:1] + cols_ref[1:2]
    keep = keep_rows(rows, step * rows, begins)
    diff = rows_down(normed, prior[prior.shape[0] - 1 :]) * keep - normed
    low = SmallWeights(small_ref[...], up_ref[...])
    width = grads_ref.shape[2]
    g_r, g_k, g_v, g_decay, g_rate, g_vup, g_gate = [grads_ref[i] for i in range(7)]
    pair, sig = pair_ref[...], gs_ref[...]
    pair_low = pair.astype(LOW)
    is_decay = lane_below(DECAY_RANK)
    m_pair = jnp.where(
        is_decay, dot(g_decay, low.up_pair, NN) * (1.0 - pair * pair), dot(g_rate, low.up_pair, NN)
    ).astype(LOW)
    m_v = kept(dot(g_vup, low.up_value, NN), lane_below(DV)).astype(LOW)
    m_g = (dot(g_gate, low.up_gate, NN) * sig * (1.0 - sig)).astype(LOW)
    near = jnp.zeros_like(x)
    far = jnp.zeros_like(x)
    value_weights = jnp.concatenate([columns_ref[:, 2 * width :], low.value], 1)
    cut = DECAY_RANK + DA + 3 * width
    grads = (
        (2, g_r, columns_ref[:, :width], ((0, g_r),)),
        (3, kept(m_pair, is_decay), low.pair, ((3 * width, m_pair[:, :DECAY_RANK]),)),
        (4, g_k, columns_ref[:, width : 2 * width], ((width, g_k),)),
        (5, jnp.concatenate([g_v, m_v], 1), value_weights, ((2 * width, g_v), (cut, m_v[:, :DV]))),
        (6, kept(m_pair, ~is_decay), low.pair, ((3 * width + DECAY_RANK, m_pair[:, DECAY_RANK:]),)),
        (7, m_g, low.gate, ((cut + DV, m_g),)),
    )
    col_sums = []
    for slot, grad, weight, parts in grads:
        mix = cols_ref[slot : slot + 1]
        mixed = (normed + diff * mix).astype(LOW)
        total = dot(grad, weight, NT)
        for start, part in parts:
            sum_ref[start : start + part.shape[1]] += dot(part, mixed, TN)
        near = near + total
        far = far + total * mix
        col_sums.append(jnp.sum(total * diff, 0, keepdims=True))
    start = 0
    for mid, grad in (
        (pair_low[:, :DECAY_RANK], g_decay),
        (pair_low[:, DECAY_RANK:], g_rate),
        (vm_ref[:, :DV], g_vup),
        (sig.astype(LOW), g_gate),
    ):
        up_sum_ref[start : start + mid.shape[1]] += dot(mid, grad, TN)
        start += mid.shape[1]
    moved = far * keep
    back = near - far + rows_up(moved, edge[0:1])
    edge[0:1] = moved[0:1]
    back_ref[...] = back.astype(LOW)
    first = [jnp.sum(back * unit, 0, keepdims=True), jnp.sum(back, 0, keepdims=True)]
    sum_ref[sum_ref.shape[0] - 8 :] += jnp.concatenate(first + col_sums, 0)


def project_back(x, grads, mids, cols, weights, place, begins, per):
    blocks = place.shape[0]
    total = blocks * BLOCK
    rows = 2 * BLOCK
    steps = blocks // 2
    wide = x.shape[2]
    width = grads.shape[2]
    low_rank = DECAY_RANK + DA + DV + 128
    span = lambda w: pl.BlockSpec((rows, w), lambda i, *_: (steps - 1 - i, 0))
    shape = jax.ShapeDtypeStruct
    sums = [shape((3 * width + low_rank + 8, wide), F32), shape((low_rank, width), F32)]
    return pl.pallas_call(
        project_back_kernel,
        grid_spec=pltpu.PrefetchScalarGridSpec(
            num_scalar_prefetch=2,
            grid=(steps,),
            in_specs=[
                block_spec(per, 0, BLOCK, wide, blocks, True),
                block_spec(per, 1, BLOCK, wide, blocks, True),
                block_spec(per, -1, 16, wide, blocks, True),
                pl.BlockSpec((7, rows, width), lambda i, *_: (0, steps - 1 - i, 0)),
            ]
            + [span(m.shape[1]) for m in mids]
            + [whole_spec(cols)]
            + [whole_spec(w) for w in weights],
            out_specs=[span(wide)] + [whole_spec(s) for s in sums],
            scratch_shapes=[pltpu.VMEM((8, wide), F32)],
        ),
        out_shape=[shape((total, wide), LOW)] + sums,
        compiler_params=pltpu.CompilerParams(vmem_limit_bytes=56 * 1024 * 1024),
        cost_estimate=work(34),
    )(place, begins, x, x, x, grads, *mids, cols, *weights)


TALL = BLOCK + 16


def block_keeps(local_ref, begins_ref, j):
    begins = [begins_ref[i] for i in range(begins_ref.shape[0])]
    first = local_ref[j] * BLOCK
    after = jnp.float32(1.0)
    for b in begins:
        after = jnp.where(first + BLOCK == b, 0.0, after)
    return keep_rows(BLOCK, first, begins), after


def middle_kernel(
    per, local_ref, begins_ref, out_ref, tokens_ref, weight_ref, cols_ref, middle_ref, ffn_ref, rows_ref
):
    heads = out_ref.shape[0]
    rows = [jnp.concatenate([out_ref[h, j] for h in range(heads)], 1) for j in range(per)]
    rows = jnp.concatenate(rows, 0)
    rows_ref[...] = rows
    middle = tokens_ref[...].astype(F32) + dot(rows, weight_ref[...], NN)
    middle_ref[...] = middle
    unit, _ = norm_rows(middle)
    normed = unit * cols_ref[16:17] + cols_ref[17:18]
    c18 = cols_ref[18:19]
    extra_row = lax.broadcasted_iota(jnp.int32, (TALL - BLOCK, 1), 0)
    for j in range(per):
        main = normed[j * TALL : j * TALL + BLOCK]
        extra = normed[j * TALL + BLOCK : (j + 1) * TALL]
        keep, keep_after = block_keeps(local_ref, begins_ref, j)
        moved = rows_down(main, extra[0:1]) * keep
        ffn_ref[j * TALL : j * TALL + BLOCK] = (main + (moved - main) * c18).astype(LOW)
        after = extra + (main[BLOCK - 1 :] * keep_after - extra) * c18
        ffn_ref[j * TALL + BLOCK : (j + 1) * TALL] = jnp.where(extra_row == 1, after, 0.0).astype(LOW)


def middle_rows(out, tokens_ext, weight, cols, local, begins):
    _, per, _, _ = out.shape
    wide = weight.shape[0]
    shape = jax.ShapeDtypeStruct
    return pl.pallas_call(
        functools.partial(middle_kernel, per),
        grid_spec=pltpu.PrefetchScalarGridSpec(
            num_scalar_prefetch=2,
            grid=(1,),
            in_specs=[whole_spec(x) for x in (out, tokens_ext, weight, cols)],
            out_specs=[whole_spec(tokens_ext)] * 3,
        ),
        out_shape=[
            shape((per * TALL, wide), F32),
            shape((per * TALL, wide), LOW),
            shape((per * TALL, wide), LOW),
        ],
        compiler_params=pltpu.CompilerParams(vmem_limit_bytes=48 * 1024 * 1024),
        cost_estimate=work(6),
    )(local, begins, out, tokens_ext, weight, cols)


def with_extra(main, extra):
    per = main.shape[0] // BLOCK
    pieces = []
    for j in range(per):
        pieces += [main[j * BLOCK : (j + 1) * BLOCK], extra[j * 16 : (j + 1) * 16]]
    return pieces


def channel_kernel(
    xa_ref, xb_ref, ga_ref, gb_ref, ea_ref, eb_ref, key_ref, value_ref, hidden_ref, pre_ref, a_ref, b_ref
):
    rows = xa_ref.shape[0]
    x = jnp.concatenate([xa_ref[...], xb_ref[...]], 0)
    g = jnp.concatenate(with_extra(ga_ref, ea_ref) + with_extra(gb_ref, eb_ref), 0)
    key, value = key_ref[...], value_ref[...]
    active = jnp.maximum(dot(x, key, NN), 0.0)
    hidden_ref[...] = (active * active).astype(LOW)
    grad = (dot(g, value, NN) * 2.0 * active).astype(LOW)
    pre_ref[...] = grad
    back = dot(grad, key, NT)

    @pl.when(pl.program_id(0) == 0)
    def _():
        a_ref[...] = back[:rows]
        b_ref[...] = back[rows:]

    @pl.when(pl.program_id(0) > 0)
    def _():
        a_ref[...] += back[:rows]
        b_ref[...] += back[rows:]


def channel_mix(x, g, extra, key, value):
    rows, wide = x[0].shape
    columns = key.shape[1]
    part = columns // 4
    piece = pl.BlockSpec((2 * rows, part), lambda i: (0, i))
    shape = jax.ShapeDtypeStruct
    return pl.pallas_call(
        channel_kernel,
        grid=(4,),
        in_specs=[whole_spec(a) for a in (*x, *g, *extra)]
        + [pl.BlockSpec((wide, part), lambda i: (0, i))] * 2,
        out_specs=[piece, piece, whole_spec(x[0]), whole_spec(x[0])],
        out_shape=[
            shape((2 * rows, columns), LOW),
            shape((2 * rows, columns), LOW),
            shape((rows, wide), F32),
            shape((rows, wide), F32),
        ],
        compiler_params=pltpu.CompilerParams(vmem_limit_bytes=48 * 1024 * 1024),
        cost_estimate=work(8),
    )(*x, *g, *extra, key, value)


def main_rows(refs):
    pieces = []
    for ref in refs:
        for start in range(0, ref.shape[0], TALL):
            pieces.append(ref[start : start + BLOCK])
    return jnp.concatenate(pieces, 0)


def channel_grad_kernel(count, *refs):
    og, x = jnp.concatenate([r[...] for r in refs[:count]], 0), main_rows(refs[count : 2 * count])
    hidden, pre = main_rows(refs[2 * count : 2 * count + 2]), main_rows(refs[2 * count + 2 : 2 * count + 4])
    out = refs[2 * count + 4]
    columns = hidden.shape[1]
    out[:, :columns] = dot(og, hidden, TN).astype(LOW)
    out[:, columns : 2 * columns] = dot(x, pre, TN).astype(LOW)


def channel_grads(og, x, hidden, pre, extra):
    wide = og[0].shape[1]
    part = 256
    columns = hidden[0].shape[1]
    return pl.pallas_call(
        functools.partial(channel_grad_kernel, len(og)),
        grid=(wide // part,),
        in_specs=[pl.BlockSpec((a.shape[0], part), lambda i: (0, i)) for a in (*og, *x)]
        + [whole_spec(h) for h in (*hidden, *pre)],
        out_specs=pl.BlockSpec((part, 2 * columns + extra), lambda i: (i, 0)),
        out_shape=jax.ShapeDtypeStruct((wide, 2 * columns + extra), LOW),
        compiler_params=pltpu.CompilerParams(vmem_limit_bytes=48 * 1024 * 1024),
        cost_estimate=work(9),
    )(*og, *x, *hidden, *pre)


def output_grad_kernel(count, which_ref, *refs):
    rows, grads, out = refs[:count], refs[count : 2 * count], refs[-1]
    left = jnp.concatenate([r[...] for r in rows], 0)
    right = jnp.concatenate([r[...] for r in grads], 0)
    out[...] = dot(left, right, TN).astype(LOW)


def output_grads(rows, grads, which, room):
    tall, wide = rows[0].shape
    part = 256
    last = room.shape[1] // part - 1
    return pl.pallas_call(
        functools.partial(output_grad_kernel, len(rows)),
        grid_spec=pltpu.PrefetchScalarGridSpec(
            num_scalar_prefetch=1,
            grid=(wide // part,),
            in_specs=[pl.BlockSpec((tall, part), lambda i, w: (0, i))] * len(rows)
            + [pl.BlockSpec((tall, part), lambda i, w: (0, w[0]))] * len(grads)
            + [pl.BlockSpec(memory_space=pl.ANY)],
            out_specs=pl.BlockSpec((part, part), lambda i, w: (i, last)),
        ),
        out_shape=jax.ShapeDtypeStruct(room.shape, LOW),
        input_output_aliases={2 * len(rows) + 1: 0},
        compiler_params=pltpu.CompilerParams(vmem_limit_bytes=48 * 1024 * 1024),
        cost_estimate=work(2),
    )(which, *rows, *grads, room)


def middle_back_kernel(
    per, local_ref, begins_ref, near_ref, core_ref, far_ref, middle_ref, og_ref, weight_ref, cols_ref,
    grad_ref, low_ref, heads_ref, sums_ref,
):
    c16, c17, c18 = [cols_ref[i : i + 1] for i in (16, 17, 18)]
    grad_in = near_ref[...] + core_ref[...] + far_ref[...].astype(F32)
    sums = [jnp.zeros((1, c16.shape[1]), F32) for _ in range(3)]
    lows = []
    for j in range(per):
        start = j * TALL
        grad, after = grad_in[start : start + BLOCK], grad_in[start + BLOCK + 1 : start + BLOCK + 2]
        keep, keep_after = block_keeps(local_ref, begins_ref, j)
        ahead = rows_up(grad * keep, after * keep_after)
        grad_normed = grad + (ahead - grad) * c18
        unit, scale = norm_rows(middle_ref[start : start + BLOCK])
        prior, _ = norm_rows(middle_ref[start + BLOCK : start + TALL])
        normed = unit * c16 + c17
        diff = rows_down(normed, prior[0:1] * c16 + c17) * keep - normed
        for i, value in enumerate((grad_normed * unit, grad_normed, grad * diff)):
            sums[i] = sums[i] + jnp.sum(value, 0, keepdims=True)
        og = og_ref[j * BLOCK : (j + 1) * BLOCK].astype(F32)
        total = og + norm_back(grad_normed, unit, scale, c16)
        grad_ref[j * BLOCK : (j + 1) * BLOCK] = total
        lows.append(total.astype(LOW))
        low_ref[start : start + BLOCK] = lows[-1]
        low_ref[start + BLOCK : start + TALL] = jnp.zeros((TALL - BLOCK, c16.shape[1]), LOW)
    sums_ref[...] = jnp.concatenate(sums + [jnp.zeros((5, c16.shape[1]), F32)], 0)
    out = dot(jnp.concatenate(lows, 0), weight_ref[...], NT).astype(LOW)
    width = heads_ref.shape[2]
    for h in range(heads_ref.shape[0]):
        heads_ref[h] = out[:, h * width : (h + 1) * width]


def norm_back(grad, unit, scale, gain):
    grad = grad * gain
    return scale * (
        grad - jnp.mean(grad, -1, keepdims=True) - unit * jnp.mean(grad * unit, -1, keepdims=True)
    )


def middle_back(near, core, far, middle, og, weight, cols, local, begins, heads):
    tall, wide = near.shape
    per = tall // TALL
    shape = jax.ShapeDtypeStruct
    outs = [
        shape((per * BLOCK, wide), F32),
        shape((tall, wide), LOW),
        shape((heads, per * BLOCK, wide // heads), LOW),
        shape((8, wide), F32),
    ]
    operands = (near, core, far, middle, og, weight, cols)
    return pl.pallas_call(
        functools.partial(middle_back_kernel, per),
        grid_spec=pltpu.PrefetchScalarGridSpec(
            num_scalar_prefetch=2,
            grid=(1,),
            in_specs=[whole_spec(x) for x in operands],
            out_specs=[whole_spec(x) for x in outs],
        ),
        out_shape=outs,
        compiler_params=pltpu.CompilerParams(vmem_limit_bytes=48 * 1024 * 1024),
        cost_estimate=work(8),
    )(local, begins, *operands)


HEAD_AXES = ("hz", "hx")


def all_gather(x, axes):
    return lax.all_gather(x, axes, axis=0, tiled=True)


def steps_along(x, axis):
    size = lax.axis_size(axis)
    return [lax.ppermute(x, axis, [(i, i ^ k) for i in range(size)]) for k in range(1, size)]


def grown(x, axis):
    return jnp.concatenate([x] + steps_along(x, axis), 0)


def in_order(x, axes):
    strides, stride = {}, 1
    for axis in axes:
        strides[axis] = stride
        stride *= lax.axis_size(axis)
    index = jnp.arange(stride, dtype=jnp.int32)
    place, below = jnp.zeros((), jnp.int32), stride
    for axis in ("ys", "core") + HEAD_AXES:
        if axis in axes:
            below //= lax.axis_size(axis)
            there = (index // below) % lax.axis_size(axis)
            place = place + (there ^ lax.axis_index(axis)) * strides[axis]
    x = taken_blocks(x, place)
    return x.reshape((x.shape[0] * x.shape[1],) + x.shape[2:])


def swap(x, axis):
    return lax.ppermute(x, axis, [(0, 1), (1, 0)])


def seq_gather(x):
    if lax.axis_size("ys") != 2:
        return list(lax.all_gather(x, ("ys", "core"), axis=0))
    far = swap(x, "ys")
    return [x, swap(x, "core"), far, swap(far, "core")]


def seq_return(near, core, far, diagonal):
    return swap(core, "core"), swap((far + swap(diagonal, "core")).astype(LOW), "ys")


def seq_step(x, axis):
    if lax.axis_size("ys") != 2:
        if axis == "ys":
            return x
        return lax.psum_scatter(x, ("ys", "core"), scatter_dimension=0, tiled=True)[0].astype(F32)
    if axis == "ys":
        x = x.reshape((2, 2) + x.shape[1:])
    index = lax.axis_index(axis)
    sent = swap(lax.dynamic_index_in_dim(x, 1 - index, 0, keepdims=False).astype(LOW), axis)
    return lax.dynamic_index_in_dim(x, index, 0, keepdims=False).astype(F32) + sent.astype(F32)


def taken_blocks(x, table):
    return x.at[table].get(mode="promise_in_bounds")


def start_flags(positions, begins):
    return jnp.any(positions[..., None] == begins, -1).astype(F32)


def body(
    tokens,
    leading_layer_value,
    output_gradient,
    lengths,
    sequence_block_of,
    stored_block_of,
    channel_settings,
    receptance_matrix,
    key_matrix,
    value_matrix,
    output_matrix,
    branch_down_weight,
    branch_up_weight,
    channel_key_weight,
    channel_value_weight,
):
    rows_here, wide = tokens.shape
    per = rows_here // BLOCK
    ys, heads_axis = lax.axis_size("ys"), lax.axis_size("hz") * lax.axis_size("hx")
    seqs = 2 * ys
    head = lax.axis_index(HEAD_AXES)
    core = lax.axis_index("core")
    width = wide // heads_axis
    weight_rows = receptance_matrix.shape[0]
    low_rank = branch_down_weight.shape[1]
    order, home = sequence_block_of[0], stored_block_of[0]
    blocks = order.shape[0]
    begins = (jnp.cumsum(lengths[0]) - lengths[0]).astype(jnp.int32)
    splits = (DECAY_RANK, DECAY_RANK + DA, DECAY_RANK + DA + DV)

    og_first = output_gradient.reshape(per, BLOCK, wide)[:, 0]
    pad = jnp.zeros((16 - per, wide), LOW)
    place = home
    local = lax.dynamic_slice_in_dim(order, head * per, per)
    before_place = taken_blocks(place, jnp.maximum(local - 1, 0))
    after_place = taken_blocks(place, jnp.minimum(local + 1, blocks - 1))
    group = all_gather(jnp.concatenate([tokens, og_first, pad], 0)[None], HEAD_AXES)
    og_parts = seq_gather(output_gradient)

    quarter = channel_key_weight.shape[1] // seqs
    pair = jnp.stack([channel_key_weight, channel_value_weight], 0).reshape(2, weight_rows, seqs, quarter)
    pair = lax.all_to_all(
        pair.transpose(2, 0, 1, 3), ("ys", "core"), split_axis=0, concat_axis=0, tiled=True
    )
    to_heads = jnp.concatenate(
        [
            leading_layer_value.reshape(rows_here, heads_axis, width).transpose(1, 0, 2),
            jnp.stack([receptance_matrix, key_matrix, value_matrix], 1)
            .reshape(weight_rows * 3, heads_axis, width)
            .transpose(1, 0, 2),
        ],
        1,
    )
    def rank_columns(weight):
        return jnp.split(weight, (DECAY_RANK + DA, DECAY_RANK + DA + DV), 1)

    (down_pair, down_value, down_gate), (up_pair, up_value, up_gate) = [
        rank_columns(w) for w in (branch_down_weight, branch_up_weight)
    ]
    count = channel_settings.shape[1]
    blank = [jnp.zeros((weight_rows, n), LOW) for n in (32 - count, 32)]
    small = jnp.concatenate(
        [
            down_pair, down_gate, down_value, channel_settings, blank[0], up_value, blank[1],
            up_pair, up_gate,
        ],
        1,
    )[None]
    to_heads = lax.all_to_all(to_heads, HEAD_AXES, split_axis=0, concat_axis=0, tiled=True)
    for axis in HEAD_AXES + ("ys", "core"):
        small = grown(small, axis)
    small = in_order(small, HEAD_AXES + ("ys", "core"))
    first_group = to_heads[:, :rows_here]
    columns = to_heads[:, rows_here:].reshape(1, heads_axis * weight_rows, 3 * width)
    columns = in_order(grown(grown(columns, "ys"), "core"), ("ys", "core"))
    out_shards = grown(grown(output_matrix[None], "hz"), "hx")
    settings = small[:, 256 + DV : 256 + DV + count].astype(F32).T
    up = lax.dynamic_slice_in_dim(small, head * width, width, 0)
    own = lax.dynamic_slice_in_dim(settings, head * width, width, 1)
    own = jnp.concatenate([own[13:16], own[8:13]], 0)
    group, columns, small, settings, up, own, og_parts, out_shards, pair = lax.optimization_barrier(
        (group, columns, small, settings, up, own, og_parts, out_shards, pair)
    )
    out_shards = grown(out_shards, "ys")
    weights = [columns, small, up]

    def gathered(half):
        return all_gather(half[None], HEAD_AXES).transpose(1, 0, 2, 3)

    whole_quarter = quarter == wide
    if whole_quarter:
        every = all_gather(pair.transpose(1, 0, 2, 3).reshape(1, -1, weight_rows, wide), HEAD_AXES)
    else:
        every = (gathered(pair[:, 0]), gathered(pair[:, 1]))

    parts, gate, pre, first, *mids = project(
        group, first_group, settings, own, weights, place, home, begins, per
    )
    after_seq = local + 1
    after_live = (after_seq < blocks).astype(LOW)[:, None]
    stored = group[:, :rows_here].reshape(-1, BLOCK, wide)
    row_before = taken_blocks(stored[:, BLOCK - 1], before_place)
    row_after = taken_blocks(stored[:, 0], after_place)
    og_rows = group[:, rows_here : rows_here + per].reshape(-1, wide)
    og_after = taken_blocks(og_rows, after_place) * after_live
    none = jnp.zeros((per, 14, wide), LOW)
    og_extra = jnp.concatenate([none[:, :1], og_after[:, None], none], 1).reshape(-1, wide)
    extra_parts = seq_gather(og_extra)
    parts, og_parts, extra_parts, out_shards = lax.optimization_barrier(
        (parts, og_parts, extra_parts, out_shards)
    )
    out_shards = grown(out_shards, "core")
    out_in, joined, scanned, states, mats = scan_forward(parts, gate, own, begins, PASSES)

    before, follow = jnp.maximum(order - 1, 0), jnp.minimum(order + 1, blocks - 1)
    in_blocks = out_in.reshape(blocks, BLOCK, width)
    extended = jnp.concatenate(
        [
            taken_blocks(in_blocks, order),
            taken_blocks(in_blocks[:, BLOCK - 1], before)[:, None],
            taken_blocks(in_blocks[:, 0], follow)[:, None],
            jnp.zeros((blocks, 14, width), LOW),
        ],
        1,
    )
    extended, every = lax.optimization_barrier((extended, every))
    out_ext = lax.all_to_all(
        extended.reshape(heads_axis, per, TALL, width), HEAD_AXES, split_axis=0, concat_axis=0, tiled=True
    )
    if whole_quarter:
        key_part, value_part = [
            x.reshape(wide, quarter)
            for x in jnp.moveaxis(every.reshape(heads_axis, 2, seqs, weight_rows, wide), 0, 2)
        ]
    else:
        key_part, value_part = [x.reshape(wide, quarter) for x in every]
    out_weight = in_order(out_shards, HEAD_AXES + ("ys", "core"))
    out_ext, key_part, value_part, out_weight = lax.optimization_barrier(
        (out_ext, key_part, value_part, out_weight)
    )
    tokens_b = tokens.reshape(per, BLOCK, wide)
    tokens_ext = jnp.concatenate([tokens_b, row_before[:, None], row_after[:, None], none], 1)
    middle, ffn_in, out_rows = middle_rows(
        out_ext, tokens_ext.reshape(-1, wide), out_weight, settings, local, begins
    )
    ffn_parts = seq_gather(ffn_in)
    if whole_quarter:
        *near, own_part, core_part = channel_mix(
            ffn_parts[:2], og_parts[:2], extra_parts[:2], key_part, value_part
        )
        ffn_parts[2:], near, own_part, core_part, out_rows = lax.optimization_barrier(
            (ffn_parts[2:], near, own_part, core_part, out_rows)
        )
        *far, far_part, diagonal = channel_mix(
            ffn_parts[2:], og_parts[2:], extra_parts[2:], key_part, value_part
        )
        came_core, came_far = seq_return(own_part, core_part, far_part, diagonal)
        grads_here = channel_grads(
            og_parts, ffn_parts, (near[0], far[0]), (near[1], far[1]), wide // seqs
        )
        came_far, grads_here = lax.optimization_barrier((came_far, grads_here))
        hidden = [near[0], far[0]]
    else:
        rows = jnp.concatenate(ffn_parts, 0)
        og_rows = jnp.concatenate(
            [
                jnp.concatenate([g.reshape(per, BLOCK, wide), x.reshape(per, 16, wide)], 1).reshape(-1, wide)
                for g, x in zip(og_parts, extra_parts)
            ],
            0,
        )
        active = jax.nn.relu(dot(rows, key_part, NN))
        hidden = [(active * active).astype(LOW)]
        grad_pre = (dot(og_rows, value_part, NN) * 2.0 * active).astype(LOW)
        own_part = dot(grad_pre, key_part, NT).reshape(seqs, per * TALL, wide)
        own_part = lax.psum_scatter(own_part, ("ys", "core"), scatter_dimension=0, tiled=True)[0]
        came_core, came_far = jnp.zeros_like(own_part), jnp.zeros_like(ffn_in)
        is_main = (jnp.arange(rows.shape[0]) % TALL < BLOCK).astype(LOW)[:, None]
        grads_here = [dot(og_rows * is_main, hidden[0], TN), dot(rows * is_main, grad_pre, TN)]
    grad_middle, middle_low, grad_out, cols_ffn = middle_back(
        own_part, came_core, came_far, middle, output_gradient, out_weight, settings, local, begins, heads_axis
    )
    cols_ffn = cols_ffn[:3]
    grad_heads = lax.all_to_all(grad_out, HEAD_AXES, split_axis=0, concat_axis=0, tiled=True)
    out_parts, low_parts = seq_gather(out_rows), seq_gather(middle_low)
    which = lax.axis_index(("ys", "core"))
    if whole_quarter:
        grads_here = output_grads(out_parts, low_parts, which[None], grads_here)
    else:
        right = jnp.concatenate(low_parts, 0).reshape(seqs * per * TALL, seqs, -1)
        right = lax.dynamic_index_in_dim(right, which, 1, keepdims=False)
        grads_here.append(dot(jnp.concatenate(out_parts, 0), right, TN))
        grads_here = jnp.concatenate(grads_here, 1).astype(LOW)
    grad_heads, grads_here = lax.optimization_barrier((grad_heads, grads_here))
    grads_here = lax.psum_scatter(grads_here, HEAD_AXES, scatter_dimension=0, tiled=True)

    scan_grads, first_grad, cols_scan = scan_backward(
        parts, joined, scanned, gate, grad_heads.reshape(blocks, BLOCK, width), pre, first, own, states,
        mats, home, begins, PASSES,
    )
    first_grad = taken_blocks(first_grad.reshape(blocks, BLOCK, width), order)
    first_value_grad = lax.all_to_all(
        first_grad.reshape(heads_axis, rows_here, width), HEAD_AXES, split_axis=0, concat_axis=2, tiled=True
    ).reshape(rows_here, wide).astype(F32)

    back, down_sums, up_sums = project_back(
        group, scan_grads, mids, settings, weights, place, begins, per
    )
    back = taken_blocks(back.reshape(blocks, BLOCK, wide), order).reshape(-1, wide)
    back, grads_here, first_value_grad = lax.optimization_barrier((back, grads_here, first_value_grad))
    back = lax.psum_scatter(back, HEAD_AXES, scatter_dimension=0, tiled=True).astype(F32)
    value_sum, key_sum, out_sum = jnp.split(grads_here.astype(F32), (quarter, 2 * quarter), 1)

    share = wide // seqs
    thin = low_rank // seqs
    fold = heads_axis // seqs

    def over_ys(sums):
        down_sums, up_sums, own_cols = sums
        own_cols = lax.dynamic_update_slice(jnp.zeros((8, wide), F32), own_cols, (0, head * width))
        rows_out = jnp.concatenate([down_sums, own_cols, cols_ffn], 0)
        rows_out = jnp.pad(rows_out, ((0, -rows_out.shape[0] % 16), (0, 0)))
        rows_out = rows_out.astype(LOW).reshape(-1, seqs, share).transpose(1, 0, 2)
        both = jnp.concatenate(
            [rows_out, up_sums.astype(LOW).reshape(seqs, thin * width // share, share)], 1
        )
        return seq_step(both, "ys")

    def over_core(x):
        return seq_step(x, "core")

    def to_owners(x):
        rows_out_count = x.shape[0] - thin * width // share
        rows_out, up_sums = x[:rows_out_count], x[rows_out_count:].reshape(thin, width)
        rows_low = rows_out.astype(LOW)
        squares = rows_low[: 3 * width].reshape(3 * width, fold, width)
        mixed = rows_low[3 * width : 3 * width + low_rank].reshape(seqs, thin, fold, width)
        mixed = mixed.transpose(0, 2, 1, 3).reshape(heads_axis, thin, width)
        cols_part = rows_low[3 * width + low_rank :][:count].reshape(count, heads_axis, -1)
        cols_part = jnp.pad(
            cols_part.transpose(1, 0, 2), ((0, 0), (0, -count % 8), (0, width - cols_part.shape[2]))
        )
        mixed = lax.all_to_all(
            jnp.concatenate([mixed, cols_part], 1), HEAD_AXES, split_axis=0, concat_axis=0, tiled=True
        )
        came = []
        for k in range(fold):
            sent = lax.dynamic_index_in_dim(squares, (head + k) % fold, 1, keepdims=False)
            came.append(
                lax.ppermute(
                    sent, every_axis, [(q * heads_axis + h, owner(q, h, (h + k) % fold)) for q, h in pairs]
                )
            )
        return up_sums, mixed, came

    every_axis = ("ys", "core") + HEAD_AXES
    pairs = [(q, h) for q in range(seqs) for h in range(heads_axis)]

    def owner(q, h, j):
        return (h // fold) * heads_axis + q * fold + j

    up_sums, mixed, came = to_owners(over_core(over_ys((down_sums, up_sums, cols_scan))))
    unit, scale = norm_rows(tokens.astype(F32))
    tokens_grad = grad_middle + norm_back(back, unit, scale, settings[0])
    mixed = jnp.sum(mixed.astype(F32), 0)
    channel_grad = mixed[thin : thin + count, :weight_rows].T
    down_grad = lax.ppermute(
        mixed[:thin].astype(LOW), every_axis, [(q * heads_axis + h, owner(q, h, h % fold)) for q, h in pairs]
    ).T.astype(F32)
    outs = [dot(h, value_part, NT) for h in hidden]
    main_middle = middle.reshape(per, TALL, wide)[:, :BLOCK].reshape(rows_here, wide)

    def main_of(x):
        return x.reshape(-1, per, TALL, wide)[:, :, :BLOCK].reshape(-1, rows_here, wide)

    if whole_quarter:
        near, far = [main_of(x) for x in outs]
        came_core, came_far = seq_return(near[0], near[1], far[0], far[1])
        layer_out = main_middle + near[0] + came_core + came_far.astype(F32)
    else:
        layer_out = main_middle + lax.psum_scatter(
            main_of(outs[0]), ("ys", "core"), scatter_dimension=0, tiled=True
        )[0]
    came = jnp.stack(came, 0)
    came = taken_blocks(came, (head - jnp.arange(fold, dtype=jnp.int32)) % fold)
    came = came.reshape(fold, 3, width, width).transpose(1, 3, 0, 2).reshape(3, width, share)
    recept_grad, key_grad, value_grad = [came[i].astype(F32) for i in range(3)]
    up_grad = up_sums.T
    return (
        layer_out.astype(LOW),
        tokens_grad,
        first_value_grad,
        channel_grad,
        recept_grad,
        key_grad,
        value_grad,
        out_sum,
        down_grad,
        up_grad,
        key_sum,
        value_sum,
    )


def solution(mesh):
    seqs, heads = mesh.devices.shape
    split = Mesh(mesh.devices.reshape(seqs // 2, 2, 4, heads // 4), ("ys", "core") + HEAD_AXES)
    rows = P(("ys", "core") + HEAD_AXES, None)
    table = P(("ys", "core"), None)
    square = P(HEAD_AXES, ("ys", "core"))
    return jax.shard_map(
        body,
        mesh=split,
        in_specs=(rows,) * 3 + (table,) * 3 + (rows,) * 9,
        out_specs=(rows,) * 4 + (square,) * 8,
        check_vma=False,
    )
```

time: 3370 us -> 503 us (0.15); the launches traced: 3310 us -> 496 us
  waiting for transfers between devices: 1480 us -> 145 us
  local copies, waits for them, and re-layouts: 830 us -> 71.3 us
  matrix products: 430 us -> 5.86 us
  blocking collectives: 334 us -> 0 us
  other arithmetic: 200 us -> 23.1 us
  Pallas kernels: 0 us -> 171 us
  starting transfers between devices: 19.6 us -> 64.9 us
    reduce_scatter x15 -> x2, waiting for transfers between devices: 1230 us -> 24.6 us  [the longest x1 19.9 us: body(): lax.psum_scatter(back, HEAD_AXES, scatter_dimension=0, tiled=True)]
    pad x45 -> x0, local copies, waits for them, and re-layouts: 432 us -> none  [the longest x43 430 us: span_scan(): _, reached = lax.associative_scan(combine, (through, offset), axis=0)]
    dot_general x127 -> x2, matrix products: 406 us -> 5.86 us  [dot(): return lax.dot_general(a, b, dims, preferred_element_type=F32)]
    all_gather x7 -> x0, blocking collectives: 334 us -> none  [the longest x1 70.6 us: body(): lax.all_gather(branch_up_weight, ('seq', 'head'), axis=0, tiled=True)]
    all_to_all x4 -> x6, waiting for transfers between devices: 201 us -> 2.33 us  [the longest x1 1.62 us: body(): lax.all_to_all(to_heads, HEAD_AXES, split_axis=0, concat_axis=0, tiled=True)]
    pallas_call x0 -> x10, Pallas kernels: none -> 171 us  [the longest x1 50.3 us: scan_backward(): pl.pallas_call(functools.partial(scan_backward_kernel, heads, p), grid_sp...]
    ppermute x0 -> x40, waiting for transfers between devices: none -> 89.6 us  [the longest x23 60.9 us: swap(): return lax.ppermute(x, axis, [(0, 1), (1, 0)])]
    convert_element_type x19 -> x1, local copies, waits for them, and re-layouts: 70.7 us -> 0.05 us  [seq_step(): lax.dynamic_index_in_dim(x, 1 - index, 0, keepdims=False).astype(LOW)]
  transfers between devices with their start and end apart: 28 -> 50, of which waited for: 21 -> 21; matrix products, arithmetic and copies ran while one was open for 15% -> 16% of each run, Pallas kernels for 0% -> 32%
where the time goes in v1:
time: 503 us; the launch traced here: 496 us
  Pallas kernels  171 us (34%)
  waiting for transfers between devices  145 us (29%)
  local copies, waits for them, and re-layouts  71.3 us (14%)
  starting transfers between devices  64.9 us (13%)
  other arithmetic  23.1 us (5%)
  between operations  15.3 us (3%)
  matrix products  5.86 us (1%)
    ppermute x23, waiting for transfers between devices, swap(): return lax.ppermute(x, axis, [(0, 1), (1, 0)])  60.9 us
    pallas_call x1, Pallas kernels, scan_backward(): pl.pallas_call(functools.partial(scan_backward_kernel, heads, p), grid_sp...  50.3 us
    pallas_call x1, Pallas kernels, scan_forward(): pl.pallas_call(functools.partial(scan_forward_kernel, heads, p), grid_spe...  34.6 us
    pallas_call x1, Pallas kernels, project_back(): pl.pallas_call(project_back_kernel, grid_spec=pltpu.PrefetchScalarGridSpe...  32 us
    all_gather x2, waiting for transfers between devices, all_gather(): return lax.all_gather(x, axes, axis=0, tiled=True)  28.2 us
    ppermute x14, waiting for transfers between devices, steps_along(): lax.ppermute(x, axis, [(i, i ^ k) for i in range(size)])  21.1 us
    unnamed x142, local copies, waits for them, and re-layouts  20 us
    reduce_scatter x1, waiting for transfers between devices, body(): lax.psum_scatter(back, HEAD_AXES, scatter_dimension=0, tiled=True)  19.9 us
  transfers between devices with their start and end apart: 50, of which 21 were waited for; matrix products, arithmetic and copies ran while one was open for 16% of the time, Pallas kernels for 32%

profile of v1, /device:TPU:4, one launch (start us, length us, event | category | flops | bytes accessed | tf_op | source)
XLA Modules:
  0.0 496.0 jit_solution(13146357663030124227)
XLA Ops:
  8.3 2.0 maximum_maximum_fusion.1
  10.6 1.6 collective-permute-start.2
  12.3 2.6 collective-permute-start.3
  15.8 3.5 collective-permute-start.12
  21.1 3.5 all-to-all-start
  27.1 3.7 collective-permute-start.13
  31.4 1.5 collective-permute-start.5
  34.8 2.6 collective-permute-done.5
  38.2 1.5 collective-permute-start.6
  39.8 9.8 %collective-permute-done.6 = bf16[8,32,640]{2,1,0:T(8,128)(2,1)S(1)} collective-permute-done((bf16[8,32,640]{2,1,0:T(8,128)(2,1)S(1)}, bf16[8,32,640]{2,1,0:T(8,128)(2,1)S(1)}, u32[]{:S(2)}, u32[]{:S(2)}) %collective-permute-start.6) | collective-permute-done | bytes 327712 | tf_op jit(solution)/shard_map/ppermute | solution.py:993
  51.1 4.2 collective-permute-done.13
  56.0 1.5 collective-permute-start.14
  57.5 1.6 all-to-all-done
  59.1 4.6 all-to-all-start.1
  65.5 2.1 constant_dynamic-update-slice_fusion.11
  67.6 3.1 gather_fusion.1
  70.7 4.5 collective-permute-done
  77.4 1.6 constant_dynamic-slice_fusion.2.up_ref
  80.3 1.6 gather_fusion
  81.9 25.1 %all-gather.6.cloned.1.call-done = bf16[2176,1024]{1,0:T(8,128)(2,1)} async-done(((bf16[272,1024]{1,0:T(8,128)(2,1)}), bf16[2176,1024]{1,0:T(8,128)(2,1)}) %all-gather.6.cloned.1.call-update) | async-done | bytes 4456464 | tf_op jit(solution)/shard_map/all_gather | solution.py:988
  107.0 1.9 copy.202
  113.4 1.5 collective-permute-start.16
  115.0 1.9 slice.171.fa_ref.fb_ref
  117.7 18.6 %shard_map.238 = (bf16[6,2048,128]{2,1,0:T(8,128)(2,1)}, f32[2048,128]{1,0:T(8,128)}, f32[5,2048,128]{2,1,0:T(8,128)}, bf16[2048,128]{1,0:T(8,128)(2,1)}, f32[20...) custom-call(s32[16]{0:T(128)} %bitcast.196, s32[16]{0:T(128)} %bitcast.197, ...), custom_call_target="tpu_custom_call" | custom-call | bytes 60000 | tf_op jit(solution)/shard_map/pallas_call | solution.py:611
  138.2 34.6 %shard_map.239 = (bf16[2048,128]{1,0:T(8,128)(2,1)S(1)}, bf16[2048,128]{1,0:T(8,128)(2,1)S(1)}, f32[2048,128]{1,0:T(8,128)S(1)}, f32[32,128,128]{2,1,0:T(8,128)S(1)}, f32[32,8,128,128]{3,2,1,0:T(8,128)}) custom-call(s32[4]{0:T(128)S(1)} %copy-done.26, bf16[6,2048,128]{2,1,0:T(8,128)(2,1)} %get-tuple-element.99.parts_ref, f32[2048,128]{1,0:T(8,128)S(1)} %copy-done.4, ...), custom_call_target="tpu_custom_call" | custom-call | bytes 240000 | tf_op jit(solution)/shard_map/pallas_call | solution.py:249
  178.8 3.1 all-gather.4.cloned.1.call-done
  181.9 3.9 all-to-all-start.2
  185.9 2.7 slice.119
  190.9 2.7 pad_maximum_fusion
  193.6 2.3 gather_fusion.7
  195.9 3.4 copy.238
  199.3 2.5 fusion.60
  202.9 1.9 shard_map.240
  206.4 13.7 %collective-permute-done.20.xa_ref.refs_6_ = bf16[288,1024]{1,0:T(8,128)(2,1)S(1)} collective-permute-done((bf16[288,1024]{1,0:T(8,128)(2,1)S(1)}, bf16[288,1024]{1,0:T(8,128)(2,1)S(1)}, u32[]{:S(2)}, u32[]{:S(2)}) %collective-permute-start.20) | collective-permute-done | bytes 589856 | tf_op jit(solution)/shard_map/ppermute | solution.py:1017
  220.1 7.7 %shard_map.241 = (bf16[576,1024]{1,0:T(8,128)(2,1)S(1)}, bf16[576,1024]{1,0:T(8,128)(2,1)S(1)}, f32[288,1024]{1,0:T(8,128)S(1)}, f32[288,1024]{1,0:T(8,128)}) custom-call(bf16[288,1024]{1,0:T(8,128)(2,1)S(1)} %get-tuple-element.109.xa_ref.refs_4_, bf16[288,1024]{1,0:T(8,128)(2,1)S(1)} %collective-permute-done.22.xb_ref.refs_5_, ...), custom_call_target="tpu_custom_call" | custom-call | bytes 24000 | tf_op jit(solution)/shard_map/pallas_call | solution.py:841
  228.8 7.8 %shard_map.242 = (bf16[576,1024]{1,0:T(8,128)(2,1)S(1)}, bf16[576,1024]{1,0:T(8,128)(2,1)S(1)}, f32[288,1024]{1,0:T(8,128)S(1)}, f32[288,1024]{1,0:T(8,128)}) custom-call(bf16[288,1024]{1,0:T(8,128)(2,1)S(1)} %collective-permute-done.20.xa_ref.refs_6_, bf16[288,1024]{1,0:T(8,128)(2,1)S(1)} %collective-permute-done.21.xb_ref.refs_7_, ...), custom_call_target="tpu_custom_call" | custom-call | bytes 24000 | tf_op jit(solution)/shard_map/pallas_call | solution.py:841
  237.2 3.5 collective-permute-done.27
  241.6 1.5 collective-permute-start.30
  243.0 8.8 %shard_map.243.refs_8_ = bf16[1024,2304]{1,0:T(8,128)(2,1)} custom-call(bf16[256,1024]{1,0:T(8,128)(2,1)S(1)} %copy-done.1, bf16[256,1024]{1,0:T(8,128)(2,1)S(1)} %copy-done.11, bf16[256,1024]{1,0:T(8,128)(2,1)S(1)} %copy-done.9, bf16[256,1024]{1,0:T(8,128)(2,1)S(1)} %copy-done.13, bf16[288,1024]{1,0:T(8,128)(2,1)S(1)} %get-tuple-element.109.xa_ref.refs_4_, ...), custom_call_target="tpu_custom_call" | custom-call | bytes 27000 | tf_op jit(solution)/shard_map/pallas_call | solution.py:879
  251.8 5.4 %collective-permute-done.28.far_ref = bf16[288,1024]{1,0:T(8,128)(2,1)S(1)} collective-permute-done((bf16[288,1024]{1,0:T(8,128)(2,1)S(1)}, bf16[288,1024]{1,0:T(8,128)(2,1)S(1)}, u32[]{:S(2)}, u32[]{:S(2)}) %collective-permute-start.28) | collective-permute-done | bytes 589856 | tf_op jit(solution)/shard_map/ppermute | solution.py:1017
  257.2 4.7 shard_map.244
  263.7 5.7 %all-to-all-start.3 = ((bf16[8,256,128]{2,1,0:T(8,128)(2,1)}), bf16[8,256,128]{2,1,0:T(8,128)(2,1)}, u32[]{:S(2)}, u32[]{:S(2)}) async-start(bf16[8,256,128]{2,1,0:T(8,128)(2,1)} %copy-done.22), calls=%async_computation.3 | async-start | bytes 1048576 | tf_op jit(solution)/shard_map/all_to_all | solution.py:1235
  270.3 11.6 %collective-permute-done.33.refs_6_ = bf16[288,1024]{1,0:T(8,128)(2,1)S(1)} collective-permute-done((bf16[288,1024]{1,0:T(8,128)(2,1)S(1)}, bf16[288,1024]{1,0:T(8,128)(2,1)S(1)}, u32[]{:S(2)}, u32[]{:S(2)}) %collective-permute-start.33) | collective-permute-done | bytes 589856 | tf_op jit(solution)/shard_map/ppermute | solution.py:1017
  281.9 2.1 collective-permute-done.34.refs_7_
  284.0 4.4 shard_map.245
  288.5 50.3 %shard_map.246 = (bf16[7,2048,128]{2,1,0:T(8,128)(2,1)}, bf16[2048,128]{1,0:T(8,128)(2,1)}, f32[8,128]{1,0:T(8,128)}) custom-call(s32[16]{0:T(128)} %bitcast.198, s32[4]{0:T(128)} %bitcast_subtract_fusion.begins_ref, bf16[6,2048,128]{2,1,0:T(8,128)(2,1)} %get-tuple-element.99.parts_ref, bf16[2048,128]{1,0:T(8,128)(2,1)} %copy-done.21, ...), custom_call_target="tpu_custom_call" | custom-call | bytes 180000 | tf_op jit(solution)/shard_map/pallas_call | solution.py:461
  338.8 2.4 gather_fusion.12
  341.2 5.7 %all-to-all-start.4 = ((bf16[8,256,128]{2,1,0:T(8,128)(2,1)}), bf16[8,256,128]{2,1,0:T(8,128)(2,1)S(1)}, u32[]{:S(2)}, u32[]{:S(2)}) async-start(bf16[8,256,128]{2,1,0:T(8,128)(2,1)} %bitcast.69), calls=%async_computation.5 | async-start | bytes 1048576 | tf_op jit(solution)/shard_map/all_to_all | solution.py:1253
  347.2 32.0 %shard_map.247 = (bf16[2048,1024]{1,0:T(8,128)(2,1)}, f32[680,1024]{1,0:T(8,128)}, f32[288,128]{1,0:T(8,128)}) custom-call(s32[16]{0:T(128)} %bitcast.199, s32[4]{0:T(128)} %bitcast_subtract_fusion.begins_ref, bf16[8,272,1024]{2,1,0:T(8,128)(2,1)} %bitcast.206, bf16[8,272,1024]{2,1,0:T(8,128)(2,1)} %bitcast.207, bf16[8,272,1024]{2,1,0:T(8,128)(2,1)} %bitcast.208, ...), custom_call_target="tpu_custom_call" | custom-call | bytes 102000 | tf_op jit(solution)/shard_map/pallas_call | solution.py:723
  379.1 5.1 %gather_fusion.11 = bf16[16,128,1024]{2,1,0:T(8,128)(2,1)} fusion(bf16[16,128,1024]{2,1,0:T(8,128)(2,1)} %bitcast.229, s32[1024]{0:T(1024)S(1)} %pad_clamp_fusion.5), kind=kCustom, calls=%fused_computation.11 | custom fusion | bytes 8388672 | tf_op jit(solution)/shard_map/gather | solution.py:1044
  385.6 4.7 reduce-scatter.3.cloned.1.call-done
  391.8 3.0 fusion.69
  394.8 1.5 fusion.61
  397.2 2.9 fusion.68
  408.4 15.1 %collective-permute-done.35 = bf16[2,740,256]{2,0,1:T(2,128)(2,1)S(1)} collective-permute-done((bf16[2,740,256]{2,0,1:T(2,128)(2,1)S(1)}, bf16[2,740,256]{2,0,1:T(2,128)(2,1)S(1)}, u32[]{:S(2)}, u32[]{:S(2)}) %collective-permute-start.35) | collective-permute-done | bytes 757792 | tf_op jit(solution)/shard_map/ppermute | solution.py:1017
  425.1 8.5 %collective-permute-done.25 = bf16[256,1024]{1,0:T(8,128)(2,1)S(1)} collective-permute-done((bf16[256,1024]{1,0:T(8,128)(2,1)S(1)}, bf16[256,1024]{1,0:T(8,128)(2,1)S(1)}, u32[]{:S(2)}, u32[]{:S(2)}) %collective-permute-start.25) | collective-permute-done | bytes 524320 | tf_op jit(solution)/shard_map/ppermute | solution.py:1017
  435.2 4.2 collective-permute-start.37
  439.5 2.5 collective-permute-start.38
  443.0 3.4 all-to-all-start.5
  447.0 3.7 collective-permute-done.38
  454.4 3.0 collective-permute-start.39
  458.1 3.8 collective-permute-done.39
  465.6 19.9 %reduce-scatter.5.cloned.1.call-done = bf16[256,1024]{1,0:T(8,128)(2,1)} async-done(((bf16[2048,1024]{1,0:T(8,128)(2,1)}), bf16[256,1024]{1,0:T(8,128)(2,1)}) %reduce-scatter.5.cloned.1.call-update) | async-done | bytes 524304 | tf_op jit(solution)/shard_map/reduce_scatter | solution.py:1262
  486.9 2.4 fusion.12
  (346 shorter events, 66.3 us)
Async XLA Ops:
  7.2 99.7 %all-gather.6.cloned.1.call-start = ((), (), s32[]{:S(2)}) async-start(), calls=%async_computation.11 | async-start | bytes 5013504 | tf_op jit(solution)/shard_map/all_gather | solution.py:988
  10.6 16.5 %collective-permute-start.2 = (bf16[1,32,640]{2,1,0:T(8,128)(2,1)S(1)}, bf16[1,32,640]{2,1,0:T(8,128)(2,1)S(1)}, u32[]{:S(2)}, u32[]{:S(2)}) collective-permute-start(bf16[1,32,640]{2,1,0:T(8,128)(2,1)S(1)} %bitcast.244), channel_id=1, source_target_pairs={{0,2},{2,0},{4,6},{6,4},{1,3},{3,1},{5,7},{7,5},{8,10},{10,8},{12,... | collective-permute-start | bytes 122888 | tf_op jit(solution)/shard_map/ppermute | solution.py:993
  12.3 18.6 %collective-permute-start.3 = (bf16[1,32,640]{2,1,0:T(8,128)(2,1)S(1)}, bf16[1,32,640]{2,1,0:T(8,128)(2,1)S(1)}, u32[]{:S(2)}, u32[]{:S(2)}) collective-permute-start(bf16[1,32,640]{2,1,0:T(8,128)(2,1)S(1)} %bitcast.245), channel_id=1, source_target_pairs={{0,4},{2,6},{4,0},{6,2},{1,5},{3,7},{5,1},{7,3},{8,12},{10,14},{12... | collective-permute-start | bytes 122888 | tf_op jit(solution)/shard_map/ppermute | solution.py:993
  14.9 16.5 %collective-permute-start.4 = (bf16[1,32,640]{2,1,0:T(8,128)(2,1)S(1)}, bf16[1,32,640]{2,1,0:T(8,128)(2,1)S(1)}, u32[]{:S(2)}, u32[]{:S(2)}) collective-permute-start(bf16[1,32,640]{2,1,0:T(8,128)(2,1)S(1)} %bitcast.246), channel_id=1, source_target_pairs={{0,6},{2,4},{4,2},{6,0},{1,7},{3,5},{5,3},{7,1},{8,14},{10,12},{12... | collective-permute-start | bytes 122888 | tf_op jit(solution)/shard_map/ppermute | solution.py:993
  15.1 35.4 %collective-permute-start.11 = (bf16[1,32,1024]{2,1,0:T(8,128)(2,1)S(1)}, bf16[1,32,1024]{2,1,0:T(8,128)(2,1)S(1)}, u32[]{:S(2)}, u32[]{:S(2)}) collective-permute-start(bf16[1,32,1024]{2,1,0:T(8,128)(2,1)S(1)} %bitcast.250), channel_id=1, source_target_pairs={{0,2},{2,0},{4,6},{6,4},{1,3},{3,1},{5,7},{7,5},{8,10},{10,8},{12,... | collective-permute-start | bytes 196616 | tf_op jit(solution)/shard_map/ppermute | solution.py:993
  15.8 35.3 %collective-permute-start.12 = (bf16[1,32,1024]{2,1,0:T(8,128)(2,1)S(1)}, bf16[1,32,1024]{2,1,0:T(8,128)(2,1)S(1)}, u32[]{:S(2)}, u32[]{:S(2)}) collective-permute-start(bf16[1,32,1024]{2,1,0:T(8,128)(2,1)S(1)} %bitcast.251), channel_id=1, source_target_pairs={{0,4},{2,6},{4,0},{6,2},{1,5},{3,7},{5,1},{7,3},{8,12},{10,14},{12... | collective-permute-start | bytes 196616 | tf_op jit(solution)/shard_map/ppermute | solution.py:993
  21.1 38.0 %all-to-all-start = ((bf16[8,352,128]{2,1,0:T(8,128)(2,1)}), bf16[8,352,128]{2,1,0:T(8,128)(2,1)S(1)}, u32[]{:S(2)}, u32[]{:S(2)}) async-start(bf16[8,352,128]{2,1,0:T(8,128)(2,1)} %pad_maximum_fusion.3), calls=%async_computation | async-start | bytes 1441792 | tf_op jit(solution)/shard_map/all_to_all | solution.py:1120
  27.1 28.2 %collective-permute-start.13 = (bf16[1,32,1024]{2,1,0:T(8,128)(2,1)S(1)}, bf16[1,32,1024]{2,1,0:T(8,128)(2,1)S(1)}, u32[]{:S(2)}, u32[]{:S(2)}) collective-permute-start(bf16[1,32,1024]{2,1,0:T(8,128)(2,1)S(1)} %bitcast.252), channel_id=1, source_target_pairs={{0,6},{2,4},{4,2},{6,0},{1,7},{3,5},{5,3},{7,1},{8,14},{10,12},{12... | collective-permute-start | bytes 196616 | tf_op jit(solution)/shard_map/ppermute | solution.py:993
  30.8 34.4 %collective-permute-start.9 = (bf16[256,1024]{1,0:T(8,128)(2,1)S(1)}, bf16[256,1024]{1,0:T(8,128)(2,1)S(1)}, u32[]{:S(2)}, u32[]{:S(2)}) collective-permute-start(bf16[256,1024]{1,0:T(8,128)(2,1)S(1)} %copy-done.1), channel_id=1, source_target_pairs={{0,16},{16,0},{1,17},{17,1},{2,18},{18,2},{3,19},{19,3},{4,20},{20... | collective-permute-start | bytes 1572872 | tf_op jit(solution)/shard_map/ppermute | solution.py:1017
  31.4 6.1 %collective-permute-start.5 = (bf16[4,32,640]{2,1,0:T(8,128)(2,1)S(1)}, bf16[4,32,640]{2,1,0:T(8,128)(2,1)S(1)}, u32[]{:S(2)}, u32[]{:S(2)}) collective-permute-start(bf16[4,32,640]{2,1,0:T(8,128)(2,1)S(1)} %pad_maximum_fusion.9), channel_id=1, source_target_pairs={{0,1},{1,0},{2,3},{3,2},{4,5},{5,4},{6,7},{7,6},{8,9},{9,8},{10,11... | collective-permute-start | bytes 491528 | tf_op jit(solution)/shard_map/ppermute | solution.py:993
  38.2 11.3 %collective-permute-start.6 = (bf16[8,32,640]{2,1,0:T(8,128)(2,1)S(1)}, bf16[8,32,640]{2,1,0:T(8,128)(2,1)S(1)}, u32[]{:S(2)}, u32[]{:S(2)}) collective-permute-start(bf16[8,32,640]{2,1,0:T(8,128)(2,1)S(1)} %get-tuple-element.251), channel_id=1, source_target_pairs={{0,16},{16,0},{1,17},{17,1},{2,18},{18,2},{3,19},{19,3},{4,20},{20... | collective-permute-start | bytes 983048 | tf_op jit(solution)/shard_map/ppermute | solution.py:993
  50.5 15.0 %collective-permute-start.7 = (bf16[16,32,640]{2,1,0:T(8,128)(2,1)}, bf16[16,32,640]{2,1,0:T(8,128)(2,1)}, u32[]{:S(2)}, u32[]{:S(2)}) collective-permute-start(bf16[16,32,640]{2,1,0:T(8,128)(2,1)} %get-tuple-element.242), channel_id=1, source_target_pairs={{0,8},{8,0},{1,9},{9,1},{2,10},{10,2},{3,11},{11,3},{4,12},{12,4},... | collective-permute-start | bytes 1966088 | tf_op jit(solution)/shard_map/ppermute | solution.py:993
  50.5 31.4 %collective-permute-start.8 = (bf16[256,1024]{1,0:T(8,128)(2,1)S(1)}, bf16[256,1024]{1,0:T(8,128)(2,1)S(1)}, u32[]{:S(2)}, u32[]{:S(2)}) collective-permute-start(bf16[256,1024]{1,0:T(8,128)(2,1)S(1)} %copy-done.1), channel_id=1, source_target_pairs={{0,8},{8,0},{1,9},{9,1},{2,10},{10,2},{3,11},{11,3},{4,12},{12,4},... | collective-permute-start | bytes 1572872 | tf_op jit(solution)/shard_map/ppermute | solution.py:1017
  56.0 8.2 %collective-permute-start.14 = (bf16[4,32,1024]{2,1,0:T(8,128)(2,1)}, bf16[4,32,1024]{2,1,0:T(8,128)(2,1)}, u32[]{:S(2)}, u32[]{:S(2)}) collective-permute-start(bf16[4,32,1024]{2,1,0:T(8,128)(2,1)} %pad_maximum_fusion.6), channel_id=1, source_target_pairs={{0,1},{1,0},{2,3},{3,2},{4,5},{5,4},{6,7},{7,6},{8,9},{9,8},{10,11... | collective-permute-start | bytes 786440 | tf_op jit(solution)/shard_map/ppermute | solution.py:993
  59.1 22.8 %all-to-all-start.1 = ((bf16[4,2,32,1024]{3,2,1,0:T(8,128)(2,1)}), bf16[4,2,32,1024]{3,2,1,0:T(8,128)(2,1)}, u32[]{:S(2)}, u32[]{:S(2)}) async-start(bf16[4,2,32,1024]{3,2,1,0:T(8,128)(2,1)} %copy.195), calls=%async_computation.1 | async-start | bytes 1048576 | tf_op jit(solution)/shard_map/all_to_all | solution.py:1093
  63.8 118.2 %all-gather.4.cloned.1.call-start = ((), (), s32[]{:S(2)}) async-start(), calls=%async_computation.8 | async-start | bytes 4718592 | tf_op jit(solution)/shard_map/all_gather | solution.py:988
  64.1 11.1 %collective-permute-start = (bf16[1,256,384]{2,1,0:T(8,128)(2,1)S(1)}, bf16[1,256,384]{2,1,0:T(8,128)(2,1)S(1)}, u32[]{:S(2)}, u32[]{:S(2)}) collective-permute-start(bf16[1,256,384]{2,1,0:T(8,128)(2,1)S(1)} %reshape.764), channel_id=1, source_target_pairs={{0,16},{16,0},{1,17},{17,1},{2,18},{18,2},{3,19},{19,3},{4,20},{20... | collective-permute-start | bytes 589832 | tf_op jit(solution)/shard_map/ppermute | solution.py:993
  65.3 16.6 %collective-permute-start.10 = (bf16[256,1024]{1,0:T(8,128)(2,1)S(1)}, bf16[256,1024]{1,0:T(8,128)(2,1)S(1)}, u32[]{:S(2)}, u32[]{:S(2)}) collective-permute-start(bf16[256,1024]{1,0:T(8,128)(2,1)S(1)} %collective-permute-done.9.ga_ref.refs_2_), channel_id=1, source_target_pairs={{0,8},{8,0},{1,9},{9,1},{2,10},{10,2},{3,11},{11,3},{4,12},{12,4},... | collective-permute-start | bytes 1572872 | tf_op jit(solution)/shard_map/ppermute | solution.py:1017
  75.2 3.7 collective-permute-start.1
  76.4 40.5 %copy-start.32 = (f32[19,1024]{0,1:T(8,128)}, f32[19,1024]{0,1:T(8,128)S(1)}, u32[]{:S(2)}) copy-start(f32[19,1024]{0,1:T(8,128)S(1)} %get-tuple-element.88) | copy-start | bytes 233476
  80.2 28.8 %copy-start.60 = (s32[1,4]{1,0:T(1,128)S(1)}, s32[1,4]{1,0:T(1,128)}, u32[]{:S(2)}) copy-start(s32[1,4]{1,0:T(1,128)} %param.18) | copy-start | bytes 52
  80.2 28.9 %copy-start.58 = (s32[1,16]{1,0:T(1,128)S(1)}, s32[1,16]{1,0:T(1,128)}, u32[]{:S(2)}) copy-start(s32[1,16]{1,0:T(1,128)} %param.19) | copy-start | bytes 196
  80.2 29.0 %copy-start.27 = (s32[1,16]{1,0:T(1,128)S(1)}, s32[1,16]{1,0:T(1,128)}, u32[]{:S(2)}) copy-start(s32[1,16]{1,0:T(1,128)} %param.20) | copy-start | bytes 196
  81.9 29.2 %copy-start.43 = (bf16[8,32,1024]{2,1,0:T(8,128)(2,1)S(1)}, bf16[8,32,1024]{2,1,0:T(8,128)(2,1)}, u32[]{:S(2)}) copy-start(bf16[8,32,1024]{2,1,0:T(8,128)(2,1)} %copy-done.42) | copy-start | bytes 1572868
  81.9 31.4 %copy-start.10 = (bf16[256,1024]{1,0:T(8,128)(2,1)}, bf16[256,1024]{1,0:T(8,128)(2,1)S(1)}, u32[]{:S(2)}) copy-start(bf16[256,1024]{1,0:T(8,128)(2,1)S(1)} %collective-permute-done.8.gb_ref.refs_1_) | copy-start | bytes 1572868
  81.9 31.4 %copy-start.12 = (bf16[256,1024]{1,0:T(8,128)(2,1)}, bf16[256,1024]{1,0:T(8,128)(2,1)S(1)}, u32[]{:S(2)}) copy-start(bf16[256,1024]{1,0:T(8,128)(2,1)S(1)} %collective-permute-done.10.gb_ref.refs_3_) | copy-start | bytes 1572868
  111.1 25.8 %collective-permute-start.18 = (bf16[8,32,1024]{2,1,0:T(8,128)(2,1)S(1)}, bf16[8,32,1024]{2,1,0:T(8,128)(2,1)S(1)}, u32[]{:S(2)}, u32[]{:S(2)}) collective-permute-start(bf16[8,32,1024]{2,1,0:T(8,128)(2,1)S(1)} %copy-done.43), channel_id=1, source_target_pairs={{0,16},{16,0},{1,17},{17,1},{2,18},{18,2},{3,19},{19,3},{4,20},{20... | collective-permute-start | bytes 1572872 | tf_op jit(solution)/shard_map/ppermute | solution.py:993
  113.3 23.0 %copy-start.44 = (bf16[2,14,1024]{2,1,0:T(8,128)(2,1)}, bf16[2,14,1024]{2,1,0:T(8,128)(2,1)S(1)}, u32[]{:S(2)}) copy-start(bf16[2,14,1024]{2,1,0:T(8,128)(2,1)S(1)} %broadcast_in_dim.68) | copy-start | bytes 172036
  113.4 22.9 %collective-permute-start.16 = (bf16[32,1024]{1,0:T(8,128)(2,1)S(1)}, bf16[32,1024]{1,0:T(8,128)(2,1)S(1)}, u32[]{:S(2)}, u32[]{:S(2)}) collective-permute-start(bf16[32,1024]{1,0:T(8,128)(2,1)S(1)} %bitcast.191), channel_id=1, source_target_pairs={{0,16},{16,0},{1,17},{17,1},{2,18},{18,2},{3,19},{19,3},{4,20},{20... | collective-permute-start | bytes 196616 | tf_op jit(solution)/shard_map/ppermute | solution.py:1017
  116.9 20.2 %collective-permute-start.15 = (bf16[32,1024]{1,0:T(8,128)(2,1)S(1)}, bf16[32,1024]{1,0:T(8,128)(2,1)S(1)}, u32[]{:S(2)}, u32[]{:S(2)}) collective-permute-start(bf16[32,1024]{1,0:T(8,128)(2,1)S(1)} %bitcast.192), channel_id=1, source_target_pairs={{0,8},{8,0},{1,9},{9,1},{2,10},{10,2},{3,11},{11,3},{4,12},{12,4},... | collective-permute-start | bytes 196616 | tf_op jit(solution)/shard_map/ppermute | solution.py:1017
  136.3 1.5 collective-permute-start.17
  137.8 35.0 %copy-start.23 = (bf16[32,1024]{1,0:T(8,128)(2,1)}, bf16[32,1024]{1,0:T(8,128)(2,1)S(1)}, u32[]{:S(2)}) copy-start(bf16[32,1024]{1,0:T(8,128)(2,1)S(1)} %collective-permute-done.17.eb_ref) | copy-start | bytes 196612
  137.8 53.1 %collective-permute-start.19 = (bf16[16,32,1024]{2,1,0:T(8,128)(2,1)S(1)}, bf16[16,32,1024]{2,1,0:T(8,128)(2,1)}, u32[]{:S(2)}, u32[]{:S(2)}) collective-permute-start(bf16[16,32,1024]{2,1,0:T(8,128)(2,1)S(1)} %pad_maximum_fusion.1), channel_id=1, source_target_pairs={{0,8},{8,0},{1,9},{9,1},{2,10},{10,2},{3,11},{11,3},{4,12},{12,4},... | collective-permute-start | bytes 3145736 | tf_op jit(solution)/shard_map/ppermute | solution.py:993
  181.9 19.9 %all-to-all-start.2 = ((bf16[8,2,144,128]{3,2,1,0:T(8,128)(2,1)}), bf16[8,2,144,128]{3,2,1,0:T(8,128)(2,1)S(1)}, u32[]{:S(2)}, u32[]{:S(2)}) async-start(bf16[8,2,144,128]{3,2,1,0:T(8,128)(2,1)} %bitcast.231), calls=%async_computation.2 | async-start | bytes 1179648 | tf_op jit(solution)/shard_map/all_to_all | solution.py:1178
  205.8 23.0 %copy-start.9 = (bf16[256,1024]{1,0:T(8,128)(2,1)S(1)}, bf16[256,1024]{1,0:T(8,128)(2,1)}, u32[]{:S(2)}) copy-start(bf16[256,1024]{1,0:T(8,128)(2,1)} %copy-done.8) | copy-start | bytes 1572868
  205.8 23.0 %copy-start.13 = (bf16[256,1024]{1,0:T(8,128)(2,1)S(1)}, bf16[256,1024]{1,0:T(8,128)(2,1)}, u32[]{:S(2)}) copy-start(bf16[256,1024]{1,0:T(8,128)(2,1)} %copy-done.12) | copy-start | bytes 1572868
  205.8 23.0 %copy-start.24 = (bf16[32,1024]{1,0:T(8,128)(2,1)S(1)}, bf16[32,1024]{1,0:T(8,128)(2,1)}, u32[]{:S(2)}) copy-start(bf16[32,1024]{1,0:T(8,128)(2,1)} %copy-done.23) | copy-start | bytes 196612
  205.8 14.2 %collective-permute-start.20 = (bf16[288,1024]{1,0:T(8,128)(2,1)S(1)}, bf16[288,1024]{1,0:T(8,128)(2,1)S(1)}, u32[]{:S(2)}, u32[]{:S(2)}) collective-permute-start(bf16[288,1024]{1,0:T(8,128)(2,1)S(1)} %get-tuple-element.109.xa_ref.refs_4_), channel_id=1, source_target_pairs={{0,16},{16,0},{1,17},{17,1},{2,18},{18,2},{3,19},{19,3},{4,20},{20... | collective-permute-start | bytes 1769480 | tf_op jit(solution)/shard_map/ppermute | solution.py:1017
  206.3 13.7 %collective-permute-start.22 = (bf16[288,1024]{1,0:T(8,128)(2,1)S(1)}, bf16[288,1024]{1,0:T(8,128)(2,1)S(1)}, u32[]{:S(2)}, u32[]{:S(2)}) collective-permute-start(bf16[288,1024]{1,0:T(8,128)(2,1)S(1)} %get-tuple-element.109.xa_ref.refs_4_), channel_id=1, source_target_pairs={{0,8},{8,0},{1,9},{9,1},{2,10},{10,2},{3,11},{11,3},{4,12},{12,4},... | collective-permute-start | bytes 1769480 | tf_op jit(solution)/shard_map/ppermute | solution.py:1017
  220.0 8.8 %collective-permute-start.21 = (bf16[288,1024]{1,0:T(8,128)(2,1)S(1)}, bf16[288,1024]{1,0:T(8,128)(2,1)S(1)}, u32[]{:S(2)}, u32[]{:S(2)}) collective-permute-start(bf16[288,1024]{1,0:T(8,128)(2,1)S(1)} %collective-permute-done.20.xa_ref.refs_6_), channel_id=1, source_target_pairs={{0,8},{8,0},{1,9},{9,1},{2,10},{10,2},{3,11},{11,3},{4,12},{12,4},... | collective-permute-start | bytes 1769480 | tf_op jit(solution)/shard_map/ppermute | solution.py:1017
  236.7 4.0 collective-permute-start.27
  237.2 20.0 %collective-permute-start.26 = (f32[288,1024]{1,0:T(8,128)S(1)}, f32[288,1024]{1,0:T(8,128)S(1)}, u32[]{:S(2)}, u32[]{:S(2)}) collective-permute-start(f32[288,1024]{1,0:T(8,128)S(1)} %copy-done.59), channel_id=1, source_target_pairs={{0,8},{8,0},{1,9},{9,1},{2,10},{10,2},{3,11},{11,3},{4,12},{12,4},... | collective-permute-start | bytes 3538952 | tf_op jit(solution)/shard_map/ppermute | solution.py:1017
  240.9 16.2 %collective-permute-start.28 = (bf16[288,1024]{1,0:T(8,128)(2,1)S(1)}, bf16[288,1024]{1,0:T(8,128)(2,1)S(1)}, u32[]{:S(2)}, u32[]{:S(2)}) collective-permute-start(bf16[288,1024]{1,0:T(8,128)(2,1)S(1)} %add_convert_fusion), channel_id=1, source_target_pairs={{0,16},{16,0},{1,17},{17,1},{2,18},{18,2},{3,19},{19,3},{4,20},{20... | collective-permute-start | bytes 1769480 | tf_op jit(solution)/shard_map/ppermute | solution.py:1017
  241.6 28.2 %collective-permute-start.30 = (bf16[288,1024]{1,0:T(8,128)(2,1)}, bf16[288,1024]{1,0:T(8,128)(2,1)S(1)}, u32[]{:S(2)}, u32[]{:S(2)}) collective-permute-start(bf16[288,1024]{1,0:T(8,128)(2,1)} %get-tuple-element.140.refs_0_), channel_id=1, source_target_pairs={{0,16},{16,0},{1,17},{17,1},{2,18},{18,2},{3,19},{19,3},{4,20},{20... | collective-permute-start | bytes 1769480 | tf_op jit(solution)/shard_map/ppermute | solution.py:1017
  262.9 19.0 %collective-permute-start.33 = (bf16[288,1024]{1,0:T(8,128)(2,1)S(1)}, bf16[288,1024]{1,0:T(8,128)(2,1)S(1)}, u32[]{:S(2)}, u32[]{:S(2)}) collective-permute-start(bf16[288,1024]{1,0:T(8,128)(2,1)S(1)} %get-tuple-element.141.refs_4_), channel_id=1, source_target_pairs={{0,16},{16,0},{1,17},{17,1},{2,18},{18,2},{3,19},{19,3},{4,20},{20... | collective-permute-start | bytes 1769480 | tf_op jit(solution)/shard_map/ppermute | solution.py:1017
  263.7 24.8 %all-to-all-start.3 = ((bf16[8,256,128]{2,1,0:T(8,128)(2,1)}), bf16[8,256,128]{2,1,0:T(8,128)(2,1)}, u32[]{:S(2)}, u32[]{:S(2)}) async-start(bf16[8,256,128]{2,1,0:T(8,128)(2,1)} %copy-done.22), calls=%async_computation.3 | async-start | bytes 1048576 | tf_op jit(solution)/shard_map/all_to_all | solution.py:1235
  269.4 120.9 %reduce-scatter.3.cloned.1.call-start = ((), (), s32[]{:S(2)}) async-start(), calls=%async_computation.9 | async-start | bytes 5308416 | tf_op jit(solution)/shard_map/reduce_scatter | solution.py:1246
  269.4 12.5 %collective-permute-start.29 = (bf16[288,1024]{1,0:T(8,128)(2,1)}, bf16[288,1024]{1,0:T(8,128)(2,1)}, u32[]{:S(2)}, u32[]{:S(2)}) collective-permute-start(bf16[288,1024]{1,0:T(8,128)(2,1)} %get-tuple-element.140.refs_0_), channel_id=1, source_target_pairs={{0,8},{8,0},{1,9},{9,1},{2,10},{10,2},{3,11},{11,3},{4,12},{12,4},... | collective-permute-start | bytes 1769480 | tf_op jit(solution)/shard_map/ppermute | solution.py:1017
  269.8 12.1 %collective-permute-start.31 = (bf16[288,1024]{1,0:T(8,128)(2,1)S(1)}, bf16[288,1024]{1,0:T(8,128)(2,1)}, u32[]{:S(2)}, u32[]{:S(2)}) collective-permute-start(bf16[288,1024]{1,0:T(8,128)(2,1)S(1)} %collective-permute-done.30.refs_2_), channel_id=1, source_target_pairs={{0,8},{8,0},{1,9},{9,1},{2,10},{10,2},{3,11},{11,3},{4,12},{12,4},... | collective-permute-start | bytes 1769480 | tf_op jit(solution)/shard_map/ppermute | solution.py:1017
  270.0 11.9 %collective-permute-start.32 = (bf16[288,1024]{1,0:T(8,128)(2,1)S(1)}, bf16[288,1024]{1,0:T(8,128)(2,1)}, u32[]{:S(2)}, u32[]{:S(2)}) collective-permute-start(bf16[288,1024]{1,0:T(8,128)(2,1)S(1)} %get-tuple-element.141.refs_4_), channel_id=1, source_target_pairs={{0,8},{8,0},{1,9},{9,1},{2,10},{10,2},{3,11},{11,3},{4,12},{12,4},... | collective-permute-start | bytes 1769480 | tf_op jit(solution)/shard_map/ppermute | solution.py:1017
  281.9 2.1 collective-permute-start.34
  341.2 43.0 %all-to-all-start.4 = ((bf16[8,256,128]{2,1,0:T(8,128)(2,1)}), bf16[8,256,128]{2,1,0:T(8,128)(2,1)S(1)}, u32[]{:S(2)}, u32[]{:S(2)}) async-start(bf16[8,256,128]{2,1,0:T(8,128)(2,1)} %bitcast.69), calls=%async_computation.5 | async-start | bytes 1048576 | tf_op jit(solution)/shard_map/all_to_all | solution.py:1253
  347.0 138.5 %reduce-scatter.5.cloned.1.call-start = ((), (), s32[]{:S(2)}) async-start(), calls=%async_computation.10 | async-start | bytes 4718592 | tf_op jit(solution)/shard_map/reduce_scatter | solution.py:1262
  396.3 8.7 %collective-permute-start.24 = (f32[256,1024]{1,0:T(8,128)}, f32[256,1024]{1,0:T(8,128)}, u32[]{:S(2)}, u32[]{:S(2)}) collective-permute-start(f32[256,1024]{1,0:T(8,128)} %bitcast.63), channel_id=1, source_target_pairs={{0,8},{8,0},{1,9},{9,1},{2,10},{10,2},{3,11},{11,3},{4,12},{12,4},... | collective-permute-start | bytes 3145736 | tf_op jit(solution)/shard_map/ppermute | solution.py:1017
  403.6 19.9 %collective-permute-start.35 = (bf16[2,740,256]{2,0,1:T(2,128)(2,1)S(1)}, bf16[2,740,256]{2,0,1:T(2,128)(2,1)S(1)}, u32[]{:S(2)}, u32[]{:S(2)}) collective-permute-start(bf16[2,740,256]{2,0,1:T(2,128)(2,1)S(1)} %copy.213), channel_id=1, source_target_pairs={{0,16},{16,0},{1,17},{17,1},{2,18},{18,2},{3,19},{19,3},{4,20},{20... | collective-permute-start | bytes 2273288 | tf_op jit(solution)/shard_map/ppermute | solution.py:1017
  404.9 20.2 %collective-permute-start.23 = (f32[256,1024]{1,0:T(8,128)S(1)}, f32[256,1024]{1,0:T(8,128)S(1)}, u32[]{:S(2)}, u32[]{:S(2)}) collective-permute-start(f32[256,1024]{1,0:T(8,128)S(1)} %bitcast.237), channel_id=1, source_target_pairs={{0,8},{8,0},{1,9},{9,1},{2,10},{10,2},{3,11},{11,3},{4,12},{12,4},... | collective-permute-start | bytes 3145736 | tf_op jit(solution)/shard_map/ppermute | solution.py:1017
  407.2 26.3 %collective-permute-start.25 = (bf16[256,1024]{1,0:T(8,128)(2,1)S(1)}, bf16[256,1024]{1,0:T(8,128)(2,1)S(1)}, u32[]{:S(2)}, u32[]{:S(2)}) collective-permute-start(bf16[256,1024]{1,0:T(8,128)(2,1)S(1)} %fusion.14), channel_id=1, source_target_pairs={{0,16},{16,0},{1,17},{17,1},{2,18},{18,2},{3,19},{19,3},{4,20},{20... | collective-permute-start | bytes 1572872 | tf_op jit(solution)/shard_map/ppermute | solution.py:1017
  423.8 11.0 %collective-permute-start.36 = (bf16[740,256]{1,0:T(8,128)(2,1)S(1)}, bf16[740,256]{1,0:T(8,128)(2,1)S(1)}, u32[]{:S(2)}, u32[]{:S(2)}) collective-permute-start(bf16[740,256]{1,0:T(8,128)(2,1)S(1)} %fusion.24), channel_id=1, source_target_pairs={{0,8},{8,0},{1,9},{9,1},{2,10},{10,2},{3,11},{11,3},{4,12},{12,4},... | collective-permute-start | bytes 1136648 | tf_op jit(solution)/shard_map/ppermute | solution.py:1017
  435.2 11.8 %collective-permute-start.37 = (bf16[384,128]{1,0:T(8,128)(2,1)S(1)}, bf16[384,128]{1,0:T(8,128)(2,1)S(1)}, u32[]{:S(2)}, u32[]{:S(2)}) collective-permute-start(bf16[384,128]{1,0:T(8,128)(2,1)S(1)} %bitcast.257), channel_id=1, source_target_pairs={{0,0},{1,1},{2,8},{3,9},{4,16},{5,17},{6,24},{7,25},{8,2},{9,3},{1... | collective-permute-start | bytes 294920 | tf_op jit(solution)/shard_map/ppermute | solution.py:1301
  439.5 11.2 %collective-permute-start.38 = (bf16[384,128]{1,0:T(8,128)(2,1)S(1)}, bf16[384,128]{1,0:T(8,128)(2,1)S(1)}, u32[]{:S(2)}, u32[]{:S(2)}) collective-permute-start(bf16[384,128]{1,0:T(8,128)(2,1)S(1)} %bitcast.258), channel_id=1, source_target_pairs={{0,1},{1,0},{2,9},{3,8},{4,17},{5,16},{6,25},{7,24},{8,3},{9,2},{1... | collective-permute-start | bytes 294920 | tf_op jit(solution)/shard_map/ppermute | solution.py:1301
  443.0 11.4 %all-to-all-start.5 = ((bf16[8,96,128]{2,1,0:T(8,128)(2,1)}), bf16[8,96,128]{2,1,0:T(8,128)(2,1)S(1)}, u32[]{:S(2)}, u32[]{:S(2)}) async-start(bf16[8,96,128]{2,1,0:T(8,128)(2,1)} %fusion.25), calls=%async_computation.7 | async-start | bytes 393216 | tf_op jit(solution)/shard_map/all_to_all | solution.py:1294
  454.4 7.5 %collective-permute-start.39 = (bf16[72,128]{1,0:T(8,128)(2,1)S(1)}, bf16[72,128]{1,0:T(8,128)(2,1)S(1)}, u32[]{:S(2)}, u32[]{:S(2)}) collective-permute-start(bf16[72,128]{1,0:T(8,128)(2,1)S(1)} %slice.198), channel_id=1, source_target_pairs={{0,0},{1,1},{2,8},{3,9},{4,16},{5,17},{6,24},{7,25},{8,2},{9,3},{1... | collective-permute-start | bytes 55304 | tf_op jit(solution)/shard_map/ppermute | solution.py:1318
  463.8 21.7 %copy-start.31 = (bf16[256,1024]{1,0:T(8,128)(2,1)S(1)}, bf16[256,1024]{1,0:T(8,128)(2,1)}, u32[]{:S(2)}) copy-start(bf16[256,1024]{1,0:T(8,128)(2,1)} %param.15) | copy-start | bytes 1572868
  464.5 22.4 %copy-start.19 = (f32[256,1024]{1,0:T(8,128)S(1)}, f32[256,1024]{1,0:T(8,128)}, u32[]{:S(2)}) copy-start(f32[256,1024]{1,0:T(8,128)} %copy-done.18) | copy-start | bytes 3145732
  (49 other events, 228.5 us)
Sparse Core Ops, SparseCore 0:
  10.4 96.5 all-gather.5
  109.1 72.7 all-gather.3
  288.6 101.6 reduce-scatter.2
  393.8 91.6 reduce-scatter.4

commit v2 on v1

--- a/solution.py
+++ b/solution.py
@@ -152,9 +152,10 @@
 
 
 def scan_forward_kernel(
-    heads, p, begins_ref, parts_ref, gate_ref, cols_ref,
-    out_ref, joined_ref, scanned_ref, state_ref, mats_ref, state,
+    heads, p, home_ref, begins_ref, parts_ref, pre_ref, gate_ref, cols_ref, *rest,
 ):
+    first_refs, rest = rest[: FORWARD_CHUNKS * SPAN // BLOCK], rest[FORWARD_CHUNKS * SPAN // BLOCK :]
+    values_ref, out_ref, joined_ref, scanned_ref, state_ref, mats_ref, state = rest
     step = pl.program_id(0)
     width = heads * HEAD
 
@@ -169,10 +170,15 @@
         lax.broadcasted_iota(jnp.int32, (width, width), 0)
         == lax.broadcasted_iota(jnp.int32, (width, width), 1)
     ).astype(F32)
+    first = jnp.concatenate([ref[0] for ref in first_refs], 0).astype(F32)
+    mix = jax.nn.sigmoid(cols_ref[5:6] + pre_ref[4])
+    values = (pre_ref[1] + (first - pre_ref[1]) * mix).astype(LOW)
+    values_ref[...] = values
     held = []
     for c in range(FORWARD_CHUNKS):
         rows = pl.ds(c * SPAN, SPAN)
-        r, lw, k, kn, a, v = [parts_ref[i, rows] for i in range(6)]
+        r, lw, k, kn, a = [parts_ref[i, rows] for i in range(5)]
+        v = values[c * SPAN : (c + 1) * SPAN]
         q = Chunk(r, lw, k, kn, a, begins, (step * FORWARD_CHUNKS + c) * SPAN, heads)
         v_st = stacked(v.astype(F32), masks).astype(LOW)
         held.append((q, r, k, v, v_st))
@@ -238,34 +244,43 @@
         out_ref[rows] = (joined.astype(F32) * gate_ref[rows]).astype(LOW)
 
 
-def scan_forward(parts, gate, cols, begins, p):
+def scan_forward(parts, pre, first, gate, cols, home, begins, p):
     _, total, width = parts.shape
     heads = width // HEAD
     rows = FORWARD_CHUNKS * SPAN
     n = heads * SPAN
     spans = total // SPAN
     assert n == width
-    row_spec = pl.BlockSpec((rows, width), lambda i, b: (i, 0))
+    row_spec = pl.BlockSpec((rows, width), lambda i, *_: (i, 0))
+    per_step = rows // BLOCK
+
+    def stored(which):
+        return pl.BlockSpec((1, BLOCK, width), lambda i, home, b: (home[per_step * i + which], 0, 0))
+
     return pl.pallas_call(
         functools.partial(scan_forward_kernel, heads, p),
         grid_spec=pltpu.PrefetchScalarGridSpec(
-            num_scalar_prefetch=1,
+            num_scalar_prefetch=2,
             grid=(total // rows,),
             in_specs=[
-                pl.BlockSpec((6, rows, width), lambda i, b: (0, i, 0)),
+                pl.BlockSpec((5, rows, width), lambda i, *_: (0, i, 0)),
+                pl.BlockSpec((5, rows, width), lambda i, *_: (0, i, 0)),
                 row_spec,
-                pl.BlockSpec(cols.shape, lambda i, b: (0, 0)),
-            ],
+                pl.BlockSpec(cols.shape, lambda i, *_: (0, 0)),
+            ]
+            + [stored(w) for w in range(per_step)],
             out_specs=[
                 row_spec,
                 row_spec,
                 row_spec,
-                pl.BlockSpec((FORWARD_CHUNKS, width, width), lambda i, b: (i, 0, 0)),
-                pl.BlockSpec((FORWARD_CHUNKS, 8, n, width), lambda i, b: (i, 0, 0, 0)),
+                row_spec,
+                pl.BlockSpec((FORWARD_CHUNKS, width, width), lambda i, *_: (i, 0, 0)),
+                pl.BlockSpec((FORWARD_CHUNKS, 8, n, width), lambda i, *_: (i, 0, 0, 0)),
             ],
             scratch_shapes=[pltpu.VMEM((width, width), F32)],
         ),
         out_shape=[
+            jax.ShapeDtypeStruct((total, width), LOW),
             jax.ShapeDtypeStruct((total, width), LOW),
             jax.ShapeDtypeStruct((total, width), LOW),
             jax.ShapeDtypeStruct((total, width), F32),
@@ -274,12 +289,12 @@
         ],
         compiler_params=pltpu.CompilerParams(vmem_limit_bytes=48 * 1024 * 1024),
         cost_estimate=work(80),
-    )(begins, parts, gate, cols)
+    )(home, begins, parts, pre, gate, cols, *[first] * per_step)
 
 
 def scan_backward_kernel(
-    heads, p, home_ref, begins_ref, parts_ref, joined_ref, scanned_ref, gate_ref, grad_a_ref, grad_b_ref,
-    pre_ref, first_ref, cols_ref, state_ref, mats_ref, *rest,
+    heads, p, home_ref, begins_ref, parts_ref, values_ref, joined_ref, scanned_ref, gate_ref, grad_a_ref,
+    grad_b_ref, pre_ref, first_a_ref, first_b_ref, cols_ref, state_ref, mats_ref, *rest,
 ):
     steps = pl.num_programs(0)
     step = steps - 1 - pl.program_id(0)
@@ -306,10 +321,12 @@
 
     c13, c14 = cols_ref[0:1], cols_ref[1:2]
     grads = jnp.concatenate([grad_a_ref[0], grad_b_ref[0]], 0).astype(F32)
+    firsts = jnp.concatenate([first_a_ref[0], first_b_ref[0]], 0).astype(F32)
     ready = []
     for c in range(BACKWARD_CHUNKS):
         rows = pl.ds(c * SPAN, SPAN)
-        r, lw, k, kn, a, v = [parts_ref[i, rows] for i in range(6)]
+        r, lw, k, kn, a = [parts_ref[i, rows] for i in range(5)]
+        v = values_ref[rows]
         q = Chunk(r, lw, k, kn, a, begins, (step * BACKWARD_CHUNKS + c) * SPAN, heads)
         r, k, v = r.astype(F32), k.astype(F32), v.astype(F32)
         unit, scale = group_norm_parts(scanned_ref[rows], ones)
@@ -344,7 +361,7 @@
     begin = [state_ref[c] for c in span]
     chunks = [ready[c][0] for c in span]
     d_outs = [ready[c][1] for c in span]
-    v_st = [stacked(parts_ref[5, pl.ds(c * SPAN, SPAN)].astype(F32), masks) for c in span]
+    v_st = [stacked(values_ref[pl.ds(c * SPAN, SPAN)].astype(F32), masks) for c in span]
     update = [mats[c][5] + product(mats[c][4], begin[c], NT, p["val"]) for c in span]
     through = [product(mats[c][2], d_outs[c], TN, p["val"]) for c in span]
     through = [
@@ -384,7 +401,8 @@
         rows = pl.ds(c * SPAN, SPAN)
         q, _, _, own_r, own_k, own_v, grad_gate = ready[c]
         end_grad, begin_now = ended[c], begin[c]
-        r, lw, k, kn, a, v = [parts_ref[i, rows].astype(F32) for i in range(6)]
+        r, lw, k, kn, a = [parts_ref[i, rows].astype(F32) for i in range(5)]
+        v = values_ref[rows].astype(F32)
         d_asks, d_keys, d_val = all_asks[c], all_keys[c], all_vals[c]
         d_ends = all_ends[c] * jnp.concatenate([q.final, q.final], 0)
         d_a, d_r = unstacked(d_asks[:n], heads) * q.before, unstacked(d_asks[n:], heads) * q.decay
@@ -416,7 +434,7 @@
             x.astype(LOW).astype(F32) for x in (d_r, d_lw, d_k, d_kn, d_rate, d_v)
         ]
         key_pre, value_pre, decay_up, rate_up, value_up = [pre_ref[i, rows] for i in range(5)]
-        first = first_ref[rows].astype(F32)
+        first = firsts[c * SPAN : (c + 1) * SPAN]
         c8, c9, c10, c11, c12 = [cols_ref[i : i + 1] for i in range(3, 8)]
         sig = jax.nn.sigmoid(c8 + decay_up)
         log_decay = -0.6065306597126334 * sig
@@ -444,7 +462,7 @@
     col_grad_ref[...] += jnp.concatenate(sums, 0)
 
 
-def scan_backward(parts, joined, scanned, gate, grad, pre, first, cols, states, mats, home, begins, p):
+def scan_backward(parts, values, joined, scanned, gate, grad, pre, first, cols, states, mats, home, begins, p):
     _, total, width = parts.shape
     heads = width // HEAD
     rows = BACKWARD_CHUNKS * SPAN
@@ -464,14 +482,16 @@
             num_scalar_prefetch=2,
             grid=(steps,),
             in_specs=[
-                pl.BlockSpec((6, rows, width), lambda i, *_: (0, steps - 1 - i, 0)),
+                pl.BlockSpec((5, rows, width), lambda i, *_: (0, steps - 1 - i, 0)),
+                row_spec,
                 row_spec,
                 row_spec,
                 row_spec,
                 stored(0),
                 stored(1),
                 pl.BlockSpec((5, rows, width), lambda i, *_: (0, steps - 1 - i, 0)),
-                row_spec,
+                stored(0),
+                stored(1),
                 pl.BlockSpec(cols.shape, lambda i, *_: (0, 0)),
                 pl.BlockSpec((BACKWARD_CHUNKS, width, width), lambda i, *_: (steps - 1 - i, 0, 0)),
                 pl.BlockSpec((BACKWARD_CHUNKS, 8, n, width), lambda i, *_: (steps - 1 - i, 0, 0, 0)),
@@ -490,7 +510,7 @@
         ],
         compiler_params=pltpu.CompilerParams(vmem_limit_bytes=56 * 1024 * 1024),
         cost_estimate=work(60),
-    )(home, begins, parts, joined, scanned, gate, grad, grad, pre, first, cols, states, mats)
+    )(home, begins, parts, values, joined, scanned, gate, grad, grad, pre, first, first, cols, states, mats)
 
 
 def norm_rows(x):
@@ -533,8 +553,8 @@
 
 
 def project_kernel(
-    place_ref, home_ref, begins_ref, xa_ref, xb_ref, fa_ref, fb_ref, cols_ref, own_ref, columns_ref,
-    small_ref, up_ref, parts_ref, gate_ref, pre_ref, first_ref, pair_ref, vm_ref, gs_ref, edge,
+    place_ref, begins_ref, xa_ref, xb_ref, cols_ref, own_ref, columns_ref,
+    small_ref, up_ref, ends_ref, parts_ref, gate_ref, pre_ref, pair_ref, vm_ref, gs_ref, edge,
 ):
     step = pl.program_id(0)
 
@@ -543,6 +563,8 @@
         edge[...] = jnp.zeros_like(edge)
 
     begins = [begins_ref[i] for i in range(begins_ref.shape[0])]
+    for i, ref in enumerate((xa_ref, xb_ref)):
+        ends_ref[i] = jnp.concatenate([ref[0, :16], ref[0, BLOCK - 16 :]], 0)
     x = jnp.concatenate([xa_ref[0], xb_ref[0]], 0).astype(F32)
     rows = x.shape[0]
     unit, _ = norm_rows(x)
@@ -570,20 +592,16 @@
     pair_ref[...] = pair
     vm_ref[...] = value_mid
     gs_ref[...] = gate_sig
-    first_low = jnp.concatenate([fa_ref[0], fb_ref[0]], 0)
-    first_ref[...] = first_low
-    first = first_low.astype(F32)
     for i, value in enumerate((key_pre, value_pre, decay_up, rate_up, value_up)):
         pre_ref[i] = value
-    c8, c9, c10, c11, c12 = [own_ref[i : i + 1] for i in range(3, 8)]
+    c8, c9, _, c11, c12 = [own_ref[i : i + 1] for i in range(3, 8)]
     ones = head_ones(recept.shape[1])
     log_decay = -jnp.exp(-jax.nn.softplus(-(c8 + decay_up)) - 0.5)
     rate = jax.nn.sigmoid(c9 + rate_up)
     scaled = key_pre * c11
     key_norm = scaled * lax.rsqrt(head_sum(scaled * scaled, ones) + 1e-06)
     key_main = key_pre * (1.0 + (rate - 1.0) * c12)
-    values = value_pre + (first - value_pre) * jax.nn.sigmoid(c10 + value_up)
-    for i, value in enumerate((recept, log_decay, key_main, key_norm, rate, values)):
+    for i, value in enumerate((recept, log_decay, key_main, key_norm, rate)):
         parts_ref[i] = value.astype(LOW)
 
 
@@ -600,8 +618,8 @@
     return pl.BlockSpec(array.shape, lambda i, *_: (0,) * array.ndim)
 
 
-def project(x, first, cols, own, weights, place, home, begins, per):
-    blocks = home.shape[0]
+def project(x, cols, own, weights, place, begins, per):
+    blocks = place.shape[0]
     total = blocks * BLOCK
     rows = 2 * BLOCK
     width = own.shape[1]
@@ -611,67 +629,81 @@
     return pl.pallas_call(
         project_kernel,
         grid_spec=pltpu.PrefetchScalarGridSpec(
-            num_scalar_prefetch=3,
+            num_scalar_prefetch=2,
             grid=(blocks // 2,),
             in_specs=[
                 block_spec(per, 0, BLOCK, x.shape[2], blocks, False),
                 block_spec(per, 1, BLOCK, x.shape[2], blocks, False),
-                block_spec(per, 0, BLOCK, width, blocks, False, 1),
-                block_spec(per, 1, BLOCK, width, blocks, False, 1),
                 whole_spec(cols),
                 whole_spec(own),
             ]
             + [whole_spec(w) for w in weights],
-            out_specs=[deep(6), span(width), deep(5), span(width), span(128), span(128), span(128)],
+            out_specs=[
+                pl.BlockSpec((2, 32, x.shape[2]), lambda i, *_: (i, 0, 0)),
+                deep(5), span(width), deep(5), span(128), span(128), span(128),
+            ],
             scratch_shapes=[pltpu.VMEM((8, x.shape[2]), F32)],
         ),
         out_shape=[
-            shape((6, total, width), LOW),
+            shape((blocks, 32, x.shape[2]), LOW),
+            shape((5, total, width), LOW),
             shape((total, width), F32),
             shape((5, total, width), F32),
-            shape((total, width), LOW),
             shape((total, 128), F32),
             shape((total, 128), LOW),
             shape((total, 128), F32),
         ],
         compiler_params=pltpu.CompilerParams(vmem_limit_bytes=56 * 1024 * 1024),
         cost_estimate=work(20),
-    )(place, home, begins, x, x, first, first, cols, own, *weights)
+    )(place, begins, x, x, cols, own, *weights)
 
 
 def project_back_kernel(
-    place_ref, begins_ref, xa_ref, xb_ref, xp_ref, grads_ref, pair_ref, vm_ref, gs_ref, cols_ref,
-    columns_ref, small_ref, up_ref, back_ref, sum_ref, up_sum_ref, edge,
+    part, parts, place_ref, turn_ref, row_ref, begins_ref, head_ref, xa_ref, xb_ref, xp_ref, grads_ref,
+    pair_ref, vm_ref, gs_ref, scan_ref, ffn_ref, cols_ref, columns_ref, small_ref, up_ref, *rest,
 ):
-    step = pl.num_programs(0) - 1 - pl.program_id(0)
-
-    @pl.when(pl.program_id(0) == 0)
+    sizes_x = len(rest) - 4 - (2 if part == 0 else 1)
+    back_refs, rest = rest[:sizes_x], rest[sizes_x:]
+    if part == 0:
+        low_sum_ref, up_sum_ref, edge, sum_ref, buffer, sems = rest
+    else:
+        low_sum_ref, edge, sum_ref, buffer, sems = rest
+    turn = pl.program_id(0)
+    step = pl.num_programs(0) - 1 - turn
+    wide = columns_ref.shape[0]
+    lanes = slice(part * wide, (part + 1) * wide)
+
+    @pl.when(turn == 0)
     def _():
-        for ref in (edge, sum_ref, up_sum_ref):
+        for ref in (edge, sum_ref) + ((up_sum_ref,) if part == 0 else ()):
             ref[...] = jnp.zeros_like(ref)
 
     begins = [begins_ref[i] for i in range(begins_ref.shape[0])]
-    x = jnp.concatenate([xa_ref[0], xb_ref[0]], 0).astype(F32)
-    rows = x.shape[0]
-    unit, _ = norm_rows(x)
+
+    def normal(x):
+        x = x.astype(F32)
+        mean = jnp.mean(x, -1, keepdims=True)
+        spread = jnp.mean((x - mean) * (x - mean), -1, keepdims=True)
+        return (x[:, lanes] - mean) * lax.rsqrt(spread + 1e-05)
+
+    unit = normal(jnp.concatenate([xa_ref[0], xb_ref[0]], 0))
+    rows = unit.shape[0]
     normed = unit * cols_ref[0:1] + cols_ref[1:2]
-    prior_unit, _ = norm_rows(xp_ref[0].astype(F32))
-    prior = prior_unit * cols_ref[0:1] + cols_ref[1:2]
+    prior = normal(xp_ref[0]) * cols_ref[0:1] + cols_ref[1:2]
     keep = keep_rows(rows, step * rows, begins)
     diff = rows_down(normed, prior[prior.shape[0] - 1 :]) * keep - normed
     low = SmallWeights(small_ref[...], up_ref[...])
     width = grads_ref.shape[2]
     g_r, g_k, g_v, g_decay, g_rate, g_vup, g_gate = [grads_ref[i] for i in range(7)]
     pair, sig = pair_ref[...], gs_ref[...]
-    pair_low = pair.astype(LOW)
     is_decay = lane_below(DECAY_RANK)
     m_pair = jnp.where(
         is_decay, dot(g_decay, low.up_pair, NN) * (1.0 - pair * pair), dot(g_rate, low.up_pair, NN)
     ).astype(LOW)
     m_v = kept(dot(g_vup, low.up_value, NN), lane_below(DV)).astype(LOW)
     m_g = (dot(g_gate, low.up_gate, NN) * sig * (1.0 - sig)).astype(LOW)
-    near = jnp.zeros_like(x)
-    far = jnp.zeros_like(x)
+    near = jnp.zeros_like(unit)
+    far = jnp.zeros_like(unit)
     value_weights = jnp.concatenate([columns_ref[:, 2 * width :], low.value], 1)
     cut = DECAY_RANK + DA + 3 * width
     grads = (
@@ -683,64 +715,120 @@
         (7, m_g, low.gate, ((cut + DV, m_g),)),
     )
     col_sums = []
-    for slot, grad, weight, parts in grads:
+    for slot, grad, weight, pieces in grads:
         mix = cols_ref[slot : slot + 1]
         mixed = (normed + diff * mix).astype(LOW)
         total = dot(grad, weight, NT)
-        for start, part in parts:
-            sum_ref[start : start + part.shape[1]] += dot(part, mixed, TN)
+        for start, piece in pieces:
+            sum_ref[start : start + piece.shape[1]] += dot(piece, mixed, TN)
         near = near + total
         far = far + total * mix
         col_sums.append(jnp.sum(total * diff, 0, keepdims=True))
-    start = 0
-    for mid, grad in (
-        (pair_low[:, :DECAY_RANK], g_decay),
-        (pair_low[:, DECAY_RANK:], g_rate),
-        (vm_ref[:, :DV], g_vup),
-        (sig.astype(LOW), g_gate),
-    ):
-        up_sum_ref[start : start + mid.shape[1]] += dot(mid, grad, TN)
-        start += mid.shape[1]
+    if part == 0:
+        start = 0
+        pair_low = pair.astype(LOW)
+        for mid, grad in (
+            (pair_low[:, :DECAY_RANK], g_decay),
+            (pair_low[:, DECAY_RANK:], g_rate),
+            (vm_ref[:, :DV], g_vup),
+            (sig.astype(LOW), g_gate),
+        ):
+            up_sum_ref[start : start + mid.shape[1]] += dot(mid, grad, TN)
+            start += mid.shape[1]
     moved = far * keep
     back = near - far + rows_up(moved, edge[0:1])
     edge[0:1] = moved[0:1]
-    back_ref[...] = back.astype(LOW)
     first = [jnp.sum(back * unit, 0, keepdims=True), jnp.sum(back, 0, keepdims=True)]
     sum_ref[sum_ref.shape[0] - 8 :] += jnp.concatenate(first + col_sums, 0)
 
-
-def project_back(x, grads, mids, cols, weights, place, begins, per):
+    slot = turn % 2
+
+    def leave(where):
+        for which in range(2):
+            pltpu.make_async_copy(
+                buffer.at[where, which], back_refs[0].at[0], sems.at[where, which]
+            ).wait()
+
+    @pl.when(turn >= 2)
+    def _():
+        leave(slot)
+
+    buffer[slot] = back.astype(LOW).reshape(2, BLOCK, wide)
+    for which in range(2):
+        block = 2 * step + which
+        for x, ref in enumerate(back_refs):
+
+            @pl.when(turn_ref[block] == x)
+            def _():
+                pltpu.make_async_copy(
+                    buffer.at[slot, which], ref.at[row_ref[block]], sems.at[slot, which]
+                ).start()
+
+    @pl.when(step == 0)
+    def _():
+        held = sum_ref.shape[0]
+        low_sum_ref[:held] = sum_ref[...].astype(LOW)
+        lane = lax.broadcasted_iota(jnp.int32, (1, wide), 1) + part * wide
+        spread = jnp.concatenate([scan_ref[...]] * (wide // width), 1)
+        spread = jnp.where(lane // width == head_ref[0], spread, 0.0)
+        low_sum_ref[held : held + 16] = jnp.concatenate([spread, ffn_ref[...]], 0).astype(LOW)
+        low_sum_ref[held + 16 :] = jnp.zeros_like(low_sum_ref[held + 16 :])
+        leave(1 - slot)
+        leave(slot)
+
+
+def project_back(
+    part, parts, x, grads, mids, extra_cols, cols, weights, place, turn, row, begins, head, per, sizes
+):
     blocks = place.shape[0]
-    total = blocks * BLOCK
     rows = 2 * BLOCK
     steps = blocks // 2
-    wide = x.shape[2]
+    wide = x.shape[2] // parts
     width = grads.shape[2]
+    size_z, size_x = sizes
     low_rank = DECAY_RANK + DA + DV + 128
     span = lambda w: pl.BlockSpec((rows, w), lambda i, *_: (steps - 1 - i, 0))
     shape = jax.ShapeDtypeStruct
-    sums = [shape((3 * width + low_rank + 8, wide), F32), shape((low_rank, width), F32)]
+    held = 3 * width + low_rank + 8
+    sums = [shape((held + 16 + -(held + 16) % 16, wide), LOW)]
+    if part == 0:
+        sums.append(shape((low_rank, width), F32))
+    columns, small, up = weights
+    assert steps > 1
     return pl.pallas_call(
-        project_back_kernel,
+        functools.partial(project_back_kernel, part, parts),
         grid_spec=pltpu.PrefetchScalarGridSpec(
-            num_scalar_prefetch=2,
+            num_scalar_prefetch=5,
             grid=(steps,),
             in_specs=[
-                block_spec(per, 0, BLOCK, wide, blocks, True),
-                block_spec(per, 1, BLOCK, wide, blocks, True),
-                block_spec(per, -1, 16, wide, blocks, True),
+                block_spec(per, 0, BLOCK, x.shape[2], blocks, True),
+                block_spec(per, 1, BLOCK, x.shape[2], blocks, True),
+                block_spec(per, -1, 16, x.shape[2], blocks, True),
                 pl.BlockSpec((7, rows, width), lambda i, *_: (0, steps - 1 - i, 0)),
             ]
             + [span(m.shape[1]) for m in mids]
-            + [whole_spec(cols)]
-            + [whole_spec(w) for w in weights],
-            out_specs=[span(wide)] + [whole_spec(s) for s in sums],
-            scratch_shapes=[pltpu.VMEM((8, wide), F32)],
+            + [
+                whole_spec(extra_cols[0]),
+                pl.BlockSpec((8, wide), lambda i, *_: (0, part)),
+                pl.BlockSpec((cols.shape[0], wide), lambda i, *_: (0, part)),
+                pl.BlockSpec((wide, columns.shape[1]), lambda i, *_: (part, 0)),
+                pl.BlockSpec((wide, small.shape[1]), lambda i, *_: (part, 0)),
+                whole_spec(up),
+            ],
+            out_specs=[pl.BlockSpec(memory_space=pl.ANY)] * size_x + [whole_spec(s) for s in sums],
+            scratch_shapes=[
+                pltpu.VMEM((8, wide), F32),
+                pltpu.VMEM((held, wide), F32),
+                pltpu.VMEM((2, 2, BLOCK, wide), LOW),
+                pltpu.SemaphoreType.DMA((2, 2)),
+            ],
         ),
-        out_shape=[shape((total, wide), LOW)] + sums,
+        out_shape=[shape((size_z * per, BLOCK, wide), LOW)] * size_x + sums,
         compiler_params=pltpu.CompilerParams(vmem_limit_bytes=56 * 1024 * 1024),
-        cost_estimate=work(34),
-    )(place, begins, x, x, x, grads, *mids, cols, *weights)
+        cost_estimate=work(17000),
+    )(
+        place, turn, row, begins, head, x, x, x, grads, *mids, *extra_cols, cols, columns, small, up
+    )
 
 
 TALL = BLOCK + 16
@@ -808,13 +896,18 @@
     return pieces
 
 
+def weight_rows_of(ref):
+    heads, _, seqs, _, _ = ref.shape
+    return jnp.concatenate([ref[h, 0, s] for s in range(seqs) for h in range(heads)], 0)
+
+
 def channel_kernel(
     xa_ref, xb_ref, ga_ref, gb_ref, ea_ref, eb_ref, key_ref, value_ref, hidden_ref, pre_ref, a_ref, b_ref
 ):
     rows = xa_ref.shape[0]
     x = jnp.concatenate([xa_ref[...], xb_ref[...]], 0)
     g = jnp.concatenate(with_extra(ga_ref, ea_ref) + with_extra(gb_ref, eb_ref), 0)
-    key, value = key_ref[...], value_ref[...]
+    key, value = weight_rows_of(key_ref), weight_rows_of(value_ref)
     active = jnp.maximum(dot(x, key, NN), 0.0)
     hidden_ref[...] = (active * active).astype(LOW)
     grad = (dot(g, value, NN) * 2.0 * active).astype(LOW)
@@ -832,17 +925,23 @@
         b_ref[...] += back[rows:]
 
 
-def channel_mix(x, g, extra, key, value):
+def channel_mix(x, g, extra, weights):
     rows, wide = x[0].shape
-    columns = key.shape[1]
+    heads, _, seqs, weight_rows, columns = weights.shape
     part = columns // 4
+
+    def weight(which):
+        return pl.BlockSpec(
+            (heads, 1, seqs, weight_rows, part), lambda i: (0, which, 0, 0, i)
+        )
+
     piece = pl.BlockSpec((2 * rows, part), lambda i: (0, i))
     shape = jax.ShapeDtypeStruct
     return pl.pallas_call(
         channel_kernel,
         grid=(4,),
         in_specs=[whole_spec(a) for a in (*x, *g, *extra)]
-        + [pl.BlockSpec((wide, part), lambda i: (0, i))] * 2,
+        + [weight(0), weight(1)],
         out_specs=[piece, piece, whole_spec(x[0]), whole_spec(x[0])],
         out_shape=[
             shape((2 * rows, columns), LOW),
@@ -852,7 +951,7 @@
         ],
         compiler_params=pltpu.CompilerParams(vmem_limit_bytes=48 * 1024 * 1024),
         cost_estimate=work(8),
-    )(*x, *g, *extra, key, value)
+    )(*x, *g, *extra, weights, weights)
 
 
 def main_rows(refs):
@@ -1080,12 +1179,13 @@
     splits = (DECAY_RANK, DECAY_RANK + DA, DECAY_RANK + DA + DV)
 
     og_first = output_gradient.reshape(per, BLOCK, wide)[:, 0]
-    pad = jnp.zeros((16 - per, wide), LOW)
     place = home
+    size_z, size_x = lax.axis_size("hz"), lax.axis_size("hx")
+    apart = (home // per) ^ head
+    turn_x, turn_row = apart % size_x, (apart // size_x) * per + home % per
     local = lax.dynamic_slice_in_dim(order, head * per, per)
-    before_place = taken_blocks(place, jnp.maximum(local - 1, 0))
-    after_place = taken_blocks(place, jnp.minimum(local + 1, blocks - 1))
-    group = all_gather(jnp.concatenate([tokens, og_first, pad], 0)[None], HEAD_AXES)
+    group = all_gather(tokens[None], HEAD_AXES)
+    og_rows = in_order(grown(grown(og_first[None], "hz"), "hx"), HEAD_AXES)
     og_parts = seq_gather(output_gradient)
 
     quarter = channel_key_weight.shape[1] // seqs
@@ -1093,15 +1193,12 @@
     pair = lax.all_to_all(
         pair.transpose(2, 0, 1, 3), ("ys", "core"), split_axis=0, concat_axis=0, tiled=True
     )
-    to_heads = jnp.concatenate(
-        [
-            leading_layer_value.reshape(rows_here, heads_axis, width).transpose(1, 0, 2),
-            jnp.stack([receptance_matrix, key_matrix, value_matrix], 1)
-            .reshape(weight_rows * 3, heads_axis, width)
-            .transpose(1, 0, 2),
-        ],
-        1,
-    )
+    columns = (
+        jnp.stack([receptance_matrix, key_matrix, value_matrix], 1)
+        .reshape(weight_rows * 3, heads_axis, width)
+        .transpose(1, 0, 2)
+    )
+    columns = lax.all_to_all(columns, HEAD_AXES, split_axis=0, concat_axis=0, tiled=True)
     def rank_columns(weight):
         return jnp.split(weight, (DECAY_RANK + DA, DECAY_RANK + DA + DV), 1)
 
@@ -1117,23 +1214,30 @@
         ],
         1,
     )[None]
-    to_heads = lax.all_to_all(to_heads, HEAD_AXES, split_axis=0, concat_axis=0, tiled=True)
     for axis in HEAD_AXES + ("ys", "core"):
         small = grown(small, axis)
     small = in_order(small, HEAD_AXES + ("ys", "core"))
-    first_group = to_heads[:, :rows_here]
-    columns = to_heads[:, rows_here:].reshape(1, heads_axis * weight_rows, 3 * width)
+    columns = columns.reshape(1, heads_axis * weight_rows, 3 * width)
     columns = in_order(grown(grown(columns, "ys"), "core"), ("ys", "core"))
-    out_shards = grown(grown(output_matrix[None], "hz"), "hx")
     settings = small[:, 256 + DV : 256 + DV + count].astype(F32).T
     up = lax.dynamic_slice_in_dim(small, head * width, width, 0)
     own = lax.dynamic_slice_in_dim(settings, head * width, width, 1)
     own = jnp.concatenate([own[13:16], own[8:13]], 0)
-    group, columns, small, settings, up, own, og_parts, out_shards, pair = lax.optimization_barrier(
-        (group, columns, small, settings, up, own, og_parts, out_shards, pair)
-    )
+    out_shards = grown(grown(output_matrix[None], "hz"), "hx")
+    columns, small, settings, up, own, og_parts, pair, first_sent, out_shards = (
+        lax.optimization_barrier(
+            (
+                columns, small, settings, up, own, og_parts, pair, leading_layer_value, out_shards,
+            )
+        )
+    )
+    first_group = lax.all_to_all(
+        first_sent.reshape(rows_here, heads_axis, width).transpose(1, 0, 2),
+        HEAD_AXES, split_axis=0, concat_axis=0, tiled=True,
+    ).reshape(blocks, BLOCK, width)
+    weights = [columns, small, up]
+
     out_shards = grown(out_shards, "ys")
-    weights = [columns, small, up]
 
     def gathered(half):
         return all_gather(half[None], HEAD_AXES).transpose(1, 0, 2, 3)
@@ -1144,24 +1248,12 @@
     else:
         every = (gathered(pair[:, 0]), gathered(pair[:, 1]))
 
-    parts, gate, pre, first, *mids = project(
-        group, first_group, settings, own, weights, place, home, begins, per
-    )
-    after_seq = local + 1
-    after_live = (after_seq < blocks).astype(LOW)[:, None]
-    stored = group[:, :rows_here].reshape(-1, BLOCK, wide)
-    row_before = taken_blocks(stored[:, BLOCK - 1], before_place)
-    row_after = taken_blocks(stored[:, 0], after_place)
-    og_rows = group[:, rows_here : rows_here + per].reshape(-1, wide)
-    og_after = taken_blocks(og_rows, after_place) * after_live
-    none = jnp.zeros((per, 14, wide), LOW)
-    og_extra = jnp.concatenate([none[:, :1], og_after[:, None], none], 1).reshape(-1, wide)
-    extra_parts = seq_gather(og_extra)
-    parts, og_parts, extra_parts, out_shards = lax.optimization_barrier(
-        (parts, og_parts, extra_parts, out_shards)
-    )
+    ends, parts, gate, pre, *mids = project(group, settings, own, weights, place, begins, per)
+    parts, out_shards = lax.optimization_barrier((parts, out_shards))
     out_shards = grown(out_shards, "core")
-    out_in, joined, scanned, states, mats = scan_forward(parts, gate, own, begins, PASSES)
+    values, out_in, joined, scanned, states, mats = scan_forward(
+        parts, pre, first_group, gate, own, home, begins, PASSES
+    )
 
     before, follow = jnp.maximum(order - 1, 0), jnp.minimum(order + 1, blocks - 1)
     in_blocks = out_in.reshape(blocks, BLOCK, width)
@@ -1174,37 +1266,37 @@
         ],
         1,
     )
-    extended, every = lax.optimization_barrier((extended, every))
+    extended, out_shards, ends, og_rows = lax.optimization_barrier((extended, out_shards, ends, og_rows))
     out_ext = lax.all_to_all(
         extended.reshape(heads_axis, per, TALL, width), HEAD_AXES, split_axis=0, concat_axis=0, tiled=True
     )
-    if whole_quarter:
-        key_part, value_part = [
-            x.reshape(wide, quarter)
-            for x in jnp.moveaxis(every.reshape(heads_axis, 2, seqs, weight_rows, wide), 0, 2)
-        ]
-    else:
-        key_part, value_part = [x.reshape(wide, quarter) for x in every]
     out_weight = in_order(out_shards, HEAD_AXES + ("ys", "core"))
-    out_ext, key_part, value_part, out_weight = lax.optimization_barrier(
-        (out_ext, key_part, value_part, out_weight)
-    )
+    local = lax.dynamic_slice_in_dim(order, head * per, per)
+    after_seq = local + 1
+    after_live = (after_seq < blocks).astype(LOW)[:, None]
+    after = jnp.minimum(after_seq, blocks - 1)
+    row_before = taken_blocks(ends, jnp.maximum(local - 1, 0))[:, 31]
+    row_after = taken_blocks(ends, after)[:, 0]
+    og_after = taken_blocks(og_rows, taken_blocks(home, after)) * after_live
+    none = jnp.zeros((per, 14, wide), LOW)
+    extra_parts = seq_gather(jnp.concatenate([none[:, :1], og_after[:, None], none], 1).reshape(-1, wide))
+    out_ext, out_weight = lax.optimization_barrier((out_ext, out_weight))
     tokens_b = tokens.reshape(per, BLOCK, wide)
     tokens_ext = jnp.concatenate([tokens_b, row_before[:, None], row_after[:, None], none], 1)
     middle, ffn_in, out_rows = middle_rows(
         out_ext, tokens_ext.reshape(-1, wide), out_weight, settings, local, begins
     )
-    ffn_parts = seq_gather(ffn_in)
+    ffn_in, every = lax.optimization_barrier((ffn_in, every))
     if whole_quarter:
-        *near, own_part, core_part = channel_mix(
-            ffn_parts[:2], og_parts[:2], extra_parts[:2], key_part, value_part
+        every = every.reshape(heads_axis, 2, seqs, weight_rows, wide)
+        value_part = every[:, 1].transpose(1, 0, 2, 3).reshape(wide, wide)
+        ffn_parts = [ffn_in, swap(ffn_in, "core"), swap(ffn_in, "ys")]
+        *near, own_part, core_part = channel_mix(ffn_parts[:2], og_parts[:2], extra_parts[:2], every)
+        ffn_parts[2], near, own_part, core_part, out_rows = lax.optimization_barrier(
+            (ffn_parts[2], near, own_part, core_part, out_rows)
         )
-        ffn_parts[2:], near, own_part, core_part, out_rows = lax.optimization_barrier(
-            (ffn_parts[2:], near, own_part, core_part, out_rows)
-        )
-        *far, far_part, diagonal = channel_mix(
-            ffn_parts[2:], og_parts[2:], extra_parts[2:], key_part, value_part
-        )
+        ffn_parts.append(swap(ffn_parts[2], "core"))
+        *far, far_part, diagonal = channel_mix(ffn_parts[2:], og_parts[2:], extra_parts[2:], every)
         came_core, came_far = seq_return(own_part, core_part, far_part, diagonal)
         grads_here = channel_grads(
             og_parts, ffn_parts, (near[0], far[0]), (near[1], far[1]), wide // seqs
@@ -1212,6 +1304,8 @@
         came_far, grads_here = lax.optimization_barrier((came_far, grads_here))
         hidden = [near[0], far[0]]
     else:
+        key_part, value_part = [x.reshape(wide, quarter) for x in every]
+        ffn_parts = seq_gather(ffn_in)
         rows = jnp.concatenate(ffn_parts, 0)
         og_rows = jnp.concatenate(
             [
@@ -1231,7 +1325,6 @@
     grad_middle, middle_low, grad_out, cols_ffn = middle_back(
         own_part, came_core, came_far, middle, output_gradient, out_weight, settings, local, begins, heads_axis
     )
-    cols_ffn = cols_ffn[:3]
     grad_heads = lax.all_to_all(grad_out, HEAD_AXES, split_axis=0, concat_axis=0, tiled=True)
     out_parts, low_parts = seq_gather(out_rows), seq_gather(middle_low)
     which = lax.axis_index(("ys", "core"))
@@ -1246,43 +1339,39 @@
     grads_here = lax.psum_scatter(grads_here, HEAD_AXES, scatter_dimension=0, tiled=True)
 
     scan_grads, first_grad, cols_scan = scan_backward(
-        parts, joined, scanned, gate, grad_heads.reshape(blocks, BLOCK, width), pre, first, own, states,
-        mats, home, begins, PASSES,
+        parts, values, joined, scanned, gate, grad_heads.reshape(blocks, BLOCK, width), pre, first_group,
+        own, states, mats, home, begins, PASSES,
     )
     first_grad = taken_blocks(first_grad.reshape(blocks, BLOCK, width), order)
     first_value_grad = lax.all_to_all(
         first_grad.reshape(heads_axis, rows_here, width), HEAD_AXES, split_axis=0, concat_axis=2, tiled=True
     ).reshape(rows_here, wide).astype(F32)
 
-    back, down_sums, up_sums = project_back(
-        group, scan_grads, mids, settings, weights, place, begins, per
-    )
-    back = taken_blocks(back.reshape(blocks, BLOCK, wide), order).reshape(-1, wide)
-    back, grads_here, first_value_grad = lax.optimization_barrier((back, grads_here, first_value_grad))
-    back = lax.psum_scatter(back, HEAD_AXES, scatter_dimension=0, tiled=True).astype(F32)
-    value_sum, key_sum, out_sum = jnp.split(grads_here.astype(F32), (quarter, 2 * quarter), 1)
-
     share = wide // seqs
     thin = low_rank // seqs
     fold = heads_axis // seqs
 
-    def over_ys(sums):
-        down_sums, up_sums, own_cols = sums
-        own_cols = lax.dynamic_update_slice(jnp.zeros((8, wide), F32), own_cols, (0, head * width))
-        rows_out = jnp.concatenate([down_sums, own_cols, cols_ffn], 0)
-        rows_out = jnp.pad(rows_out, ((0, -rows_out.shape[0] % 16), (0, 0)))
-        rows_out = rows_out.astype(LOW).reshape(-1, seqs, share).transpose(1, 0, 2)
-        both = jnp.concatenate(
-            [rows_out, up_sums.astype(LOW).reshape(seqs, thin * width // share, share)], 1
-        )
-        return seq_step(both, "ys")
-
-    def over_core(x):
-        return seq_step(x, "core")
-
-    def to_owners(x):
-        rows_out_count = x.shape[0] - thin * width // share
-        rows_out, up_sums = x[:rows_out_count], x[rows_out_count:].reshape(thin, width)
+    def over_ys(left, right, up_sums):
+        up_sums = up_sums.astype(LOW).reshape(seqs, thin, width)
+        if ys != 2:
+            rows_out = jnp.concatenate([left, right], 1)
+            return rows_out.reshape(-1, seqs, share).transpose(1, 0, 2), up_sums
+        index = lax.axis_index("ys")
+        came = swap(jnp.where(index == 0, right, left), "ys")
+        total = jnp.where(index == 0, left, right).astype(F32) + came.astype(F32)
+        return total.reshape(-1, 2, share), seq_step(up_sums, "ys")
+
+    def over_core(rows_out, up_sums):
+        if ys != 2:
+            return [
+                lax.psum_scatter(x, ("ys", "core"), scatter_dimension=0, tiled=True)[0].astype(F32)
+                for x in (rows_out, up_sums)
+            ]
+        sent = lax.dynamic_index_in_dim(rows_out, 1 - core, 1, keepdims=False).astype(LOW)
+        kept_rows = lax.dynamic_index_in_dim(rows_out, core, 1, keepdims=False)
+        return kept_rows + swap(sent, "core").astype(F32), seq_step(up_sums, "core")
+
+    def to_owners(rows_out):
         rows_low = rows_out.astype(LOW)
         squares = rows_low[: 3 * width].reshape(3 * width, fold, width)
         mixed = rows_low[3 * width : 3 * width + low_rank].reshape(seqs, thin, fold, width)
@@ -1302,7 +1391,7 @@
                     sent, every_axis, [(q * heads_axis + h, owner(q, h, (h + k) % fold)) for q, h in pairs]
                 )
             )
-        return up_sums, mixed, came
+        return mixed, came
 
     every_axis = ("ys", "core") + HEAD_AXES
     pairs = [(q, h) for q in range(seqs) for h in range(heads_axis)]
@@ -1310,7 +1399,63 @@
     def owner(q, h, j):
         return (h // fold) * heads_axis + q * fold + j
 
-    up_sums, mixed, came = to_owners(over_core(over_ys((down_sums, up_sums, cols_scan))))
+    sizes = (size_z, size_x)
+
+    def others_x(blocks_back):
+        return [
+            lax.ppermute(blocks_back[k], "hx", [(i, i ^ k) for i in range(size_x)])
+            for k in range(1, size_x)
+        ]
+
+    def after_x(kept_blocks, came):
+        total = kept_blocks.astype(F32)
+        for x in came:
+            total = total + x.astype(F32)
+        total = total.reshape(size_z, rows_here, -1)
+        return total[0], [total[k].astype(LOW) for k in range(1, size_z)]
+
+    def others_z(sent):
+        return [
+            lax.ppermute(x, "hz", [(i, i ^ k) for i in range(size_z)]) for k, x in enumerate(sent, 1)
+        ]
+
+    def half_back(part, grads):
+        outs = project_back(
+            part, 2, group, grads, mids, (cols_scan, cols_ffn), settings, weights, place, turn_x, turn_row,
+            begins, head[None], per, sizes,
+        )
+        return outs[:size_x], outs[size_x:]
+
+    left_blocks, (left_sum, up_sums) = half_back(0, scan_grads)
+    left_came = others_x(left_blocks)
+    scan_grads, left_sum = lax.optimization_barrier((scan_grads, left_sum))
+    right_blocks, (right_sum,) = half_back(1, scan_grads)
+    right_blocks, left_came, right_sum, first_value_grad = lax.optimization_barrier(
+        (right_blocks, left_came, right_sum, first_value_grad)
+    )
+    right_came = others_x(right_blocks)
+    left_own, left_sent = after_x(left_blocks[0], left_came)
+    left_sent, right_sum, hidden = lax.optimization_barrier((left_sent, right_sum, hidden))
+    left_z = others_z(left_sent)
+    rows_out, up_sums = over_ys(left_sum, right_sum, up_sums)
+    outs = [dot(h, value_part, NT) for h in hidden]
+    right_came, outs, grads_here = lax.optimization_barrier((right_came, outs, grads_here))
+    right_own, right_sent = after_x(right_blocks[0], right_came)
+    right_sent, left_z, rows_out, up_sums, outs = lax.optimization_barrier(
+        (right_sent, left_z, rows_out, up_sums, outs)
+    )
+    right_z = others_z(right_sent)
+    rows_out, up_sums = over_core(rows_out, up_sums)
+    mixed, came = to_owners(rows_out)
+    if whole_quarter:
+        came_core, came_far = seq_return(*[x for out in outs for x in jnp.split(out, 2, 0)])
+        right_z, came_core, came_far = lax.optimization_barrier((right_z, came_core, came_far))
+    right_z, up_sums, mixed, came = lax.optimization_barrier((right_z, up_sums, mixed, came))
+    back = jnp.concatenate(
+        [own + sum(x.astype(F32) for x in z) for own, z in ((left_own, left_z), (right_own, right_z))], 1
+    )
+    value_sum, key_sum, out_sum = jnp.split(grads_here.astype(F32), (quarter, 2 * quarter), 1)
+
     unit, scale = norm_rows(tokens.astype(F32))
     tokens_grad = grad_middle + norm_back(back, unit, scale, settings[0])
     mixed = jnp.sum(mixed.astype(F32), 0)
@@ -1318,18 +1463,16 @@
     down_grad = lax.ppermute(
         mixed[:thin].astype(LOW), every_axis, [(q * heads_axis + h, owner(q, h, h % fold)) for q, h in pairs]
     ).T.astype(F32)
-    outs = [dot(h, value_part, NT) for h in hidden]
-    main_middle = middle.reshape(per, TALL, wide)[:, :BLOCK].reshape(rows_here, wide)
 
     def main_of(x):
         return x.reshape(-1, per, TALL, wide)[:, :, :BLOCK].reshape(-1, rows_here, wide)
 
+    layer_out = main_of(middle)[0]
     if whole_quarter:
-        near, far = [main_of(x) for x in outs]
-        came_core, came_far = seq_return(near[0], near[1], far[0], far[1])
-        layer_out = main_middle + near[0] + came_core + came_far.astype(F32)
+        own_out = jnp.split(outs[0], 2, 0)[0]
+        layer_out = layer_out + main_of(own_out)[0] + main_of(came_core)[0] + main_of(came_far)[0].astype(F32)
     else:
-        layer_out = main_middle + lax.psum_scatter(
+        layer_out = layer_out + lax.psum_scatter(
             main_of(outs[0]), ("ys", "core"), scatter_dimension=0, tiled=True
         )[0]
     came = jnp.stack(came, 0)

time: 503 us -> 490 us (0.974)
  waiting for transfers between devices: 145 us -> 91.6 us
  starting transfers between devices: 64.9 us -> 85.5 us
  Pallas kernels: 171 us -> 181 us
  other arithmetic: 23.1 us -> 32.9 us
    all_gather x2, waiting for transfers between devices: 28.2 us -> 0.01 us  [all_gather(): return lax.all_gather(x, axes, axis=0, tiled=True)]
    reduce_scatter x1 -> x0, waiting for transfers between devices: 19.9 us -> none  [body(): lax.psum_scatter(back, HEAD_AXES, scatter_dimension=0, tiled=True)]
    ppermute x23 -> x25, waiting for transfers between devices: 60.9 us -> 41.9 us  [swap(): return lax.ppermute(x, axis, [(0, 1), (1, 0)])]
    ppermute x0 -> x8, starting transfers between devices: none -> 14.3 us  [the longest x6 11.9 us: others_z(): lax.ppermute(x, 'hz', [(i, i ^ k) for i in range(size_z)])]
    ppermute x2, waiting for transfers between devices: 3.72 us -> 17.3 us  [to_owners(): lax.ppermute(sent, every_axis, [(q * heads_axis + h, owner(q, h, (h + k)...]
    pallas_call x1 -> x2, Pallas kernels: 32 us -> 42.3 us  [project_back(): pl.pallas_call(functools.partial(project_back_kernel, part, parts), grid_...]
    add x0 -> x6, other arithmetic: none -> 8.37 us  [the longest x2 3.93 us: after_x(): total = total + x.astype(F32)]
    unnamed x142 -> x138, local copies, waits for them, and re-layouts: 20 us -> 26.7 us
  transfers between devices with their start and end apart: 50 -> 64, of which waited for: 21 -> 19; matrix products, arithmetic and copies ran while one was open for 16% -> 19% of each run, Pallas kernels for 32% -> 36%
where the time goes in v2:
time: 490 us; the launch traced here: 482 us
  Pallas kernels  181 us (37%)
  waiting for transfers between devices  91.6 us (19%)
  starting transfers between devices  85.5 us (17%)
  local copies, waits for them, and re-layouts  70.3 us (14%)
  other arithmetic  32.9 us (7%)
  between operations  15.1 us (3%)
  matrix products  5.76 us (1%)
    pallas_call x1, Pallas kernels, scan_backward(): pl.pallas_call(functools.partial(scan_backward_kernel, heads, p), grid_sp...  50.4 us
    pallas_call x2, Pallas kernels, project_back(): pl.pallas_call(functools.partial(project_back_kernel, part, parts), grid_...  42.3 us
    ppermute x25, waiting for transfers between devices, swap(): return lax.ppermute(x, axis, [(0, 1), (1, 0)])  41.9 us
    pallas_call x1, Pallas kernels, scan_forward(): pl.pallas_call(functools.partial(scan_forward_kernel, heads, p), grid_spe...  35.2 us
    unnamed x138, local copies, waits for them, and re-layouts  26.7 us
    ppermute x18, waiting for transfers between devices, steps_along(): lax.ppermute(x, axis, [(i, i ^ k) for i in range(size)])  22.7 us
    ppermute x18, starting transfers between devices, steps_along(): lax.ppermute(x, axis, [(i, i ^ k) for i in range(size)])  21.8 us
    pallas_call x1, Pallas kernels, project(): pl.pallas_call(project_kernel, grid_spec=pltpu.PrefetchScalarGridSpec(num...  18 us
  transfers between devices with their start and end apart: 64, of which 19 were waited for; matrix products, arithmetic and copies ran while one was open for 19% of the time, Pallas kernels for 36%

profile of v2, /device:TPU:4, one launch (start us, length us, event | category | flops | bytes accessed | tf_op | source)
XLA Modules:
  0.0 482.4 jit_solution(23027378123068811)
XLA Ops:
  11.1 3.7 collective-permute-start.4
  15.6 3.6 collective-permute-start.13
  21.2 5.2 %all-to-all-start = ((bf16[8,96,128]{2,1,0:T(8,128)(2,1)}), bf16[8,96,128]{2,1,0:T(8,128)(2,1)S(1)}, u32[]{:S(2)}, u32[]{:S(2)}) async-start(bf16[8,96,128]{2,1,0:T(8,128)(2,1)} %copy.102), calls=%async_computation | async-start | bytes 393216 | tf_op jit(solution)/shard_map/all_to_all | solution.py:1201
  29.5 2.0 collective-permute-start.11
  35.6 2.0 collective-permute-done.5
  40.1 4.5 all-to-all-start.1
  47.0 6.5 %collective-permute-done.6 = bf16[8,32,640]{2,1,0:T(8,128)(2,1)S(1)} collective-permute-done((bf16[8,32,640]{2,1,0:T(8,128)(2,1)}, bf16[8,32,640]{2,1,0:T(8,128)(2,1)S(1)}, u32[]{:S(2)}, u32[]{:S(2)}) %collective-permute-start.6) | collective-permute-done | bytes 327712 | tf_op jit(solution)/shard_map/ppermute | solution.py:1092
  54.3 5.5 %collective-permute-done = bf16[1,256,384]{2,1,0:T(8,128)(2,1)S(1)} collective-permute-done((bf16[1,256,384]{2,1,0:T(8,128)(2,1)S(1)}, bf16[1,256,384]{2,1,0:T(8,128)(2,1)S(1)}, u32[]{:S(2)}, u32[]{:S(2)}) %collective-permute-start) | collective-permute-done | bytes 196640 | tf_op jit(solution)/shard_map/ppermute | solution.py:1092
  65.7 2.0 constant_dynamic-update-slice_fusion.11
  67.7 3.2 gather_fusion.1
  74.6 2.2 copy.115
  76.9 2.4 collective-permute-start.19
  79.4 1.9 collective-permute-start.17
  83.6 4.8 all-to-all-start.2
  89.2 6.4 %collective-permute-done.15 = bf16[8,32,1024]{2,1,0:T(8,128)(2,1)} collective-permute-done((bf16[8,32,1024]{2,1,0:T(8,128)(2,1)}, bf16[8,32,1024]{2,1,0:T(8,128)(2,1)}, u32[]{:S(2)}, u32[]{:S(2)}) %collective-permute-start.15) | collective-permute-done | bytes 524320 | tf_op jit(solution)/shard_map/ppermute | solution.py:1092
  95.7 2.3 pad_maximum_fusion.1
  97.9 18.0 %shard_map.238 = (bf16[16,32,1024]{2,1,0:T(8,128)(2,1)}, bf16[5,2048,128]{2,1,0:T(8,128)(2,1)}, f32[2048,128]{1,0:T(8,128)}, f32[5,2048,128]{2,1,0:T(8,128)}, f3...) custom-call(s32[16]{0:T(128)} %bitcast.183, s32[4]{0:T(128)} %bitcast_subtract_fusion.begins_ref, ...), custom_call_target="tpu_custom_call" | custom-call | bytes 60000 | tf_op jit(solution)/shard_map/pallas_call | solution.py:629
  117.7 2.2 collective-permute-done.20
  122.0 35.2 %shard_map.239 = (bf16[2048,128]{1,0:T(8,128)(2,1)S(1)}, bf16[2048,128]{1,0:T(8,128)(2,1)S(1)}, bf16[2048,128]{1,0:T(8,128)(2,1)S(1)}, f32[2048,128]{1,0:T(8,128...) custom-call(s32[16]{0:T(128)S(1)} %bitcast.187, s32[4]{0:T(128)S(1)} %copy-done.35, ...), custom_call_target="tpu_custom_call" | custom-call | bytes 240000 | tf_op jit(solution)/shard_map/pallas_call | solution.py:260
  161.8 3.1 pad_maximum_fusion
  164.9 4.9 %all-to-all-start.3 = ((bf16[8,2,144,128]{3,2,1,0:T(8,128)(2,1)}), bf16[8,2,144,128]{3,2,1,0:T(8,128)(2,1)S(1)}, u32[]{:S(2)}, u32[]{:S(2)}) async-start(bf16[8,2,144,128]{3,2,1,0:T(8,128)(2,1)} %bitcast.231), calls=%async_computation.3 | async-start | bytes 1179648 | tf_op jit(solution)/shard_map/all_to_all | solution.py:1270
  170.4 1.8 gather_fusion.8
  172.2 1.8 gather_fusion.7
  174.0 2.3 gather_fusion.6
  176.3 2.5 pad_maximum_fusion.3
  178.8 6.7 %all-to-all-done.3.out_ref = bf16[8,2,144,128]{3,2,1,0:T(8,128)(2,1)S(1)} async-done(((bf16[8,2,144,128]{3,2,1,0:T(8,128)(2,1)}), bf16[8,2,144,128]{3,2,1,0:T(8,128)(2,1)S(1)}, u32[]{:S(2)}, u32[]{:S(2)}) %all-to-all-start.3) | async-done | bytes 589856 | tf_op jit(solution)/shard_map/all_to_all | solution.py:1270
  186.5 1.9 shard_map.240
  195.8 7.8 %shard_map.241 = (bf16[576,1024]{1,0:T(8,128)(2,1)S(1)}, bf16[576,1024]{1,0:T(8,128)(2,1)S(1)}, f32[288,1024]{1,0:T(8,128)S(1)}, f32[288,1024]{1,0:T(8,128)}) custom-call(bf16[288,1024]{1,0:T(8,128)(2,1)S(1)} %copy-done.12, bf16[288,1024]{1,0:T(8,128)(2,1)S(1)} %collective-permute-done.22.xb_ref.refs_5_, bf16[256,1024]{1,0:T(8,128)(2,1)S(1)} %copy-done.5, ...), custom_call_target="tpu_custom_call" | custom-call | bytes 24000 | tf_op jit(solution)/shard_map/pallas_call | solution.py:940
  204.6 2.5 collective-permute-done.21.xa_ref.refs_6_
  207.6 4.0 collective-permute-done.26.ea_ref
  212.9 7.7 %shard_map.242 = (bf16[576,1024]{1,0:T(8,128)(2,1)S(1)}, bf16[576,1024]{1,0:T(8,128)(2,1)S(1)}, f32[288,1024]{1,0:T(8,128)S(1)}, f32[288,1024]{1,0:T(8,128)}) custom-call(bf16[288,1024]{1,0:T(8,128)(2,1)S(1)} %collective-permute-done.21.xa_ref.refs_6_, bf16[288,1024]{1,0:T(8,128)(2,1)S(1)} %collective-permute-done.25.xb_ref.refs_7_, ...), custom_call_target="tpu_custom_call" | custom-call | bytes 24000 | tf_op jit(solution)/shard_map/pallas_call | solution.py:940
  221.1 2.7 collective-permute-done.28
  226.2 8.8 %shard_map.243.refs_8_ = bf16[1024,2304]{1,0:T(8,128)(2,1)} custom-call(bf16[256,1024]{1,0:T(8,128)(2,1)S(1)} %copy-done.5, bf16[256,1024]{1,0:T(8,128)(2,1)S(1)} %copy-done.18, bf16[256,1024]{1,0:T(8,128)(2,1)S(1)} %copy-done.15, bf16[256,1024]{1,0:T(8,128)(2,1)S(1)} %copy-done.20, bf16[288,1024]{1,0:T(8,128)(2,1)S(1)} %copy-done.13, ...), custom_call_target="tpu_custom_call" | custom-call | bytes 27000 | tf_op jit(solution)/shard_map/pallas_call | solution.py:978
  234.9 5.4 %collective-permute-done.29.far_ref = bf16[288,1024]{1,0:T(8,128)(2,1)S(1)} collective-permute-done((bf16[288,1024]{1,0:T(8,128)(2,1)S(1)}, bf16[288,1024]{1,0:T(8,128)(2,1)S(1)}, u32[]{:S(2)}, u32[]{:S(2)}) %collective-permute-start.29) | collective-permute-done | bytes 589856 | tf_op jit(solution)/shard_map/ppermute | solution.py:1116
  240.3 4.8 shard_map.244
  246.5 4.1 all-to-all-start.4
  250.8 2.3 collective-permute-done.31.refs_2_
  253.5 11.2 %collective-permute-done.34.refs_6_ = bf16[288,1024]{1,0:T(8,128)(2,1)S(1)} collective-permute-done((bf16[288,1024]{1,0:T(8,128)(2,1)S(1)}, bf16[288,1024]{1,0:T(8,128)(2,1)S(1)}, u32[]{:S(2)}, u32[]{:S(2)}) %collective-permute-start.34) | collective-permute-done | bytes 589856 | tf_op jit(solution)/shard_map/ppermute | solution.py:1116
  264.8 2.1 collective-permute-done.35.refs_7_
  266.9 4.5 shard_map.245
  273.4 50.4 %shard_map.246 = (bf16[7,2048,128]{2,1,0:T(8,128)(2,1)}, bf16[2048,128]{1,0:T(8,128)(2,1)}, f32[8,128]{1,0:T(8,128)}) custom-call(s32[16]{0:T(128)} %bitcast.184, s32[4]{0:T(128)} %bitcast_subtract_fusion.begins_ref, bf16[5,2048,128]{2,1,0:T(8,128)(2,1)} %get-tuple-element.128.parts_ref, bf16[2048,128]{1,0:T(8,128)(2,1)} %copy-done.30, ...), custom_call_target="tpu_custom_call" | custom-call | bytes 180000 | tf_op jit(solution)/shard_map/pallas_call | solution.py:479
  323.7 2.5 gather_fusion.11
  326.2 3.9 all-to-all-start.5
  330.6 21.6 %shard_map.247 = (bf16[8,128,512]{2,1,0:T(8,128)(2,1)}, bf16[8,128,512]{2,1,0:T(8,128)(2,1)}, bf16[704,512]{1,0:T(8,128)(2,1)}, f32[288,128]{1,0:T(8,128)}) custom-call(s32[16]{0:T(128)} %bitcast.185, s32[16]{0:T(128)} %and_select_fusion.3.turn_ref, s32[16]{0:T(128)} %get-tuple-element.272.row_ref, s32[4]{0:T(128)} %bitcast_subtract_fusion.begins_ref, ...), custom_call_target="tpu_custom_call" | custom-call | bytes 51000000 | tf_op jit(solution)/shard_map/pallas_call | solution.py:798
  352.2 2.1 collective-permute-start.36
  357.6 20.7 %shard_map.248 = (bf16[8,128,512]{2,1,0:T(8,128)(2,1)}, bf16[8,128,512]{2,1,0:T(8,128)(2,1)}, bf16[704,512]{1,0:T(8,128)(2,1)}) custom-call(s32[16]{0:T(128)} %bitcast.186, s32[16]{0:T(128)} %and_select_fusion.3.turn_ref, s32[16]{0:T(128)} %get-tuple-element.272.row_ref, s32[4]{0:T(128)} %bitcast_subtract_fusion.begins_ref, s32[1]{0:T(128)} %bitcast.41.head_ref, ...), custom_call_target="tpu_custom_call" | custom-call | bytes 51000000 | tf_op jit(solution)/shard_map/pallas_call | solution.py:798
  381.0 2.0 convert_add_fusion.1
  384.0 1.7 collective-permute-start.38
  385.7 2.4 collective-permute-start.39
  389.7 2.9 fusion.67
  392.6 2.9 fusion.68
  395.5 9.4 %collective-permute-done.41 = bf16[704,512]{1,0:T(8,128)(2,1)S(1)} collective-permute-done((bf16[704,512]{1,0:T(8,128)(2,1)S(1)}, bf16[704,512]{1,0:T(8,128)(2,1)S(1)}, u32[]{:S(2)}, u32[]{:S(2)}) %collective-permute-start.41) | collective-permute-done | bytes 720928 | tf_op jit(solution)/shard_map/ppermute | solution.py:1116
  406.3 2.4 reshape.881
  408.7 2.0 convert_add_fusion
  421.2 3.3 collective-permute-start.44
  427.9 3.4 all-to-all-start.6
  431.4 3.7 collective-permute-start.45
  435.6 2.3 collective-permute-start.51
  437.9 4.4 collective-permute-start.52
  442.9 2.3 collective-permute-done.45
  445.2 14.2 %collective-permute-done.51 = bf16[384,128]{1,0:T(8,128)(2,1)S(1)} collective-permute-done((bf16[384,128]{1,0:T(8,128)(2,1)S(1)}, bf16[384,128]{1,0:T(8,128)(2,1)S(1)}, u32[]{:S(2)}, u32[]{:S(2)}) %collective-permute-start.51) | collective-permute-done | bytes 98336 | tf_op jit(solution)/shard_map/ppermute | solution.py:1390
  459.4 3.0 collective-permute-done.52
  464.8 1.9 collective-permute-start.53
  469.5 2.6 fusion.10
  (363 shorter events, 93.1 us)
Async XLA Ops:
  7.2 90.7 %all-gather.6.cloned.1.call-start = ((), (), s32[]{:S(2)}) async-start(), calls=%async_computation.10 | async-start | bytes 4718592 | tf_op jit(solution)/shard_map/all_gather | solution.py:1087
  11.1 18.4 %collective-permute-start.4 = (bf16[1,32,640]{2,1,0:T(8,128)(2,1)S(1)}, bf16[1,32,640]{2,1,0:T(8,128)(2,1)S(1)}, u32[]{:S(2)}, u32[]{:S(2)}) collective-permute-start(bf16[1,32,640]{2,1,0:T(8,128)(2,1)S(1)} %bitcast.242), channel_id=1, source_target_pairs={{0,6},{2,4},{4,2},{6,0},{1,7},{3,5},{5,3},{7,1},{8,14},{10,12},{12... | collective-permute-start | bytes 122888 | tf_op jit(solution)/shard_map/ppermute | solution.py:1092
  14.8 16.8 %collective-permute-start.3 = (bf16[1,32,640]{2,1,0:T(8,128)(2,1)S(1)}, bf16[1,32,640]{2,1,0:T(8,128)(2,1)S(1)}, u32[]{:S(2)}, u32[]{:S(2)}) collective-permute-start(bf16[1,32,640]{2,1,0:T(8,128)(2,1)S(1)} %bitcast.243), channel_id=1, source_target_pairs={{0,4},{2,6},{4,0},{6,2},{1,5},{3,7},{5,1},{7,3},{8,12},{10,14},{12... | collective-permute-start | bytes 122888 | tf_op jit(solution)/shard_map/ppermute | solution.py:1092
  14.8 17.3 %collective-permute-start.2 = (bf16[1,32,640]{2,1,0:T(8,128)(2,1)S(1)}, bf16[1,32,640]{2,1,0:T(8,128)(2,1)S(1)}, u32[]{:S(2)}, u32[]{:S(2)}) collective-permute-start(bf16[1,32,640]{2,1,0:T(8,128)(2,1)S(1)} %bitcast.244), channel_id=1, source_target_pairs={{0,2},{2,0},{4,6},{6,4},{1,3},{3,1},{5,7},{7,5},{8,10},{10,8},{12,... | collective-permute-start | bytes 122888 | tf_op jit(solution)/shard_map/ppermute | solution.py:1092
  15.6 29.1 %collective-permute-start.13 = (bf16[1,32,1024]{2,1,0:T(8,128)(2,1)}, bf16[1,32,1024]{2,1,0:T(8,128)(2,1)S(1)}, u32[]{:S(2)}, u32[]{:S(2)}) collective-permute-start(bf16[1,32,1024]{2,1,0:T(8,128)(2,1)} %bitcast.251), channel_id=1, source_target_pairs={{0,6},{2,4},{4,2},{6,0},{1,7},{3,5},{5,3},{7,1},{8,14},{10,12},{12... | collective-permute-start | bytes 196616 | tf_op jit(solution)/shard_map/ppermute | solution.py:1092
  19.2 25.8 %collective-permute-start.12 = (bf16[1,32,1024]{2,1,0:T(8,128)(2,1)}, bf16[1,32,1024]{2,1,0:T(8,128)(2,1)S(1)}, u32[]{:S(2)}, u32[]{:S(2)}) collective-permute-start(bf16[1,32,1024]{2,1,0:T(8,128)(2,1)} %bitcast.252), channel_id=1, source_target_pairs={{0,4},{2,6},{4,0},{6,2},{1,5},{3,7},{5,1},{7,3},{8,12},{10,14},{12... | collective-permute-start | bytes 196616 | tf_op jit(solution)/shard_map/ppermute | solution.py:1092
  21.2 18.9 %all-to-all-start = ((bf16[8,96,128]{2,1,0:T(8,128)(2,1)}), bf16[8,96,128]{2,1,0:T(8,128)(2,1)S(1)}, u32[]{:S(2)}, u32[]{:S(2)}) async-start(bf16[8,96,128]{2,1,0:T(8,128)(2,1)} %copy.102), calls=%async_computation | async-start | bytes 393216 | tf_op jit(solution)/shard_map/all_to_all | solution.py:1201
  29.5 15.8 %collective-permute-start.11 = (bf16[1,32,1024]{2,1,0:T(8,128)(2,1)S(1)}, bf16[1,32,1024]{2,1,0:T(8,128)(2,1)S(1)}, u32[]{:S(2)}, u32[]{:S(2)}) collective-permute-start(bf16[1,32,1024]{2,1,0:T(8,128)(2,1)S(1)} %bitcast.253), channel_id=1, source_target_pairs={{0,2},{2,0},{4,6},{6,4},{1,3},{3,1},{5,7},{7,5},{8,10},{10,8},{12,... | collective-permute-start | bytes 196616 | tf_op jit(solution)/shard_map/ppermute | solution.py:1092
  31.6 31.1 %collective-permute-start.9 = (bf16[256,1024]{1,0:T(8,128)(2,1)S(1)}, bf16[256,1024]{1,0:T(8,128)(2,1)S(1)}, u32[]{:S(2)}, u32[]{:S(2)}) collective-permute-start(bf16[256,1024]{1,0:T(8,128)(2,1)S(1)} %copy-done.5), channel_id=1, source_target_pairs={{0,16},{16,0},{1,17},{17,1},{2,18},{18,2},{3,19},{19,3},{4,20},{20... | collective-permute-start | bytes 1572872 | tf_op jit(solution)/shard_map/ppermute | solution.py:1116
  32.1 5.5 %collective-permute-start.5 = (bf16[4,32,640]{2,1,0:T(8,128)(2,1)S(1)}, bf16[4,32,640]{2,1,0:T(8,128)(2,1)S(1)}, u32[]{:S(2)}, u32[]{:S(2)}) collective-permute-start(bf16[4,32,640]{2,1,0:T(8,128)(2,1)S(1)} %pad_maximum_fusion.8), channel_id=1, source_target_pairs={{0,1},{1,0},{2,3},{3,2},{4,5},{5,4},{6,7},{7,6},{8,9},{9,8},{10,11... | collective-permute-start | bytes 491528 | tf_op jit(solution)/shard_map/ppermute | solution.py:1092
  38.4 15.0 %collective-permute-start.6 = (bf16[8,32,640]{2,1,0:T(8,128)(2,1)}, bf16[8,32,640]{2,1,0:T(8,128)(2,1)S(1)}, u32[]{:S(2)}, u32[]{:S(2)}) collective-permute-start(bf16[8,32,640]{2,1,0:T(8,128)(2,1)} %get-tuple-element.301), channel_id=1, source_target_pairs={{0,16},{16,0},{1,17},{17,1},{2,18},{18,2},{3,19},{19,3},{4,20},{20... | collective-permute-start | bytes 983048 | tf_op jit(solution)/shard_map/ppermute | solution.py:1092
  40.1 34.5 %all-to-all-start.1 = ((bf16[4,2,32,1024]{3,2,1,0:T(8,128)(2,1)}), bf16[4,2,32,1024]{3,2,1,0:T(8,128)(2,1)}, u32[]{:S(2)}, u32[]{:S(2)}) async-start(bf16[4,2,32,1024]{3,2,1,0:T(8,128)(2,1)} %copy.106), calls=%async_computation.1 | async-start | bytes 1048576 | tf_op jit(solution)/shard_map/all_to_all | solution.py:1193
  44.6 146.5 %all-gather.4.cloned.1.call-start = ((), (), s32[]{:S(2)}) async-start(), calls=%async_computation.8 | async-start | bytes 4718592 | tf_op jit(solution)/shard_map/all_gather | solution.py:1087
  44.7 29.9 %collective-permute-start.8 = (bf16[256,1024]{1,0:T(8,128)(2,1)S(1)}, bf16[256,1024]{1,0:T(8,128)(2,1)S(1)}, u32[]{:S(2)}, u32[]{:S(2)}) collective-permute-start(bf16[256,1024]{1,0:T(8,128)(2,1)S(1)} %copy-done.5), channel_id=1, source_target_pairs={{0,8},{8,0},{1,9},{9,1},{2,10},{10,2},{3,11},{11,3},{4,12},{12,4},... | collective-permute-start | bytes 1572872 | tf_op jit(solution)/shard_map/ppermute | solution.py:1116
  44.9 14.9 %collective-permute-start = (bf16[1,256,384]{2,1,0:T(8,128)(2,1)S(1)}, bf16[1,256,384]{2,1,0:T(8,128)(2,1)S(1)}, u32[]{:S(2)}, u32[]{:S(2)}) collective-permute-start(bf16[1,256,384]{2,1,0:T(8,128)(2,1)S(1)} %reshape.861), channel_id=1, source_target_pairs={{0,16},{16,0},{1,17},{17,1},{2,18},{18,2},{3,19},{19,3},{4,20},{20... | collective-permute-start | bytes 589832 | tf_op jit(solution)/shard_map/ppermute | solution.py:1092
  45.3 16.5 %collective-permute-start.14 = (bf16[4,32,1024]{2,1,0:T(8,128)(2,1)S(1)}, bf16[4,32,1024]{2,1,0:T(8,128)(2,1)S(1)}, u32[]{:S(2)}, u32[]{:S(2)}) collective-permute-start(bf16[4,32,1024]{2,1,0:T(8,128)(2,1)S(1)} %pad_maximum_fusion.5), channel_id=1, source_target_pairs={{0,1},{1,0},{2,3},{3,2},{4,5},{5,4},{6,7},{7,6},{8,9},{9,8},{10,11... | collective-permute-start | bytes 786440 | tf_op jit(solution)/shard_map/ppermute | solution.py:1092
  54.3 11.4 %collective-permute-start.7 = (bf16[16,32,640]{2,1,0:T(8,128)(2,1)}, bf16[16,32,640]{2,1,0:T(8,128)(2,1)}, u32[]{:S(2)}, u32[]{:S(2)}) collective-permute-start(bf16[16,32,640]{2,1,0:T(8,128)(2,1)} %get-tuple-element.292), channel_id=1, source_target_pairs={{0,8},{8,0},{1,9},{9,1},{2,10},{10,2},{3,11},{11,3},{4,12},{12,4},... | collective-permute-start | bytes 1966088 | tf_op jit(solution)/shard_map/ppermute | solution.py:1092
  59.9 3.2 collective-permute-start.1
  62.6 12.0 %collective-permute-start.10 = (bf16[256,1024]{1,0:T(8,128)(2,1)S(1)}, bf16[256,1024]{1,0:T(8,128)(2,1)S(1)}, u32[]{:S(2)}, u32[]{:S(2)}) collective-permute-start(bf16[256,1024]{1,0:T(8,128)(2,1)S(1)} %collective-permute-done.9.ga_ref.refs_2_), channel_id=1, source_target_pairs={{0,8},{8,0},{1,9},{9,1},{2,10},{10,2},{3,11},{11,3},{4,12},{12,4},... | collective-permute-start | bytes 1572872 | tf_op jit(solution)/shard_map/ppermute | solution.py:1116
  76.9 39.1 %collective-permute-start.19 = (bf16[1,2,1024]{2,1,0:T(2,128)(2,1)S(1)}, bf16[1,2,1024]{2,1,0:T(2,128)(2,1)S(1)}, u32[]{:S(2)}, u32[]{:S(2)}) collective-permute-start(bf16[1,2,1024]{2,1,0:T(2,128)(2,1)S(1)} %get-tuple-element.271), channel_id=1, source_target_pairs={{0,6},{2,4},{4,2},{6,0},{1,7},{3,5},{5,3},{7,1},{8,14},{10,12},{12... | collective-permute-start | bytes 12296 | tf_op jit(solution)/shard_map/ppermute | solution.py:1092
  79.3 36.7 %collective-permute-start.18 = (bf16[1,2,1024]{2,1,0:T(2,128)(2,1)S(1)}, bf16[1,2,1024]{2,1,0:T(2,128)(2,1)S(1)}, u32[]{:S(2)}, u32[]{:S(2)}) collective-permute-start(bf16[1,2,1024]{2,1,0:T(2,128)(2,1)S(1)} %get-tuple-element.271), channel_id=1, source_target_pairs={{0,4},{2,6},{4,0},{6,2},{1,5},{3,7},{5,1},{7,3},{8,12},{10,14},{12... | collective-permute-start | bytes 12296 | tf_op jit(solution)/shard_map/ppermute | solution.py:1092
  79.4 36.6 %collective-permute-start.17 = (bf16[1,2,1024]{2,1,0:T(2,128)(2,1)S(1)}, bf16[1,2,1024]{2,1,0:T(2,128)(2,1)S(1)}, u32[]{:S(2)}, u32[]{:S(2)}) collective-permute-start(bf16[1,2,1024]{2,1,0:T(2,128)(2,1)S(1)} %get-tuple-element.271), channel_id=1, source_target_pairs={{0,2},{2,0},{4,6},{6,4},{1,3},{3,1},{5,7},{7,5},{8,10},{10,8},{12,... | collective-permute-start | bytes 12296 | tf_op jit(solution)/shard_map/ppermute | solution.py:1092
  82.2 13.5 %collective-permute-start.15 = (bf16[8,32,1024]{2,1,0:T(8,128)(2,1)}, bf16[8,32,1024]{2,1,0:T(8,128)(2,1)}, u32[]{:S(2)}, u32[]{:S(2)}) collective-permute-start(bf16[8,32,1024]{2,1,0:T(8,128)(2,1)} %constant_dynamic-update-slice_fusion.18), channel_id=1, source_target_pairs={{0,16},{16,0},{1,17},{17,1},{2,18},{18,2},{3,19},{19,3},{4,20},{20... | collective-permute-start | bytes 1572872 | tf_op jit(solution)/shard_map/ppermute | solution.py:1092
  83.6 37.0 %all-to-all-start.2 = ((bf16[8,256,128]{2,1,0:T(8,128)(2,1)}), bf16[8,256,128]{2,1,0:T(8,128)(2,1)S(1)}, u32[]{:S(2)}, u32[]{:S(2)}) async-start(bf16[8,256,128]{2,1,0:T(8,128)(2,1)} %bitcast_bitcast_fusion), calls=%async_computation.2 | async-start | bytes 1048576 | tf_op jit(solution)/shard_map/all_to_all | solution.py:1234
  115.9 45.9 %collective-permute-start.16 = (bf16[16,32,1024]{2,1,0:T(8,128)(2,1)}, bf16[16,32,1024]{2,1,0:T(8,128)(2,1)}, u32[]{:S(2)}, u32[]{:S(2)}) collective-permute-start(bf16[16,32,1024]{2,1,0:T(8,128)(2,1)} %pad_maximum_fusion.1), channel_id=1, source_target_pairs={{0,8},{8,0},{1,9},{9,1},{2,10},{10,2},{3,11},{11,3},{4,12},{12,4},... | collective-permute-start | bytes 3145736 | tf_op jit(solution)/shard_map/ppermute | solution.py:1092
  116.1 3.8 collective-permute-start.20
  164.9 20.6 %all-to-all-start.3 = ((bf16[8,2,144,128]{3,2,1,0:T(8,128)(2,1)}), bf16[8,2,144,128]{3,2,1,0:T(8,128)(2,1)S(1)}, u32[]{:S(2)}, u32[]{:S(2)}) async-start(bf16[8,2,144,128]{3,2,1,0:T(8,128)(2,1)} %bitcast.231), calls=%async_computation.3 | async-start | bytes 1179648 | tf_op jit(solution)/shard_map/all_to_all | solution.py:1270
  191.1 2.6 collective-permute-start.22
  191.1 16.0 %collective-permute-start.21 = (bf16[288,1024]{1,0:T(8,128)(2,1)}, bf16[288,1024]{1,0:T(8,128)(2,1)S(1)}, u32[]{:S(2)}, u32[]{:S(2)}) collective-permute-start(bf16[288,1024]{1,0:T(8,128)(2,1)} %copy-done.11), channel_id=1, source_target_pairs={{0,16},{16,0},{1,17},{17,1},{2,18},{18,2},{3,19},{19,3},{4,20},{20... | collective-permute-start | bytes 1769480 | tf_op jit(solution)/shard_map/ppermute | solution.py:1116
  192.4 1.3 collective-permute-start.23
  207.1 5.8 %collective-permute-start.25 = (bf16[288,1024]{1,0:T(8,128)(2,1)S(1)}, bf16[288,1024]{1,0:T(8,128)(2,1)S(1)}, u32[]{:S(2)}, u32[]{:S(2)}) collective-permute-start(bf16[288,1024]{1,0:T(8,128)(2,1)S(1)} %collective-permute-done.21.xa_ref.refs_6_), channel_id=1, source_target_pairs={{0,8},{8,0},{1,9},{9,1},{2,10},{10,2},{3,11},{11,3},{4,12},{12,4},... | collective-permute-start | bytes 1769480 | tf_op jit(solution)/shard_map/ppermute | solution.py:1116
  207.1 4.5 collective-permute-start.26
  211.6 1.3 collective-permute-start.27
  220.6 3.2 collective-permute-start.28
  220.7 19.5 %collective-permute-start.24 = (f32[288,1024]{1,0:T(8,128)S(1)}, f32[288,1024]{1,0:T(8,128)S(1)}, u32[]{:S(2)}, u32[]{:S(2)}) collective-permute-start(f32[288,1024]{1,0:T(8,128)S(1)} %copy-done.56), channel_id=1, source_target_pairs={{0,8},{8,0},{1,9},{9,1},{2,10},{10,2},{3,11},{11,3},{4,12},{12,4},... | collective-permute-start | bytes 3538952 | tf_op jit(solution)/shard_map/ppermute | solution.py:1116
  224.1 16.2 %collective-permute-start.29 = (bf16[288,1024]{1,0:T(8,128)(2,1)S(1)}, bf16[288,1024]{1,0:T(8,128)(2,1)S(1)}, u32[]{:S(2)}, u32[]{:S(2)}) collective-permute-start(bf16[288,1024]{1,0:T(8,128)(2,1)S(1)} %add_convert_fusion.1), channel_id=1, source_target_pairs={{0,16},{16,0},{1,17},{17,1},{2,18},{18,2},{3,19},{19,3},{4,20},{20... | collective-permute-start | bytes 1769480 | tf_op jit(solution)/shard_map/ppermute | solution.py:1116
  224.9 28.2 %collective-permute-start.31 = (bf16[288,1024]{1,0:T(8,128)(2,1)S(1)}, bf16[288,1024]{1,0:T(8,128)(2,1)}, u32[]{:S(2)}, u32[]{:S(2)}) collective-permute-start(bf16[288,1024]{1,0:T(8,128)(2,1)S(1)} %copy-done.29), channel_id=1, source_target_pairs={{0,16},{16,0},{1,17},{17,1},{2,18},{18,2},{3,19},{19,3},{4,20},{20... | collective-permute-start | bytes 1769480 | tf_op jit(solution)/shard_map/ppermute | solution.py:1116
  245.7 19.1 %collective-permute-start.34 = (bf16[288,1024]{1,0:T(8,128)(2,1)S(1)}, bf16[288,1024]{1,0:T(8,128)(2,1)S(1)}, u32[]{:S(2)}, u32[]{:S(2)}) collective-permute-start(bf16[288,1024]{1,0:T(8,128)(2,1)S(1)} %get-tuple-element.170.refs_4_), channel_id=1, source_target_pairs={{0,16},{16,0},{1,17},{17,1},{2,18},{18,2},{3,19},{19,3},{4,20},{20... | collective-permute-start | bytes 1769480 | tf_op jit(solution)/shard_map/ppermute | solution.py:1116
  246.5 24.9 %all-to-all-start.4 = ((bf16[8,256,128]{2,1,0:T(8,128)(2,1)}), bf16[8,256,128]{2,1,0:T(8,128)(2,1)}, u32[]{:S(2)}, u32[]{:S(2)}) async-start(bf16[8,256,128]{2,1,0:T(8,128)(2,1)} %copy-done.32), calls=%async_computation.4 | async-start | bytes 1048576 | tf_op jit(solution)/shard_map/all_to_all | solution.py:1328
  250.6 158.1 %reduce-scatter.2.cloned.1.call-start = ((), (), s32[]{:S(2)}) async-start(), calls=%async_computation.9 | async-start | bytes 5308416 | tf_op jit(solution)/shard_map/reduce_scatter | solution.py:1339
  250.7 14.1 %collective-permute-start.30 = (bf16[288,1024]{1,0:T(8,128)(2,1)S(1)}, bf16[288,1024]{1,0:T(8,128)(2,1)}, u32[]{:S(2)}, u32[]{:S(2)}) collective-permute-start(bf16[288,1024]{1,0:T(8,128)(2,1)S(1)} %copy-done.29), channel_id=1, source_target_pairs={{0,8},{8,0},{1,9},{9,1},{2,10},{10,2},{3,11},{11,3},{4,12},{12,4},... | collective-permute-start | bytes 1769480 | tf_op jit(solution)/shard_map/ppermute | solution.py:1116
  253.0 11.7 %collective-permute-start.32 = (bf16[288,1024]{1,0:T(8,128)(2,1)}, bf16[288,1024]{1,0:T(8,128)(2,1)}, u32[]{:S(2)}, u32[]{:S(2)}) collective-permute-start(bf16[288,1024]{1,0:T(8,128)(2,1)} %collective-permute-done.31.refs_2_), channel_id=1, source_target_pairs={{0,8},{8,0},{1,9},{9,1},{2,10},{10,2},{3,11},{11,3},{4,12},{12,4},... | collective-permute-start | bytes 1769480 | tf_op jit(solution)/shard_map/ppermute | solution.py:1116
  253.0 11.7 %collective-permute-start.33 = (bf16[288,1024]{1,0:T(8,128)(2,1)S(1)}, bf16[288,1024]{1,0:T(8,128)(2,1)}, u32[]{:S(2)}, u32[]{:S(2)}) collective-permute-start(bf16[288,1024]{1,0:T(8,128)(2,1)S(1)} %get-tuple-element.170.refs_4_), channel_id=1, source_target_pairs={{0,8},{8,0},{1,9},{9,1},{2,10},{10,2},{3,11},{11,3},{4,12},{12,4},... | collective-permute-start | bytes 1769480 | tf_op jit(solution)/shard_map/ppermute | solution.py:1116
  264.8 2.1 collective-permute-start.35
  326.2 52.8 %all-to-all-start.5 = ((bf16[8,256,128]{2,1,0:T(8,128)(2,1)}), bf16[8,256,128]{2,1,0:T(8,128)(2,1)S(1)}, u32[]{:S(2)}, u32[]{:S(2)}) async-start(bf16[8,256,128]{2,1,0:T(8,128)(2,1)} %bitcast.52), calls=%async_computation.5 | async-start | bytes 1048576 | tf_op jit(solution)/shard_map/all_to_all | solution.py:1346
  352.2 27.2 %collective-permute-start.36 = (bf16[8,128,512]{2,1,0:T(8,128)(2,1)}, bf16[8,128,512]{2,1,0:T(8,128)(2,1)}, u32[]{:S(2)}, u32[]{:S(2)}) collective-permute-start(bf16[8,128,512]{2,1,0:T(8,128)(2,1)} %get-tuple-element.185), channel_id=1, source_target_pairs={{0,1},{1,0},{2,3},{3,2},{4,5},{5,4},{6,7},{7,6},{8,9},{9,8},{10,11... | collective-permute-start | bytes 3145736 | tf_op jit(solution)/shard_map/ppermute | solution.py:1406
  355.4 23.0 %collective-permute-start.42 = (bf16[2,72,128]{2,1,0:T(8,128)(2,1)S(1)}, bf16[2,72,128]{2,1,0:T(8,128)(2,1)S(1)}, u32[]{:S(2)}, u32[]{:S(2)}) collective-permute-start(bf16[2,72,128]{2,1,0:T(8,128)(2,1)S(1)} %dynamic-slice_bitcast_fusion.1), channel_id=1, source_target_pairs={{0,16},{16,0},{1,17},{17,1},{2,18},{18,2},{3,19},{19,3},{4,20},{20... | collective-permute-start | bytes 110600 | tf_op jit(solution)/shard_map/ppermute | solution.py:1116
  380.7 28.0 %collective-permute-start.37 = (bf16[8,128,512]{2,1,0:T(8,128)(2,1)}, bf16[8,128,512]{2,1,0:T(8,128)(2,1)}, u32[]{:S(2)}, u32[]{:S(2)}) collective-permute-start(bf16[8,128,512]{2,1,0:T(8,128)(2,1)} %get-tuple-element.189), channel_id=1, source_target_pairs={{0,1},{1,0},{2,3},{3,2},{4,5},{5,4},{6,7},{7,6},{8,9},{9,8},{10,11... | collective-permute-start | bytes 3145736 | tf_op jit(solution)/shard_map/ppermute | solution.py:1406
  384.0 27.6 %collective-permute-start.38 = (bf16[256,512]{1,0:T(8,128)(2,1)}, bf16[256,512]{1,0:T(8,128)(2,1)}, u32[]{:S(2)}, u32[]{:S(2)}) collective-permute-start(bf16[256,512]{1,0:T(8,128)(2,1)} %bitcast.56), channel_id=1, source_target_pairs={{0,2},{2,0},{4,6},{6,4},{1,3},{3,1},{5,7},{7,5},{8,10},{10,8},{12,... | collective-permute-start | bytes 786440 | tf_op jit(solution)/shard_map/ppermute | solution.py:1419
  385.7 25.9 %collective-permute-start.39 = (bf16[256,512]{1,0:T(8,128)(2,1)}, bf16[256,512]{1,0:T(8,128)(2,1)}, u32[]{:S(2)}, u32[]{:S(2)}) collective-permute-start(bf16[256,512]{1,0:T(8,128)(2,1)} %bitcast.57), channel_id=1, source_target_pairs={{0,4},{2,6},{4,0},{6,2},{1,5},{3,7},{5,1},{7,3},{8,12},{10,14},{12... | collective-permute-start | bytes 786440 | tf_op jit(solution)/shard_map/ppermute | solution.py:1419
  388.1 23.5 %collective-permute-start.40 = (bf16[256,512]{1,0:T(8,128)(2,1)}, bf16[256,512]{1,0:T(8,128)(2,1)}, u32[]{:S(2)}, u32[]{:S(2)}) collective-permute-start(bf16[256,512]{1,0:T(8,128)(2,1)} %bitcast.58), channel_id=1, source_target_pairs={{0,6},{2,4},{4,2},{6,0},{1,7},{3,5},{5,3},{7,1},{8,14},{10,12},{12... | collective-permute-start | bytes 786440 | tf_op jit(solution)/shard_map/ppermute | solution.py:1419
  388.4 16.5 %collective-permute-start.41 = (bf16[704,512]{1,0:T(8,128)(2,1)S(1)}, bf16[704,512]{1,0:T(8,128)(2,1)S(1)}, u32[]{:S(2)}, u32[]{:S(2)}) collective-permute-start(bf16[704,512]{1,0:T(8,128)(2,1)S(1)} %broadcast_select_fusion), channel_id=1, source_target_pairs={{0,16},{16,0},{1,17},{17,1},{2,18},{18,2},{3,19},{19,3},{4,20},{20... | collective-permute-start | bytes 2162696 | tf_op jit(solution)/shard_map/ppermute | solution.py:1116
  412.8 8.4 %collective-permute-start.47 = (f32[288,1024]{1,0:T(8,128)S(1)}, f32[288,1024]{1,0:T(8,128)S(1)}, u32[]{:S(2)}, u32[]{:S(2)}) collective-permute-start(f32[288,1024]{1,0:T(8,128)S(1)} %split.48), channel_id=1, source_target_pairs={{0,8},{8,0},{1,9},{9,1},{2,10},{10,2},{3,11},{11,3},{4,12},{12,4},... | collective-permute-start | bytes 3538952 | tf_op jit(solution)/shard_map/ppermute | solution.py:1116
  415.9 29.3 %collective-permute-start.46 = (f32[288,1024]{1,0:T(8,128)}, f32[288,1024]{1,0:T(8,128)}, u32[]{:S(2)}, u32[]{:S(2)}) collective-permute-start(f32[288,1024]{1,0:T(8,128)} %get-tuple-element.275), channel_id=1, source_target_pairs={{0,8},{8,0},{1,9},{9,1},{2,10},{10,2},{3,11},{11,3},{4,12},{12,4},... | collective-permute-start | bytes 3538952 | tf_op jit(solution)/shard_map/ppermute | solution.py:1116
  420.1 5.4 %collective-permute-start.50 = (bf16[704,256]{1,0:T(8,128)(2,1)S(1)}, bf16[704,256]{1,0:T(8,128)(2,1)S(1)}, u32[]{:S(2)}, u32[]{:S(2)}) collective-permute-start(bf16[704,256]{1,0:T(8,128)(2,1)S(1)} %fusion.14), channel_id=1, source_target_pairs={{0,8},{8,0},{1,9},{9,1},{2,10},{10,2},{3,11},{11,3},{4,12},{12,4},... | collective-permute-start | bytes 1081352 | tf_op jit(solution)/shard_map/ppermute | solution.py:1116
  420.2 11.1 %collective-permute-start.49 = (bf16[72,128]{1,0:T(8,128)(2,1)S(1)}, bf16[72,128]{1,0:T(8,128)(2,1)S(1)}, u32[]{:S(2)}, u32[]{:S(2)}) collective-permute-start(bf16[72,128]{1,0:T(8,128)(2,1)S(1)} %fusion.17), channel_id=1, source_target_pairs={{0,8},{8,0},{1,9},{9,1},{2,10},{10,2},{3,11},{11,3},{4,12},{12,4},... | collective-permute-start | bytes 55304 | tf_op jit(solution)/shard_map/ppermute | solution.py:1116
  420.7 14.9 %collective-permute-start.43 = (bf16[256,512]{1,0:T(8,128)(2,1)}, bf16[256,512]{1,0:T(8,128)(2,1)}, u32[]{:S(2)}, u32[]{:S(2)}) collective-permute-start(bf16[256,512]{1,0:T(8,128)(2,1)} %bitcast.62), channel_id=1, source_target_pairs={{0,2},{2,0},{4,6},{6,4},{1,3},{3,1},{5,7},{7,5},{8,10},{10,8},{12,... | collective-permute-start | bytes 786440 | tf_op jit(solution)/shard_map/ppermute | solution.py:1419
  421.2 16.8 %collective-permute-start.44 = (bf16[256,512]{1,0:T(8,128)(2,1)}, bf16[256,512]{1,0:T(8,128)(2,1)}, u32[]{:S(2)}, u32[]{:S(2)}) collective-permute-start(bf16[256,512]{1,0:T(8,128)(2,1)} %bitcast.63), channel_id=1, source_target_pairs={{0,4},{2,6},{4,0},{6,2},{1,5},{3,7},{5,1},{7,3},{8,12},{10,14},{12... | collective-permute-start | bytes 786440 | tf_op jit(solution)/shard_map/ppermute | solution.py:1419
  425.4 19.8 %collective-permute-start.48 = (bf16[288,1024]{1,0:T(8,128)(2,1)}, bf16[288,1024]{1,0:T(8,128)(2,1)}, u32[]{:S(2)}, u32[]{:S(2)}) collective-permute-start(bf16[288,1024]{1,0:T(8,128)(2,1)} %add_convert_fusion), channel_id=1, source_target_pairs={{0,16},{16,0},{1,17},{17,1},{2,18},{18,2},{3,19},{19,3},{4,20},{20... | collective-permute-start | bytes 1769480 | tf_op jit(solution)/shard_map/ppermute | solution.py:1116
  427.9 34.5 %all-to-all-start.6 = ((bf16[8,96,128]{2,1,0:T(8,128)(2,1)}), bf16[8,96,128]{2,1,0:T(8,128)(2,1)S(1)}, u32[]{:S(2)}, u32[]{:S(2)}) async-start(bf16[8,96,128]{2,1,0:T(8,128)(2,1)} %fusion.15), calls=%async_computation.7 | async-start | bytes 393216 | tf_op jit(solution)/shard_map/all_to_all | solution.py:1383
  431.4 13.8 %collective-permute-start.45 = (bf16[256,512]{1,0:T(8,128)(2,1)}, bf16[256,512]{1,0:T(8,128)(2,1)S(1)}, u32[]{:S(2)}, u32[]{:S(2)}) collective-permute-start(bf16[256,512]{1,0:T(8,128)(2,1)} %bitcast.250), channel_id=1, source_target_pairs={{0,6},{2,4},{4,2},{6,0},{1,7},{3,5},{5,3},{7,1},{8,14},{10,12},{12... | collective-permute-start | bytes 786440 | tf_op jit(solution)/shard_map/ppermute | solution.py:1419
  435.6 23.9 %collective-permute-start.51 = (bf16[384,128]{1,0:T(8,128)(2,1)S(1)}, bf16[384,128]{1,0:T(8,128)(2,1)S(1)}, u32[]{:S(2)}, u32[]{:S(2)}) collective-permute-start(bf16[384,128]{1,0:T(8,128)(2,1)S(1)} %bitcast.259), channel_id=1, source_target_pairs={{0,0},{1,1},{2,8},{3,9},{4,16},{5,17},{6,24},{7,25},{8,2},{9,3},{1... | collective-permute-start | bytes 294920 | tf_op jit(solution)/shard_map/ppermute | solution.py:1390
  437.9 24.5 %collective-permute-start.52 = (bf16[384,128]{1,0:T(8,128)(2,1)S(1)}, bf16[384,128]{1,0:T(8,128)(2,1)S(1)}, u32[]{:S(2)}, u32[]{:S(2)}) collective-permute-start(bf16[384,128]{1,0:T(8,128)(2,1)S(1)} %bitcast.258), channel_id=1, source_target_pairs={{0,1},{1,0},{2,9},{3,8},{4,17},{5,16},{6,25},{7,24},{8,3},{9,2},{1... | collective-permute-start | bytes 294920 | tf_op jit(solution)/shard_map/ppermute | solution.py:1390
  464.8 10.2 %collective-permute-start.53 = (bf16[72,128]{1,0:T(8,128)(2,1)S(1)}, bf16[72,128]{1,0:T(8,128)(2,1)S(1)}, u32[]{:S(2)}, u32[]{:S(2)}) collective-permute-start(bf16[72,128]{1,0:T(8,128)(2,1)S(1)} %slice.216), channel_id=1, source_target_pairs={{0,0},{1,1},{2,8},{3,9},{4,16},{5,17},{6,24},{7,25},{8,2},{9,3},{1... | collective-permute-start | bytes 55304 | tf_op jit(solution)/shard_map/ppermute | solution.py:1463
  (58 other events, 519.5 us)
Sparse Core Ops, SparseCore 0:
  10.2 81.9 all-gather.5
  94.3 71.9 all-gather.3
  271.5 99.0 reduce-scatter.1

commit v3 on v2

--- a/solution.py
+++ b/solution.py
@@ -552,10 +552,14 @@
         self.up_value = jnp.concatenate([up[:, 320:352], jnp.zeros((up.shape[0], 96), LOW)], 1)
 
 
-def project_kernel(
-    place_ref, begins_ref, xa_ref, xb_ref, cols_ref, own_ref, columns_ref,
-    small_ref, up_ref, ends_ref, parts_ref, gate_ref, pre_ref, pair_ref, vm_ref, gs_ref, edge,
-):
+PROJECT_BLOCKS = 4
+BACK_BLOCKS = 4
+
+
+def project_kernel(place_ref, begins_ref, *refs):
+    x_refs, refs = refs[:PROJECT_BLOCKS], refs[PROJECT_BLOCKS:]
+    cols_ref, own_ref, columns_ref, small_ref, up_ref, ends_ref, stats_ref, parts_ref, gate_ref = refs[:9]
+    pre_ref, pair_ref, vm_ref, gs_ref, edge = refs[9:]
     step = pl.program_id(0)
 
     @pl.when(step == 0)
@@ -563,11 +567,15 @@
         edge[...] = jnp.zeros_like(edge)
 
     begins = [begins_ref[i] for i in range(begins_ref.shape[0])]
-    for i, ref in enumerate((xa_ref, xb_ref)):
+    for i, ref in enumerate(x_refs):
         ends_ref[i] = jnp.concatenate([ref[0, :16], ref[0, BLOCK - 16 :]], 0)
-    x = jnp.concatenate([xa_ref[0], xb_ref[0]], 0).astype(F32)
+    x = jnp.concatenate([ref[0] for ref in x_refs], 0).astype(F32)
     rows = x.shape[0]
-    unit, _ = norm_rows(x)
+    mean = jnp.mean(x, -1, keepdims=True)
+    center = x - mean
+    scale = lax.rsqrt(jnp.mean(center * center, -1, keepdims=True) + 1e-05)
+    unit = center * scale
+    stats_ref[...] = jnp.concatenate([mean, scale], 1)
     normed = unit * cols_ref[0:1] + cols_ref[1:2]
     moved = rows_down(normed, edge[0:1]) * keep_rows(rows, step * rows, begins)
     edge[0:1] = normed[rows - 1 : rows]
@@ -605,11 +613,11 @@
         parts_ref[i] = value.astype(LOW)
 
 
-def block_spec(per, which, rows, width, blocks, back, table=0):
+def block_spec(per, which, rows, width, blocks, back, each, lanes=0):
     def index(i, *tables):
-        step = blocks // 2 - 1 - i if back else i
-        stored = tables[table][jnp.maximum(2 * step + which, 0)]
-        return (stored // per, (stored % per) * (BLOCK // rows) + BLOCK // rows - 1, 0)
+        step = blocks // each - 1 - i if back else i
+        stored = tables[0][jnp.maximum(each * step + which, 0)]
+        return (stored // per, (stored % per) * (BLOCK // rows) + BLOCK // rows - 1, lanes)
 
     return pl.BlockSpec((1, rows, width), index)
 
@@ -621,7 +629,7 @@
 def project(x, cols, own, weights, place, begins, per):
     blocks = place.shape[0]
     total = blocks * BLOCK
-    rows = 2 * BLOCK
+    rows = PROJECT_BLOCKS * BLOCK
     width = own.shape[1]
     span = lambda w: pl.BlockSpec((rows, w), lambda i, *_: (i, 0))
     deep = lambda n: pl.BlockSpec((n, rows, width), lambda i, *_: (0, i, 0))
@@ -630,22 +638,22 @@
         project_kernel,
         grid_spec=pltpu.PrefetchScalarGridSpec(
             num_scalar_prefetch=2,
-            grid=(blocks // 2,),
+            grid=(blocks // PROJECT_BLOCKS,),
             in_specs=[
-                block_spec(per, 0, BLOCK, x.shape[2], blocks, False),
-                block_spec(per, 1, BLOCK, x.shape[2], blocks, False),
-                whole_spec(cols),
-                whole_spec(own),
+                block_spec(per, b, BLOCK, x.shape[2], blocks, False, PROJECT_BLOCKS)
+                for b in range(PROJECT_BLOCKS)
             ]
+            + [whole_spec(cols), whole_spec(own)]
             + [whole_spec(w) for w in weights],
             out_specs=[
-                pl.BlockSpec((2, 32, x.shape[2]), lambda i, *_: (i, 0, 0)),
-                deep(5), span(width), deep(5), span(128), span(128), span(128),
+                pl.BlockSpec((PROJECT_BLOCKS, 32, x.shape[2]), lambda i, *_: (i, 0, 0)),
+                span(2), deep(5), span(width), deep(5), span(128), span(128), span(128),
             ],
             scratch_shapes=[pltpu.VMEM((8, x.shape[2]), F32)],
         ),
         out_shape=[
             shape((blocks, 32, x.shape[2]), LOW),
+            shape((total, 2), F32),
             shape((5, total, width), LOW),
             shape((total, width), F32),
             shape((5, total, width), F32),
@@ -655,70 +663,72 @@
         ],
         compiler_params=pltpu.CompilerParams(vmem_limit_bytes=56 * 1024 * 1024),
         cost_estimate=work(20),
-    )(place, begins, x, x, cols, own, *weights)
+    )(place, begins, *[x] * PROJECT_BLOCKS, cols, own, *weights)
 
 
 def project_back_kernel(
-    part, parts, place_ref, turn_ref, row_ref, begins_ref, head_ref, xa_ref, xb_ref, xp_ref, grads_ref,
-    pair_ref, vm_ref, gs_ref, scan_ref, ffn_ref, cols_ref, columns_ref, small_ref, up_ref, *rest,
+    part, parts, place_ref, turn_ref, row_ref, begins_ref, head_ref, *refs,
 ):
-    sizes_x = len(rest) - 4 - (2 if part == 0 else 1)
+    x_refs, refs = refs[:BACK_BLOCKS], refs[BACK_BLOCKS:]
+    xp_ref, stats_ref, prior_stats_ref, grads_ref, pair_ref, vm_ref, gs_ref, scan_ref, ffn_ref = refs[:9]
+    cols_ref, columns_ref, small_ref, up_ref, *rest = refs[9:]
+    sizes_x = len(rest) - 6 - (2 if part == 0 else 1)
     back_refs, rest = rest[:sizes_x], rest[sizes_x:]
     if part == 0:
-        low_sum_ref, up_sum_ref, edge, sum_ref, buffer, sems = rest
+        low_sum_ref, up_sum_ref, edge, sum_ref, columns_t, small_t, buffer, sems = rest
     else:
-        low_sum_ref, edge, sum_ref, buffer, sems = rest
+        low_sum_ref, edge, sum_ref, columns_t, small_t, buffer, sems = rest
     turn = pl.program_id(0)
     step = pl.num_programs(0) - 1 - turn
     wide = columns_ref.shape[0]
-    lanes = slice(part * wide, (part + 1) * wide)
 
     @pl.when(turn == 0)
     def _():
         for ref in (edge, sum_ref) + ((up_sum_ref,) if part == 0 else ()):
             ref[...] = jnp.zeros_like(ref)
+        columns_t[...] = columns_ref[...].T
+        small_t[...] = small_ref[:, :384].T
 
     begins = [begins_ref[i] for i in range(begins_ref.shape[0])]
 
-    def normal(x):
-        x = x.astype(F32)
-        mean = jnp.mean(x, -1, keepdims=True)
-        spread = jnp.mean((x - mean) * (x - mean), -1, keepdims=True)
-        return (x[:, lanes] - mean) * lax.rsqrt(spread + 1e-05)
-
-    unit = normal(jnp.concatenate([xa_ref[0], xb_ref[0]], 0))
+    x = jnp.concatenate([ref[0] for ref in x_refs], 0).astype(F32)
+    unit = (x - stats_ref[:, 0:1]) * stats_ref[:, 1:2]
     rows = unit.shape[0]
     normed = unit * cols_ref[0:1] + cols_ref[1:2]
-    prior = normal(xp_ref[0]) * cols_ref[0:1] + cols_ref[1:2]
+    last = xp_ref[0, 8:].astype(F32)
+    prior = (last - prior_stats_ref[:, 0:1]) * prior_stats_ref[:, 1:2] * cols_ref[0:1] + cols_ref[1:2]
     keep = keep_rows(rows, step * rows, begins)
     diff = rows_down(normed, prior[prior.shape[0] - 1 :]) * keep - normed
-    low = SmallWeights(small_ref[...], up_ref[...])
+    up = up_ref[...]
+    up_pair, up_gate = up[:, 384:512], up[:, 512:640]
+    up_value = jnp.concatenate([up[:, 320:352], jnp.zeros((up.shape[0], 96), LOW)], 1)
     width = grads_ref.shape[2]
     g_r, g_k, g_v, g_decay, g_rate, g_vup, g_gate = [grads_ref[i] for i in range(7)]
     pair, sig = pair_ref[...], gs_ref[...]
     is_decay = lane_below(DECAY_RANK)
     m_pair = jnp.where(
-        is_decay, dot(g_decay, low.up_pair, NN) * (1.0 - pair * pair), dot(g_rate, low.up_pair, NN)
+        is_decay, dot(g_decay, up_pair, NN) * (1.0 - pair * pair), dot(g_rate, up_pair, NN)
     ).astype(LOW)
-    m_v = kept(dot(g_vup, low.up_value, NN), lane_below(DV)).astype(LOW)
-    m_g = (dot(g_gate, low.up_gate, NN) * sig * (1.0 - sig)).astype(LOW)
+    m_v = kept(dot(g_vup, up_value, NN), lane_below(DV)).astype(LOW)
+    m_g = (dot(g_gate, up_gate, NN) * sig * (1.0 - sig)).astype(LOW)
     near = jnp.zeros_like(unit)
     far = jnp.zeros_like(unit)
-    value_weights = jnp.concatenate([columns_ref[:, 2 * width :], low.value], 1)
+    value_weights = jnp.concatenate([columns_t[2 * width :], small_t[256:384]], 0)
+    pair_weights = small_t[:128]
     cut = DECAY_RANK + DA + 3 * width
     grads = (
-        (2, g_r, columns_ref[:, :width], ((0, g_r),)),
-        (3, kept(m_pair, is_decay), low.pair, ((3 * width, m_pair[:, :DECAY_RANK]),)),
-        (4, g_k, columns_ref[:, width : 2 * width], ((width, g_k),)),
+        (2, g_r, columns_t[:width], ((0, g_r),)),
+        (3, kept(m_pair, is_decay), pair_weights, ((3 * width, m_pair[:, :DECAY_RANK]),)),
+        (4, g_k, columns_t[width : 2 * width], ((width, g_k),)),
         (5, jnp.concatenate([g_v, m_v], 1), value_weights, ((2 * width, g_v), (cut, m_v[:, :DV]))),
-        (6, kept(m_pair, ~is_decay), low.pair, ((3 * width + DECAY_RANK, m_pair[:, DECAY_RANK:]),)),
-        (7, m_g, low.gate, ((cut + DV, m_g),)),
+        (6, kept(m_pair, ~is_decay), pair_weights, ((3 * width + DECAY_RANK, m_pair[:, DECAY_RANK:]),)),
+        (7, m_g, small_t[128:256], ((cut + DV, m_g),)),
     )
     col_sums = []
     for slot, grad, weight, pieces in grads:
         mix = cols_ref[slot : slot + 1]
         mixed = (normed + diff * mix).astype(LOW)
-        total = dot(grad, weight, NT)
+        total = dot(grad, weight, NN)
         for start, piece in pieces:
             sum_ref[start : start + piece.shape[1]] += dot(piece, mixed, TN)
         near = near + total
@@ -744,7 +754,7 @@
     slot = turn % 2
 
     def leave(where):
-        for which in range(2):
+        for which in range(BACK_BLOCKS):
             pltpu.make_async_copy(
                 buffer.at[where, which], back_refs[0].at[0], sems.at[where, which]
             ).wait()
@@ -753,9 +763,9 @@
     def _():
         leave(slot)
 
-    buffer[slot] = back.astype(LOW).reshape(2, BLOCK, wide)
-    for which in range(2):
-        block = 2 * step + which
+    buffer[slot] = back.astype(LOW).reshape(BACK_BLOCKS, BLOCK, wide)
+    for which in range(BACK_BLOCKS):
+        block = BACK_BLOCKS * step + which
         for x, ref in enumerate(back_refs):
 
             @pl.when(turn_ref[block] == x)
@@ -778,11 +788,11 @@
 
 
 def project_back(
-    part, parts, x, grads, mids, extra_cols, cols, weights, place, turn, row, begins, head, per, sizes
+    part, parts, x, stats, grads, mids, extra_cols, cols, weights, place, turn, row, begins, head, per, sizes
 ):
     blocks = place.shape[0]
-    rows = 2 * BLOCK
-    steps = blocks // 2
+    rows = BACK_BLOCKS * BLOCK
+    steps = blocks // BACK_BLOCKS
     wide = x.shape[2] // parts
     width = grads.shape[2]
     size_z, size_x = sizes
@@ -801,9 +811,15 @@
             num_scalar_prefetch=5,
             grid=(steps,),
             in_specs=[
-                block_spec(per, 0, BLOCK, x.shape[2], blocks, True),
-                block_spec(per, 1, BLOCK, x.shape[2], blocks, True),
-                block_spec(per, -1, 16, x.shape[2], blocks, True),
+                *[
+                    block_spec(per, b, BLOCK, wide, blocks, True, BACK_BLOCKS, part)
+                    for b in range(BACK_BLOCKS)
+                ],
+                block_spec(per, -1, 16, wide, blocks, True, BACK_BLOCKS, part),
+                span(2),
+                pl.BlockSpec(
+                    (8, 2), lambda i, *_: (jnp.maximum((steps - 1 - i) * (rows // 8) - 1, 0), 0)
+                ),
                 pl.BlockSpec((7, rows, width), lambda i, *_: (0, steps - 1 - i, 0)),
             ]
             + [span(m.shape[1]) for m in mids]
@@ -819,15 +835,17 @@
             scratch_shapes=[
                 pltpu.VMEM((8, wide), F32),
                 pltpu.VMEM((held, wide), F32),
-                pltpu.VMEM((2, 2, BLOCK, wide), LOW),
-                pltpu.SemaphoreType.DMA((2, 2)),
+                pltpu.VMEM((columns.shape[1], wide), LOW),
+                pltpu.VMEM((384, wide), LOW),
+                pltpu.VMEM((2, BACK_BLOCKS, BLOCK, wide), LOW),
+                pltpu.SemaphoreType.DMA((2, BACK_BLOCKS)),
             ],
         ),
         out_shape=[shape((size_z * per, BLOCK, wide), LOW)] * size_x + sums,
         compiler_params=pltpu.CompilerParams(vmem_limit_bytes=56 * 1024 * 1024),
         cost_estimate=work(17000),
     )(
-        place, turn, row, begins, head, x, x, x, grads, *mids, *extra_cols, cols, columns, small, up
+        place, turn, row, begins, head, *[x] * (BACK_BLOCKS + 1), stats, stats, grads, *mids, *extra_cols, cols, columns, small, up
     )
 
 
@@ -844,8 +862,14 @@
 
 
 def middle_kernel(
-    per, local_ref, begins_ref, out_ref, tokens_ref, weight_ref, cols_ref, middle_ref, ffn_ref, rows_ref
+    per, local_ref, begins_ref, table_ref, out_ref, tokens_ref, cols_ref, near_ref, far_ref, middle_ref, ffn_ref,
+    rows_ref, weight_ref,
 ):
+    count, height, _ = near_ref.shape
+    for i in range(2 * count):
+        slot = table_ref[i]
+        other = lax.rem(slot, count)
+        weight_ref[i * height : (i + 1) * height] = jnp.where(slot < count, near_ref[other], far_ref[other])
     heads = out_ref.shape[0]
     rows = [jnp.concatenate([out_ref[h, j] for h in range(heads)], 1) for j in range(per)]
     rows = jnp.concatenate(rows, 0)
@@ -866,26 +890,28 @@
         ffn_ref[j * TALL + BLOCK : (j + 1) * TALL] = jnp.where(extra_row == 1, after, 0.0).astype(LOW)
 
 
-def middle_rows(out, tokens_ext, weight, cols, local, begins):
+def middle_rows(out, tokens_ext, near, far, table, cols, local, begins):
     _, per, _, _ = out.shape
-    wide = weight.shape[0]
+    wide = near.shape[2]
     shape = jax.ShapeDtypeStruct
+    weight = shape((wide, wide), LOW)
     return pl.pallas_call(
         functools.partial(middle_kernel, per),
         grid_spec=pltpu.PrefetchScalarGridSpec(
-            num_scalar_prefetch=2,
+            num_scalar_prefetch=3,
             grid=(1,),
-            in_specs=[whole_spec(x) for x in (out, tokens_ext, weight, cols)],
-            out_specs=[whole_spec(tokens_ext)] * 3,
+            in_specs=[whole_spec(x) for x in (out, tokens_ext, cols, near, far)],
+            out_specs=[whole_spec(tokens_ext)] * 3 + [whole_spec(weight)],
         ),
         out_shape=[
             shape((per * TALL, wide), F32),
             shape((per * TALL, wide), LOW),
             shape((per * TALL, wide), LOW),
+            weight,
         ],
         compiler_params=pltpu.CompilerParams(vmem_limit_bytes=48 * 1024 * 1024),
         cost_estimate=work(6),
-    )(local, begins, out, tokens_ext, weight, cols)
+    )(local, begins, table, out, tokens_ext, cols, near, far)
 
 
 def with_extra(main, extra):
@@ -987,32 +1013,29 @@
     )(*og, *x, *hidden, *pre)
 
 
-def output_grad_kernel(count, which_ref, *refs):
+def output_grad_kernel(count, *refs):
     rows, grads, out = refs[:count], refs[count : 2 * count], refs[-1]
     left = jnp.concatenate([r[...] for r in rows], 0)
     right = jnp.concatenate([r[...] for r in grads], 0)
     out[...] = dot(left, right, TN).astype(LOW)
 
 
-def output_grads(rows, grads, which, room):
+def output_grads(rows, grads, room):
     tall, wide = rows[0].shape
-    part = 256
+    part = grads[0].shape[1]
     last = room.shape[1] // part - 1
     return pl.pallas_call(
         functools.partial(output_grad_kernel, len(rows)),
-        grid_spec=pltpu.PrefetchScalarGridSpec(
-            num_scalar_prefetch=1,
-            grid=(wide // part,),
-            in_specs=[pl.BlockSpec((tall, part), lambda i, w: (0, i))] * len(rows)
-            + [pl.BlockSpec((tall, part), lambda i, w: (0, w[0]))] * len(grads)
-            + [pl.BlockSpec(memory_space=pl.ANY)],
-            out_specs=pl.BlockSpec((part, part), lambda i, w: (i, last)),
-        ),
+        grid=(wide // part,),
+        in_specs=[pl.BlockSpec((tall, part), lambda i: (0, i))] * len(rows)
+        + [whole_spec(g) for g in grads]
+        + [pl.BlockSpec(memory_space=pl.ANY)],
+        out_specs=pl.BlockSpec((part, part), lambda i: (i, last)),
         out_shape=jax.ShapeDtypeStruct(room.shape, LOW),
-        input_output_aliases={2 * len(rows) + 1: 0},
+        input_output_aliases={2 * len(rows): 0},
         compiler_params=pltpu.CompilerParams(vmem_limit_bytes=48 * 1024 * 1024),
         cost_estimate=work(2),
-    )(which, *rows, *grads, room)
+    )(*rows, *grads, room)
 
 
 def middle_back_kernel(
@@ -1039,8 +1062,10 @@
         total = og + norm_back(grad_normed, unit, scale, c16)
         grad_ref[j * BLOCK : (j + 1) * BLOCK] = total
         lows.append(total.astype(LOW))
-        low_ref[start : start + BLOCK] = lows[-1]
-        low_ref[start + BLOCK : start + TALL] = jnp.zeros((TALL - BLOCK, c16.shape[1]), LOW)
+        quarter = low_ref.shape[2]
+        for s in range(low_ref.shape[0]):
+            low_ref[s, start : start + BLOCK] = lows[-1][:, s * quarter : (s + 1) * quarter]
+            low_ref[s, start + BLOCK : start + TALL] = jnp.zeros((TALL - BLOCK, quarter), LOW)
     sums_ref[...] = jnp.concatenate(sums + [jnp.zeros((5, c16.shape[1]), F32)], 0)
     out = dot(jnp.concatenate(lows, 0), weight_ref[...], NT).astype(LOW)
     width = heads_ref.shape[2]
@@ -1055,13 +1080,13 @@
     )
 
 
-def middle_back(near, core, far, middle, og, weight, cols, local, begins, heads):
+def middle_back(near, core, far, middle, og, weight, cols, local, begins, heads, seqs):
     tall, wide = near.shape
     per = tall // TALL
     shape = jax.ShapeDtypeStruct
     outs = [
         shape((per * BLOCK, wide), F32),
-        shape((tall, wide), LOW),
+        shape((seqs, tall, wide // seqs), LOW),
         shape((heads, per * BLOCK, wide // heads), LOW),
         shape((8, wide), F32),
     ]
@@ -1096,7 +1121,7 @@
     return jnp.concatenate([x] + steps_along(x, axis), 0)
 
 
-def in_order(x, axes):
+def order_table(axes):
     strides, stride = {}, 1
     for axis in axes:
         strides[axis] = stride
@@ -1108,7 +1133,11 @@
             below //= lax.axis_size(axis)
             there = (index // below) % lax.axis_size(axis)
             place = place + (there ^ lax.axis_index(axis)) * strides[axis]
-    x = taken_blocks(x, place)
+    return place
+
+
+def in_order(x, axes):
+    x = taken_blocks(x, order_table(axes))
     return x.reshape((x.shape[0] * x.shape[1],) + x.shape[2:])
 
 
@@ -1180,6 +1209,7 @@
 
     og_first = output_gradient.reshape(per, BLOCK, wide)[:, 0]
     place = home
+    out_table = order_table(HEAD_AXES + ("ys", "core"))
     size_z, size_x = lax.axis_size("hz"), lax.axis_size("hx")
     apart = (home // per) ^ head
     turn_x, turn_row = apart % size_x, (apart // size_x) * per + home % per
@@ -1248,9 +1278,9 @@
     else:
         every = (gathered(pair[:, 0]), gathered(pair[:, 1]))
 
-    ends, parts, gate, pre, *mids = project(group, settings, own, weights, place, begins, per)
+    ends, stats, parts, gate, pre, *mids = project(group, settings, own, weights, place, begins, per)
     parts, out_shards = lax.optimization_barrier((parts, out_shards))
-    out_shards = grown(out_shards, "core")
+    far_shards = swap(out_shards, "core")
     values, out_in, joined, scanned, states, mats = scan_forward(
         parts, pre, first_group, gate, own, home, begins, PASSES
     )
@@ -1266,11 +1296,10 @@
         ],
         1,
     )
-    extended, out_shards, ends, og_rows = lax.optimization_barrier((extended, out_shards, ends, og_rows))
+    extended, far_shards, ends, og_rows = lax.optimization_barrier((extended, far_shards, ends, og_rows))
     out_ext = lax.all_to_all(
         extended.reshape(heads_axis, per, TALL, width), HEAD_AXES, split_axis=0, concat_axis=0, tiled=True
     )
-    out_weight = in_order(out_shards, HEAD_AXES + ("ys", "core"))
     local = lax.dynamic_slice_in_dim(order, head * per, per)
     after_seq = local + 1
     after_live = (after_seq < blocks).astype(LOW)[:, None]
@@ -1280,11 +1309,10 @@
     og_after = taken_blocks(og_rows, taken_blocks(home, after)) * after_live
     none = jnp.zeros((per, 14, wide), LOW)
     extra_parts = seq_gather(jnp.concatenate([none[:, :1], og_after[:, None], none], 1).reshape(-1, wide))
-    out_ext, out_weight = lax.optimization_barrier((out_ext, out_weight))
     tokens_b = tokens.reshape(per, BLOCK, wide)
     tokens_ext = jnp.concatenate([tokens_b, row_before[:, None], row_after[:, None], none], 1)
-    middle, ffn_in, out_rows = middle_rows(
-        out_ext, tokens_ext.reshape(-1, wide), out_weight, settings, local, begins
+    middle, ffn_in, out_rows, out_weight = middle_rows(
+        out_ext, tokens_ext.reshape(-1, wide), out_shards, far_shards, out_table, settings, local, begins
     )
     ffn_in, every = lax.optimization_barrier((ffn_in, every))
     if whole_quarter:
@@ -1323,17 +1351,24 @@
         is_main = (jnp.arange(rows.shape[0]) % TALL < BLOCK).astype(LOW)[:, None]
         grads_here = [dot(og_rows * is_main, hidden[0], TN), dot(rows * is_main, grad_pre, TN)]
     grad_middle, middle_low, grad_out, cols_ffn = middle_back(
-        own_part, came_core, came_far, middle, output_gradient, out_weight, settings, local, begins, heads_axis
+        own_part, came_core, came_far, middle, output_gradient, out_weight, settings, local, begins, heads_axis,
+        seqs,
     )
     grad_heads = lax.all_to_all(grad_out, HEAD_AXES, split_axis=0, concat_axis=0, tiled=True)
-    out_parts, low_parts = seq_gather(out_rows), seq_gather(middle_low)
+    out_parts = seq_gather(out_rows)
     which = lax.axis_index(("ys", "core"))
     if whole_quarter:
-        grads_here = output_grads(out_parts, low_parts, which[None], grads_here)
+
+        def quarter_from(k):
+            sent = lax.dynamic_index_in_dim(middle_low, which ^ k, 0, keepdims=False)
+            return lax.ppermute(sent, ("ys", "core"), [(i, i ^ k) for i in range(seqs)])
+
+        low_parts = [lax.dynamic_index_in_dim(middle_low, which, 0, keepdims=False)]
+        low_parts += [quarter_from(k) for k in (1, 2, 3)]
+        grads_here = output_grads(out_parts, low_parts, grads_here)
     else:
-        right = jnp.concatenate(low_parts, 0).reshape(seqs * per * TALL, seqs, -1)
-        right = lax.dynamic_index_in_dim(right, which, 1, keepdims=False)
-        grads_here.append(dot(jnp.concatenate(out_parts, 0), right, TN))
+        right = lax.all_to_all(middle_low, ("ys", "core"), split_axis=0, concat_axis=0, tiled=True)
+        grads_here.append(dot(jnp.concatenate(out_parts, 0), right.reshape(-1, right.shape[2]), TN))
         grads_here = jnp.concatenate(grads_here, 1).astype(LOW)
     grad_heads, grads_here = lax.optimization_barrier((grad_heads, grads_here))
     grads_here = lax.psum_scatter(grads_here, HEAD_AXES, scatter_dimension=0, tiled=True)
@@ -1343,40 +1378,54 @@
         own, states, mats, home, begins, PASSES,
     )
     first_grad = taken_blocks(first_grad.reshape(blocks, BLOCK, width), order)
-    first_value_grad = lax.all_to_all(
-        first_grad.reshape(heads_axis, rows_here, width), HEAD_AXES, split_axis=0, concat_axis=2, tiled=True
-    ).reshape(rows_here, wide).astype(F32)
+    first_came = lax.all_to_all(
+        first_grad.reshape(heads_axis, rows_here, width), HEAD_AXES, split_axis=0, concat_axis=0, tiled=True
+    )
 
     share = wide // seqs
     thin = low_rank // seqs
     fold = heads_axis // seqs
+
+    cut = 3 * width
+    end = cut + low_rank
 
     def over_ys(left, right, up_sums):
         up_sums = up_sums.astype(LOW).reshape(seqs, thin, width)
         if ys != 2:
             rows_out = jnp.concatenate([left, right], 1)
-            return rows_out.reshape(-1, seqs, share).transpose(1, 0, 2), up_sums
+            by_feature = jnp.concatenate([rows_out[:cut], rows_out[end:]], 0)
+            by_feature = by_feature.reshape(-1, seqs, share).transpose(1, 0, 2)
+            return by_feature, rows_out[cut:end].reshape(seqs, thin, wide), up_sums
         index = lax.axis_index("ys")
-        came = swap(jnp.where(index == 0, right, left), "ys")
-        total = jnp.where(index == 0, left, right).astype(F32) + came.astype(F32)
-        return total.reshape(-1, 2, share), seq_step(up_sums, "ys")
-
-    def over_core(rows_out, up_sums):
+
+        def part_of(which):
+            half = jnp.where(which == 0, left, right)
+            rank = [lax.dynamic_slice_in_dim(x, cut + which * 2 * thin, 2 * thin, 0) for x in (left, right)]
+            return jnp.concatenate([half[:cut], half[end:]] + rank, 0)
+
+        total = part_of(index).astype(F32) + swap(part_of(1 - index), "ys").astype(F32)
+        features = total.shape[0] - 4 * thin
+        by_rank = total[features:].reshape(2, 2, thin, -1).transpose(1, 2, 0, 3)
+        return total[:features].reshape(-1, 2, share), by_rank, seq_step(up_sums, "ys")
+
+    def over_core(by_feature, by_rank, up_sums):
         if ys != 2:
             return [
                 lax.psum_scatter(x, ("ys", "core"), scatter_dimension=0, tiled=True)[0].astype(F32)
-                for x in (rows_out, up_sums)
+                for x in (by_feature, by_rank, up_sums)
             ]
-        sent = lax.dynamic_index_in_dim(rows_out, 1 - core, 1, keepdims=False).astype(LOW)
-        kept_rows = lax.dynamic_index_in_dim(rows_out, core, 1, keepdims=False)
-        return kept_rows + swap(sent, "core").astype(F32), seq_step(up_sums, "core")
-
-    def to_owners(rows_out):
-        rows_low = rows_out.astype(LOW)
-        squares = rows_low[: 3 * width].reshape(3 * width, fold, width)
-        mixed = rows_low[3 * width : 3 * width + low_rank].reshape(seqs, thin, fold, width)
-        mixed = mixed.transpose(0, 2, 1, 3).reshape(heads_axis, thin, width)
-        cols_part = rows_low[3 * width + low_rank :][:count].reshape(count, heads_axis, -1)
+
+        def step(x, dim):
+            sent = lax.dynamic_index_in_dim(x, 1 - core, dim, keepdims=False).astype(LOW)
+            return lax.dynamic_index_in_dim(x, core, dim, keepdims=False) + swap(sent, "core").astype(F32)
+
+        return step(by_feature, 1), step(by_rank, 0).reshape(thin, wide), step(up_sums, 0)
+
+    def to_owners(by_feature, by_rank):
+        rows_low = by_feature.astype(LOW)
+        squares = rows_low[:cut].reshape(cut, fold, width)
+        mixed = by_rank.astype(LOW).reshape(thin, heads_axis, width).transpose(1, 0, 2)
+        cols_part = rows_low[cut:][:count].reshape(count, heads_axis, -1)
         cols_part = jnp.pad(
             cols_part.transpose(1, 0, 2), ((0, 0), (0, -count % 8), (0, width - cols_part.shape[2]))
         )
@@ -1421,35 +1470,34 @@
 
     def half_back(part, grads):
         outs = project_back(
-            part, 2, group, grads, mids, (cols_scan, cols_ffn), settings, weights, place, turn_x, turn_row,
+            part, 2, group, stats, grads, mids, (cols_scan, cols_ffn), settings, weights, place, turn_x, turn_row,
             begins, head[None], per, sizes,
         )
         return outs[:size_x], outs[size_x:]
 
     left_blocks, (left_sum, up_sums) = half_back(0, scan_grads)
     left_came = others_x(left_blocks)
-    scan_grads, left_sum = lax.optimization_barrier((scan_grads, left_sum))
+    scan_grads, left_sum, first_came = lax.optimization_barrier((scan_grads, left_sum, first_came))
     right_blocks, (right_sum,) = half_back(1, scan_grads)
-    right_blocks, left_came, right_sum, first_value_grad = lax.optimization_barrier(
-        (right_blocks, left_came, right_sum, first_value_grad)
-    )
+    right_blocks, left_came = lax.optimization_barrier((right_blocks, left_came))
     right_came = others_x(right_blocks)
     left_own, left_sent = after_x(left_blocks[0], left_came)
     left_sent, right_sum, hidden = lax.optimization_barrier((left_sent, right_sum, hidden))
     left_z = others_z(left_sent)
-    rows_out, up_sums = over_ys(left_sum, right_sum, up_sums)
+    sums = over_ys(left_sum, right_sum, up_sums)
     outs = [dot(h, value_part, NT) for h in hidden]
     right_came, outs, grads_here = lax.optimization_barrier((right_came, outs, grads_here))
     right_own, right_sent = after_x(right_blocks[0], right_came)
-    right_sent, left_z, rows_out, up_sums, outs = lax.optimization_barrier(
-        (right_sent, left_z, rows_out, up_sums, outs)
-    )
+    right_sent, left_z, sums, outs = lax.optimization_barrier((right_sent, left_z, sums, outs))
     right_z = others_z(right_sent)
-    rows_out, up_sums = over_core(rows_out, up_sums)
-    mixed, came = to_owners(rows_out)
+    by_feature, by_rank, up_sums = over_core(*sums)
+    right_z[0], by_feature, by_rank = lax.optimization_barrier((right_z[0], by_feature, by_rank))
+    mixed, came = to_owners(by_feature, by_rank)
     if whole_quarter:
         came_core, came_far = seq_return(*[x for out in outs for x in jnp.split(out, 2, 0)])
         right_z, came_core, came_far = lax.optimization_barrier((right_z, came_core, came_far))
+    right_z[0], first_came = lax.optimization_barrier((right_z[0], first_came))
+    first_value_grad = first_came.transpose(1, 0, 2).reshape(rows_here, wide).astype(F32)
     right_z, up_sums, mixed, came = lax.optimization_barrier((right_z, up_sums, mixed, came))
     back = jnp.concatenate(
         [own + sum(x.astype(F32) for x in z) for own, z in ((left_own, left_z), (right_own, right_z))], 1
@@ -1460,9 +1508,7 @@
     tokens_grad = grad_middle + norm_back(back, unit, scale, settings[0])
     mixed = jnp.sum(mixed.astype(F32), 0)
     channel_grad = mixed[thin : thin + count, :weight_rows].T
-    down_grad = lax.ppermute(
-        mixed[:thin].astype(LOW), every_axis, [(q * heads_axis + h, owner(q, h, h % fold)) for q, h in pairs]
-    ).T.astype(F32)
+    down_grad = mixed[:thin].T
 
     def main_of(x):
         return x.reshape(-1, per, TALL, wide)[:, :, :BLOCK].reshape(-1, rows_here, wide)

time: 490 us -> 486 us (level)
  local copies, waits for them, and re-layouts: 70.3 us -> 78.4 us
  waiting for transfers between devices: 91.6 us -> 84 us
    ppermute x25 -> x24, waiting for transfers between devices: 41.9 us -> 27.4 us  [swap(): return lax.ppermute(x, axis, [(0, 1), (1, 0)])]
    ppermute x2, waiting for transfers between devices: 17.3 us -> 9.7 us  [to_owners(): lax.ppermute(sent, every_axis, [(q * heads_axis + h, owner(q, h, (h + k)...]
    ppermute x1 -> x3, waiting for transfers between devices: 0.01 us -> 7.24 us  [quarter_from(): return lax.ppermute(sent, ('ys', 'core'), [(i, i ^ k) for i in range(seqs)])]
    ppermute x6, waiting for transfers between devices: 2.28 us -> 7.42 us  [others_z(): lax.ppermute(x, 'hz', [(i, i ^ k) for i in range(size_z)])]
    unnamed x138 -> x141, local copies, waits for them, and re-layouts: 26.7 us -> 28.7 us
    ppermute x18 -> x17, waiting for transfers between devices: 22.7 us -> 21.2 us  [steps_along(): lax.ppermute(x, axis, [(i, i ^ k) for i in range(size)])]
    gather x13 -> x12, local copies, waits for them, and re-layouts: 17.3 us -> 16.1 us  [taken_blocks(): return x.at[table].get(mode='promise_in_bounds')]
    ppermute x25 -> x24, starting transfers between devices: 9.89 us -> 9.52 us  [swap(): return lax.ppermute(x, axis, [(0, 1), (1, 0)])]
  transfers between devices with their start and end apart: 64 -> 64, of which waited for: 19 -> 21; matrix products, arithmetic and copies ran while one was open for 19% -> 17% of each run, Pallas kernels for 36% -> 36%
where the time goes in v3:
time: 486 us; the launch traced here: 479 us
  Pallas kernels  178 us (37%)
  starting transfers between devices  87.9 us (18%)
  waiting for transfers between devices  84 us (17%)
  local copies, waits for them, and re-layouts  78.4 us (16%)
  other arithmetic  29.5 us (6%)
  between operations  15.5 us (3%)
  matrix products  5.74 us (1%)
    pallas_call x1, Pallas kernels, scan_backward(): pl.pallas_call(functools.partial(scan_backward_kernel, heads, p), grid_sp...  50.4 us
    pallas_call x2, Pallas kernels, project_back(): pl.pallas_call(functools.partial(project_back_kernel, part, parts), grid_...  38.1 us
    pallas_call x1, Pallas kernels, scan_forward(): pl.pallas_call(functools.partial(scan_forward_kernel, heads, p), grid_spe...  35.2 us
    unnamed x141, local copies, waits for them, and re-layouts  28.7 us
    ppermute x24, waiting for transfers between devices, swap(): return lax.ppermute(x, axis, [(0, 1), (1, 0)])  27.4 us
    ppermute x17, starting transfers between devices, steps_along(): lax.ppermute(x, axis, [(i, i ^ k) for i in range(size)])  22 us
    ppermute x17, waiting for transfers between devices, steps_along(): lax.ppermute(x, axis, [(i, i ^ k) for i in range(size)])  21.2 us
    pallas_call x1, Pallas kernels, project(): pl.pallas_call(project_kernel, grid_spec=pltpu.PrefetchScalarGridSpec(num...  17.6 us
  transfers between devices with their start and end apart: 64, of which 21 were waited for; matrix products, arithmetic and copies ran while one was open for 17% of the time, Pallas kernels for 36%

profile of v3, /device:TPU:4, one launch (start us, length us, event | category | flops | bytes accessed | tf_op | source)
XLA Modules:
  0.0 479.0 jit_solution(8098443931330713090)
XLA Ops:
  11.1 3.7 collective-permute-start.4
  15.6 3.6 collective-permute-start.13
  21.2 5.2 %all-to-all-start = ((bf16[8,96,128]{2,1,0:T(8,128)(2,1)}), bf16[8,96,128]{2,1,0:T(8,128)(2,1)S(1)}, u32[]{:S(2)}, u32[]{:S(2)}) async-start(bf16[8,96,128]{2,1,0:T(8,128)(2,1)} %copy.101), calls=%async_computation | async-start | bytes 393216 | tf_op jit(solution)/shard_map/all_to_all | solution.py:1231
  28.9 2.0 collective-permute-start.11
  35.0 1.9 collective-permute-done.5
  37.7 1.8 collective-permute-start.6
  39.5 4.4 all-to-all-start.1
  45.4 1.8 collective-permute-start.14
  47.2 5.6 %collective-permute-done.6 = bf16[8,32,640]{2,1,0:T(8,128)(2,1)S(1)} collective-permute-done((bf16[8,32,640]{2,1,0:T(8,128)(2,1)}, bf16[8,32,640]{2,1,0:T(8,128)(2,1)S(1)}, u32[]{:S(2)}, u32[]{:S(2)}) %collective-permute-start.6) | collective-permute-done | bytes 327712 | tf_op jit(solution)/shard_map/ppermute | solution.py:1117
  53.7 5.5 %collective-permute-done = bf16[1,256,384]{2,1,0:T(8,128)(2,1)S(1)} collective-permute-done((bf16[1,256,384]{2,1,0:T(8,128)(2,1)S(1)}, bf16[1,256,384]{2,1,0:T(8,128)(2,1)S(1)}, u32[]{:S(2)}, u32[]{:S(2)}) %collective-permute-start) | collective-permute-done | bytes 196640 | tf_op jit(solution)/shard_map/ppermute | solution.py:1117
  64.2 2.0 constant_dynamic-update-slice_fusion.11
  66.2 3.2 gather_fusion.1
  71.4 1.6 constant_dynamic-slice_fusion.7.refs_8_.refs_16_
  73.1 2.2 copy.114
  75.4 2.4 collective-permute-start.19
  77.9 1.9 collective-permute-start.17
  82.0 5.0 %all-to-all-start.2 = ((bf16[8,256,128]{2,1,0:T(8,128)(2,1)}), bf16[8,256,128]{2,1,0:T(8,128)(2,1)S(1)}, u32[]{:S(2)}, u32[]{:S(2)}) async-start(bf16[8,256,128]{2,1,0:T(8,128)(2,1)} %bitcast_bitcast_fusion), calls=%async_computation.2 | async-start | bytes 1048576 | tf_op jit(solution)/shard_map/all_to_all | solution.py:1264
  87.9 6.0 %collective-permute-done.15 = bf16[8,32,1024]{2,1,0:T(8,128)(2,1)} collective-permute-done((bf16[8,32,1024]{2,1,0:T(8,128)(2,1)S(1)}, bf16[8,32,1024]{2,1,0:T(8,128)(2,1)}, u32[]{:S(2)}, u32[]{:S(2)}) %collective-permute-start.15) | collective-permute-done | bytes 524320 | tf_op jit(solution)/shard_map/ppermute | solution.py:1117
  95.2 17.6 %shard_map.238 = (bf16[16,32,1024]{2,1,0:T(8,128)(2,1)}, f32[2048,2]{1,0:T(8,128)}, bf16[5,2048,128]{2,1,0:T(8,128)(2,1)}, f32[2048,128]{1,0:T(8,128)}, f32[5,20...) custom-call(s32[16]{0:T(128)} %bitcast.200, ...), custom_call_target="tpu_custom_call" | custom-call | bytes 60000 | tf_op jit(solution)/shard_map/pallas_call | solution.py:637
  114.7 2.2 collective-permute-done.20
  119.1 35.2 %shard_map.239 = (bf16[2048,128]{1,0:T(8,128)(2,1)S(1)}, bf16[2048,128]{1,0:T(8,128)(2,1)S(1)}, bf16[2048,128]{1,0:T(8,128)(2,1)S(1)}, f32[2048,128]{1,0:T(8,128...) custom-call(s32[16]{0:T(128)S(1)} %bitcast.204, s32[4]{0:T(128)S(1)} %copy-done.32, ...), custom_call_target="tpu_custom_call" | custom-call | bytes 240000 | tf_op jit(solution)/shard_map/pallas_call | solution.py:260
  157.7 1.7 gather_fusion.2
  163.4 4.7 all-to-all-start.3
  168.9 1.8 gather_fusion.7
  170.7 1.8 gather_fusion.6
  173.6 10.3 %all-to-all-done.3.out_ref = bf16[8,2,144,128]{3,2,1,0:T(8,128)(2,1)S(1)} async-done(((bf16[8,2,144,128]{3,2,1,0:T(8,128)(2,1)}), bf16[8,2,144,128]{3,2,1,0:T(8,128)(2,1)S(1)}, u32[]{:S(2)}, u32[]{:S(2)}) %all-to-all-start.3) | async-done | bytes 589856 | tf_op jit(solution)/shard_map/all_to_all | solution.py:1300
  185.1 3.1 shard_map.240
  194.8 7.8 %shard_map.241 = (bf16[576,1024]{1,0:T(8,128)(2,1)S(1)}, bf16[576,1024]{1,0:T(8,128)(2,1)S(1)}, f32[288,1024]{1,0:T(8,128)S(1)}, f32[288,1024]{1,0:T(8,128)}) custom-call(bf16[288,1024]{1,0:T(8,128)(2,1)S(1)} %copy-done.10, bf16[288,1024]{1,0:T(8,128)(2,1)S(1)} %collective-permute-done.22.xb_ref.refs_5_, bf16[256,1024]{1,0:T(8,128)(2,1)S(1)} %copy-done.4, ...), custom_call_target="tpu_custom_call" | custom-call | bytes 24000 | tf_op jit(solution)/shard_map/pallas_call | solution.py:966
  203.6 2.4 collective-permute-done.21.xa_ref.refs_6_
  206.5 4.0 collective-permute-done.26.ea_ref
  211.8 7.7 %shard_map.242 = (bf16[576,1024]{1,0:T(8,128)(2,1)S(1)}, bf16[576,1024]{1,0:T(8,128)(2,1)S(1)}, f32[288,1024]{1,0:T(8,128)S(1)}, f32[288,1024]{1,0:T(8,128)}) custom-call(bf16[288,1024]{1,0:T(8,128)(2,1)S(1)} %collective-permute-done.21.xa_ref.refs_6_, bf16[288,1024]{1,0:T(8,128)(2,1)S(1)} %collective-permute-done.25.xb_ref.refs_7_, ...), custom_call_target="tpu_custom_call" | custom-call | bytes 24000 | tf_op jit(solution)/shard_map/pallas_call | solution.py:966
  220.1 2.7 collective-permute-done.28
  225.1 8.8 %shard_map.243.refs_8_ = bf16[1024,2304]{1,0:T(8,128)(2,1)} custom-call(bf16[256,1024]{1,0:T(8,128)(2,1)S(1)} %copy-done.4, bf16[256,1024]{1,0:T(8,128)(2,1)S(1)} %copy-done.15, bf16[256,1024]{1,0:T(8,128)(2,1)S(1)} %copy-done.13, bf16[256,1024]{1,0:T(8,128)(2,1)S(1)} %copy-done.17, bf16[288,1024]{1,0:T(8,128)(2,1)S(1)} %copy-done.11, ...), custom_call_target="tpu_custom_call" | custom-call | bytes 27000 | tf_op jit(solution)/shard_map/pallas_call | solution.py:1004
  234.0 5.3 %collective-permute-done.29.far_ref = bf16[288,1024]{1,0:T(8,128)(2,1)S(1)} collective-permute-done((bf16[288,1024]{1,0:T(8,128)(2,1)S(1)}, bf16[288,1024]{1,0:T(8,128)(2,1)S(1)}, u32[]{:S(2)}, u32[]{:S(2)}) %collective-permute-start.29) | collective-permute-done | bytes 589856 | tf_op jit(solution)/shard_map/ppermute | solution.py:1145
  239.3 4.8 shard_map.244
  246.3 4.2 all-to-all-start.4
  254.6 3.5 collective-permute-done.35.refs_7_
  258.1 3.7 collective-permute-done.34.refs_6_
  261.8 4.2 shard_map.245
  269.3 50.4 %shard_map.246 = (bf16[7,2048,128]{2,1,0:T(8,128)(2,1)}, bf16[2048,128]{1,0:T(8,128)(2,1)}, f32[8,128]{1,0:T(8,128)}) custom-call(s32[16]{0:T(128)} %bitcast.201, s32[4]{0:T(128)} %bitcast_subtract_fusion.begins_ref, bf16[5,2048,128]{2,1,0:T(8,128)(2,1)} %get-tuple-element.133.parts_ref, bf16[2048,128]{1,0:T(8,128)(2,1)} %copy-done.27, ...), custom_call_target="tpu_custom_call" | custom-call | bytes 180000 | tf_op jit(solution)/shard_map/pallas_call | solution.py:479
  319.6 2.4 gather_fusion.10
  322.1 6.2 %all-to-all-start.5 = ((bf16[8,256,128]{2,1,0:T(8,128)(2,1)}), bf16[8,256,128]{2,1,0:T(8,128)(2,1)}, u32[]{:S(2)}, u32[]{:S(2)}) async-start(bf16[8,256,128]{2,1,0:T(8,128)(2,1)} %bitcast.54), calls=%async_computation.5 | async-start | bytes 1048576 | tf_op jit(solution)/shard_map/all_to_all | solution.py:1381
  328.3 19.5 %shard_map.247 = (bf16[8,128,512]{2,1,0:T(8,128)(2,1)}, bf16[8,128,512]{2,1,0:T(8,128)(2,1)}, bf16[704,512]{1,0:T(8,128)(2,1)}, f32[288,128]{1,0:T(8,128)}) custom-call(s32[16]{0:T(128)} %bitcast.202, s32[16]{0:T(128)} %and_select_fusion.3.turn_ref, s32[16]{0:T(128)} %get-tuple-element.282.row_ref, s32[4]{0:T(128)} %bitcast_subtract_fusion.begins_ref, ...), custom_call_target="tpu_custom_call" | custom-call | bytes 51000000 | tf_op jit(solution)/shard_map/pallas_call | solution.py:808
  347.7 2.1 collective-permute-start.36
  352.2 1.8 slice_bitcast_fusion
  356.3 18.7 %shard_map.248 = (bf16[8,128,512]{2,1,0:T(8,128)(2,1)}, bf16[8,128,512]{2,1,0:T(8,128)(2,1)}, bf16[704,512]{1,0:T(8,128)(2,1)}) custom-call(s32[16]{0:T(128)} %bitcast.203, s32[16]{0:T(128)} %and_select_fusion.3.turn_ref, s32[16]{0:T(128)} %get-tuple-element.282.row_ref, s32[4]{0:T(128)} %bitcast_subtract_fusion.begins_ref, s32[1]{0:T(128)} %bitcast.40.head_ref, ...), custom_call_target="tpu_custom_call" | custom-call | bytes 51000000 | tf_op jit(solution)/shard_map/pallas_call | solution.py:808
  375.0 1.6 convert_add_fusion.1
  379.2 2.0 collective-permute-start.38
  381.3 2.4 collective-permute-start.39
  385.2 2.8 fusion.81
  388.0 2.9 fusion.82
  390.9 8.8 %collective-permute-done.41 = bf16[704,512]{1,0:T(8,128)(2,1)S(1)} collective-permute-done((bf16[704,512]{1,0:T(8,128)(2,1)S(1)}, bf16[704,512]{1,0:T(8,128)(2,1)S(1)}, u32[]{:S(2)}, u32[]{:S(2)}) %collective-permute-start.41) | collective-permute-done | bytes 720928 | tf_op jit(solution)/shard_map/ppermute | solution.py:1145
  400.9 1.7 reshape.878
  403.9 2.0 convert_add_fusion
  415.2 3.3 collective-permute-start.46
  420.6 7.4 %collective-permute-done.43 = bf16[256,512]{1,0:T(8,128)(2,1)S(1)} collective-permute-done((bf16[256,512]{1,0:T(8,128)(2,1)S(1)}, bf16[256,512]{1,0:T(8,128)(2,1)S(1)}, u32[]{:S(2)}, u32[]{:S(2)}) %collective-permute-start.43) | collective-permute-done | bytes 262176 | tf_op jit(solution)/shard_map/ppermute | solution.py:1468
  428.0 2.0 collective-permute-start.47
  433.4 4.3 all-to-all-start.6
  438.1 4.8 collective-permute-start.52
  442.9 2.5 collective-permute-start.53
  446.8 7.0 %collective-permute-done.52 = bf16[384,128]{1,0:T(8,128)(2,1)S(1)} collective-permute-done((bf16[384,128]{1,0:T(8,128)(2,1)S(1)}, bf16[384,128]{1,0:T(8,128)(2,1)S(1)}, u32[]{:S(2)}, u32[]{:S(2)}) %collective-permute-start.52) | collective-permute-done | bytes 98336 | tf_op jit(solution)/shard_map/ppermute | solution.py:1439
  453.8 2.7 collective-permute-done.53
  464.8 2.5 copy.127
  469.4 2.6 fusion.10
  (376 shorter events, 101.7 us)
Async XLA Ops:
  7.2 88.0 %all-gather.6.cloned.1.call-start = ((), (), s32[]{:S(2)}) async-start(), calls=%async_computation.10 | async-start | bytes 4718592 | tf_op jit(solution)/shard_map/all_gather | solution.py:1112
  11.1 17.8 %collective-permute-start.4 = (bf16[1,32,640]{2,1,0:T(8,128)(2,1)S(1)}, bf16[1,32,640]{2,1,0:T(8,128)(2,1)S(1)}, u32[]{:S(2)}, u32[]{:S(2)}) collective-permute-start(bf16[1,32,640]{2,1,0:T(8,128)(2,1)S(1)} %bitcast.267), channel_id=1, source_target_pairs={{0,6},{2,4},{4,2},{6,0},{1,7},{3,5},{5,3},{7,1},{8,14},{10,12},{12... | collective-permute-start | bytes 122888 | tf_op jit(solution)/shard_map/ppermute | solution.py:1117
  14.8 16.1 %collective-permute-start.3 = (bf16[1,32,640]{2,1,0:T(8,128)(2,1)S(1)}, bf16[1,32,640]{2,1,0:T(8,128)(2,1)S(1)}, u32[]{:S(2)}, u32[]{:S(2)}) collective-permute-start(bf16[1,32,640]{2,1,0:T(8,128)(2,1)S(1)} %bitcast.268), channel_id=1, source_target_pairs={{0,4},{2,6},{4,0},{6,2},{1,5},{3,7},{5,1},{7,3},{8,12},{10,14},{12... | collective-permute-start | bytes 122888 | tf_op jit(solution)/shard_map/ppermute | solution.py:1117
  14.8 16.7 %collective-permute-start.2 = (bf16[1,32,640]{2,1,0:T(8,128)(2,1)S(1)}, bf16[1,32,640]{2,1,0:T(8,128)(2,1)S(1)}, u32[]{:S(2)}, u32[]{:S(2)}) collective-permute-start(bf16[1,32,640]{2,1,0:T(8,128)(2,1)S(1)} %bitcast.269), channel_id=1, source_target_pairs={{0,2},{2,0},{4,6},{6,4},{1,3},{3,1},{5,7},{7,5},{8,10},{10,8},{12,... | collective-permute-start | bytes 122888 | tf_op jit(solution)/shard_map/ppermute | solution.py:1117
  15.6 28.4 %collective-permute-start.13 = (bf16[1,32,1024]{2,1,0:T(8,128)(2,1)}, bf16[1,32,1024]{2,1,0:T(8,128)(2,1)S(1)}, u32[]{:S(2)}, u32[]{:S(2)}) collective-permute-start(bf16[1,32,1024]{2,1,0:T(8,128)(2,1)} %bitcast.276), channel_id=1, source_target_pairs={{0,6},{2,4},{4,2},{6,0},{1,7},{3,5},{5,3},{7,1},{8,14},{10,12},{12... | collective-permute-start | bytes 196616 | tf_op jit(solution)/shard_map/ppermute | solution.py:1117
  19.2 25.0 %collective-permute-start.12 = (bf16[1,32,1024]{2,1,0:T(8,128)(2,1)}, bf16[1,32,1024]{2,1,0:T(8,128)(2,1)S(1)}, u32[]{:S(2)}, u32[]{:S(2)}) collective-permute-start(bf16[1,32,1024]{2,1,0:T(8,128)(2,1)} %bitcast.277), channel_id=1, source_target_pairs={{0,4},{2,6},{4,0},{6,2},{1,5},{3,7},{5,1},{7,3},{8,12},{10,14},{12... | collective-permute-start | bytes 196616 | tf_op jit(solution)/shard_map/ppermute | solution.py:1117
  21.2 18.2 %all-to-all-start = ((bf16[8,96,128]{2,1,0:T(8,128)(2,1)}), bf16[8,96,128]{2,1,0:T(8,128)(2,1)S(1)}, u32[]{:S(2)}, u32[]{:S(2)}) async-start(bf16[8,96,128]{2,1,0:T(8,128)(2,1)} %copy.101), calls=%async_computation | async-start | bytes 393216 | tf_op jit(solution)/shard_map/all_to_all | solution.py:1231
  28.9 15.7 %collective-permute-start.11 = (bf16[1,32,1024]{2,1,0:T(8,128)(2,1)S(1)}, bf16[1,32,1024]{2,1,0:T(8,128)(2,1)}, u32[]{:S(2)}, u32[]{:S(2)}) collective-permute-start(bf16[1,32,1024]{2,1,0:T(8,128)(2,1)S(1)} %bitcast.278), channel_id=1, source_target_pairs={{0,2},{2,0},{4,6},{6,4},{1,3},{3,1},{5,7},{7,5},{8,10},{10,8},{12,... | collective-permute-start | bytes 196616 | tf_op jit(solution)/shard_map/ppermute | solution.py:1117
  30.9 30.1 %collective-permute-start.9 = (bf16[256,1024]{1,0:T(8,128)(2,1)S(1)}, bf16[256,1024]{1,0:T(8,128)(2,1)S(1)}, u32[]{:S(2)}, u32[]{:S(2)}) collective-permute-start(bf16[256,1024]{1,0:T(8,128)(2,1)S(1)} %copy-done.4), channel_id=1, source_target_pairs={{0,16},{16,0},{1,17},{17,1},{2,18},{18,2},{3,19},{19,3},{4,20},{20... | collective-permute-start | bytes 1572872 | tf_op jit(solution)/shard_map/ppermute | solution.py:1145
  31.5 5.4 %collective-permute-start.5 = (bf16[4,32,640]{2,1,0:T(8,128)(2,1)S(1)}, bf16[4,32,640]{2,1,0:T(8,128)(2,1)S(1)}, u32[]{:S(2)}, u32[]{:S(2)}) collective-permute-start(bf16[4,32,640]{2,1,0:T(8,128)(2,1)S(1)} %pad_maximum_fusion.8), channel_id=1, source_target_pairs={{0,1},{1,0},{2,3},{3,2},{4,5},{5,4},{6,7},{7,6},{8,9},{9,8},{10,11... | collective-permute-start | bytes 491528 | tf_op jit(solution)/shard_map/ppermute | solution.py:1117
  37.7 15.1 %collective-permute-start.6 = (bf16[8,32,640]{2,1,0:T(8,128)(2,1)}, bf16[8,32,640]{2,1,0:T(8,128)(2,1)S(1)}, u32[]{:S(2)}, u32[]{:S(2)}) collective-permute-start(bf16[8,32,640]{2,1,0:T(8,128)(2,1)} %get-tuple-element.321), channel_id=1, source_target_pairs={{0,16},{16,0},{1,17},{17,1},{2,18},{18,2},{3,19},{19,3},{4,20},{20... | collective-permute-start | bytes 983048 | tf_op jit(solution)/shard_map/ppermute | solution.py:1117
  39.5 33.5 %all-to-all-start.1 = ((bf16[4,2,32,1024]{3,2,1,0:T(8,128)(2,1)}), bf16[4,2,32,1024]{3,2,1,0:T(8,128)(2,1)}, u32[]{:S(2)}, u32[]{:S(2)}) async-start(bf16[4,2,32,1024]{3,2,1,0:T(8,128)(2,1)} %copy.105), calls=%async_computation.1 | async-start | bytes 1048576 | tf_op jit(solution)/shard_map/all_to_all | solution.py:1223
  43.9 146.2 %all-gather.4.cloned.1.call-start = ((), (), s32[]{:S(2)}) async-start(), calls=%async_computation.8 | async-start | bytes 4718592 | tf_op jit(solution)/shard_map/all_gather | solution.py:1112
  44.0 29.0 %collective-permute-start.8 = (bf16[256,1024]{1,0:T(8,128)(2,1)S(1)}, bf16[256,1024]{1,0:T(8,128)(2,1)S(1)}, u32[]{:S(2)}, u32[]{:S(2)}) collective-permute-start(bf16[256,1024]{1,0:T(8,128)(2,1)S(1)} %copy-done.4), channel_id=1, source_target_pairs={{0,8},{8,0},{1,9},{9,1},{2,10},{10,2},{3,11},{11,3},{4,12},{12,4},... | collective-permute-start | bytes 1572872 | tf_op jit(solution)/shard_map/ppermute | solution.py:1145
  44.2 15.0 %collective-permute-start = (bf16[1,256,384]{2,1,0:T(8,128)(2,1)S(1)}, bf16[1,256,384]{2,1,0:T(8,128)(2,1)S(1)}, u32[]{:S(2)}, u32[]{:S(2)}) collective-permute-start(bf16[1,256,384]{2,1,0:T(8,128)(2,1)S(1)} %reshape.859), channel_id=1, source_target_pairs={{0,16},{16,0},{1,17},{17,1},{2,18},{18,2},{3,19},{19,3},{4,20},{20... | collective-permute-start | bytes 589832 | tf_op jit(solution)/shard_map/ppermute | solution.py:1117
  45.4 14.8 %collective-permute-start.14 = (bf16[4,32,1024]{2,1,0:T(8,128)(2,1)S(1)}, bf16[4,32,1024]{2,1,0:T(8,128)(2,1)S(1)}, u32[]{:S(2)}, u32[]{:S(2)}) collective-permute-start(bf16[4,32,1024]{2,1,0:T(8,128)(2,1)S(1)} %pad_maximum_fusion.5), channel_id=1, source_target_pairs={{0,1},{1,0},{2,3},{3,2},{4,5},{5,4},{6,7},{7,6},{8,9},{9,8},{10,11... | collective-permute-start | bytes 786440 | tf_op jit(solution)/shard_map/ppermute | solution.py:1117
  53.7 10.5 %collective-permute-start.7 = (bf16[16,32,640]{2,1,0:T(8,128)(2,1)}, bf16[16,32,640]{2,1,0:T(8,128)(2,1)}, u32[]{:S(2)}, u32[]{:S(2)}) collective-permute-start(bf16[16,32,640]{2,1,0:T(8,128)(2,1)} %get-tuple-element.312), channel_id=1, source_target_pairs={{0,8},{8,0},{1,9},{9,1},{2,10},{10,2},{3,11},{11,3},{4,12},{12,4},... | collective-permute-start | bytes 1966088 | tf_op jit(solution)/shard_map/ppermute | solution.py:1117
  59.3 2.3 collective-permute-start.1
  61.1 12.0 %collective-permute-start.10 = (bf16[256,1024]{1,0:T(8,128)(2,1)S(1)}, bf16[256,1024]{1,0:T(8,128)(2,1)S(1)}, u32[]{:S(2)}, u32[]{:S(2)}) collective-permute-start(bf16[256,1024]{1,0:T(8,128)(2,1)S(1)} %collective-permute-done.9.ga_ref.refs_2_), channel_id=1, source_target_pairs={{0,8},{8,0},{1,9},{9,1},{2,10},{10,2},{3,11},{11,3},{4,12},{12,4},... | collective-permute-start | bytes 1572872 | tf_op jit(solution)/shard_map/ppermute | solution.py:1145
  75.4 37.7 %collective-permute-start.19 = (bf16[1,2,1024]{2,1,0:T(2,128)(2,1)S(1)}, bf16[1,2,1024]{2,1,0:T(2,128)(2,1)S(1)}, u32[]{:S(2)}, u32[]{:S(2)}) collective-permute-start(bf16[1,2,1024]{2,1,0:T(2,128)(2,1)S(1)} %get-tuple-element.281), channel_id=1, source_target_pairs={{0,6},{2,4},{4,2},{6,0},{1,7},{3,5},{5,3},{7,1},{8,14},{10,12},{12... | collective-permute-start | bytes 12296 | tf_op jit(solution)/shard_map/ppermute | solution.py:1117
  77.8 35.3 %collective-permute-start.18 = (bf16[1,2,1024]{2,1,0:T(2,128)(2,1)S(1)}, bf16[1,2,1024]{2,1,0:T(2,128)(2,1)S(1)}, u32[]{:S(2)}, u32[]{:S(2)}) collective-permute-start(bf16[1,2,1024]{2,1,0:T(2,128)(2,1)S(1)} %get-tuple-element.281), channel_id=1, source_target_pairs={{0,4},{2,6},{4,0},{6,2},{1,5},{3,7},{5,1},{7,3},{8,12},{10,14},{12... | collective-permute-start | bytes 12296 | tf_op jit(solution)/shard_map/ppermute | solution.py:1117
  77.9 35.2 %collective-permute-start.17 = (bf16[1,2,1024]{2,1,0:T(2,128)(2,1)S(1)}, bf16[1,2,1024]{2,1,0:T(2,128)(2,1)S(1)}, u32[]{:S(2)}, u32[]{:S(2)}) collective-permute-start(bf16[1,2,1024]{2,1,0:T(2,128)(2,1)S(1)} %get-tuple-element.281), channel_id=1, source_target_pairs={{0,2},{2,0},{4,6},{6,4},{1,3},{3,1},{5,7},{7,5},{8,10},{10,8},{12,... | collective-permute-start | bytes 12296 | tf_op jit(solution)/shard_map/ppermute | solution.py:1117
  80.5 13.3 %collective-permute-start.15 = (bf16[8,32,1024]{2,1,0:T(8,128)(2,1)S(1)}, bf16[8,32,1024]{2,1,0:T(8,128)(2,1)}, u32[]{:S(2)}, u32[]{:S(2)}) collective-permute-start(bf16[8,32,1024]{2,1,0:T(8,128)(2,1)S(1)} %copy-done.48), channel_id=1, source_target_pairs={{0,16},{16,0},{1,17},{17,1},{2,18},{18,2},{3,19},{19,3},{4,20},{20... | collective-permute-start | bytes 1572872 | tf_op jit(solution)/shard_map/ppermute | solution.py:1117
  82.0 35.6 %all-to-all-start.2 = ((bf16[8,256,128]{2,1,0:T(8,128)(2,1)}), bf16[8,256,128]{2,1,0:T(8,128)(2,1)S(1)}, u32[]{:S(2)}, u32[]{:S(2)}) async-start(bf16[8,256,128]{2,1,0:T(8,128)(2,1)} %bitcast_bitcast_fusion), calls=%async_computation.2 | async-start | bytes 1048576 | tf_op jit(solution)/shard_map/all_to_all | solution.py:1264
  112.8 49.6 %collective-permute-start.16 = (bf16[16,32,1024]{2,1,0:T(8,128)(2,1)S(1)}, bf16[16,32,1024]{2,1,0:T(8,128)(2,1)S(1)}, u32[]{:S(2)}, u32[]{:S(2)}) collective-permute-start(bf16[16,32,1024]{2,1,0:T(8,128)(2,1)S(1)} %pad_maximum_fusion.near_ref), channel_id=1, source_target_pairs={{0,8},{8,0},{1,9},{9,1},{2,10},{10,2},{3,11},{11,3},{4,12},{12,4},... | collective-permute-start | bytes 3145736 | tf_op jit(solution)/shard_map/ppermute | solution.py:1145
  113.1 3.8 collective-permute-start.20
  163.4 20.5 %all-to-all-start.3 = ((bf16[8,2,144,128]{3,2,1,0:T(8,128)(2,1)}), bf16[8,2,144,128]{3,2,1,0:T(8,128)(2,1)S(1)}, u32[]{:S(2)}, u32[]{:S(2)}) async-start(bf16[8,2,144,128]{3,2,1,0:T(8,128)(2,1)} %bitcast.252), calls=%async_computation.3 | async-start | bytes 1179648 | tf_op jit(solution)/shard_map/all_to_all | solution.py:1300
  190.1 2.6 collective-permute-start.22
  190.1 16.0 %collective-permute-start.21 = (bf16[288,1024]{1,0:T(8,128)(2,1)}, bf16[288,1024]{1,0:T(8,128)(2,1)S(1)}, u32[]{:S(2)}, u32[]{:S(2)}) collective-permute-start(bf16[288,1024]{1,0:T(8,128)(2,1)} %copy-done.9), channel_id=1, source_target_pairs={{0,16},{16,0},{1,17},{17,1},{2,18},{18,2},{3,19},{19,3},{4,20},{20... | collective-permute-start | bytes 1769480 | tf_op jit(solution)/shard_map/ppermute | solution.py:1145
  191.3 1.3 collective-permute-start.23
  206.0 5.8 %collective-permute-start.25 = (bf16[288,1024]{1,0:T(8,128)(2,1)S(1)}, bf16[288,1024]{1,0:T(8,128)(2,1)S(1)}, u32[]{:S(2)}, u32[]{:S(2)}) collective-permute-start(bf16[288,1024]{1,0:T(8,128)(2,1)S(1)} %collective-permute-done.21.xa_ref.refs_6_), channel_id=1, source_target_pairs={{0,8},{8,0},{1,9},{9,1},{2,10},{10,2},{3,11},{11,3},{4,12},{12,4},... | collective-permute-start | bytes 1769480 | tf_op jit(solution)/shard_map/ppermute | solution.py:1145
  206.0 4.5 collective-permute-start.26
  210.5 1.3 collective-permute-start.27
  219.5 3.2 collective-permute-start.28
  219.7 19.6 %collective-permute-start.24 = (f32[288,1024]{1,0:T(8,128)S(1)}, f32[288,1024]{1,0:T(8,128)S(1)}, u32[]{:S(2)}, u32[]{:S(2)}) collective-permute-start(f32[288,1024]{1,0:T(8,128)S(1)} %copy-done.57), channel_id=1, source_target_pairs={{0,8},{8,0},{1,9},{9,1},{2,10},{10,2},{3,11},{11,3},{4,12},{12,4},... | collective-permute-start | bytes 3538952 | tf_op jit(solution)/shard_map/ppermute | solution.py:1145
  223.0 16.3 %collective-permute-start.29 = (bf16[288,1024]{1,0:T(8,128)(2,1)S(1)}, bf16[288,1024]{1,0:T(8,128)(2,1)S(1)}, u32[]{:S(2)}, u32[]{:S(2)}) collective-permute-start(bf16[288,1024]{1,0:T(8,128)(2,1)S(1)} %add_convert_fusion.1), channel_id=1, source_target_pairs={{0,16},{16,0},{1,17},{17,1},{2,18},{18,2},{3,19},{19,3},{4,20},{20... | collective-permute-start | bytes 1769480 | tf_op jit(solution)/shard_map/ppermute | solution.py:1145
  223.6 27.6 %collective-permute-start.31 = (bf16[288,1024]{1,0:T(8,128)(2,1)}, bf16[288,1024]{1,0:T(8,128)(2,1)}, u32[]{:S(2)}, u32[]{:S(2)}) collective-permute-start(bf16[288,1024]{1,0:T(8,128)(2,1)} %get-tuple-element.174.refs_0_), channel_id=1, source_target_pairs={{0,16},{16,0},{1,17},{17,1},{2,18},{18,2},{3,19},{19,3},{4,20},{20... | collective-permute-start | bytes 1769480 | tf_op jit(solution)/shard_map/ppermute | solution.py:1145
  246.3 19.8 %all-to-all-start.4 = ((bf16[8,256,128]{2,1,0:T(8,128)(2,1)}), bf16[8,256,128]{2,1,0:T(8,128)(2,1)}, u32[]{:S(2)}, u32[]{:S(2)}) async-start(bf16[8,256,128]{2,1,0:T(8,128)(2,1)} %copy-done.29), calls=%async_computation.4 | async-start | bytes 1048576 | tf_op jit(solution)/shard_map/all_to_all | solution.py:1357
  250.4 153.4 %reduce-scatter.2.cloned.1.call-start = ((), (), s32[]{:S(2)}) async-start(), calls=%async_computation.9 | async-start | bytes 5308416 | tf_op jit(solution)/shard_map/reduce_scatter | solution.py:1374
  250.7 3.9 collective-permute-start.30
  251.2 3.4 collective-permute-start.32
  252.4 5.7 %collective-permute-start.35 = (bf16[288,256]{1,0:T(8,128)(2,1)S(1)}, bf16[288,256]{1,0:T(8,128)(2,1)S(1)}, u32[]{:S(2)}, u32[]{:S(2)}) collective-permute-start(bf16[288,256]{1,0:T(8,128)(2,1)S(1)} %get-tuple-element.306), channel_id=1, source_target_pairs={{0,24},{8,16},{16,8},{24,0},{1,25},{9,17},{17,9},{25,1},{2,26},{10... | collective-permute-start | bytes 442376 | tf_op jit(solution)/shard_map/ppermute | solution.py:1364
  253.0 8.8 %collective-permute-start.34 = (bf16[288,256]{1,0:T(8,128)(2,1)S(1)}, bf16[288,256]{1,0:T(8,128)(2,1)S(1)}, u32[]{:S(2)}, u32[]{:S(2)}) collective-permute-start(bf16[288,256]{1,0:T(8,128)(2,1)S(1)} %get-tuple-element.307), channel_id=1, source_target_pairs={{0,16},{8,24},{16,0},{24,8},{1,17},{9,25},{17,1},{25,9},{2,18},{10... | collective-permute-start | bytes 442376 | tf_op jit(solution)/shard_map/ppermute | solution.py:1364
  254.6 7.3 %collective-permute-start.33 = (bf16[288,256]{1,0:T(8,128)(2,1)S(1)}, bf16[288,256]{1,0:T(8,128)(2,1)S(1)}, u32[]{:S(2)}, u32[]{:S(2)}) collective-permute-start(bf16[288,256]{1,0:T(8,128)(2,1)S(1)} %get-tuple-element.308), channel_id=1, source_target_pairs={{0,8},{8,0},{16,24},{24,16},{1,9},{9,1},{17,25},{25,17},{2,10},{10... | collective-permute-start | bytes 442376 | tf_op jit(solution)/shard_map/ppermute | solution.py:1364
  322.1 34.2 %all-to-all-start.5 = ((bf16[8,256,128]{2,1,0:T(8,128)(2,1)}), bf16[8,256,128]{2,1,0:T(8,128)(2,1)}, u32[]{:S(2)}, u32[]{:S(2)}) async-start(bf16[8,256,128]{2,1,0:T(8,128)(2,1)} %bitcast.54), calls=%async_computation.5 | async-start | bytes 1048576 | tf_op jit(solution)/shard_map/all_to_all | solution.py:1381
  347.7 27.3 %collective-permute-start.36 = (bf16[8,128,512]{2,1,0:T(8,128)(2,1)}, bf16[8,128,512]{2,1,0:T(8,128)(2,1)}, u32[]{:S(2)}, u32[]{:S(2)}) collective-permute-start(bf16[8,128,512]{2,1,0:T(8,128)(2,1)} %get-tuple-element.191), channel_id=1, source_target_pairs={{0,1},{1,0},{2,3},{3,2},{4,5},{5,4},{6,7},{7,6},{8,9},{9,8},{10,11... | collective-permute-start | bytes 3145736 | tf_op jit(solution)/shard_map/ppermute | solution.py:1455
  351.6 4.0 collective-permute-start.42
  378.3 25.6 %collective-permute-start.37 = (bf16[8,128,512]{2,1,0:T(8,128)(2,1)}, bf16[8,128,512]{2,1,0:T(8,128)(2,1)}, u32[]{:S(2)}, u32[]{:S(2)}) collective-permute-start(bf16[8,128,512]{2,1,0:T(8,128)(2,1)} %get-tuple-element.193), channel_id=1, source_target_pairs={{0,1},{1,0},{2,3},{3,2},{4,5},{5,4},{6,7},{7,6},{8,9},{9,8},{10,11... | collective-permute-start | bytes 3145736 | tf_op jit(solution)/shard_map/ppermute | solution.py:1455
  379.2 29.0 %collective-permute-start.38 = (bf16[256,512]{1,0:T(8,128)(2,1)}, bf16[256,512]{1,0:T(8,128)(2,1)}, u32[]{:S(2)}, u32[]{:S(2)}) collective-permute-start(bf16[256,512]{1,0:T(8,128)(2,1)} %bitcast.55), channel_id=1, source_target_pairs={{0,2},{2,0},{4,6},{6,4},{1,3},{3,1},{5,7},{7,5},{8,10},{10,8},{12,... | collective-permute-start | bytes 786440 | tf_op jit(solution)/shard_map/ppermute | solution.py:1468
  381.3 26.9 %collective-permute-start.39 = (bf16[256,512]{1,0:T(8,128)(2,1)}, bf16[256,512]{1,0:T(8,128)(2,1)}, u32[]{:S(2)}, u32[]{:S(2)}) collective-permute-start(bf16[256,512]{1,0:T(8,128)(2,1)} %bitcast.56), channel_id=1, source_target_pairs={{0,4},{2,6},{4,0},{6,2},{1,5},{3,7},{5,1},{7,3},{8,12},{10,14},{12... | collective-permute-start | bytes 786440 | tf_op jit(solution)/shard_map/ppermute | solution.py:1468
  383.7 24.5 %collective-permute-start.40 = (bf16[256,512]{1,0:T(8,128)(2,1)}, bf16[256,512]{1,0:T(8,128)(2,1)}, u32[]{:S(2)}, u32[]{:S(2)}) collective-permute-start(bf16[256,512]{1,0:T(8,128)(2,1)} %bitcast.57), channel_id=1, source_target_pairs={{0,6},{2,4},{4,2},{6,0},{1,7},{3,5},{5,3},{7,1},{8,14},{10,12},{12... | collective-permute-start | bytes 786440 | tf_op jit(solution)/shard_map/ppermute | solution.py:1468
  383.8 15.9 %collective-permute-start.41 = (bf16[704,512]{1,0:T(8,128)(2,1)S(1)}, bf16[704,512]{1,0:T(8,128)(2,1)S(1)}, u32[]{:S(2)}, u32[]{:S(2)}) collective-permute-start(bf16[704,512]{1,0:T(8,128)(2,1)S(1)} %pad_maximum_fusion.2), channel_id=1, source_target_pairs={{0,16},{16,0},{1,17},{17,1},{2,18},{18,2},{3,19},{19,3},{4,20},{20... | collective-permute-start | bytes 2162696 | tf_op jit(solution)/shard_map/ppermute | solution.py:1145
  408.4 21.7 %collective-permute-start.49 = (f32[288,1024]{1,0:T(8,128)S(1)}, f32[288,1024]{1,0:T(8,128)S(1)}, u32[]{:S(2)}, u32[]{:S(2)}) collective-permute-start(f32[288,1024]{1,0:T(8,128)S(1)} %split.48), channel_id=1, source_target_pairs={{0,8},{8,0},{1,9},{9,1},{2,10},{10,2},{3,11},{11,3},{4,12},{12,4},... | collective-permute-start | bytes 3538952 | tf_op jit(solution)/shard_map/ppermute | solution.py:1145
  410.8 8.1 %collective-permute-start.45 = (bf16[72,2,512]{2,1,0:T(2,128)(2,1)S(1)}, bf16[72,2,512]{2,1,0:T(2,128)(2,1)S(1)}, u32[]{:S(2)}, u32[]{:S(2)}) collective-permute-start(bf16[72,2,512]{2,1,0:T(2,128)(2,1)S(1)} %fusion.15), channel_id=1, source_target_pairs={{0,8},{8,0},{1,9},{9,1},{2,10},{10,2},{3,11},{11,3},{4,12},{12,4},... | collective-permute-start | bytes 442376 | tf_op jit(solution)/shard_map/ppermute | solution.py:1145
  414.1 24.1 %collective-permute-start.51 = (bf16[72,128]{1,0:T(8,128)(2,1)}, bf16[72,128]{1,0:T(8,128)(2,1)}, u32[]{:S(2)}, u32[]{:S(2)}) collective-permute-start(bf16[72,128]{1,0:T(8,128)(2,1)} %fusion.17), channel_id=1, source_target_pairs={{0,8},{8,0},{1,9},{9,1},{2,10},{10,2},{3,11},{11,3},{4,12},{12,4},... | collective-permute-start | bytes 55304 | tf_op jit(solution)/shard_map/ppermute | solution.py:1145
  414.4 13.6 %collective-permute-start.43 = (bf16[256,512]{1,0:T(8,128)(2,1)S(1)}, bf16[256,512]{1,0:T(8,128)(2,1)S(1)}, u32[]{:S(2)}, u32[]{:S(2)}) collective-permute-start(bf16[256,512]{1,0:T(8,128)(2,1)S(1)} %bitcast.275), channel_id=1, source_target_pairs={{0,2},{2,0},{4,6},{6,4},{1,3},{3,1},{5,7},{7,5},{8,10},{10,8},{12,... | collective-permute-start | bytes 786440 | tf_op jit(solution)/shard_map/ppermute | solution.py:1468
  415.2 27.7 %collective-permute-start.46 = (bf16[256,512]{1,0:T(8,128)(2,1)}, bf16[256,512]{1,0:T(8,128)(2,1)}, u32[]{:S(2)}, u32[]{:S(2)}) collective-permute-start(bf16[256,512]{1,0:T(8,128)(2,1)} %bitcast.62), channel_id=1, source_target_pairs={{0,4},{2,6},{4,0},{6,2},{1,5},{3,7},{5,1},{7,3},{8,12},{10,14},{12... | collective-permute-start | bytes 786440 | tf_op jit(solution)/shard_map/ppermute | solution.py:1468
  418.9 1.5 collective-permute-start.44
  420.4 26.3 %collective-permute-start.48 = (f32[288,1024]{1,0:T(8,128)}, f32[288,1024]{1,0:T(8,128)}, u32[]{:S(2)}, u32[]{:S(2)}) collective-permute-start(f32[288,1024]{1,0:T(8,128)} %get-tuple-element.285), channel_id=1, source_target_pairs={{0,8},{8,0},{1,9},{9,1},{2,10},{10,2},{3,11},{11,3},{4,12},{12,4},... | collective-permute-start | bytes 3538952 | tf_op jit(solution)/shard_map/ppermute | solution.py:1145
  428.0 18.7 %collective-permute-start.47 = (bf16[256,512]{1,0:T(8,128)(2,1)}, bf16[256,512]{1,0:T(8,128)(2,1)}, u32[]{:S(2)}, u32[]{:S(2)}) collective-permute-start(bf16[256,512]{1,0:T(8,128)(2,1)} %bitcast.63), channel_id=1, source_target_pairs={{0,6},{2,4},{4,2},{6,0},{1,7},{3,5},{5,3},{7,1},{8,14},{10,12},{12... | collective-permute-start | bytes 786440 | tf_op jit(solution)/shard_map/ppermute | solution.py:1468
  431.0 15.8 %collective-permute-start.50 = (bf16[288,1024]{1,0:T(8,128)(2,1)}, bf16[288,1024]{1,0:T(8,128)(2,1)}, u32[]{:S(2)}, u32[]{:S(2)}) collective-permute-start(bf16[288,1024]{1,0:T(8,128)(2,1)} %add_convert_fusion), channel_id=1, source_target_pairs={{0,16},{16,0},{1,17},{17,1},{2,18},{18,2},{3,19},{19,3},{4,20},{20... | collective-permute-start | bytes 1769480 | tf_op jit(solution)/shard_map/ppermute | solution.py:1145
  433.4 23.1 %all-to-all-start.6 = ((bf16[8,96,128]{2,1,0:T(8,128)(2,1)}), bf16[8,96,128]{2,1,0:T(8,128)(2,1)S(1)}, u32[]{:S(2)}, u32[]{:S(2)}) async-start(bf16[8,96,128]{2,1,0:T(8,128)(2,1)} %fusion.14), calls=%async_computation.7 | async-start | bytes 393216 | tf_op jit(solution)/shard_map/all_to_all | solution.py:1432
  438.1 15.7 %collective-permute-start.52 = (bf16[384,128]{1,0:T(8,128)(2,1)S(1)}, bf16[384,128]{1,0:T(8,128)(2,1)S(1)}, u32[]{:S(2)}, u32[]{:S(2)}) collective-permute-start(bf16[384,128]{1,0:T(8,128)(2,1)S(1)} %bitcast.284), channel_id=1, source_target_pairs={{0,0},{1,1},{2,8},{3,9},{4,16},{5,17},{6,24},{7,25},{8,2},{9,3},{1... | collective-permute-start | bytes 294920 | tf_op jit(solution)/shard_map/ppermute | solution.py:1439
  442.9 13.5 %collective-permute-start.53 = (bf16[384,128]{1,0:T(8,128)(2,1)S(1)}, bf16[384,128]{1,0:T(8,128)(2,1)S(1)}, u32[]{:S(2)}, u32[]{:S(2)}) collective-permute-start(bf16[384,128]{1,0:T(8,128)(2,1)S(1)} %bitcast.283), channel_id=1, source_target_pairs={{0,1},{1,0},{2,9},{3,8},{4,17},{5,16},{6,25},{7,24},{8,3},{9,2},{1... | collective-permute-start | bytes 294920 | tf_op jit(solution)/shard_map/ppermute | solution.py:1439
  (59 other events, 496.2 us)
Sparse Core Ops, SparseCore 0:
  10.2 83.2 all-gather.5
  95.6 72.8 all-gather.3
  266.2 96.6 reduce-scatter.1

commit v4 on v3

--- a/solution.py
+++ b/solution.py
@@ -287,7 +287,7 @@
             jax.ShapeDtypeStruct((spans, width, width), F32),
             jax.ShapeDtypeStruct((spans, 8, n, width), F32),
         ],
-        compiler_params=pltpu.CompilerParams(vmem_limit_bytes=48 * 1024 * 1024),
+        compiler_params=pltpu.CompilerParams(vmem_limit_bytes=60 * 1024 * 1024),
         cost_estimate=work(80),
     )(home, begins, parts, pre, gate, cols, *[first] * per_step)
 
@@ -508,7 +508,7 @@
             jax.ShapeDtypeStruct((total, width), LOW),
             jax.ShapeDtypeStruct((8, width), F32),
         ],
-        compiler_params=pltpu.CompilerParams(vmem_limit_bytes=56 * 1024 * 1024),
+        compiler_params=pltpu.CompilerParams(vmem_limit_bytes=60 * 1024 * 1024),
         cost_estimate=work(60),
     )(home, begins, parts, values, joined, scanned, gate, grad, grad, pre, first, first, cols, states, mats)
 
@@ -695,7 +695,7 @@
     unit = (x - stats_ref[:, 0:1]) * stats_ref[:, 1:2]
     rows = unit.shape[0]
     normed = unit * cols_ref[0:1] + cols_ref[1:2]
-    last = xp_ref[0, 8:].astype(F32)
+    last = xp_ref[0].astype(F32)[8:]
     prior = (last - prior_stats_ref[:, 0:1]) * prior_stats_ref[:, 1:2] * cols_ref[0:1] + cols_ref[1:2]
     keep = keep_rows(rows, step * rows, begins)
     diff = rows_down(normed, prior[prior.shape[0] - 1 :]) * keep - normed
@@ -776,13 +776,13 @@
 
     @pl.when(step == 0)
     def _():
-        held = sum_ref.shape[0]
-        low_sum_ref[:held] = sum_ref[...].astype(LOW)
         lane = lax.broadcasted_iota(jnp.int32, (1, wide), 1) + part * wide
         spread = jnp.concatenate([scan_ref[...]] * (wide // width), 1)
         spread = jnp.where(lane // width == head_ref[0], spread, 0.0)
-        low_sum_ref[held : held + 16] = jnp.concatenate([spread, ffn_ref[...]], 0).astype(LOW)
-        low_sum_ref[held + 16 :] = jnp.zeros_like(low_sum_ref[held + 16 :])
+        rest_rows = low_sum_ref.shape[0] - sum_ref.shape[0] - 16
+        low_sum_ref[...] = jnp.concatenate(
+            [sum_ref[...], spread, ffn_ref[...], jnp.zeros((rest_rows, wide), F32)], 0
+        ).astype(LOW)
         leave(1 - slot)
         leave(slot)
 
@@ -1311,6 +1311,10 @@
     extra_parts = seq_gather(jnp.concatenate([none[:, :1], og_after[:, None], none], 1).reshape(-1, wide))
     tokens_b = tokens.reshape(per, BLOCK, wide)
     tokens_ext = jnp.concatenate([tokens_b, row_before[:, None], row_after[:, None], none], 1)
+    if weight_rows % 16:
+        ordered = in_order(jnp.concatenate([out_shards, far_shards], 0), HEAD_AXES + ("ys", "core"))
+        out_shards, far_shards = ordered.reshape(2, -1, 32, wide)
+        out_table = jnp.arange(2 * out_shards.shape[0], dtype=jnp.int32)
     middle, ffn_in, out_rows, out_weight = middle_rows(
         out_ext, tokens_ext.reshape(-1, wide), out_shards, far_shards, out_table, settings, local, begins
     )

time: 486 us -> 483 us (level)
    unnamed x141 -> x129, local copies, waits for them, and re-layouts: 28.7 us -> 23.9 us
where the time goes in v4:
time: 483 us; the launch traced here: 477 us
  Pallas kernels  179 us (37%)
  starting transfers between devices  87.9 us (18%)
  waiting for transfers between devices  84 us (17%)
  local copies, waits for them, and re-layouts  74.5 us (15%)
  other arithmetic  30.3 us (6%)
  between operations  15.5 us (3%)
  matrix products  5.72 us (1%)
    pallas_call x1, Pallas kernels, scan_backward(): pl.pallas_call(functools.partial(scan_backward_kernel, heads, p), grid_sp...  50.4 us
    pallas_call x2, Pallas kernels, project_back(): pl.pallas_call(functools.partial(project_back_kernel, part, parts), grid_...  38.2 us
    pallas_call x1, Pallas kernels, scan_forward(): pl.pallas_call(functools.partial(scan_forward_kernel, heads, p), grid_spe...  36.3 us
    ppermute x24, waiting for transfers between devices, swap(): return lax.ppermute(x, axis, [(0, 1), (1, 0)])  27.6 us
    unnamed x129, local copies, waits for them, and re-layouts  23.9 us
    ppermute x17, starting transfers between devices, steps_along(): lax.ppermute(x, axis, [(i, i ^ k) for i in range(size)])  22 us
    ppermute x17, waiting for transfers between devices, steps_along(): lax.ppermute(x, axis, [(i, i ^ k) for i in range(size)])  21.1 us
    pallas_call x1, Pallas kernels, project(): pl.pallas_call(project_kernel, grid_spec=pltpu.PrefetchScalarGridSpec(num...  17.6 us
  transfers between devices with their start and end apart: 64, of which 21 were waited for; matrix products, arithmetic and copies ran while one was open for 17% of the time, Pallas kernels for 36%

profile of v4, /device:TPU:4, one launch (start us, length us, event | category | flops | bytes accessed | tf_op | source)
XLA Modules:
  0.0 476.8 jit_solution(14118817334052765364)
XLA Ops:
  11.1 3.7 collective-permute-start.4
  15.6 3.6 collective-permute-start.13
  21.2 5.2 %all-to-all-start = ((bf16[8,96,128]{2,1,0:T(8,128)(2,1)}), bf16[8,96,128]{2,1,0:T(8,128)(2,1)S(1)}, u32[]{:S(2)}, u32[]{:S(2)}) async-start(bf16[8,96,128]{2,1,0:T(8,128)(2,1)} %copy.101), calls=%async_computation | async-start | bytes 393216 | tf_op jit(solution)/shard_map/all_to_all | solution.py:1231
  28.9 2.0 collective-permute-start.11
  35.0 1.9 collective-permute-done.5
  37.7 1.8 collective-permute-start.6
  39.5 4.4 all-to-all-start.1
  45.4 1.8 collective-permute-start.14
  47.2 5.6 %collective-permute-done.6 = bf16[8,32,640]{2,1,0:T(8,128)(2,1)S(1)} collective-permute-done((bf16[8,32,640]{2,1,0:T(8,128)(2,1)}, bf16[8,32,640]{2,1,0:T(8,128)(2,1)S(1)}, u32[]{:S(2)}, u32[]{:S(2)}) %collective-permute-start.6) | collective-permute-done | bytes 327712 | tf_op jit(solution)/shard_map/ppermute | solution.py:1117
  53.7 5.5 %collective-permute-done = bf16[1,256,384]{2,1,0:T(8,128)(2,1)S(1)} collective-permute-done((bf16[1,256,384]{2,1,0:T(8,128)(2,1)S(1)}, bf16[1,256,384]{2,1,0:T(8,128)(2,1)S(1)}, u32[]{:S(2)}, u32[]{:S(2)}) %collective-permute-start) | collective-permute-done | bytes 196640 | tf_op jit(solution)/shard_map/ppermute | solution.py:1117
  64.2 2.0 constant_dynamic-update-slice_fusion.11
  66.2 3.1 gather_fusion.1
  73.1 2.3 copy.114
  75.4 2.4 collective-permute-start.19
  77.9 1.9 collective-permute-start.17
  82.0 5.2 %all-to-all-start.2 = ((bf16[8,256,128]{2,1,0:T(8,128)(2,1)}), bf16[8,256,128]{2,1,0:T(8,128)(2,1)}, u32[]{:S(2)}, u32[]{:S(2)}) async-start(bf16[8,256,128]{2,1,0:T(8,128)(2,1)} %bitcast_bitcast_fusion), calls=%async_computation.2 | async-start | bytes 1048576 | tf_op jit(solution)/shard_map/all_to_all | solution.py:1264
  88.1 5.8 %collective-permute-done.15 = bf16[8,32,1024]{2,1,0:T(8,128)(2,1)} collective-permute-done((bf16[8,32,1024]{2,1,0:T(8,128)(2,1)S(1)}, bf16[8,32,1024]{2,1,0:T(8,128)(2,1)}, u32[]{:S(2)}, u32[]{:S(2)}) %collective-permute-start.15) | collective-permute-done | bytes 524320 | tf_op jit(solution)/shard_map/ppermute | solution.py:1117
  95.0 17.6 %shard_map.238 = (bf16[16,32,1024]{2,1,0:T(8,128)(2,1)}, f32[2048,2]{1,0:T(8,128)}, bf16[5,2048,128]{2,1,0:T(8,128)(2,1)}, f32[2048,128]{1,0:T(8,128)}, f32[5,20...) custom-call(s32[16]{0:T(128)} %bitcast.222, ...), custom_call_target="tpu_custom_call" | custom-call | bytes 60000 | tf_op jit(solution)/shard_map/pallas_call | solution.py:637
  114.5 2.2 collective-permute-done.20
  117.4 36.3 %shard_map.239 = (bf16[2048,128]{1,0:T(8,128)(2,1)}, bf16[2048,128]{1,0:T(8,128)(2,1)}, bf16[2048,128]{1,0:T(8,128)(2,1)}, f32[2048,128]{1,0:T(8,128)}, f32[32,1...) custom-call(s32[16]{0:T(128)} %bitcast.223, s32[4]{0:T(128)} %bitcast_subtract_fusion.begins_ref, ...), custom_call_target="tpu_custom_call" | custom-call | bytes 240000 | tf_op jit(solution)/shard_map/pallas_call | solution.py:260
  153.7 2.5 gather_fusion.2
  158.2 2.1 maximum_maximum_fusion
  161.2 4.7 all-to-all-start.3
  166.7 1.8 gather_fusion.7
  168.5 1.8 gather_fusion.6
  171.5 10.2 %all-to-all-done.3.out_ref = bf16[8,2,144,128]{3,2,1,0:T(8,128)(2,1)S(1)} async-done(((bf16[8,2,144,128]{3,2,1,0:T(8,128)(2,1)}), bf16[8,2,144,128]{3,2,1,0:T(8,128)(2,1)S(1)}, u32[]{:S(2)}, u32[]{:S(2)}) %all-to-all-start.3) | async-done | bytes 589856 | tf_op jit(solution)/shard_map/all_to_all | solution.py:1300
  183.0 3.1 shard_map.240
  192.6 7.8 %shard_map.241 = (bf16[576,1024]{1,0:T(8,128)(2,1)S(1)}, bf16[576,1024]{1,0:T(8,128)(2,1)S(1)}, f32[288,1024]{1,0:T(8,128)S(1)}, f32[288,1024]{1,0:T(8,128)}) custom-call(bf16[288,1024]{1,0:T(8,128)(2,1)S(1)} %copy-done.7, bf16[288,1024]{1,0:T(8,128)(2,1)S(1)} %collective-permute-done.22.xb_ref.refs_5_, bf16[256,1024]{1,0:T(8,128)(2,1)S(1)} %copy-done.2, ...), custom_call_target="tpu_custom_call" | custom-call | bytes 24000 | tf_op jit(solution)/shard_map/pallas_call | solution.py:966
  201.4 2.4 collective-permute-done.21.xa_ref.refs_6_
  204.4 4.0 collective-permute-done.26.ea_ref
  209.6 7.7 %shard_map.242 = (bf16[576,1024]{1,0:T(8,128)(2,1)S(1)}, bf16[576,1024]{1,0:T(8,128)(2,1)S(1)}, f32[288,1024]{1,0:T(8,128)S(1)}, f32[288,1024]{1,0:T(8,128)}) custom-call(bf16[288,1024]{1,0:T(8,128)(2,1)S(1)} %collective-permute-done.21.xa_ref.refs_6_, bf16[288,1024]{1,0:T(8,128)(2,1)S(1)} %collective-permute-done.25.xb_ref.refs_7_, ...), custom_call_target="tpu_custom_call" | custom-call | bytes 24000 | tf_op jit(solution)/shard_map/pallas_call | solution.py:966
  217.9 2.7 collective-permute-done.28
  222.9 8.8 %shard_map.243.refs_8_ = bf16[1024,2304]{1,0:T(8,128)(2,1)} custom-call(bf16[256,1024]{1,0:T(8,128)(2,1)S(1)} %copy-done.2, bf16[256,1024]{1,0:T(8,128)(2,1)S(1)} %copy-done.12, bf16[256,1024]{1,0:T(8,128)(2,1)S(1)} %copy-done.10, bf16[256,1024]{1,0:T(8,128)(2,1)S(1)} %copy-done.14, bf16[288,1024]{1,0:T(8,128)(2,1)S(1)} %copy-done.8, ...), custom_call_target="tpu_custom_call" | custom-call | bytes 27000 | tf_op jit(solution)/shard_map/pallas_call | solution.py:1004
  231.7 5.4 %collective-permute-done.29.far_ref = bf16[288,1024]{1,0:T(8,128)(2,1)S(1)} collective-permute-done((bf16[288,1024]{1,0:T(8,128)(2,1)S(1)}, bf16[288,1024]{1,0:T(8,128)(2,1)S(1)}, u32[]{:S(2)}, u32[]{:S(2)}) %collective-permute-start.29) | collective-permute-done | bytes 589856 | tf_op jit(solution)/shard_map/ppermute | solution.py:1145
  237.1 4.7 shard_map.244
  244.1 4.1 all-to-all-start.4
  252.4 3.4 collective-permute-done.35.refs_7_
  255.9 3.8 collective-permute-done.34.refs_6_
  259.6 4.3 shard_map.245
  267.0 50.4 %shard_map.246 = (bf16[7,2048,128]{2,1,0:T(8,128)(2,1)}, bf16[2048,128]{1,0:T(8,128)(2,1)}, f32[8,128]{1,0:T(8,128)}) custom-call(s32[16]{0:T(128)} %bitcast.224, s32[4]{0:T(128)} %bitcast_subtract_fusion.begins_ref, bf16[5,2048,128]{2,1,0:T(8,128)(2,1)} %get-tuple-element.133.parts_ref, bf16[2048,128]{1,0:T(8,128)(2,1)} %get-tuple-element.145.values_ref, ...), custom_call_target="tpu_custom_call" | custom-call | bytes 180000 | tf_op jit(solution)/shard_map/pallas_call | solution.py:479
  317.4 2.4 gather_fusion.10
  319.9 6.2 %all-to-all-start.5 = ((bf16[8,256,128]{2,1,0:T(8,128)(2,1)}), bf16[8,256,128]{2,1,0:T(8,128)(2,1)}, u32[]{:S(2)}, u32[]{:S(2)}) async-start(bf16[8,256,128]{2,1,0:T(8,128)(2,1)} %bitcast.54), calls=%async_computation.5 | async-start | bytes 1048576 | tf_op jit(solution)/shard_map/all_to_all | solution.py:1385
  326.1 19.5 %shard_map.247 = (bf16[8,128,512]{2,1,0:T(8,128)(2,1)}, bf16[8,128,512]{2,1,0:T(8,128)(2,1)}, bf16[704,512]{1,0:T(8,128)(2,1)}, f32[288,128]{1,0:T(8,128)}) custom-call(s32[16]{0:T(128)} %bitcast.225, s32[16]{0:T(128)} %and_select_fusion.3.turn_ref, s32[16]{0:T(128)} %get-tuple-element.282.row_ref, s32[4]{0:T(128)} %bitcast_subtract_fusion.begins_ref, ...), custom_call_target="tpu_custom_call" | custom-call | bytes 51000000 | tf_op jit(solution)/shard_map/pallas_call | solution.py:808
  345.5 2.1 collective-permute-start.36
  350.0 1.8 slice_bitcast_fusion
  354.1 18.7 %shard_map.248 = (bf16[8,128,512]{2,1,0:T(8,128)(2,1)}, bf16[8,128,512]{2,1,0:T(8,128)(2,1)}, bf16[704,512]{1,0:T(8,128)(2,1)}) custom-call(s32[16]{0:T(128)} %bitcast.226, s32[16]{0:T(128)} %and_select_fusion.3.turn_ref, s32[16]{0:T(128)} %get-tuple-element.282.row_ref, s32[4]{0:T(128)} %bitcast_subtract_fusion.begins_ref, s32[1]{0:T(128)} %bitcast.40.head_ref, ...), custom_call_target="tpu_custom_call" | custom-call | bytes 51000000 | tf_op jit(solution)/shard_map/pallas_call | solution.py:808
  372.9 1.6 convert_add_fusion.1
  377.1 2.1 collective-permute-start.38
  379.1 2.3 collective-permute-start.39
  382.9 2.8 fusion.81
  385.8 2.9 fusion.82
  388.7 8.8 %collective-permute-done.41 = bf16[704,512]{1,0:T(8,128)(2,1)S(1)} collective-permute-done((bf16[704,512]{1,0:T(8,128)(2,1)S(1)}, bf16[704,512]{1,0:T(8,128)(2,1)S(1)}, u32[]{:S(2)}, u32[]{:S(2)}) %collective-permute-start.41) | collective-permute-done | bytes 720928 | tf_op jit(solution)/shard_map/ppermute | solution.py:1145
  398.7 1.7 reshape.878
  401.7 2.0 convert_add_fusion
  413.0 3.3 collective-permute-start.46
  418.5 7.4 %collective-permute-done.43 = bf16[256,512]{1,0:T(8,128)(2,1)S(1)} collective-permute-done((bf16[256,512]{1,0:T(8,128)(2,1)S(1)}, bf16[256,512]{1,0:T(8,128)(2,1)S(1)}, u32[]{:S(2)}, u32[]{:S(2)}) %collective-permute-start.43) | collective-permute-done | bytes 262176 | tf_op jit(solution)/shard_map/ppermute | solution.py:1472
  425.9 1.9 collective-permute-start.47
  431.3 4.2 all-to-all-start.6
  436.0 4.8 %collective-permute-start.52 = (bf16[384,128]{1,0:T(8,128)(2,1)S(1)}, bf16[384,128]{1,0:T(8,128)(2,1)S(1)}, u32[]{:S(2)}, u32[]{:S(2)}) collective-permute-start(bf16[384,128]{1,0:T(8,128)(2,1)S(1)} %bitcast.278), channel_id=1, source_target_pairs={{0,0},{1,1},{2,8},{3,9},{4,16},{5,17},{6,24},{7,25},{8,2},{9,3},{1... | collective-permute-start | bytes 294920 | tf_op jit(solution)/shard_map/ppermute | solution.py:1443
  440.8 2.5 collective-permute-start.53
  444.6 7.1 %collective-permute-done.52 = bf16[384,128]{1,0:T(8,128)(2,1)S(1)} collective-permute-done((bf16[384,128]{1,0:T(8,128)(2,1)S(1)}, bf16[384,128]{1,0:T(8,128)(2,1)S(1)}, u32[]{:S(2)}, u32[]{:S(2)}) %collective-permute-start.52) | collective-permute-done | bytes 98336 | tf_op jit(solution)/shard_map/ppermute | solution.py:1443
  451.7 2.6 collective-permute-done.53
  462.6 2.5 copy.127
  467.2 2.6 fusion.10
  (364 shorter events, 97.3 us)
Async XLA Ops:
  7.2 87.8 %all-gather.6.cloned.1.call-start = ((), (), s32[]{:S(2)}) async-start(), calls=%async_computation.10 | async-start | bytes 4718592 | tf_op jit(solution)/shard_map/all_gather | solution.py:1112
  11.1 17.8 %collective-permute-start.4 = (bf16[1,32,640]{2,1,0:T(8,128)(2,1)S(1)}, bf16[1,32,640]{2,1,0:T(8,128)(2,1)S(1)}, u32[]{:S(2)}, u32[]{:S(2)}) collective-permute-start(bf16[1,32,640]{2,1,0:T(8,128)(2,1)S(1)} %bitcast.261), channel_id=1, source_target_pairs={{0,6},{2,4},{4,2},{6,0},{1,7},{3,5},{5,3},{7,1},{8,14},{10,12},{12... | collective-permute-start | bytes 122888 | tf_op jit(solution)/shard_map/ppermute | solution.py:1117
  14.8 16.1 %collective-permute-start.3 = (bf16[1,32,640]{2,1,0:T(8,128)(2,1)S(1)}, bf16[1,32,640]{2,1,0:T(8,128)(2,1)S(1)}, u32[]{:S(2)}, u32[]{:S(2)}) collective-permute-start(bf16[1,32,640]{2,1,0:T(8,128)(2,1)S(1)} %bitcast.262), channel_id=1, source_target_pairs={{0,4},{2,6},{4,0},{6,2},{1,5},{3,7},{5,1},{7,3},{8,12},{10,14},{12... | collective-permute-start | bytes 122888 | tf_op jit(solution)/shard_map/ppermute | solution.py:1117
  14.8 16.7 %collective-permute-start.2 = (bf16[1,32,640]{2,1,0:T(8,128)(2,1)S(1)}, bf16[1,32,640]{2,1,0:T(8,128)(2,1)S(1)}, u32[]{:S(2)}, u32[]{:S(2)}) collective-permute-start(bf16[1,32,640]{2,1,0:T(8,128)(2,1)S(1)} %bitcast.263), channel_id=1, source_target_pairs={{0,2},{2,0},{4,6},{6,4},{1,3},{3,1},{5,7},{7,5},{8,10},{10,8},{12,... | collective-permute-start | bytes 122888 | tf_op jit(solution)/shard_map/ppermute | solution.py:1117
  15.6 28.4 %collective-permute-start.13 = (bf16[1,32,1024]{2,1,0:T(8,128)(2,1)}, bf16[1,32,1024]{2,1,0:T(8,128)(2,1)S(1)}, u32[]{:S(2)}, u32[]{:S(2)}) collective-permute-start(bf16[1,32,1024]{2,1,0:T(8,128)(2,1)} %bitcast.270), channel_id=1, source_target_pairs={{0,6},{2,4},{4,2},{6,0},{1,7},{3,5},{5,3},{7,1},{8,14},{10,12},{12... | collective-permute-start | bytes 196616 | tf_op jit(solution)/shard_map/ppermute | solution.py:1117
  19.2 25.0 %collective-permute-start.12 = (bf16[1,32,1024]{2,1,0:T(8,128)(2,1)}, bf16[1,32,1024]{2,1,0:T(8,128)(2,1)S(1)}, u32[]{:S(2)}, u32[]{:S(2)}) collective-permute-start(bf16[1,32,1024]{2,1,0:T(8,128)(2,1)} %bitcast.271), channel_id=1, source_target_pairs={{0,4},{2,6},{4,0},{6,2},{1,5},{3,7},{5,1},{7,3},{8,12},{10,14},{12... | collective-permute-start | bytes 196616 | tf_op jit(solution)/shard_map/ppermute | solution.py:1117
  21.2 18.2 %all-to-all-start = ((bf16[8,96,128]{2,1,0:T(8,128)(2,1)}), bf16[8,96,128]{2,1,0:T(8,128)(2,1)S(1)}, u32[]{:S(2)}, u32[]{:S(2)}) async-start(bf16[8,96,128]{2,1,0:T(8,128)(2,1)} %copy.101), calls=%async_computation | async-start | bytes 393216 | tf_op jit(solution)/shard_map/all_to_all | solution.py:1231
  28.9 15.7 %collective-permute-start.11 = (bf16[1,32,1024]{2,1,0:T(8,128)(2,1)S(1)}, bf16[1,32,1024]{2,1,0:T(8,128)(2,1)}, u32[]{:S(2)}, u32[]{:S(2)}) collective-permute-start(bf16[1,32,1024]{2,1,0:T(8,128)(2,1)S(1)} %bitcast.272), channel_id=1, source_target_pairs={{0,2},{2,0},{4,6},{6,4},{1,3},{3,1},{5,7},{7,5},{8,10},{10,8},{12,... | collective-permute-start | bytes 196616 | tf_op jit(solution)/shard_map/ppermute | solution.py:1117
  30.9 30.1 %collective-permute-start.9 = (bf16[256,1024]{1,0:T(8,128)(2,1)S(1)}, bf16[256,1024]{1,0:T(8,128)(2,1)S(1)}, u32[]{:S(2)}, u32[]{:S(2)}) collective-permute-start(bf16[256,1024]{1,0:T(8,128)(2,1)S(1)} %copy-done.2), channel_id=1, source_target_pairs={{0,16},{16,0},{1,17},{17,1},{2,18},{18,2},{3,19},{19,3},{4,20},{20... | collective-permute-start | bytes 1572872 | tf_op jit(solution)/shard_map/ppermute | solution.py:1145
  31.5 5.4 %collective-permute-start.5 = (bf16[4,32,640]{2,1,0:T(8,128)(2,1)S(1)}, bf16[4,32,640]{2,1,0:T(8,128)(2,1)S(1)}, u32[]{:S(2)}, u32[]{:S(2)}) collective-permute-start(bf16[4,32,640]{2,1,0:T(8,128)(2,1)S(1)} %pad_maximum_fusion.8), channel_id=1, source_target_pairs={{0,1},{1,0},{2,3},{3,2},{4,5},{5,4},{6,7},{7,6},{8,9},{9,8},{10,11... | collective-permute-start | bytes 491528 | tf_op jit(solution)/shard_map/ppermute | solution.py:1117
  37.7 15.1 %collective-permute-start.6 = (bf16[8,32,640]{2,1,0:T(8,128)(2,1)}, bf16[8,32,640]{2,1,0:T(8,128)(2,1)S(1)}, u32[]{:S(2)}, u32[]{:S(2)}) collective-permute-start(bf16[8,32,640]{2,1,0:T(8,128)(2,1)} %get-tuple-element.321), channel_id=1, source_target_pairs={{0,16},{16,0},{1,17},{17,1},{2,18},{18,2},{3,19},{19,3},{4,20},{20... | collective-permute-start | bytes 983048 | tf_op jit(solution)/shard_map/ppermute | solution.py:1117
  39.5 33.5 %all-to-all-start.1 = ((bf16[4,2,32,1024]{3,2,1,0:T(8,128)(2,1)}), bf16[4,2,32,1024]{3,2,1,0:T(8,128)(2,1)}, u32[]{:S(2)}, u32[]{:S(2)}) async-start(bf16[4,2,32,1024]{3,2,1,0:T(8,128)(2,1)} %copy.105), calls=%async_computation.1 | async-start | bytes 1048576 | tf_op jit(solution)/shard_map/all_to_all | solution.py:1223
  43.9 144.1 %all-gather.4.cloned.1.call-start = ((), (), s32[]{:S(2)}) async-start(), calls=%async_computation.8 | async-start | bytes 4718592 | tf_op jit(solution)/shard_map/all_gather | solution.py:1112
  44.0 29.1 %collective-permute-start.8 = (bf16[256,1024]{1,0:T(8,128)(2,1)S(1)}, bf16[256,1024]{1,0:T(8,128)(2,1)S(1)}, u32[]{:S(2)}, u32[]{:S(2)}) collective-permute-start(bf16[256,1024]{1,0:T(8,128)(2,1)S(1)} %copy-done.2), channel_id=1, source_target_pairs={{0,8},{8,0},{1,9},{9,1},{2,10},{10,2},{3,11},{11,3},{4,12},{12,4},... | collective-permute-start | bytes 1572872 | tf_op jit(solution)/shard_map/ppermute | solution.py:1145
  44.2 15.0 %collective-permute-start = (bf16[1,256,384]{2,1,0:T(8,128)(2,1)S(1)}, bf16[1,256,384]{2,1,0:T(8,128)(2,1)S(1)}, u32[]{:S(2)}, u32[]{:S(2)}) collective-permute-start(bf16[1,256,384]{2,1,0:T(8,128)(2,1)S(1)} %reshape.859), channel_id=1, source_target_pairs={{0,16},{16,0},{1,17},{17,1},{2,18},{18,2},{3,19},{19,3},{4,20},{20... | collective-permute-start | bytes 589832 | tf_op jit(solution)/shard_map/ppermute | solution.py:1117
  45.4 14.8 %collective-permute-start.14 = (bf16[4,32,1024]{2,1,0:T(8,128)(2,1)S(1)}, bf16[4,32,1024]{2,1,0:T(8,128)(2,1)S(1)}, u32[]{:S(2)}, u32[]{:S(2)}) collective-permute-start(bf16[4,32,1024]{2,1,0:T(8,128)(2,1)S(1)} %pad_maximum_fusion.5), channel_id=1, source_target_pairs={{0,1},{1,0},{2,3},{3,2},{4,5},{5,4},{6,7},{7,6},{8,9},{9,8},{10,11... | collective-permute-start | bytes 786440 | tf_op jit(solution)/shard_map/ppermute | solution.py:1117
  53.7 10.5 %collective-permute-start.7 = (bf16[16,32,640]{2,1,0:T(8,128)(2,1)}, bf16[16,32,640]{2,1,0:T(8,128)(2,1)}, u32[]{:S(2)}, u32[]{:S(2)}) collective-permute-start(bf16[16,32,640]{2,1,0:T(8,128)(2,1)} %get-tuple-element.312), channel_id=1, source_target_pairs={{0,8},{8,0},{1,9},{9,1},{2,10},{10,2},{3,11},{11,3},{4,12},{12,4},... | collective-permute-start | bytes 1966088 | tf_op jit(solution)/shard_map/ppermute | solution.py:1117
  59.3 2.3 collective-permute-start.1
  61.1 12.0 %collective-permute-start.10 = (bf16[256,1024]{1,0:T(8,128)(2,1)S(1)}, bf16[256,1024]{1,0:T(8,128)(2,1)S(1)}, u32[]{:S(2)}, u32[]{:S(2)}) collective-permute-start(bf16[256,1024]{1,0:T(8,128)(2,1)S(1)} %collective-permute-done.9.ga_ref.refs_2_), channel_id=1, source_target_pairs={{0,8},{8,0},{1,9},{9,1},{2,10},{10,2},{3,11},{11,3},{4,12},{12,4},... | collective-permute-start | bytes 1572872 | tf_op jit(solution)/shard_map/ppermute | solution.py:1145
  75.4 37.5 %collective-permute-start.19 = (bf16[1,2,1024]{2,1,0:T(2,128)(2,1)S(1)}, bf16[1,2,1024]{2,1,0:T(2,128)(2,1)S(1)}, u32[]{:S(2)}, u32[]{:S(2)}) collective-permute-start(bf16[1,2,1024]{2,1,0:T(2,128)(2,1)S(1)} %get-tuple-element.281), channel_id=1, source_target_pairs={{0,6},{2,4},{4,2},{6,0},{1,7},{3,5},{5,3},{7,1},{8,14},{10,12},{12... | collective-permute-start | bytes 12296 | tf_op jit(solution)/shard_map/ppermute | solution.py:1117
  77.8 35.0 %collective-permute-start.18 = (bf16[1,2,1024]{2,1,0:T(2,128)(2,1)S(1)}, bf16[1,2,1024]{2,1,0:T(2,128)(2,1)S(1)}, u32[]{:S(2)}, u32[]{:S(2)}) collective-permute-start(bf16[1,2,1024]{2,1,0:T(2,128)(2,1)S(1)} %get-tuple-element.281), channel_id=1, source_target_pairs={{0,4},{2,6},{4,0},{6,2},{1,5},{3,7},{5,1},{7,3},{8,12},{10,14},{12... | collective-permute-start | bytes 12296 | tf_op jit(solution)/shard_map/ppermute | solution.py:1117
  77.9 35.0 %collective-permute-start.17 = (bf16[1,2,1024]{2,1,0:T(2,128)(2,1)S(1)}, bf16[1,2,1024]{2,1,0:T(2,128)(2,1)S(1)}, u32[]{:S(2)}, u32[]{:S(2)}) collective-permute-start(bf16[1,2,1024]{2,1,0:T(2,128)(2,1)S(1)} %get-tuple-element.281), channel_id=1, source_target_pairs={{0,2},{2,0},{4,6},{6,4},{1,3},{3,1},{5,7},{7,5},{8,10},{10,8},{12,... | collective-permute-start | bytes 12296 | tf_op jit(solution)/shard_map/ppermute | solution.py:1117
  80.6 13.3 %collective-permute-start.15 = (bf16[8,32,1024]{2,1,0:T(8,128)(2,1)S(1)}, bf16[8,32,1024]{2,1,0:T(8,128)(2,1)}, u32[]{:S(2)}, u32[]{:S(2)}) collective-permute-start(bf16[8,32,1024]{2,1,0:T(8,128)(2,1)S(1)} %copy-done.41), channel_id=1, source_target_pairs={{0,16},{16,0},{1,17},{17,1},{2,18},{18,2},{3,19},{19,3},{4,20},{20... | collective-permute-start | bytes 1572872 | tf_op jit(solution)/shard_map/ppermute | solution.py:1117
  82.0 35.4 %all-to-all-start.2 = ((bf16[8,256,128]{2,1,0:T(8,128)(2,1)}), bf16[8,256,128]{2,1,0:T(8,128)(2,1)}, u32[]{:S(2)}, u32[]{:S(2)}) async-start(bf16[8,256,128]{2,1,0:T(8,128)(2,1)} %bitcast_bitcast_fusion), calls=%async_computation.2 | async-start | bytes 1048576 | tf_op jit(solution)/shard_map/all_to_all | solution.py:1264
  112.6 47.7 %collective-permute-start.16 = (bf16[16,32,1024]{2,1,0:T(8,128)(2,1)S(1)}, bf16[16,32,1024]{2,1,0:T(8,128)(2,1)S(1)}, u32[]{:S(2)}, u32[]{:S(2)}) collective-permute-start(bf16[16,32,1024]{2,1,0:T(8,128)(2,1)S(1)} %pad_maximum_fusion.near_ref), channel_id=1, source_target_pairs={{0,8},{8,0},{1,9},{9,1},{2,10},{10,2},{3,11},{11,3},{4,12},{12,4},... | collective-permute-start | bytes 3145736 | tf_op jit(solution)/shard_map/ppermute | solution.py:1145
  112.9 3.8 collective-permute-start.20
  161.2 20.5 %all-to-all-start.3 = ((bf16[8,2,144,128]{3,2,1,0:T(8,128)(2,1)}), bf16[8,2,144,128]{3,2,1,0:T(8,128)(2,1)S(1)}, u32[]{:S(2)}, u32[]{:S(2)}) async-start(bf16[8,2,144,128]{3,2,1,0:T(8,128)(2,1)} %bitcast.244), calls=%async_computation.3 | async-start | bytes 1179648 | tf_op jit(solution)/shard_map/all_to_all | solution.py:1300
  187.9 2.6 collective-permute-start.22
  187.9 16.0 %collective-permute-start.21 = (bf16[288,1024]{1,0:T(8,128)(2,1)}, bf16[288,1024]{1,0:T(8,128)(2,1)S(1)}, u32[]{:S(2)}, u32[]{:S(2)}) collective-permute-start(bf16[288,1024]{1,0:T(8,128)(2,1)} %copy-done.6), channel_id=1, source_target_pairs={{0,16},{16,0},{1,17},{17,1},{2,18},{18,2},{3,19},{19,3},{4,20},{20... | collective-permute-start | bytes 1769480 | tf_op jit(solution)/shard_map/ppermute | solution.py:1145
  189.2 1.3 collective-permute-start.23
  203.9 5.8 %collective-permute-start.25 = (bf16[288,1024]{1,0:T(8,128)(2,1)S(1)}, bf16[288,1024]{1,0:T(8,128)(2,1)S(1)}, u32[]{:S(2)}, u32[]{:S(2)}) collective-permute-start(bf16[288,1024]{1,0:T(8,128)(2,1)S(1)} %collective-permute-done.21.xa_ref.refs_6_), channel_id=1, source_target_pairs={{0,8},{8,0},{1,9},{9,1},{2,10},{10,2},{3,11},{11,3},{4,12},{12,4},... | collective-permute-start | bytes 1769480 | tf_op jit(solution)/shard_map/ppermute | solution.py:1145
  203.9 4.5 collective-permute-start.26
  208.4 1.3 collective-permute-start.27
  217.4 3.2 collective-permute-start.28
  217.5 19.5 %collective-permute-start.24 = (f32[288,1024]{1,0:T(8,128)S(1)}, f32[288,1024]{1,0:T(8,128)S(1)}, u32[]{:S(2)}, u32[]{:S(2)}) collective-permute-start(f32[288,1024]{1,0:T(8,128)S(1)} %copy-done.51), channel_id=1, source_target_pairs={{0,8},{8,0},{1,9},{9,1},{2,10},{10,2},{3,11},{11,3},{4,12},{12,4},... | collective-permute-start | bytes 3538952 | tf_op jit(solution)/shard_map/ppermute | solution.py:1145
  220.9 16.2 %collective-permute-start.29 = (bf16[288,1024]{1,0:T(8,128)(2,1)S(1)}, bf16[288,1024]{1,0:T(8,128)(2,1)S(1)}, u32[]{:S(2)}, u32[]{:S(2)}) collective-permute-start(bf16[288,1024]{1,0:T(8,128)(2,1)S(1)} %add_convert_fusion.1), channel_id=1, source_target_pairs={{0,16},{16,0},{1,17},{17,1},{2,18},{18,2},{3,19},{19,3},{4,20},{20... | collective-permute-start | bytes 1769480 | tf_op jit(solution)/shard_map/ppermute | solution.py:1145
  221.4 27.6 %collective-permute-start.31 = (bf16[288,1024]{1,0:T(8,128)(2,1)}, bf16[288,1024]{1,0:T(8,128)(2,1)}, u32[]{:S(2)}, u32[]{:S(2)}) collective-permute-start(bf16[288,1024]{1,0:T(8,128)(2,1)} %get-tuple-element.174.refs_0_), channel_id=1, source_target_pairs={{0,16},{16,0},{1,17},{17,1},{2,18},{18,2},{3,19},{19,3},{4,20},{20... | collective-permute-start | bytes 1769480 | tf_op jit(solution)/shard_map/ppermute | solution.py:1145
  244.1 19.8 %all-to-all-start.4 = ((bf16[8,256,128]{2,1,0:T(8,128)(2,1)}), bf16[8,256,128]{2,1,0:T(8,128)(2,1)}, u32[]{:S(2)}, u32[]{:S(2)}) async-start(bf16[8,256,128]{2,1,0:T(8,128)(2,1)} %copy-done.22), calls=%async_computation.4 | async-start | bytes 1048576 | tf_op jit(solution)/shard_map/all_to_all | solution.py:1361
  248.2 153.4 %reduce-scatter.2.cloned.1.call-start = ((), (), s32[]{:S(2)}) async-start(), calls=%async_computation.9 | async-start | bytes 5308416 | tf_op jit(solution)/shard_map/reduce_scatter | solution.py:1378
  248.5 3.9 collective-permute-start.30
  249.0 3.4 collective-permute-start.32
  250.2 5.6 %collective-permute-start.35 = (bf16[288,256]{1,0:T(8,128)(2,1)S(1)}, bf16[288,256]{1,0:T(8,128)(2,1)S(1)}, u32[]{:S(2)}, u32[]{:S(2)}) collective-permute-start(bf16[288,256]{1,0:T(8,128)(2,1)S(1)} %get-tuple-element.306), channel_id=1, source_target_pairs={{0,24},{8,16},{16,8},{24,0},{1,25},{9,17},{17,9},{25,1},{2,26},{10... | collective-permute-start | bytes 442376 | tf_op jit(solution)/shard_map/ppermute | solution.py:1368
  250.9 8.8 %collective-permute-start.34 = (bf16[288,256]{1,0:T(8,128)(2,1)S(1)}, bf16[288,256]{1,0:T(8,128)(2,1)S(1)}, u32[]{:S(2)}, u32[]{:S(2)}) collective-permute-start(bf16[288,256]{1,0:T(8,128)(2,1)S(1)} %get-tuple-element.307), channel_id=1, source_target_pairs={{0,16},{8,24},{16,0},{24,8},{1,17},{9,25},{17,1},{25,9},{2,18},{10... | collective-permute-start | bytes 442376 | tf_op jit(solution)/shard_map/ppermute | solution.py:1368
  252.4 7.2 %collective-permute-start.33 = (bf16[288,256]{1,0:T(8,128)(2,1)S(1)}, bf16[288,256]{1,0:T(8,128)(2,1)S(1)}, u32[]{:S(2)}, u32[]{:S(2)}) collective-permute-start(bf16[288,256]{1,0:T(8,128)(2,1)S(1)} %get-tuple-element.308), channel_id=1, source_target_pairs={{0,8},{8,0},{16,24},{24,16},{1,9},{9,1},{17,25},{25,17},{2,10},{10... | collective-permute-start | bytes 442376 | tf_op jit(solution)/shard_map/ppermute | solution.py:1368
  319.9 34.2 %all-to-all-start.5 = ((bf16[8,256,128]{2,1,0:T(8,128)(2,1)}), bf16[8,256,128]{2,1,0:T(8,128)(2,1)}, u32[]{:S(2)}, u32[]{:S(2)}) async-start(bf16[8,256,128]{2,1,0:T(8,128)(2,1)} %bitcast.54), calls=%async_computation.5 | async-start | bytes 1048576 | tf_op jit(solution)/shard_map/all_to_all | solution.py:1385
  345.5 27.4 %collective-permute-start.36 = (bf16[8,128,512]{2,1,0:T(8,128)(2,1)}, bf16[8,128,512]{2,1,0:T(8,128)(2,1)}, u32[]{:S(2)}, u32[]{:S(2)}) collective-permute-start(bf16[8,128,512]{2,1,0:T(8,128)(2,1)} %get-tuple-element.191), channel_id=1, source_target_pairs={{0,1},{1,0},{2,3},{3,2},{4,5},{5,4},{6,7},{7,6},{8,9},{9,8},{10,11... | collective-permute-start | bytes 3145736 | tf_op jit(solution)/shard_map/ppermute | solution.py:1459
  349.4 4.0 collective-permute-start.42
  376.1 25.5 %collective-permute-start.37 = (bf16[8,128,512]{2,1,0:T(8,128)(2,1)}, bf16[8,128,512]{2,1,0:T(8,128)(2,1)}, u32[]{:S(2)}, u32[]{:S(2)}) collective-permute-start(bf16[8,128,512]{2,1,0:T(8,128)(2,1)} %get-tuple-element.193), channel_id=1, source_target_pairs={{0,1},{1,0},{2,3},{3,2},{4,5},{5,4},{6,7},{7,6},{8,9},{9,8},{10,11... | collective-permute-start | bytes 3145736 | tf_op jit(solution)/shard_map/ppermute | solution.py:1459
  377.1 28.9 %collective-permute-start.38 = (bf16[256,512]{1,0:T(8,128)(2,1)}, bf16[256,512]{1,0:T(8,128)(2,1)}, u32[]{:S(2)}, u32[]{:S(2)}) collective-permute-start(bf16[256,512]{1,0:T(8,128)(2,1)} %bitcast.55), channel_id=1, source_target_pairs={{0,2},{2,0},{4,6},{6,4},{1,3},{3,1},{5,7},{7,5},{8,10},{10,8},{12,... | collective-permute-start | bytes 786440 | tf_op jit(solution)/shard_map/ppermute | solution.py:1472
  379.1 26.9 %collective-permute-start.39 = (bf16[256,512]{1,0:T(8,128)(2,1)}, bf16[256,512]{1,0:T(8,128)(2,1)}, u32[]{:S(2)}, u32[]{:S(2)}) collective-permute-start(bf16[256,512]{1,0:T(8,128)(2,1)} %bitcast.56), channel_id=1, source_target_pairs={{0,4},{2,6},{4,0},{6,2},{1,5},{3,7},{5,1},{7,3},{8,12},{10,14},{12... | collective-permute-start | bytes 786440 | tf_op jit(solution)/shard_map/ppermute | solution.py:1472
  381.5 24.6 %collective-permute-start.40 = (bf16[256,512]{1,0:T(8,128)(2,1)}, bf16[256,512]{1,0:T(8,128)(2,1)}, u32[]{:S(2)}, u32[]{:S(2)}) collective-permute-start(bf16[256,512]{1,0:T(8,128)(2,1)} %bitcast.57), channel_id=1, source_target_pairs={{0,6},{2,4},{4,2},{6,0},{1,7},{3,5},{5,3},{7,1},{8,14},{10,12},{12... | collective-permute-start | bytes 786440 | tf_op jit(solution)/shard_map/ppermute | solution.py:1472
  381.6 15.9 %collective-permute-start.41 = (bf16[704,512]{1,0:T(8,128)(2,1)S(1)}, bf16[704,512]{1,0:T(8,128)(2,1)S(1)}, u32[]{:S(2)}, u32[]{:S(2)}) collective-permute-start(bf16[704,512]{1,0:T(8,128)(2,1)S(1)} %pad_maximum_fusion.2), channel_id=1, source_target_pairs={{0,16},{16,0},{1,17},{17,1},{2,18},{18,2},{3,19},{19,3},{4,20},{20... | collective-permute-start | bytes 2162696 | tf_op jit(solution)/shard_map/ppermute | solution.py:1145
  406.2 21.7 %collective-permute-start.49 = (f32[288,1024]{1,0:T(8,128)S(1)}, f32[288,1024]{1,0:T(8,128)S(1)}, u32[]{:S(2)}, u32[]{:S(2)}) collective-permute-start(f32[288,1024]{1,0:T(8,128)S(1)} %split.48), channel_id=1, source_target_pairs={{0,8},{8,0},{1,9},{9,1},{2,10},{10,2},{3,11},{11,3},{4,12},{12,4},... | collective-permute-start | bytes 3538952 | tf_op jit(solution)/shard_map/ppermute | solution.py:1145
  408.6 8.2 %collective-permute-start.45 = (bf16[72,2,512]{2,1,0:T(2,128)(2,1)S(1)}, bf16[72,2,512]{2,1,0:T(2,128)(2,1)S(1)}, u32[]{:S(2)}, u32[]{:S(2)}) collective-permute-start(bf16[72,2,512]{2,1,0:T(2,128)(2,1)S(1)} %fusion.15), channel_id=1, source_target_pairs={{0,8},{8,0},{1,9},{9,1},{2,10},{10,2},{3,11},{11,3},{4,12},{12,4},... | collective-permute-start | bytes 442376 | tf_op jit(solution)/shard_map/ppermute | solution.py:1145
  411.9 24.1 %collective-permute-start.51 = (bf16[72,128]{1,0:T(8,128)(2,1)}, bf16[72,128]{1,0:T(8,128)(2,1)}, u32[]{:S(2)}, u32[]{:S(2)}) collective-permute-start(bf16[72,128]{1,0:T(8,128)(2,1)} %fusion.17), channel_id=1, source_target_pairs={{0,8},{8,0},{1,9},{9,1},{2,10},{10,2},{3,11},{11,3},{4,12},{12,4},... | collective-permute-start | bytes 55304 | tf_op jit(solution)/shard_map/ppermute | solution.py:1145
  412.3 13.6 %collective-permute-start.43 = (bf16[256,512]{1,0:T(8,128)(2,1)S(1)}, bf16[256,512]{1,0:T(8,128)(2,1)S(1)}, u32[]{:S(2)}, u32[]{:S(2)}) collective-permute-start(bf16[256,512]{1,0:T(8,128)(2,1)S(1)} %bitcast.269), channel_id=1, source_target_pairs={{0,2},{2,0},{4,6},{6,4},{1,3},{3,1},{5,7},{7,5},{8,10},{10,8},{12,... | collective-permute-start | bytes 786440 | tf_op jit(solution)/shard_map/ppermute | solution.py:1472
  413.0 27.8 %collective-permute-start.46 = (bf16[256,512]{1,0:T(8,128)(2,1)}, bf16[256,512]{1,0:T(8,128)(2,1)}, u32[]{:S(2)}, u32[]{:S(2)}) collective-permute-start(bf16[256,512]{1,0:T(8,128)(2,1)} %bitcast.62), channel_id=1, source_target_pairs={{0,4},{2,6},{4,0},{6,2},{1,5},{3,7},{5,1},{7,3},{8,12},{10,14},{12... | collective-permute-start | bytes 786440 | tf_op jit(solution)/shard_map/ppermute | solution.py:1472
  416.8 1.5 collective-permute-start.44
  418.3 26.4 %collective-permute-start.48 = (f32[288,1024]{1,0:T(8,128)}, f32[288,1024]{1,0:T(8,128)}, u32[]{:S(2)}, u32[]{:S(2)}) collective-permute-start(f32[288,1024]{1,0:T(8,128)} %get-tuple-element.285), channel_id=1, source_target_pairs={{0,8},{8,0},{1,9},{9,1},{2,10},{10,2},{3,11},{11,3},{4,12},{12,4},... | collective-permute-start | bytes 3538952 | tf_op jit(solution)/shard_map/ppermute | solution.py:1145
  425.9 18.8 %collective-permute-start.47 = (bf16[256,512]{1,0:T(8,128)(2,1)}, bf16[256,512]{1,0:T(8,128)(2,1)}, u32[]{:S(2)}, u32[]{:S(2)}) collective-permute-start(bf16[256,512]{1,0:T(8,128)(2,1)} %bitcast.63), channel_id=1, source_target_pairs={{0,6},{2,4},{4,2},{6,0},{1,7},{3,5},{5,3},{7,1},{8,14},{10,12},{12... | collective-permute-start | bytes 786440 | tf_op jit(solution)/shard_map/ppermute | solution.py:1472
  428.8 15.8 %collective-permute-start.50 = (bf16[288,1024]{1,0:T(8,128)(2,1)}, bf16[288,1024]{1,0:T(8,128)(2,1)}, u32[]{:S(2)}, u32[]{:S(2)}) collective-permute-start(bf16[288,1024]{1,0:T(8,128)(2,1)} %add_convert_fusion), channel_id=1, source_target_pairs={{0,16},{16,0},{1,17},{17,1},{2,18},{18,2},{3,19},{19,3},{4,20},{20... | collective-permute-start | bytes 1769480 | tf_op jit(solution)/shard_map/ppermute | solution.py:1145
  431.3 23.0 %all-to-all-start.6 = ((bf16[8,96,128]{2,1,0:T(8,128)(2,1)}), bf16[8,96,128]{2,1,0:T(8,128)(2,1)S(1)}, u32[]{:S(2)}, u32[]{:S(2)}) async-start(bf16[8,96,128]{2,1,0:T(8,128)(2,1)} %fusion.14), calls=%async_computation.7 | async-start | bytes 393216 | tf_op jit(solution)/shard_map/all_to_all | solution.py:1436
  436.0 15.7 %collective-permute-start.52 = (bf16[384,128]{1,0:T(8,128)(2,1)S(1)}, bf16[384,128]{1,0:T(8,128)(2,1)S(1)}, u32[]{:S(2)}, u32[]{:S(2)}) collective-permute-start(bf16[384,128]{1,0:T(8,128)(2,1)S(1)} %bitcast.278), channel_id=1, source_target_pairs={{0,0},{1,1},{2,8},{3,9},{4,16},{5,17},{6,24},{7,25},{8,2},{9,3},{1... | collective-permute-start | bytes 294920 | tf_op jit(solution)/shard_map/ppermute | solution.py:1443
  440.8 13.5 %collective-permute-start.53 = (bf16[384,128]{1,0:T(8,128)(2,1)S(1)}, bf16[384,128]{1,0:T(8,128)(2,1)S(1)}, u32[]{:S(2)}, u32[]{:S(2)}) collective-permute-start(bf16[384,128]{1,0:T(8,128)(2,1)S(1)} %bitcast.277), channel_id=1, source_target_pairs={{0,1},{1,0},{2,9},{3,8},{4,17},{5,16},{6,25},{7,24},{8,3},{9,2},{1... | collective-permute-start | bytes 294920 | tf_op jit(solution)/shard_map/ppermute | solution.py:1443
  (53 other events, 425.3 us)
Sparse Core Ops, SparseCore 0:
  10.2 83.0 all-gather.5
  95.4 72.7 all-gather.3
  264.0 98.6 reduce-scatter.1

commit v5 on v4

--- a/solution.py
+++ b/solution.py
@@ -298,9 +298,22 @@
 ):
     steps = pl.num_programs(0)
     step = steps - 1 - pl.program_id(0)
-    grads_ref, first_grad_ref, col_grad_ref, state = rest
+    grads_ref, first_grad_ref, col_grad_ref, state, buffer, sems = rest
+    turn = pl.program_id(0)
+    slot = turn % 2
     width = heads * HEAD
     n = heads * SPAN
+
+    def first_copy(where, b, stored):
+        return pltpu.make_async_copy(buffer.at[where, b], first_grad_ref.at[stored], sems.at[where, b])
+
+    def first_done(where):
+        for b in range(2):
+            first_copy(where, b, 0).wait()
+
+    @pl.when(turn >= 2)
+    def _():
+        first_done(slot)
 
     @pl.when(pl.program_id(0) == 0)
     def _():
@@ -453,13 +466,24 @@
         add(3, g_scaled * key_pre)
         mix = jax.nn.sigmoid(c10 + value_up)
         g_value = g_v * (1.0 - mix)
-        first_grad_ref[rows] = (g_v * mix).astype(first_grad_ref.dtype)
+        inside = c * SPAN % BLOCK
+        buffer[slot, c * SPAN // BLOCK, inside : inside + SPAN] = (g_v * mix).astype(LOW)
         g_vup = g_v * (first - value_pre) * mix * (1.0 - mix)
         add(2, g_vup)
         for i, x in enumerate((g_r, g_key, g_value, g_decay, g_rate, g_vup)):
             grads_ref[i, rows] = x.astype(LOW)
         grads_ref[6, rows] = grad_gate
     col_grad_ref[...] += jnp.concatenate(sums, 0)
+    for b in range(2):
+        first_copy(slot, b, home_ref[2 * step + b]).start()
+
+    @pl.when(step == 0)
+    def _():
+        first_done(slot)
+
+        @pl.when(turn > 0)
+        def _():
+            first_done(1 - slot)
 
 
 def scan_backward(parts, values, joined, scanned, gate, grad, pre, first, cols, states, mats, home, begins, p):
@@ -498,14 +522,18 @@
             ],
             out_specs=[
                 pl.BlockSpec((7, rows, width), lambda i, *_: (0, steps - 1 - i, 0)),
-                row_spec,
+                pl.BlockSpec(memory_space=pl.ANY),
                 pl.BlockSpec((8, width), lambda i, *_: (0, 0)),
             ],
-            scratch_shapes=[pltpu.VMEM((width, width), F32)],
+            scratch_shapes=[
+                pltpu.VMEM((width, width), F32),
+                pltpu.VMEM((2, 2, BLOCK, width), LOW),
+                pltpu.SemaphoreType.DMA((2, 2)),
+            ],
         ),
         out_shape=[
             jax.ShapeDtypeStruct((7, total, width), LOW),
-            jax.ShapeDtypeStruct((total, width), LOW),
+            jax.ShapeDtypeStruct((total // BLOCK, BLOCK, width), LOW),
             jax.ShapeDtypeStruct((8, width), F32),
         ],
         compiler_params=pltpu.CompilerParams(vmem_limit_bytes=60 * 1024 * 1024),
@@ -1381,7 +1409,6 @@
         parts, values, joined, scanned, gate, grad_heads.reshape(blocks, BLOCK, width), pre, first_group,
         own, states, mats, home, begins, PASSES,
     )
-    first_grad = taken_blocks(first_grad.reshape(blocks, BLOCK, width), order)
     first_came = lax.all_to_all(
         first_grad.reshape(heads_axis, rows_here, width), HEAD_AXES, split_axis=0, concat_axis=0, tiled=True
     )

time: 483 us -> 482 us (level)
  local copies, waits for them, and re-layouts: 74.5 us -> 68.2 us
  waiting for transfers between devices: 84 us -> 89.8 us
    unnamed x129 -> x128, local copies, waits for them, and re-layouts: 23.9 us -> 21.4 us
    gather x12 -> x11, local copies, waits for them, and re-layouts: 16.9 us -> 14.4 us  [taken_blocks(): return x.at[table].get(mode='promise_in_bounds')]
  transfers between devices with their start and end apart: 64 -> 64, of which waited for: 21 -> 22; matrix products, arithmetic and copies ran while one was open for 17% -> 17% of each run, Pallas kernels for 36% -> 36%
where the time goes in v5:
time: 482 us; the launch traced here: 476 us
  Pallas kernels  179 us (37%)
  waiting for transfers between devices  89.8 us (19%)
  starting transfers between devices  86.3 us (18%)
  local copies, waits for them, and re-layouts  68.2 us (14%)
  other arithmetic  31.3 us (6%)
  between operations  15.2 us (3%)
  matrix products  5.72 us (1%)
    pallas_call x1, Pallas kernels, scan_backward(): pl.pallas_call(functools.partial(scan_backward_kernel, heads, p), grid_sp...  50.8 us
    pallas_call x2, Pallas kernels, project_back(): pl.pallas_call(functools.partial(project_back_kernel, part, parts), grid_...  38.1 us
    pallas_call x1, Pallas kernels, scan_forward(): pl.pallas_call(functools.partial(scan_forward_kernel, heads, p), grid_spe...  36.3 us
    ppermute x24, waiting for transfers between devices, swap(): return lax.ppermute(x, axis, [(0, 1), (1, 0)])  28.9 us
    ppermute x17, starting transfers between devices, steps_along(): lax.ppermute(x, axis, [(i, i ^ k) for i in range(size)])  22 us
    unnamed x128, local copies, waits for them, and re-layouts  21.4 us
    ppermute x17, waiting for transfers between devices, steps_along(): lax.ppermute(x, axis, [(i, i ^ k) for i in range(size)])  21.3 us
    pallas_call x1, Pallas kernels, project(): pl.pallas_call(project_kernel, grid_spec=pltpu.PrefetchScalarGridSpec(num...  17.6 us
  transfers between devices with their start and end apart: 64, of which 22 were waited for; matrix products, arithmetic and copies ran while one was open for 17% of the time, Pallas kernels for 36%

profile of v5, /device:TPU:4, one launch (start us, length us, event | category | flops | bytes accessed | tf_op | source)
XLA Modules:
  0.0 475.7 jit_solution(16213252202543999288)
XLA Ops:
  11.1 3.7 collective-permute-start.4
  15.6 3.6 collective-permute-start.13
  21.2 5.2 %all-to-all-start = ((bf16[8,96,128]{2,1,0:T(8,128)(2,1)}), bf16[8,96,128]{2,1,0:T(8,128)(2,1)S(1)}, u32[]{:S(2)}, u32[]{:S(2)}) async-start(bf16[8,96,128]{2,1,0:T(8,128)(2,1)} %copy.102), calls=%async_computation | async-start | bytes 393216 | tf_op jit(solution)/shard_map/all_to_all | solution.py:1259
  28.9 2.0 collective-permute-start.11
  35.0 1.9 collective-permute-done.5
  37.7 1.8 collective-permute-start.6
  39.5 4.4 all-to-all-start.1
  45.4 1.8 collective-permute-start.14
  47.2 5.6 %collective-permute-done.6 = bf16[8,32,640]{2,1,0:T(8,128)(2,1)S(1)} collective-permute-done((bf16[8,32,640]{2,1,0:T(8,128)(2,1)}, bf16[8,32,640]{2,1,0:T(8,128)(2,1)S(1)}, u32[]{:S(2)}, u32[]{:S(2)}) %collective-permute-start.6) | collective-permute-done | bytes 327712 | tf_op jit(solution)/shard_map/ppermute | solution.py:1145
  53.7 5.5 %collective-permute-done = bf16[1,256,384]{2,1,0:T(8,128)(2,1)S(1)} collective-permute-done((bf16[1,256,384]{2,1,0:T(8,128)(2,1)S(1)}, bf16[1,256,384]{2,1,0:T(8,128)(2,1)S(1)}, u32[]{:S(2)}, u32[]{:S(2)}) %collective-permute-start) | collective-permute-done | bytes 196640 | tf_op jit(solution)/shard_map/ppermute | solution.py:1145
  64.2 2.0 constant_dynamic-update-slice_fusion.11
  66.2 3.1 gather_fusion.1
  71.4 1.6 constant_dynamic-slice_fusion.7.refs_8_.refs_16_
  73.1 2.3 copy.115
  75.4 2.4 collective-permute-start.19
  77.9 1.9 collective-permute-start.17
  82.0 4.9 %all-to-all-start.2 = ((bf16[8,256,128]{2,1,0:T(8,128)(2,1)}), bf16[8,256,128]{2,1,0:T(8,128)(2,1)}, u32[]{:S(2)}, u32[]{:S(2)}) async-start(bf16[8,256,128]{2,1,0:T(8,128)(2,1)} %bitcast_bitcast_fusion), calls=%async_computation.2 | async-start | bytes 1048576 | tf_op jit(solution)/shard_map/all_to_all | solution.py:1292
  87.8 6.0 %collective-permute-done.15 = bf16[8,32,1024]{2,1,0:T(8,128)(2,1)} collective-permute-done((bf16[8,32,1024]{2,1,0:T(8,128)(2,1)S(1)}, bf16[8,32,1024]{2,1,0:T(8,128)(2,1)}, u32[]{:S(2)}, u32[]{:S(2)}) %collective-permute-start.15) | collective-permute-done | bytes 524320 | tf_op jit(solution)/shard_map/ppermute | solution.py:1145
  95.0 17.6 %shard_map.238 = (bf16[16,32,1024]{2,1,0:T(8,128)(2,1)}, f32[2048,2]{1,0:T(8,128)}, bf16[5,2048,128]{2,1,0:T(8,128)(2,1)}, f32[2048,128]{1,0:T(8,128)}, f32[5,20...) custom-call(s32[16]{0:T(128)} %bitcast.224, ...), custom_call_target="tpu_custom_call" | custom-call | bytes 60000 | tf_op jit(solution)/shard_map/pallas_call | solution.py:665
  114.5 2.2 collective-permute-done.20
  117.4 36.3 %shard_map.239 = (bf16[2048,128]{1,0:T(8,128)(2,1)}, bf16[2048,128]{1,0:T(8,128)(2,1)}, bf16[2048,128]{1,0:T(8,128)(2,1)}, f32[2048,128]{1,0:T(8,128)}, f32[32,1...) custom-call(s32[16]{0:T(128)} %bitcast.225, s32[4]{0:T(128)} %bitcast_subtract_fusion.begins_ref, ...), custom_call_target="tpu_custom_call" | custom-call | bytes 240000 | tf_op jit(solution)/shard_map/pallas_call | solution.py:260
  153.7 2.5 gather_fusion.2
  158.2 2.1 maximum_maximum_fusion
  161.2 4.8 %all-to-all-start.3 = ((bf16[8,2,144,128]{3,2,1,0:T(8,128)(2,1)}), bf16[8,2,144,128]{3,2,1,0:T(8,128)(2,1)S(1)}, u32[]{:S(2)}, u32[]{:S(2)}) async-start(bf16[8,2,144,128]{3,2,1,0:T(8,128)(2,1)} %bitcast.245), calls=%async_computation.3 | async-start | bytes 1179648 | tf_op jit(solution)/shard_map/all_to_all | solution.py:1328
  166.8 1.8 gather_fusion.7
  168.6 1.8 gather_fusion.6
  171.5 10.2 %all-to-all-done.3.out_ref = bf16[8,2,144,128]{3,2,1,0:T(8,128)(2,1)S(1)} async-done(((bf16[8,2,144,128]{3,2,1,0:T(8,128)(2,1)}), bf16[8,2,144,128]{3,2,1,0:T(8,128)(2,1)S(1)}, u32[]{:S(2)}, u32[]{:S(2)}) %all-to-all-start.3) | async-done | bytes 589856 | tf_op jit(solution)/shard_map/all_to_all | solution.py:1328
  183.0 3.1 shard_map.240
  192.6 7.8 %shard_map.241 = (bf16[576,1024]{1,0:T(8,128)(2,1)S(1)}, bf16[576,1024]{1,0:T(8,128)(2,1)S(1)}, f32[288,1024]{1,0:T(8,128)S(1)}, f32[288,1024]{1,0:T(8,128)}) custom-call(bf16[288,1024]{1,0:T(8,128)(2,1)S(1)} %copy-done.7, bf16[288,1024]{1,0:T(8,128)(2,1)S(1)} %collective-permute-done.22.xb_ref.refs_5_, bf16[256,1024]{1,0:T(8,128)(2,1)S(1)} %copy-done.2, ...), custom_call_target="tpu_custom_call" | custom-call | bytes 24000 | tf_op jit(solution)/shard_map/pallas_call | solution.py:994
  201.5 2.4 collective-permute-done.21.xa_ref.refs_6_
  204.4 4.0 collective-permute-done.26.ea_ref
  209.7 7.7 %shard_map.242 = (bf16[576,1024]{1,0:T(8,128)(2,1)S(1)}, bf16[576,1024]{1,0:T(8,128)(2,1)S(1)}, f32[288,1024]{1,0:T(8,128)S(1)}, f32[288,1024]{1,0:T(8,128)}) custom-call(bf16[288,1024]{1,0:T(8,128)(2,1)S(1)} %collective-permute-done.21.xa_ref.refs_6_, bf16[288,1024]{1,0:T(8,128)(2,1)S(1)} %collective-permute-done.25.xb_ref.refs_7_, ...), custom_call_target="tpu_custom_call" | custom-call | bytes 24000 | tf_op jit(solution)/shard_map/pallas_call | solution.py:994
  217.9 2.7 collective-permute-done.28
  223.0 8.8 %shard_map.243.refs_8_ = bf16[1024,2304]{1,0:T(8,128)(2,1)} custom-call(bf16[256,1024]{1,0:T(8,128)(2,1)S(1)} %copy-done.2, bf16[256,1024]{1,0:T(8,128)(2,1)S(1)} %copy-done.12, bf16[256,1024]{1,0:T(8,128)(2,1)S(1)} %copy-done.10, bf16[256,1024]{1,0:T(8,128)(2,1)S(1)} %copy-done.14, bf16[288,1024]{1,0:T(8,128)(2,1)S(1)} %copy-done.8, ...), custom_call_target="tpu_custom_call" | custom-call | bytes 27000 | tf_op jit(solution)/shard_map/pallas_call | solution.py:1032
  231.8 5.4 %collective-permute-done.29.far_ref = bf16[288,1024]{1,0:T(8,128)(2,1)S(1)} collective-permute-done((bf16[288,1024]{1,0:T(8,128)(2,1)S(1)}, bf16[288,1024]{1,0:T(8,128)(2,1)S(1)}, u32[]{:S(2)}, u32[]{:S(2)}) %collective-permute-start.29) | collective-permute-done | bytes 589856 | tf_op jit(solution)/shard_map/ppermute | solution.py:1173
  237.1 4.7 shard_map.244
  244.1 4.1 all-to-all-start.4
  252.5 4.0 collective-permute-done.35.refs_7_
  256.5 3.4 collective-permute-done.34.refs_6_
  259.9 4.3 shard_map.245
  267.3 50.8 %shard_map.246 = (bf16[7,2048,128]{2,1,0:T(8,128)(2,1)}, bf16[16,128,128]{2,1,0:T(8,128)(2,1)}, f32[8,128]{1,0:T(8,128)}) custom-call(s32[16]{0:T(128)} %bitcast.226, s32[4]{0:T(128)} %bitcast_subtract_fusion.begins_ref, bf16[5,2048,128]{2,1,0:T(8,128)(2,1)} %get-tuple-element.133.parts_ref, bf16[2048,128]{1,0:T(8,128)(2,1)} %get-tuple-element.145.values_ref, ...), custom_call_target="tpu_custom_call" | custom-call | bytes 180000 | tf_op jit(solution)/shard_map/pallas_call | solution.py:503
  318.1 6.1 %all-to-all-start.5 = ((bf16[8,256,128]{2,1,0:T(8,128)(2,1)}), bf16[8,256,128]{2,1,0:T(8,128)(2,1)}, u32[]{:S(2)}, u32[]{:S(2)}) async-start(bf16[8,256,128]{2,1,0:T(8,128)(2,1)} %bitcast.260), calls=%async_computation.5 | async-start | bytes 1048576 | tf_op jit(solution)/shard_map/all_to_all | solution.py:1412
  324.2 19.4 %shard_map.247 = (bf16[8,128,512]{2,1,0:T(8,128)(2,1)}, bf16[8,128,512]{2,1,0:T(8,128)(2,1)}, bf16[704,512]{1,0:T(8,128)(2,1)}, f32[288,128]{1,0:T(8,128)}) custom-call(s32[16]{0:T(128)} %bitcast.227, s32[16]{0:T(128)} %and_select_fusion.3.turn_ref, s32[16]{0:T(128)} %get-tuple-element.282.row_ref, s32[4]{0:T(128)} %bitcast_subtract_fusion.begins_ref, ...), custom_call_target="tpu_custom_call" | custom-call | bytes 51000000 | tf_op jit(solution)/shard_map/pallas_call | solution.py:836
  343.7 2.1 collective-permute-start.36
  348.1 1.8 slice_bitcast_fusion
  352.3 18.6 %shard_map.248 = (bf16[8,128,512]{2,1,0:T(8,128)(2,1)}, bf16[8,128,512]{2,1,0:T(8,128)(2,1)}, bf16[704,512]{1,0:T(8,128)(2,1)}) custom-call(s32[16]{0:T(128)} %bitcast.228, s32[16]{0:T(128)} %and_select_fusion.3.turn_ref, s32[16]{0:T(128)} %get-tuple-element.282.row_ref, s32[4]{0:T(128)} %bitcast_subtract_fusion.begins_ref, s32[1]{0:T(128)} %bitcast.40.head_ref, ...), custom_call_target="tpu_custom_call" | custom-call | bytes 51000000 | tf_op jit(solution)/shard_map/pallas_call | solution.py:836
  370.9 3.9 collective-permute-done.36
  374.9 1.6 convert_add_fusion.1
  381.1 2.4 collective-permute-start.39
  384.5 2.8 fusion.81
  387.3 2.9 fusion.82
  390.2 10.4 %collective-permute-done.41 = bf16[704,512]{1,0:T(8,128)(2,1)S(1)} collective-permute-done((bf16[704,512]{1,0:T(8,128)(2,1)S(1)}, bf16[704,512]{1,0:T(8,128)(2,1)S(1)}, u32[]{:S(2)}, u32[]{:S(2)}) %collective-permute-start.41) | collective-permute-done | bytes 720928 | tf_op jit(solution)/shard_map/ppermute | solution.py:1173
  401.8 1.7 reshape.874
  404.7 2.0 convert_add_fusion
  412.0 1.6 fusion.73
  415.9 3.3 collective-permute-start.46
  421.3 7.6 %collective-permute-done.43 = bf16[256,512]{1,0:T(8,128)(2,1)S(1)} collective-permute-done((bf16[256,512]{1,0:T(8,128)(2,1)S(1)}, bf16[256,512]{1,0:T(8,128)(2,1)S(1)}, u32[]{:S(2)}, u32[]{:S(2)}) %collective-permute-start.43) | collective-permute-done | bytes 262176 | tf_op jit(solution)/shard_map/ppermute | solution.py:1499
  428.9 1.7 collective-permute-start.47
  433.2 4.5 all-to-all-start.6
  438.1 5.7 %collective-permute-start.52 = (bf16[384,128]{1,0:T(8,128)(2,1)S(1)}, bf16[384,128]{1,0:T(8,128)(2,1)S(1)}, u32[]{:S(2)}, u32[]{:S(2)}) collective-permute-start(bf16[384,128]{1,0:T(8,128)(2,1)S(1)} %bitcast.279), channel_id=1, source_target_pairs={{0,0},{1,1},{2,8},{3,9},{4,16},{5,17},{6,24},{7,25},{8,2},{9,3},{1... | collective-permute-start | bytes 294920 | tf_op jit(solution)/shard_map/ppermute | solution.py:1470
  446.7 6.9 %collective-permute-done.52 = bf16[384,128]{1,0:T(8,128)(2,1)S(1)} collective-permute-done((bf16[384,128]{1,0:T(8,128)(2,1)S(1)}, bf16[384,128]{1,0:T(8,128)(2,1)S(1)}, u32[]{:S(2)}, u32[]{:S(2)}) %collective-permute-start.52) | collective-permute-done | bytes 98336 | tf_op jit(solution)/shard_map/ppermute | solution.py:1470
  453.6 2.7 collective-permute-done.53
  462.3 2.1 copy_bitcast_fusion
  466.4 2.6 fusion.10
  (361 shorter events, 93.7 us)
Async XLA Ops:
  7.2 87.8 %all-gather.6.cloned.1.call-start = ((), (), s32[]{:S(2)}) async-start(), calls=%async_computation.10 | async-start | bytes 4718592 | tf_op jit(solution)/shard_map/all_gather | solution.py:1140
  11.1 17.8 %collective-permute-start.4 = (bf16[1,32,640]{2,1,0:T(8,128)(2,1)S(1)}, bf16[1,32,640]{2,1,0:T(8,128)(2,1)S(1)}, u32[]{:S(2)}, u32[]{:S(2)}) collective-permute-start(bf16[1,32,640]{2,1,0:T(8,128)(2,1)S(1)} %bitcast.262), channel_id=1, source_target_pairs={{0,6},{2,4},{4,2},{6,0},{1,7},{3,5},{5,3},{7,1},{8,14},{10,12},{12... | collective-permute-start | bytes 122888 | tf_op jit(solution)/shard_map/ppermute | solution.py:1145
  14.8 16.1 %collective-permute-start.3 = (bf16[1,32,640]{2,1,0:T(8,128)(2,1)S(1)}, bf16[1,32,640]{2,1,0:T(8,128)(2,1)S(1)}, u32[]{:S(2)}, u32[]{:S(2)}) collective-permute-start(bf16[1,32,640]{2,1,0:T(8,128)(2,1)S(1)} %bitcast.263), channel_id=1, source_target_pairs={{0,4},{2,6},{4,0},{6,2},{1,5},{3,7},{5,1},{7,3},{8,12},{10,14},{12... | collective-permute-start | bytes 122888 | tf_op jit(solution)/shard_map/ppermute | solution.py:1145
  14.8 16.7 %collective-permute-start.2 = (bf16[1,32,640]{2,1,0:T(8,128)(2,1)S(1)}, bf16[1,32,640]{2,1,0:T(8,128)(2,1)S(1)}, u32[]{:S(2)}, u32[]{:S(2)}) collective-permute-start(bf16[1,32,640]{2,1,0:T(8,128)(2,1)S(1)} %bitcast.264), channel_id=1, source_target_pairs={{0,2},{2,0},{4,6},{6,4},{1,3},{3,1},{5,7},{7,5},{8,10},{10,8},{12,... | collective-permute-start | bytes 122888 | tf_op jit(solution)/shard_map/ppermute | solution.py:1145
  15.6 28.4 %collective-permute-start.13 = (bf16[1,32,1024]{2,1,0:T(8,128)(2,1)}, bf16[1,32,1024]{2,1,0:T(8,128)(2,1)S(1)}, u32[]{:S(2)}, u32[]{:S(2)}) collective-permute-start(bf16[1,32,1024]{2,1,0:T(8,128)(2,1)} %bitcast.271), channel_id=1, source_target_pairs={{0,6},{2,4},{4,2},{6,0},{1,7},{3,5},{5,3},{7,1},{8,14},{10,12},{12... | collective-permute-start | bytes 196616 | tf_op jit(solution)/shard_map/ppermute | solution.py:1145
  19.2 25.0 %collective-permute-start.12 = (bf16[1,32,1024]{2,1,0:T(8,128)(2,1)}, bf16[1,32,1024]{2,1,0:T(8,128)(2,1)S(1)}, u32[]{:S(2)}, u32[]{:S(2)}) collective-permute-start(bf16[1,32,1024]{2,1,0:T(8,128)(2,1)} %bitcast.272), channel_id=1, source_target_pairs={{0,4},{2,6},{4,0},{6,2},{1,5},{3,7},{5,1},{7,3},{8,12},{10,14},{12... | collective-permute-start | bytes 196616 | tf_op jit(solution)/shard_map/ppermute | solution.py:1145
  21.2 18.2 %all-to-all-start = ((bf16[8,96,128]{2,1,0:T(8,128)(2,1)}), bf16[8,96,128]{2,1,0:T(8,128)(2,1)S(1)}, u32[]{:S(2)}, u32[]{:S(2)}) async-start(bf16[8,96,128]{2,1,0:T(8,128)(2,1)} %copy.102), calls=%async_computation | async-start | bytes 393216 | tf_op jit(solution)/shard_map/all_to_all | solution.py:1259
  28.9 15.7 %collective-permute-start.11 = (bf16[1,32,1024]{2,1,0:T(8,128)(2,1)S(1)}, bf16[1,32,1024]{2,1,0:T(8,128)(2,1)}, u32[]{:S(2)}, u32[]{:S(2)}) collective-permute-start(bf16[1,32,1024]{2,1,0:T(8,128)(2,1)S(1)} %bitcast.273), channel_id=1, source_target_pairs={{0,2},{2,0},{4,6},{6,4},{1,3},{3,1},{5,7},{7,5},{8,10},{10,8},{12,... | collective-permute-start | bytes 196616 | tf_op jit(solution)/shard_map/ppermute | solution.py:1145
  30.9 30.1 %collective-permute-start.9 = (bf16[256,1024]{1,0:T(8,128)(2,1)S(1)}, bf16[256,1024]{1,0:T(8,128)(2,1)S(1)}, u32[]{:S(2)}, u32[]{:S(2)}) collective-permute-start(bf16[256,1024]{1,0:T(8,128)(2,1)S(1)} %copy-done.2), channel_id=1, source_target_pairs={{0,16},{16,0},{1,17},{17,1},{2,18},{18,2},{3,19},{19,3},{4,20},{20... | collective-permute-start | bytes 1572872 | tf_op jit(solution)/shard_map/ppermute | solution.py:1173
  31.5 5.4 %collective-permute-start.5 = (bf16[4,32,640]{2,1,0:T(8,128)(2,1)S(1)}, bf16[4,32,640]{2,1,0:T(8,128)(2,1)S(1)}, u32[]{:S(2)}, u32[]{:S(2)}) collective-permute-start(bf16[4,32,640]{2,1,0:T(8,128)(2,1)S(1)} %pad_maximum_fusion.8), channel_id=1, source_target_pairs={{0,1},{1,0},{2,3},{3,2},{4,5},{5,4},{6,7},{7,6},{8,9},{9,8},{10,11... | collective-permute-start | bytes 491528 | tf_op jit(solution)/shard_map/ppermute | solution.py:1145
  37.7 15.1 %collective-permute-start.6 = (bf16[8,32,640]{2,1,0:T(8,128)(2,1)}, bf16[8,32,640]{2,1,0:T(8,128)(2,1)S(1)}, u32[]{:S(2)}, u32[]{:S(2)}) collective-permute-start(bf16[8,32,640]{2,1,0:T(8,128)(2,1)} %get-tuple-element.321), channel_id=1, source_target_pairs={{0,16},{16,0},{1,17},{17,1},{2,18},{18,2},{3,19},{19,3},{4,20},{20... | collective-permute-start | bytes 983048 | tf_op jit(solution)/shard_map/ppermute | solution.py:1145
  39.5 33.5 %all-to-all-start.1 = ((bf16[4,2,32,1024]{3,2,1,0:T(8,128)(2,1)}), bf16[4,2,32,1024]{3,2,1,0:T(8,128)(2,1)}, u32[]{:S(2)}, u32[]{:S(2)}) async-start(bf16[4,2,32,1024]{3,2,1,0:T(8,128)(2,1)} %copy.106), calls=%async_computation.1 | async-start | bytes 1048576 | tf_op jit(solution)/shard_map/all_to_all | solution.py:1251
  43.9 144.1 %all-gather.4.cloned.1.call-start = ((), (), s32[]{:S(2)}) async-start(), calls=%async_computation.8 | async-start | bytes 4718592 | tf_op jit(solution)/shard_map/all_gather | solution.py:1140
  44.0 29.1 %collective-permute-start.8 = (bf16[256,1024]{1,0:T(8,128)(2,1)S(1)}, bf16[256,1024]{1,0:T(8,128)(2,1)S(1)}, u32[]{:S(2)}, u32[]{:S(2)}) collective-permute-start(bf16[256,1024]{1,0:T(8,128)(2,1)S(1)} %copy-done.2), channel_id=1, source_target_pairs={{0,8},{8,0},{1,9},{9,1},{2,10},{10,2},{3,11},{11,3},{4,12},{12,4},... | collective-permute-start | bytes 1572872 | tf_op jit(solution)/shard_map/ppermute | solution.py:1173
  44.2 15.0 %collective-permute-start = (bf16[1,256,384]{2,1,0:T(8,128)(2,1)S(1)}, bf16[1,256,384]{2,1,0:T(8,128)(2,1)S(1)}, u32[]{:S(2)}, u32[]{:S(2)}) collective-permute-start(bf16[1,256,384]{2,1,0:T(8,128)(2,1)S(1)} %reshape.856), channel_id=1, source_target_pairs={{0,16},{16,0},{1,17},{17,1},{2,18},{18,2},{3,19},{19,3},{4,20},{20... | collective-permute-start | bytes 589832 | tf_op jit(solution)/shard_map/ppermute | solution.py:1145
  45.4 14.8 %collective-permute-start.14 = (bf16[4,32,1024]{2,1,0:T(8,128)(2,1)S(1)}, bf16[4,32,1024]{2,1,0:T(8,128)(2,1)S(1)}, u32[]{:S(2)}, u32[]{:S(2)}) collective-permute-start(bf16[4,32,1024]{2,1,0:T(8,128)(2,1)S(1)} %pad_maximum_fusion.5), channel_id=1, source_target_pairs={{0,1},{1,0},{2,3},{3,2},{4,5},{5,4},{6,7},{7,6},{8,9},{9,8},{10,11... | collective-permute-start | bytes 786440 | tf_op jit(solution)/shard_map/ppermute | solution.py:1145
  53.7 10.5 %collective-permute-start.7 = (bf16[16,32,640]{2,1,0:T(8,128)(2,1)}, bf16[16,32,640]{2,1,0:T(8,128)(2,1)}, u32[]{:S(2)}, u32[]{:S(2)}) collective-permute-start(bf16[16,32,640]{2,1,0:T(8,128)(2,1)} %get-tuple-element.312), channel_id=1, source_target_pairs={{0,8},{8,0},{1,9},{9,1},{2,10},{10,2},{3,11},{11,3},{4,12},{12,4},... | collective-permute-start | bytes 1966088 | tf_op jit(solution)/shard_map/ppermute | solution.py:1145
  59.3 2.3 collective-permute-start.1
  61.1 12.0 %collective-permute-start.10 = (bf16[256,1024]{1,0:T(8,128)(2,1)S(1)}, bf16[256,1024]{1,0:T(8,128)(2,1)S(1)}, u32[]{:S(2)}, u32[]{:S(2)}) collective-permute-start(bf16[256,1024]{1,0:T(8,128)(2,1)S(1)} %collective-permute-done.9.ga_ref.refs_2_), channel_id=1, source_target_pairs={{0,8},{8,0},{1,9},{9,1},{2,10},{10,2},{3,11},{11,3},{4,12},{12,4},... | collective-permute-start | bytes 1572872 | tf_op jit(solution)/shard_map/ppermute | solution.py:1173
  75.4 37.5 %collective-permute-start.19 = (bf16[1,2,1024]{2,1,0:T(2,128)(2,1)S(1)}, bf16[1,2,1024]{2,1,0:T(2,128)(2,1)S(1)}, u32[]{:S(2)}, u32[]{:S(2)}) collective-permute-start(bf16[1,2,1024]{2,1,0:T(2,128)(2,1)S(1)} %get-tuple-element.281), channel_id=1, source_target_pairs={{0,6},{2,4},{4,2},{6,0},{1,7},{3,5},{5,3},{7,1},{8,14},{10,12},{12... | collective-permute-start | bytes 12296 | tf_op jit(solution)/shard_map/ppermute | solution.py:1145
  77.8 35.0 %collective-permute-start.18 = (bf16[1,2,1024]{2,1,0:T(2,128)(2,1)S(1)}, bf16[1,2,1024]{2,1,0:T(2,128)(2,1)S(1)}, u32[]{:S(2)}, u32[]{:S(2)}) collective-permute-start(bf16[1,2,1024]{2,1,0:T(2,128)(2,1)S(1)} %get-tuple-element.281), channel_id=1, source_target_pairs={{0,4},{2,6},{4,0},{6,2},{1,5},{3,7},{5,1},{7,3},{8,12},{10,14},{12... | collective-permute-start | bytes 12296 | tf_op jit(solution)/shard_map/ppermute | solution.py:1145
  77.9 35.0 %collective-permute-start.17 = (bf16[1,2,1024]{2,1,0:T(2,128)(2,1)S(1)}, bf16[1,2,1024]{2,1,0:T(2,128)(2,1)S(1)}, u32[]{:S(2)}, u32[]{:S(2)}) collective-permute-start(bf16[1,2,1024]{2,1,0:T(2,128)(2,1)S(1)} %get-tuple-element.281), channel_id=1, source_target_pairs={{0,2},{2,0},{4,6},{6,4},{1,3},{3,1},{5,7},{7,5},{8,10},{10,8},{12,... | collective-permute-start | bytes 12296 | tf_op jit(solution)/shard_map/ppermute | solution.py:1145
  80.6 13.3 %collective-permute-start.15 = (bf16[8,32,1024]{2,1,0:T(8,128)(2,1)S(1)}, bf16[8,32,1024]{2,1,0:T(8,128)(2,1)}, u32[]{:S(2)}, u32[]{:S(2)}) collective-permute-start(bf16[8,32,1024]{2,1,0:T(8,128)(2,1)S(1)} %copy-done.41), channel_id=1, source_target_pairs={{0,16},{16,0},{1,17},{17,1},{2,18},{18,2},{3,19},{19,3},{4,20},{20... | collective-permute-start | bytes 1572872 | tf_op jit(solution)/shard_map/ppermute | solution.py:1145
  82.0 35.4 %all-to-all-start.2 = ((bf16[8,256,128]{2,1,0:T(8,128)(2,1)}), bf16[8,256,128]{2,1,0:T(8,128)(2,1)}, u32[]{:S(2)}, u32[]{:S(2)}) async-start(bf16[8,256,128]{2,1,0:T(8,128)(2,1)} %bitcast_bitcast_fusion), calls=%async_computation.2 | async-start | bytes 1048576 | tf_op jit(solution)/shard_map/all_to_all | solution.py:1292
  112.6 47.6 %collective-permute-start.16 = (bf16[16,32,1024]{2,1,0:T(8,128)(2,1)S(1)}, bf16[16,32,1024]{2,1,0:T(8,128)(2,1)S(1)}, u32[]{:S(2)}, u32[]{:S(2)}) collective-permute-start(bf16[16,32,1024]{2,1,0:T(8,128)(2,1)S(1)} %pad_maximum_fusion.near_ref), channel_id=1, source_target_pairs={{0,8},{8,0},{1,9},{9,1},{2,10},{10,2},{3,11},{11,3},{4,12},{12,4},... | collective-permute-start | bytes 3145736 | tf_op jit(solution)/shard_map/ppermute | solution.py:1173
  112.9 3.8 collective-permute-start.20
  161.2 20.6 %all-to-all-start.3 = ((bf16[8,2,144,128]{3,2,1,0:T(8,128)(2,1)}), bf16[8,2,144,128]{3,2,1,0:T(8,128)(2,1)S(1)}, u32[]{:S(2)}, u32[]{:S(2)}) async-start(bf16[8,2,144,128]{3,2,1,0:T(8,128)(2,1)} %bitcast.245), calls=%async_computation.3 | async-start | bytes 1179648 | tf_op jit(solution)/shard_map/all_to_all | solution.py:1328
  187.9 2.6 collective-permute-start.22
  187.9 16.0 %collective-permute-start.21 = (bf16[288,1024]{1,0:T(8,128)(2,1)}, bf16[288,1024]{1,0:T(8,128)(2,1)S(1)}, u32[]{:S(2)}, u32[]{:S(2)}) collective-permute-start(bf16[288,1024]{1,0:T(8,128)(2,1)} %copy-done.6), channel_id=1, source_target_pairs={{0,16},{16,0},{1,17},{17,1},{2,18},{18,2},{3,19},{19,3},{4,20},{20... | collective-permute-start | bytes 1769480 | tf_op jit(solution)/shard_map/ppermute | solution.py:1173
  189.2 1.3 collective-permute-start.23
  203.9 5.8 %collective-permute-start.25 = (bf16[288,1024]{1,0:T(8,128)(2,1)S(1)}, bf16[288,1024]{1,0:T(8,128)(2,1)S(1)}, u32[]{:S(2)}, u32[]{:S(2)}) collective-permute-start(bf16[288,1024]{1,0:T(8,128)(2,1)S(1)} %collective-permute-done.21.xa_ref.refs_6_), channel_id=1, source_target_pairs={{0,8},{8,0},{1,9},{9,1},{2,10},{10,2},{3,11},{11,3},{4,12},{12,4},... | collective-permute-start | bytes 1769480 | tf_op jit(solution)/shard_map/ppermute | solution.py:1173
  203.9 4.5 collective-permute-start.26
  208.4 1.3 collective-permute-start.27
  217.4 3.2 collective-permute-start.28
  217.6 19.5 %collective-permute-start.24 = (f32[288,1024]{1,0:T(8,128)S(1)}, f32[288,1024]{1,0:T(8,128)S(1)}, u32[]{:S(2)}, u32[]{:S(2)}) collective-permute-start(f32[288,1024]{1,0:T(8,128)S(1)} %copy-done.51), channel_id=1, source_target_pairs={{0,8},{8,0},{1,9},{9,1},{2,10},{10,2},{3,11},{11,3},{4,12},{12,4},... | collective-permute-start | bytes 3538952 | tf_op jit(solution)/shard_map/ppermute | solution.py:1173
  220.9 16.3 %collective-permute-start.29 = (bf16[288,1024]{1,0:T(8,128)(2,1)S(1)}, bf16[288,1024]{1,0:T(8,128)(2,1)S(1)}, u32[]{:S(2)}, u32[]{:S(2)}) collective-permute-start(bf16[288,1024]{1,0:T(8,128)(2,1)S(1)} %add_convert_fusion.1), channel_id=1, source_target_pairs={{0,16},{16,0},{1,17},{17,1},{2,18},{18,2},{3,19},{19,3},{4,20},{20... | collective-permute-start | bytes 1769480 | tf_op jit(solution)/shard_map/ppermute | solution.py:1173
  221.4 27.6 %collective-permute-start.31 = (bf16[288,1024]{1,0:T(8,128)(2,1)}, bf16[288,1024]{1,0:T(8,128)(2,1)}, u32[]{:S(2)}, u32[]{:S(2)}) collective-permute-start(bf16[288,1024]{1,0:T(8,128)(2,1)} %get-tuple-element.174.refs_0_), channel_id=1, source_target_pairs={{0,16},{16,0},{1,17},{17,1},{2,18},{18,2},{3,19},{19,3},{4,20},{20... | collective-permute-start | bytes 1769480 | tf_op jit(solution)/shard_map/ppermute | solution.py:1173
  244.1 20.1 %all-to-all-start.4 = ((bf16[8,256,128]{2,1,0:T(8,128)(2,1)}), bf16[8,256,128]{2,1,0:T(8,128)(2,1)}, u32[]{:S(2)}, u32[]{:S(2)}) async-start(bf16[8,256,128]{2,1,0:T(8,128)(2,1)} %copy-done.22), calls=%async_computation.4 | async-start | bytes 1048576 | tf_op jit(solution)/shard_map/all_to_all | solution.py:1389
  248.3 156.5 %reduce-scatter.2.cloned.1.call-start = ((), (), s32[]{:S(2)}) async-start(), calls=%async_computation.9 | async-start | bytes 5308416 | tf_op jit(solution)/shard_map/reduce_scatter | solution.py:1406
  248.8 3.7 collective-permute-start.30
  249.0 3.4 collective-permute-start.32
  250.5 5.9 %collective-permute-start.35 = (bf16[288,256]{1,0:T(8,128)(2,1)S(1)}, bf16[288,256]{1,0:T(8,128)(2,1)S(1)}, u32[]{:S(2)}, u32[]{:S(2)}) collective-permute-start(bf16[288,256]{1,0:T(8,128)(2,1)S(1)} %get-tuple-element.306), channel_id=1, source_target_pairs={{0,24},{8,16},{16,8},{24,0},{1,25},{9,17},{17,9},{25,1},{2,26},{10... | collective-permute-start | bytes 442376 | tf_op jit(solution)/shard_map/ppermute | solution.py:1396
  250.9 9.0 %collective-permute-start.34 = (bf16[288,256]{1,0:T(8,128)(2,1)S(1)}, bf16[288,256]{1,0:T(8,128)(2,1)S(1)}, u32[]{:S(2)}, u32[]{:S(2)}) collective-permute-start(bf16[288,256]{1,0:T(8,128)(2,1)S(1)} %get-tuple-element.307), channel_id=1, source_target_pairs={{0,16},{8,24},{16,0},{24,8},{1,17},{9,25},{17,1},{25,9},{2,18},{10... | collective-permute-start | bytes 442376 | tf_op jit(solution)/shard_map/ppermute | solution.py:1396
  252.4 7.5 %collective-permute-start.33 = (bf16[288,256]{1,0:T(8,128)(2,1)S(1)}, bf16[288,256]{1,0:T(8,128)(2,1)S(1)}, u32[]{:S(2)}, u32[]{:S(2)}) collective-permute-start(bf16[288,256]{1,0:T(8,128)(2,1)S(1)} %get-tuple-element.308), channel_id=1, source_target_pairs={{0,8},{8,0},{16,24},{24,16},{1,9},{9,1},{17,25},{25,17},{2,10},{10... | collective-permute-start | bytes 442376 | tf_op jit(solution)/shard_map/ppermute | solution.py:1396
  318.1 34.1 %all-to-all-start.5 = ((bf16[8,256,128]{2,1,0:T(8,128)(2,1)}), bf16[8,256,128]{2,1,0:T(8,128)(2,1)}, u32[]{:S(2)}, u32[]{:S(2)}) async-start(bf16[8,256,128]{2,1,0:T(8,128)(2,1)} %bitcast.260), calls=%async_computation.5 | async-start | bytes 1048576 | tf_op jit(solution)/shard_map/all_to_all | solution.py:1412
  343.7 31.2 %collective-permute-start.36 = (bf16[8,128,512]{2,1,0:T(8,128)(2,1)}, bf16[8,128,512]{2,1,0:T(8,128)(2,1)}, u32[]{:S(2)}, u32[]{:S(2)}) collective-permute-start(bf16[8,128,512]{2,1,0:T(8,128)(2,1)} %get-tuple-element.191), channel_id=1, source_target_pairs={{0,1},{1,0},{2,3},{3,2},{4,5},{5,4},{6,7},{7,6},{8,9},{9,8},{10,11... | collective-permute-start | bytes 3145736 | tf_op jit(solution)/shard_map/ppermute | solution.py:1486
  347.6 4.0 collective-permute-start.42
  378.1 26.6 %collective-permute-start.37 = (bf16[8,128,512]{2,1,0:T(8,128)(2,1)}, bf16[8,128,512]{2,1,0:T(8,128)(2,1)}, u32[]{:S(2)}, u32[]{:S(2)}) collective-permute-start(bf16[8,128,512]{2,1,0:T(8,128)(2,1)} %get-tuple-element.193), channel_id=1, source_target_pairs={{0,1},{1,0},{2,3},{3,2},{4,5},{5,4},{6,7},{7,6},{8,9},{9,8},{10,11... | collective-permute-start | bytes 3145736 | tf_op jit(solution)/shard_map/ppermute | solution.py:1486
  379.6 29.5 %collective-permute-start.38 = (bf16[256,512]{1,0:T(8,128)(2,1)}, bf16[256,512]{1,0:T(8,128)(2,1)}, u32[]{:S(2)}, u32[]{:S(2)}) collective-permute-start(bf16[256,512]{1,0:T(8,128)(2,1)} %bitcast.54), channel_id=1, source_target_pairs={{0,2},{2,0},{4,6},{6,4},{1,3},{3,1},{5,7},{7,5},{8,10},{10,8},{12,... | collective-permute-start | bytes 786440 | tf_op jit(solution)/shard_map/ppermute | solution.py:1499
  381.1 28.0 %collective-permute-start.39 = (bf16[256,512]{1,0:T(8,128)(2,1)}, bf16[256,512]{1,0:T(8,128)(2,1)}, u32[]{:S(2)}, u32[]{:S(2)}) collective-permute-start(bf16[256,512]{1,0:T(8,128)(2,1)} %bitcast.55), channel_id=1, source_target_pairs={{0,4},{2,6},{4,0},{6,2},{1,5},{3,7},{5,1},{7,3},{8,12},{10,14},{12... | collective-permute-start | bytes 786440 | tf_op jit(solution)/shard_map/ppermute | solution.py:1499
  383.5 25.6 %collective-permute-start.40 = (bf16[256,512]{1,0:T(8,128)(2,1)}, bf16[256,512]{1,0:T(8,128)(2,1)}, u32[]{:S(2)}, u32[]{:S(2)}) collective-permute-start(bf16[256,512]{1,0:T(8,128)(2,1)} %bitcast.56), channel_id=1, source_target_pairs={{0,6},{2,4},{4,2},{6,0},{1,7},{3,5},{5,3},{7,1},{8,14},{10,12},{12... | collective-permute-start | bytes 786440 | tf_op jit(solution)/shard_map/ppermute | solution.py:1499
  384.1 16.5 %collective-permute-start.41 = (bf16[704,512]{1,0:T(8,128)(2,1)S(1)}, bf16[704,512]{1,0:T(8,128)(2,1)S(1)}, u32[]{:S(2)}, u32[]{:S(2)}) collective-permute-start(bf16[704,512]{1,0:T(8,128)(2,1)S(1)} %pad_maximum_fusion.2), channel_id=1, source_target_pairs={{0,16},{16,0},{1,17},{17,1},{2,18},{18,2},{3,19},{19,3},{4,20},{20... | collective-permute-start | bytes 2162696 | tf_op jit(solution)/shard_map/ppermute | solution.py:1173
  409.2 21.5 %collective-permute-start.49 = (f32[288,1024]{1,0:T(8,128)S(1)}, f32[288,1024]{1,0:T(8,128)S(1)}, u32[]{:S(2)}, u32[]{:S(2)}) collective-permute-start(f32[288,1024]{1,0:T(8,128)S(1)} %split.48), channel_id=1, source_target_pairs={{0,8},{8,0},{1,9},{9,1},{2,10},{10,2},{3,11},{11,3},{4,12},{12,4},... | collective-permute-start | bytes 3538952 | tf_op jit(solution)/shard_map/ppermute | solution.py:1173
  411.6 7.9 %collective-permute-start.45 = (bf16[72,2,512]{2,1,0:T(2,128)(2,1)S(1)}, bf16[72,2,512]{2,1,0:T(2,128)(2,1)S(1)}, u32[]{:S(2)}, u32[]{:S(2)}) collective-permute-start(bf16[72,2,512]{2,1,0:T(2,128)(2,1)S(1)} %fusion.15), channel_id=1, source_target_pairs={{0,8},{8,0},{1,9},{9,1},{2,10},{10,2},{3,11},{11,3},{4,12},{12,4},... | collective-permute-start | bytes 442376 | tf_op jit(solution)/shard_map/ppermute | solution.py:1173
  415.0 23.1 %collective-permute-start.51 = (bf16[72,128]{1,0:T(8,128)(2,1)}, bf16[72,128]{1,0:T(8,128)(2,1)}, u32[]{:S(2)}, u32[]{:S(2)}) collective-permute-start(bf16[72,128]{1,0:T(8,128)(2,1)} %fusion.17), channel_id=1, source_target_pairs={{0,8},{8,0},{1,9},{9,1},{2,10},{10,2},{3,11},{11,3},{4,12},{12,4},... | collective-permute-start | bytes 55304 | tf_op jit(solution)/shard_map/ppermute | solution.py:1173
  415.3 13.6 %collective-permute-start.43 = (bf16[256,512]{1,0:T(8,128)(2,1)S(1)}, bf16[256,512]{1,0:T(8,128)(2,1)S(1)}, u32[]{:S(2)}, u32[]{:S(2)}) collective-permute-start(bf16[256,512]{1,0:T(8,128)(2,1)S(1)} %bitcast.270), channel_id=1, source_target_pairs={{0,2},{2,0},{4,6},{6,4},{1,3},{3,1},{5,7},{7,5},{8,10},{10,8},{12,... | collective-permute-start | bytes 786440 | tf_op jit(solution)/shard_map/ppermute | solution.py:1499
  415.9 27.9 %collective-permute-start.46 = (bf16[256,512]{1,0:T(8,128)(2,1)}, bf16[256,512]{1,0:T(8,128)(2,1)}, u32[]{:S(2)}, u32[]{:S(2)}) collective-permute-start(bf16[256,512]{1,0:T(8,128)(2,1)} %bitcast.61), channel_id=1, source_target_pairs={{0,4},{2,6},{4,0},{6,2},{1,5},{3,7},{5,1},{7,3},{8,12},{10,14},{12... | collective-permute-start | bytes 786440 | tf_op jit(solution)/shard_map/ppermute | solution.py:1499
  419.6 1.5 collective-permute-start.44
  421.1 25.6 %collective-permute-start.48 = (f32[288,1024]{1,0:T(8,128)}, f32[288,1024]{1,0:T(8,128)}, u32[]{:S(2)}, u32[]{:S(2)}) collective-permute-start(f32[288,1024]{1,0:T(8,128)} %get-tuple-element.285), channel_id=1, source_target_pairs={{0,8},{8,0},{1,9},{9,1},{2,10},{10,2},{3,11},{11,3},{4,12},{12,4},... | collective-permute-start | bytes 3538952 | tf_op jit(solution)/shard_map/ppermute | solution.py:1173
  428.9 17.8 %collective-permute-start.47 = (bf16[256,512]{1,0:T(8,128)(2,1)}, bf16[256,512]{1,0:T(8,128)(2,1)}, u32[]{:S(2)}, u32[]{:S(2)}) collective-permute-start(bf16[256,512]{1,0:T(8,128)(2,1)} %bitcast.62), channel_id=1, source_target_pairs={{0,6},{2,4},{4,2},{6,0},{1,7},{3,5},{5,3},{7,1},{8,14},{10,12},{12... | collective-permute-start | bytes 786440 | tf_op jit(solution)/shard_map/ppermute | solution.py:1499
  431.7 15.1 %collective-permute-start.50 = (bf16[288,1024]{1,0:T(8,128)(2,1)}, bf16[288,1024]{1,0:T(8,128)(2,1)}, u32[]{:S(2)}, u32[]{:S(2)}) collective-permute-start(bf16[288,1024]{1,0:T(8,128)(2,1)} %add_convert_fusion), channel_id=1, source_target_pairs={{0,16},{16,0},{1,17},{17,1},{2,18},{18,2},{3,19},{19,3},{4,20},{20... | collective-permute-start | bytes 1769480 | tf_op jit(solution)/shard_map/ppermute | solution.py:1173
  433.2 23.1 %all-to-all-start.6 = ((bf16[8,96,128]{2,1,0:T(8,128)(2,1)}), bf16[8,96,128]{2,1,0:T(8,128)(2,1)S(1)}, u32[]{:S(2)}, u32[]{:S(2)}) async-start(bf16[8,96,128]{2,1,0:T(8,128)(2,1)} %fusion.14), calls=%async_computation.7 | async-start | bytes 393216 | tf_op jit(solution)/shard_map/all_to_all | solution.py:1463
  438.1 15.5 %collective-permute-start.52 = (bf16[384,128]{1,0:T(8,128)(2,1)S(1)}, bf16[384,128]{1,0:T(8,128)(2,1)S(1)}, u32[]{:S(2)}, u32[]{:S(2)}) collective-permute-start(bf16[384,128]{1,0:T(8,128)(2,1)S(1)} %bitcast.279), channel_id=1, source_target_pairs={{0,0},{1,1},{2,8},{3,9},{4,16},{5,17},{6,24},{7,25},{8,2},{9,3},{1... | collective-permute-start | bytes 294920 | tf_op jit(solution)/shard_map/ppermute | solution.py:1470
  443.8 12.4 %collective-permute-start.53 = (bf16[384,128]{1,0:T(8,128)(2,1)S(1)}, bf16[384,128]{1,0:T(8,128)(2,1)S(1)}, u32[]{:S(2)}, u32[]{:S(2)}) collective-permute-start(bf16[384,128]{1,0:T(8,128)(2,1)S(1)} %bitcast.278), channel_id=1, source_target_pairs={{0,1},{1,0},{2,9},{3,8},{4,17},{5,16},{6,25},{7,24},{8,3},{9,2},{1... | collective-permute-start | bytes 294920 | tf_op jit(solution)/shard_map/ppermute | solution.py:1470
  (53 other events, 428.5 us)
Sparse Core Ops, SparseCore 0:
  10.2 83.3 all-gather.5
  95.7 73.1 all-gather.3
  264.3 105.6 reduce-scatter.1
